TPU v7x, 32 devices: a whole 2x2x4 slice. The times are simulated.
32 devices in a mesh: frm: 8 (over z, core), col: 4 (over y, x).
Axes of the slice: x: 2, y: 2, z: 4, core: 2. Of those that a mesh axis runs over, the one named last changes fastest.
Arguments:
- video: bfloat16 [64, 8, 128, 512], P('frm', None, 'col'), may hold values from -6 to 6
- norm_gain: float32 [512], replicated, may hold values from 0.25 to 1.75
- w_query: bfloat16 [512, 512], replicated, may hold values from -1 to 1
- w_key: bfloat16 [512, 512], replicated, may hold values from -1 to 1
- w_value: bfloat16 [512, 512], replicated, may hold values from -0.25 to 0.25
- w_out: bfloat16 [512, 512], replicated, may hold values from -0.25 to 0.25
- w_time: bfloat16 [3, 512, 512], replicated, may hold values from -0.15625 to 0.15625
- w_depth: float32 [3, 3, 512], replicated, may hold values from -2 to 2
Outputs:
- encoded: bfloat16 [32, 8, 128, 512], P('frm', None, 'col')
All inputs are finite; a program needn't handle non-finite values.
Results may differ from a plain program's by a relative error of at most 0.012.
The roundings to bfloat16 on the way count: a program that leaves them out, or rounds other values in their place, can miss the bound.
Values may be sent and summed in bfloat16 or wider, within the bound.
No kernel may reach another device: no remote copies, remote signals or barrier semaphores. Data moves between devices by JAX's collectives and lax.ppermute only.
A program may use at most 64 MiB of HBM per device.

v0:
```python
import math

import jax
import jax.numpy as jnp
from jax import lax
from jax.sharding import PartitionSpec as P

FRAMES = 64
VIDEOS = 1
FRAMES_OUT = 32


epsilon = 1e-06


def padded_2(block, sides, width):
    for axis, dim in sides:
        count = lax.axis_size(axis)
        forward = [(i, i + 1) for i in range(count - 1)]
        backward = [(target, source) for source, target in forward]
        low = lax.ppermute(
            lax.slice_in_dim(block, block.shape[dim] - width, None, axis=dim), axis, forward
        )
        high = lax.ppermute(lax.slice_in_dim(block, 0, width, axis=dim), axis, backward)
        block = jnp.concatenate([low, block, high], axis=dim)
    return block


def attend_block(block_in, norm_gain, w_query, w_key, w_value, w_out):
    channels = block_in.shape[-1]
    widened = block_in.reshape(-1, channels).astype(jnp.float32)
    normed = (
        widened
        * lax.rsqrt(jnp.mean(widened * widened, axis=-1, keepdims=True) + epsilon)
        * norm_gain
    ).astype(jnp.bfloat16)
    grid_shape = (VIDEOS, FRAMES, -1, channels)
    queries = (
        jnp.dot(normed, w_query, preferred_element_type=jnp.float32)
        .astype(jnp.bfloat16)
        .reshape(grid_shape)
    )
    key_proj = (
        jnp.dot(normed, w_key, preferred_element_type=jnp.float32)
        .astype(jnp.bfloat16)
        .reshape(grid_shape)
    )
    values = (
        jnp.dot(normed, w_value, preferred_element_type=jnp.float32)
        .astype(jnp.bfloat16)
        .reshape(grid_shape)
    )
    scores = jnp.einsum(
        "bqpc,bkpc->bpqk", queries, key_proj, preferred_element_type=jnp.float32
    ) / math.sqrt(channels)
    causal = jnp.arange(FRAMES)[:, None] >= jnp.arange(FRAMES)[None, :]
    scores = jnp.where(causal, scores, -1e30)
    raised = jnp.exp(scores - jnp.max(scores, axis=-1, keepdims=True))
    weights = (raised / jnp.sum(raised, axis=-1, keepdims=True)).astype(jnp.bfloat16)
    attended = jnp.einsum(
        "bpqk,bkpc->bqpc", weights, values, preferred_element_type=jnp.float32
    ).astype(jnp.bfloat16)
    projected = jnp.dot(attended.reshape(-1, channels), w_out, preferred_element_type=jnp.float32)
    return (widened + projected).astype(jnp.bfloat16).reshape(block_in.shape)


def time_conv(prior_frames, even_frames, odd_frames, w_time):
    channels = even_frames.shape[-1]
    summed = jnp.dot(
        prior_frames.reshape(-1, channels), w_time[0], preferred_element_type=jnp.float32
    )
    summed = summed + jnp.dot(
        even_frames.reshape(-1, channels), w_time[1], preferred_element_type=jnp.float32
    )
    summed = summed + jnp.dot(
        odd_frames.reshape(-1, channels), w_time[2], preferred_element_type=jnp.float32
    )
    return jax.nn.silu(summed).astype(jnp.bfloat16).reshape(even_frames.shape)


def local(video, norm_gain, w_query, w_key, w_value, w_out, w_time, w_depth):
    mixed_rows = attend_block(
        lax.all_to_all(video, "frm", split_axis=1, concat_axis=0, tiled=True),
        norm_gain,
        w_query,
        w_key,
        w_value,
        w_out,
    )
    band_rows = mixed_rows.shape[1]
    piece_cols = mixed_rows.shape[2]
    channels = mixed_rows.shape[3]
    grouped = mixed_rows.reshape(VIDEOS, FRAMES, band_rows, piece_cols, channels)
    even_frames = grouped[:, 0::2]
    odd_frames = grouped[:, 1::2]
    prior_frames = jnp.concatenate([grouped[:, :1], odd_frames[:, :-1]], axis=1)
    activated_band = time_conv(prior_frames, even_frames, odd_frames, w_time)
    banded = activated_band.reshape(VIDEOS * FRAMES_OUT, band_rows, piece_cols, channels)
    activated = lax.all_to_all(banded, "frm", split_axis=0, concat_axis=1, tiled=True)
    rimmed = padded_2(activated, (("col", 2),), 1)
    rows = activated.shape[1]
    cols = activated.shape[2]
    padded = jnp.pad(rimmed.astype(jnp.float32), ((0, 0), (1, 1), (0, 0), (0, 0)))
    summed = jnp.zeros(activated.shape, jnp.float32)
    for row_step in range(3):
        for col_step in range(3):
            summed = (
                summed
                + padded[:, row_step : row_step + rows, col_step : col_step + cols]
                * w_depth[row_step, col_step]
            )
    return summed.astype(jnp.bfloat16)


def solution(mesh):
    return jax.shard_map(
        local,
        mesh=mesh,
        in_specs=(P("frm", None, "col", None), P(), P(), P(), P(), P(), P(), P()),
        out_specs=P("frm", None, "col", None),
        check_vma=False,
    )
```

profile of v0, /device:TPU:0, one launch (start us, length us, event | category | flops | bytes accessed | tf_op | source)
XLA Modules:
  0.0 125.1 jit_solution(9855558011978051738)
XLA Ops:
  0.0 0.0 copy-start
  0.0 3.2 %copy.21 = bf16[8,8,32,512]{3,2,0,1:T(8,128)(2,1)} copy(bf16[8,8,32,512]{3,2,1,0:T(8,128)(2,1)} %param.8) | data formatting | bytes 4194304 | tf_op args[0]
  3.2 6.3 %all-to-all-start = ((bf16[8,8,32,512]{3,2,0,1:T(8,128)(2,1)}), bf16[8,8,32,512]{3,2,0,1:T(8,128)(2,1)S(1)}, u32[]{:S(2)}, u32[]{:S(2)}) async-start(bf16[8,8,32,512]{3,2,0,1:T(8,128)(2,1)} %copy.21), calls=%async_computation | async-start | bytes 4194304 | tf_op jit(solution)/shard_map/all_to_all | solution.py:83
  9.6 0.0 copy-start.3
  9.6 49.0 %all-to-all-done = bf16[8,8,32,512]{3,2,0,1:T(8,128)(2,1)S(1)} async-done(((bf16[8,8,32,512]{3,2,0,1:T(8,128)(2,1)}), bf16[8,8,32,512]{3,2,0,1:T(8,128)(2,1)S(1)}, u32[]{:S(2)}, u32[]{:S(2)}) %all-to-all-start) | async-done | bytes 2097184 | tf_op jit(solution)/shard_map/all_to_all | solution.py:83
  58.6 0.5 fusion.1
  59.1 0.1 rsqrt.12
  59.2 0.0 copy-done.3
  59.2 0.5 fusion.3
  59.8 0.0 copy-done
  59.8 0.0 copy-start.4
  59.8 1.3 %convolution_convert_fusion.1 = bf16[2048,512]{1,0:T(8,128)(2,1)S(1)} fusion(bf16[2048,512]{1,0:T(8,128)(2,1)S(1)} %fusion.3, bf16[512,512]{1,0:T(8,128)(2,1)S(1)} %copy-done), kind=kOutput, calls=%fused_computation.15 | convolution fusion | flops 1074790400 | bytes 4718592 | tf_op jit(solution)/shard_map/dot_general | solution.py:39
  61.1 0.0 copy-done.4
  61.1 1.3 %convolution_convert_fusion = bf16[2048,512]{1,0:T(8,128)(2,1)S(1)} fusion(bf16[2048,512]{1,0:T(8,128)(2,1)S(1)} %fusion.3, bf16[512,512]{1,0:T(8,128)(2,1)S(1)} %copy-done.4), kind=kOutput, calls=%fused_computation.14 | convolution fusion | flops 1074790400 | bytes 4718592 | tf_op jit(solution)/shard_map/dot_general | solution.py:44
  62.4 0.0 copy-start.5
  62.4 2.4 %fusion.34 = f32[32,64,64]{1,2,0:T(8,128)S(1)} fusion(bf16[64,32,512]{2,1,0:T(8,128)(2,1)S(1)} %bitcast.86, bf16[64,32,512]{2,1,0:T(8,128)(2,1)S(1)} %bitcast.85, pred[64,64]{0,1:T(8,128)(4,1)S(1)} %iota_compare_fusion), kind=kOutput, calls=%fused_computation.46 | convolution fusion | flops 134479872 | bytes 4722688 | tf_op jit(solution)/shard_map/bqpc,bkpc->bpqk/dot_general | solution.py:53
  64.8 0.0 copy-start.7
  64.8 0.3 fusion.55
  65.1 0.0 copy-done.5
  65.1 2.6 %convolution_convert_fusion.2 = bf16[2048,512]{1,0:T(8,128)(2,1)} fusion(bf16[2048,512]{1,0:T(8,128)(2,1)S(1)} %fusion.3, bf16[512,512]{1,0:T(8,128)(2,1)S(1)} %copy-done.5), kind=kOutput, calls=%fused_computation.16 | convolution fusion | flops 1074790400 | bytes 4718592 | tf_op jit(solution)/shard_map/dot_general | solution.py:49
  67.7 0.0 copy-done.7
  67.7 6.4 %convert_bitcast_fusion = bf16[1,64,32,512]{3,1,2,0:T(8,128)(2,1)} fusion(bf16[64,32,512]{2,1,0:T(8,128)(2,1)} %bitcast.84, f32[32,64]{1,0:T(8,128)S(1)} %fusion.55, f32[32,64,64]{1,2,0:T(8,128)} %copy-done.7), kind=kOutput, calls=%fused_computation.41 | convolution fusion | flops 135661632 | bytes 4726784 | tf_op jit(solution)/shard_map/bpqk,bkpc->bqpc/dot_general | solution.py:60
  74.1 0.0 copy-start.6
  74.1 2.8 %copy.28 = bf16[1,64,32,512]{3,2,1,0:T(8,128)(2,1)S(1)} copy(bf16[1,64,32,512]{3,1,2,0:T(8,128)(2,1)} %convert_bitcast_fusion) | data formatting | bytes 4194304 | tf_op jit(solution)/shard_map/convert_element_type | solution.py:62
  76.9 0.0 copy-done.6
  76.9 1.2 fusion.4
  78.2 0.2 fusion.52
  78.4 0.0 copy-start.1
  78.4 0.1 slice.112
  78.5 0.1 pad_maximum_fusion
  78.6 1.2 copy-done.1
  79.8 0.9 fusion.42
  80.7 0.7 fusion.40
  81.4 1.0 multiply_convert_fusion
  82.4 0.0 copy-start.2
  82.4 29.0 %all_to_all.27 = bf16[32,1,32,512]{3,2,1,0:T(8,128)(2,1)S(1)} all-to-all(bf16[32,1,32,512]{3,2,1,0:T(8,128)(2,1)S(1)} %bitcast.74), channel_id=1, replica_groups=mesh['frm'=8,'col'=4] {'frm'}, dimensions={0} | all-to-all | bytes 2097152 | tf_op jit(solution)/shard_map/all_to_all | solution.py:99
  111.5 0.1 fusion.53
  111.6 3.4 %collective-permute-start = (bf16[4,8,1,512]{3,2,0,1:T(2,128)(2,1)S(1)}, bf16[4,8,1,512]{3,2,0,1:T(2,128)(2,1)S(1)}, u32[]{:S(2)}, u32[]{:S(2)}) collective-permute-start(bf16[4,8,1,512]{3,2,0,1:T(2,128)(2,1)S(1)} %get-tuple-element.7), channel_id=1, source_target_pairs={{0,1},{1,2},{2,3},{4,5},{5,6},{6,7},{8,9},{9,10},{10,11},{12,13},{... | collective-permute-start | bytes 98312 | tf_op jit(solution)/shard_map/ppermute | solution.py:21
  115.0 1.3 %collective-permute-start.1 = (bf16[4,8,1,512]{3,2,0,1:T(2,128)(2,1)S(1)}, bf16[4,8,1,512]{3,2,0,1:T(2,128)(2,1)S(1)}, u32[]{:S(2)}, u32[]{:S(2)}) collective-permute-start(bf16[4,8,1,512]{3,2,0,1:T(2,128)(2,1)S(1)} %get-tuple-element.8), channel_id=1, source_target_pairs={{1,0},{2,1},{3,2},{5,4},{6,5},{7,6},{9,8},{10,9},{11,10},{13,12},{... | collective-permute-start | bytes 98312 | tf_op jit(solution)/shard_map/ppermute | solution.py:24
  116.3 0.0 copy-done.2
  116.3 0.6 collective-permute-done
  116.9 4.3 %collective-permute-done.1 = bf16[4,8,1,512]{3,2,0,1:T(2,128)(2,1)S(1)} collective-permute-done((bf16[4,8,1,512]{3,2,0,1:T(2,128)(2,1)S(1)}, bf16[4,8,1,512]{3,2,0,1:T(2,128)(2,1)S(1)}, u32[]{:S(2)}, u32[]{:S(2)}) %collective-permute-start.1) | collective-permute-done | bytes 32800 | tf_op jit(solution)/shard_map/ppermute | solution.py:24
  121.1 0.5 maximum_convert_fusion
  121.7 2.3 %fusion.14 = bf16[4,8,32,512]{3,2,0,1:T(8,128)(2,1)S(1)} fusion(f32[4,8,34,512]{3,2,0,1:T(8,128)S(1)} %maximum_convert_fusion, f32[512]{0:T(512)S(1)} %bitcast.82, f32[512]{0:T(512)S(1)} %bitcast.83, f32[512]{0:T(512)S(1)} %bitcast.76, f32[512]{0:T(512)S(1)} %bitcast.77, f32[512]{0:T(512)S(1)} %bitcast.78, f32[512]{0:T(512)S(1)} %bitcast.79, ...), kind=kLoop, calls=%fused_computation.26 | loop fusion | flops 9437184 | bytes 9979904 | tf_op jit(solution)/shard_map/convert_element_type | solution.py:112
  124.0 1.0 copy.30
  (5 shorter events, 0.1 us)
Async XLA Ops:
  0.0 59.8 %copy-start = (bf16[512,512]{1,0:T(8,128)(2,1)S(1)}, bf16[512,512]{1,0:T(8,128)(2,1)}, u32[]{:S(2)}) copy-start(bf16[512,512]{1,0:T(8,128)(2,1)} %param.10) | copy-start | bytes 1572868
  3.2 55.4 %all-to-all-start = ((bf16[8,8,32,512]{3,2,0,1:T(8,128)(2,1)}), bf16[8,8,32,512]{3,2,0,1:T(8,128)(2,1)S(1)}, u32[]{:S(2)}, u32[]{:S(2)}) async-start(bf16[8,8,32,512]{3,2,0,1:T(8,128)(2,1)} %copy.21), calls=%async_computation | async-start | bytes 4194304 | tf_op jit(solution)/shard_map/all_to_all | solution.py:83
  9.6 49.6 %copy-start.3 = (f32[512]{0:T(512)S(1)}, f32[512]{0:T(512)}, u32[]{:S(2)}) copy-start(f32[512]{0:T(512)} %param.9) | copy-start | bytes 6148
  59.8 1.3 %copy-start.4 = (bf16[512,512]{1,0:T(8,128)(2,1)S(1)}, bf16[512,512]{1,0:T(8,128)(2,1)}, u32[]{:S(2)}) copy-start(bf16[512,512]{1,0:T(8,128)(2,1)} %param.11) | copy-start | bytes 1572868
  62.4 2.7 %copy-start.5 = (bf16[512,512]{1,0:T(8,128)(2,1)S(1)}, bf16[512,512]{1,0:T(8,128)(2,1)}, u32[]{:S(2)}) copy-start(bf16[512,512]{1,0:T(8,128)(2,1)} %param.12) | copy-start | bytes 1572868
  64.8 2.9 %copy-start.7 = (f32[32,64,64]{1,2,0:T(8,128)}, f32[32,64,64]{1,2,0:T(8,128)S(1)}, u32[]{:S(2)}) copy-start(f32[32,64,64]{1,2,0:T(8,128)S(1)} %fusion.34) | copy-start | bytes 1572868
  74.1 2.8 %copy-start.6 = (bf16[512,512]{1,0:T(8,128)(2,1)S(1)}, bf16[512,512]{1,0:T(8,128)(2,1)}, u32[]{:S(2)}) copy-start(bf16[512,512]{1,0:T(8,128)(2,1)} %param.13) | copy-start | bytes 1572868
  78.4 1.4 %copy-start.1 = (bf16[3,512,512]{2,1,0:T(8,128)(2,1)S(1)}, bf16[3,512,512]{2,1,0:T(8,128)(2,1)}, u32[]{:S(2)}) copy-start(bf16[3,512,512]{2,1,0:T(8,128)(2,1)} %param.14) | copy-start | bytes 4718596
  82.4 33.8 %copy-start.2 = (f32[3,3,512]{2,1,0:T(4,128)S(1)}, f32[3,3,512]{2,1,0:T(4,128)}, u32[]{:S(2)}) copy-start(f32[3,3,512]{2,1,0:T(4,128)} %param.15) | copy-start | bytes 55300
  111.6 5.3 %collective-permute-start = (bf16[4,8,1,512]{3,2,0,1:T(2,128)(2,1)S(1)}, bf16[4,8,1,512]{3,2,0,1:T(2,128)(2,1)S(1)}, u32[]{:S(2)}, u32[]{:S(2)}) collective-permute-start(bf16[4,8,1,512]{3,2,0,1:T(2,128)(2,1)S(1)} %get-tuple-element.7), channel_id=1, source_target_pairs={{0,1},{1,2},{2,3},{4,5},{5,6},{6,7},{8,9},{9,10},{10,11},{12,13},{... | collective-permute-start | bytes 98312 | tf_op jit(solution)/shard_map/ppermute | solution.py:21
  115.0 6.2 %collective-permute-start.1 = (bf16[4,8,1,512]{3,2,0,1:T(2,128)(2,1)S(1)}, bf16[4,8,1,512]{3,2,0,1:T(2,128)(2,1)S(1)}, u32[]{:S(2)}, u32[]{:S(2)}) collective-permute-start(bf16[4,8,1,512]{3,2,0,1:T(2,128)(2,1)S(1)} %get-tuple-element.8), channel_id=1, source_target_pairs={{1,0},{2,1},{3,2},{5,4},{6,5},{7,6},{9,8},{10,9},{11,10},{13,12},{... | collective-permute-start | bytes 98312 | tf_op jit(solution)/shard_map/ppermute | solution.py:24
where the time goes:
time: 125 us
  waiting for transfers between devices  53.9 us (43%)
  blocking collectives  29 us (23%)
  matrix products  17.8 us (14%)
  starting transfers between devices  11 us (9%)
  local copies, waits for them, and re-layouts  8.84 us (7%)
  other arithmetic  4.25 us (3%)
    all_to_all x1, waiting for transfers between devices, local(): lax.all_to_all(video, 'frm', split_axis=1, concat_axis=0, tiled=True)  49 us
    all_to_all x1, blocking collectives, local(): lax.all_to_all(banded, 'frm', split_axis=0, concat_axis=1, tiled=True)  29 us
    dot_general x1, matrix products, attend_block(): jnp.einsum('bpqk,bkpc->bqpc', weights, values, preferred_element_type=jnp...  6.39 us
    all_to_all x1, starting transfers between devices, local(): lax.all_to_all(video, 'frm', split_axis=1, concat_axis=0, tiled=True)  6.33 us
    unnamed x17, local copies, waits for them, and re-layouts  4.48 us
    ppermute x1, waiting for transfers between devices, padded_2(): lax.ppermute(lax.slice_in_dim(block, 0, width, axis=dim), axis, backward)  4.27 us
    ppermute x1, starting transfers between devices, padded_2(): lax.ppermute(lax.slice_in_dim(block, block.shape[dim] - width, None, axis...  3.4 us
    convert_element_type x1, local copies, waits for them, and re-layouts, attend_block(): attended = jnp.einsum('bpqk,bkpc->bqpc', weights, values, preferred_eleme...  2.81 us
  transfers between devices with their start and end apart: 3, of which 3 were waited for; matrix products, arithmetic and copies ran while one was open for 0% of the time, Pallas kernels for 0%

commit v1 on v0

v1 whole, which is shorter than its diff:
```python
import functools
import math

import jax
import jax.numpy as jnp
from jax import lax
from jax.experimental import pallas as pl
from jax.experimental.pallas import tpu as pltpu
from jax.sharding import PartitionSpec as P

epsilon = 1e-06
GROUP = 8
MEMORY = 56 * 1024 * 1024


def attend_group(x, gain, w_query, w_key, w_value, w_out, w_time, frames):
    channels = x.shape[-1]
    rows = frames * GROUP
    x = x.reshape(rows, channels)
    normed = (x * lax.rsqrt(jnp.mean(x * x, axis=-1, keepdims=True) + epsilon) * gain).astype(jnp.bfloat16)

    def project(weight):
        return jnp.dot(normed, weight[...], preferred_element_type=jnp.float32).astype(jnp.bfloat16)

    queries, key_proj, values = project(w_query), project(w_key), project(w_value)
    blocks = 2
    height = rows // blocks
    mixed = []
    for block in range(blocks):
        begin = block * height
        span = begin + height
        scores = lax.dot_general(
            queries[begin:span],
            key_proj[:span],
            (((1,), (1,)), ((), ())),
            preferred_element_type=jnp.float32,
        ) * (1.0 / math.sqrt(channels))
        to_row = lax.broadcasted_iota(jnp.int32, scores.shape, 0) + begin
        from_row = lax.broadcasted_iota(jnp.int32, scores.shape, 1)
        allowed = (from_row <= to_row) & (lax.rem(from_row, GROUP) == lax.rem(to_row, GROUP))
        scores = jnp.where(allowed, scores, -1e30)
        raised = jnp.exp(scores - jnp.max(scores, axis=-1, keepdims=True))
        weights = (raised / jnp.sum(raised, axis=-1, keepdims=True)).astype(jnp.bfloat16)
        attended = jnp.dot(weights, values[:span], preferred_element_type=jnp.float32).astype(jnp.bfloat16)
        projected = jnp.dot(attended, w_out[...], preferred_element_type=jnp.float32)
        mixed.append(x[begin:span] + projected)
    mixed = jnp.concatenate(mixed, axis=0).reshape(frames // 2, 2, GROUP, channels)
    even = mixed[:, 0]
    odd = mixed[:, 1]
    prior = jnp.concatenate([even[:1], odd[:-1]], axis=0)
    summed = jnp.zeros((rows // 2, channels), jnp.float32)
    for tap, part in enumerate((prior, even, odd)):
        part = part.reshape(rows // 2, channels).astype(jnp.bfloat16)
        summed = summed + jnp.dot(part, w_time[tap], preferred_element_type=jnp.float32)
    return (summed / (1.0 + jnp.exp(-summed))).reshape(frames // 2, GROUP, channels)


def attend_kernel(count, *refs):
    pieces = refs[:count]
    gain, w_query, w_key, w_value, w_out, w_time = refs[count : count + 6]
    results = refs[count + 6 : 2 * count + 6]
    band, done, sems = refs[2 * count + 6 :]
    me = lax.axis_index("frm")
    span = pieces[0].shape[0]
    made = results[0].shape[0]
    copies = [
        pltpu.make_async_copy(pieces[k], band.at[pl.ds((me ^ k) * span, span)], sems.at[k]) for k in range(count)
    ]
    for copy in copies:
        copy.start()
    for copy in copies:
        copy.wait()
    frames, cols, channels = band.shape
    x = band[...].astype(jnp.float32)
    parts = [
        attend_group(x[:, g : g + GROUP], gain[...], w_query, w_key, w_value, w_out, w_time, frames)
        for g in range(0, cols, GROUP)
    ]
    done[...] = jnp.concatenate(parts, axis=1).astype(jnp.bfloat16)
    copies = [
        pltpu.make_async_copy(done.at[pl.ds((me ^ k) * made, made)], results[k], sems.at[k]) for k in range(count)
    ]
    for copy in copies:
        copy.start()
    for copy in copies:
        copy.wait()


def attend(pieces, norm_gain, w_query, w_key, w_value, w_out, w_time):
    count = len(pieces)
    span, cols, channels = pieces[0].shape
    frames = span * count
    made = span // 2
    anywhere = pl.BlockSpec(memory_space=pl.ANY)
    inside = pl.BlockSpec(memory_space=pltpu.VMEM)
    rows = frames * cols
    return pl.pallas_call(
        functools.partial(attend_kernel, count),
        out_shape=[jax.ShapeDtypeStruct((made, cols, channels), jnp.bfloat16)] * count,
        in_specs=[anywhere] * count + [inside] * 6,
        out_specs=[anywhere] * count,
        scratch_shapes=[
            pltpu.VMEM((frames, cols, channels), jnp.bfloat16),
            pltpu.VMEM((frames // 2, cols, channels), jnp.bfloat16),
            pltpu.SemaphoreType.DMA((count,)),
        ],
        compiler_params=pltpu.CompilerParams(vmem_limit_bytes=MEMORY),
        cost_estimate=pl.CostEstimate(
            flops=rows * channels * (channels * 11 + GROUP * frames * 4),
            bytes_accessed=rows * channels * 3 + channels * channels * 14,
            transcendentals=rows * frames,
        ),
        name="attend",
    )(*pieces, norm_gain[None], w_query, w_key, w_value, w_out, w_time)


def filter_kernel(count, *refs):
    outer = refs[:count]
    inner = refs[count : 2 * count]
    left, right, w_depth, out, outer_rows, inner_rows, sems = refs[2 * count :]
    me = lax.axis_index("frm")
    copies = []
    for k in range(count):
        copies.append(pltpu.make_async_copy(outer[k], outer_rows.at[me ^ k], sems.at[2 * k]))
        copies.append(pltpu.make_async_copy(inner[k], inner_rows.at[me ^ k], sems.at[2 * k + 1]))
    for copy in copies:
        copy.start()
    for copy in copies:
        copy.wait()
    frames, height, cols, channels = out.shape
    edge = outer_rows.shape[2] // 2
    lanes = 128

    def one_part(step, carry):
        part = pl.ds(pl.multiple_of(step * lanes, lanes), lanes)
        for frame in range(frames):
            taps = [[w_depth[a, b, part] for b in range(3)] for a in range(3)]

            def filtered(row):
                rim = outer_rows[row, frame, :, part].astype(jnp.float32)
                core = inner_rows[row, frame, :, part].astype(jnp.float32)
                mid = jnp.concatenate([rim[:edge], core, rim[edge:]], axis=0)
                place = lax.broadcasted_iota(jnp.int32, mid.shape, 0)
                low = left[me ^ row, frame, part].astype(jnp.float32)[None]
                high = right[me ^ row, frame, part].astype(jnp.float32)[None]
                before = jnp.where(place == 0, low, pltpu.roll(mid, 1, 0))
                after = jnp.where(place == cols - 1, high, pltpu.roll(mid, cols - 1, 0))
                return [
                    before * taps[a][0][None] + mid * taps[a][1][None] + after * taps[a][2][None] for a in range(3)
                ]

            above = None
            here = filtered(0)
            for row in range(height):
                below = filtered(row + 1) if row + 1 < height else None
                total = here[1]
                if above is not None:
                    total = total + above[0]
                if below is not None:
                    total = total + below[2]
                out[frame, row, :, part] = total.astype(jnp.bfloat16)
                above, here = here, below
        return carry

    lax.fori_loop(0, channels // lanes, one_part, 0)


def depth_filter(outer, inner, left, right, w_depth):
    count = len(outer)
    frames, width, channels = outer[0].shape
    cols = 2 * width
    anywhere = pl.BlockSpec(memory_space=pl.ANY)
    inside = pl.BlockSpec(memory_space=pltpu.VMEM)
    size = frames * count * cols * channels
    return pl.pallas_call(
        functools.partial(filter_kernel, count),
        out_shape=jax.ShapeDtypeStruct((frames, count, cols, channels), jnp.bfloat16),
        in_specs=[anywhere] * (2 * count) + [inside] * 3,
        out_specs=inside,
        scratch_shapes=[
            pltpu.VMEM((count, frames, width, channels), jnp.bfloat16),
            pltpu.VMEM((count, frames, width, channels), jnp.bfloat16),
            pltpu.SemaphoreType.DMA((2 * count,)),
        ],
        compiler_params=pltpu.CompilerParams(vmem_limit_bytes=MEMORY),
        cost_estimate=pl.CostEstimate(flops=18 * size, bytes_accessed=4 * size, transcendentals=0),
        name="depth_filter",
    )(*outer, *inner, left, right, w_depth)


def swap(block, k, count):
    if k == 0:
        return block
    return lax.ppermute(block, "frm", [(i, i ^ k) for i in range(count)])


def local(video, norm_gain, w_query, w_key, w_value, w_out, w_time, w_depth):
    count = lax.axis_size("frm")
    me = lax.axis_index("frm")
    frames, height, cols, channels = video.shape
    assert height == count and count & (count - 1) == 0
    edge = cols // 4
    weights = (norm_gain, w_query, w_key, w_value, w_out, w_time)
    order = sorted(range(count), key=lambda k: -k)

    def forward(cut):
        return {k: swap(cut(lax.dynamic_index_in_dim(video, me ^ k, 1, keepdims=False)), k, count) for k in order}

    def back(pieces):
        results = attend([pieces[k] for k in range(count)], *weights)
        return {k: swap(results[k], k, count) for k in order}

    outer = forward(lambda row: jnp.concatenate([row[:, :edge], row[:, cols - edge :]], axis=1))
    inner = forward(lambda row: row[:, edge : cols - edge])
    outer = back(outer)
    outer = [outer[k] for k in range(count)]
    line = lax.axis_size("col")
    upward = [(i, i + 1) for i in range(line - 1)]
    left = lax.ppermute(jnp.stack([piece[:, 2 * edge - 1] for piece in outer]), "col", upward)
    right = lax.ppermute(jnp.stack([piece[:, 0] for piece in outer]), "col", [(b, a) for a, b in upward])
    inner = back(inner)
    inner = [inner[k] for k in range(count)]
    return depth_filter(outer, inner, left, right, w_depth)


def solution(mesh):
    return jax.shard_map(
        local,
        mesh=mesh,
        in_specs=(P("frm", None, "col", None), P(), P(), P(), P(), P(), P(), P()),
        out_specs=P("frm", None, "col", None),
        check_vma=False,
    )
```

time: 125 us -> 113 us (0.904); the launches traced: 125 us -> 112 us
  starting transfers between devices: 11 us -> 61.1 us
  waiting for transfers between devices: 53.9 us -> 11.3 us
  blocking collectives: 29 us -> 0 us
  Pallas kernels: 0 us -> 24.9 us
  matrix products: 17.8 us -> 0 us
  local copies, waits for them, and re-layouts: 8.84 us -> 13.1 us
  other arithmetic: 4.25 us -> 0.74 us
    ppermute x2 -> x30, starting transfers between devices: 4.69 us -> 61.1 us  [the longest x28 55.3 us: swap(): return lax.ppermute(block, 'frm', [(i, i ^ k) for i in range(count)])]
    all_to_all x1 -> x0, waiting for transfers between devices: 49 us -> none  [local(): lax.all_to_all(video, 'frm', split_axis=1, concat_axis=0, tiled=True)]
    all_to_all x1 -> x0, blocking collectives: 29 us -> none  [local(): lax.all_to_all(banded, 'frm', split_axis=0, concat_axis=1, tiled=True)]
    pallas_call x0 -> x3, Pallas kernels: none -> 24.9 us  [the longest x2 20.2 us: attend(): pl.pallas_call(functools.partial(attend_kernel, count), out_shape=[jax.Sh...]
    dot_general x9 -> x0, matrix products: 17.8 us -> none  [the longest x1 6.39 us: attend_block(): jnp.einsum('bpqk,bkpc->bqpc', weights, values, preferred_element_type=jnp...]
    ppermute x2 -> x30, waiting for transfers between devices: 4.82 us -> 11.3 us  [the longest x28 11.3 us: swap(): return lax.ppermute(block, 'frm', [(i, i ^ k) for i in range(count)])]
    all_to_all x1 -> x0, starting transfers between devices: 6.33 us -> none  [local(): lax.all_to_all(video, 'frm', split_axis=1, concat_axis=0, tiled=True)]
    pallas_call x0 -> x8, local copies, waits for them, and re-layouts: none -> 5.47 us  [attend(): pl.pallas_call(functools.partial(attend_kernel, count), out_shape=[jax.Sh...]
  transfers between devices with their start and end apart: 3 -> 30, of which waited for: 3 -> 6; matrix products, arithmetic and copies ran while one was open for 0% -> 10% of each run, Pallas kernels for 0% -> 18%
where the time goes in v1:
time: 113 us; the launch traced here: 112 us
  starting transfers between devices  61.1 us (54%)
  Pallas kernels  24.9 us (22%)
  local copies, waits for them, and re-layouts  13.1 us (12%)
  waiting for transfers between devices  11.3 us (10%)
    ppermute x28, starting transfers between devices, swap(): return lax.ppermute(block, 'frm', [(i, i ^ k) for i in range(count)])  55.3 us
    pallas_call x2, Pallas kernels, attend(): pl.pallas_call(functools.partial(attend_kernel, count), out_shape=[jax.Sh...  20.2 us
    ppermute x28, waiting for transfers between devices, swap(): return lax.ppermute(block, 'frm', [(i, i ^ k) for i in range(count)])  11.3 us
    pallas_call x8, local copies, waits for them, and re-layouts, attend(): pl.pallas_call(functools.partial(attend_kernel, count), out_shape=[jax.Sh...  5.47 us
    pallas_call x1, Pallas kernels, depth_filter(): pl.pallas_call(functools.partial(filter_kernel, count), out_shape=jax.Sha...  4.7 us
    ppermute x1, starting transfers between devices, local(): lax.ppermute(jnp.stack([piece[:, 2 * edge - 1] for piece in outer]), 'col...  4.55 us
    ppermute x7, local copies, waits for them, and re-layouts, swap(): return lax.ppermute(block, 'frm', [(i, i ^ k) for i in range(count)])  4.43 us
  transfers between devices with their start and end apart: 30, of which 6 were waited for; matrix products, arithmetic and copies ran while one was open for 10% of the time, Pallas kernels for 18%

profile of v1, /device:TPU:0, one launch (start us, length us, event | category | flops | bytes accessed | tf_op | source)
XLA Modules:
  0.0 111.8 jit_solution(3848240603756036352)
XLA Ops:
  0.0 1.6 %dynamic-slice_bitcast_fusion = (bf16[8,32,512]{2,1,0:T(8,128)(2,1)S(1)}, bf16[8,32,512]{2,1,0:T(8,128)(2,1)S(1)}, bf16[8,32,512]{2,1,0:T(8,128)(2,1)S(1)}, bf16...) fusion(bf16[8,8,32,512]{3,2,1,0:T(8,128)(2,1)} %param.8, ...), kind=kLoop, calls=%fused_computation | loop fusion | bytes 4194336 | tf_op jit(solution)/shard_map/jit(dynamic_index_in_dim)/squeeze | solution.py:207
  1.7 0.5 collective-permute-start
  2.3 2.7 %collective-permute-start.1 = (bf16[8,16,512]{2,1,0:T(8,128)(2,1)S(1)}, bf16[8,16,512]{2,1,0:T(8,128)(2,1)S(1)}, u32[]{:S(2)}, u32[]{:S(2)}) collective-permute-start(bf16[8,16,512]{2,1,0:T(8,128)(2,1)S(1)} %pad_maximum_fusion.2), channel_id=1, source_target_pairs={{0,8},{4,12},{8,0},{12,4},{16,24},{20,28},{24,16},{28,20},{1,9},{5... | collective-permute-start | bytes 393224 | tf_op jit(solution)/shard_map/ppermute | solution.py:194
  4.9 0.2 collective-permute-start.2
  5.2 2.8 %collective-permute-start.3 = (bf16[8,16,512]{2,1,0:T(8,128)(2,1)S(1)}, bf16[8,16,512]{2,1,0:T(8,128)(2,1)S(1)}, u32[]{:S(2)}, u32[]{:S(2)}) collective-permute-start(bf16[8,16,512]{2,1,0:T(8,128)(2,1)S(1)} %pad_maximum_fusion.4), channel_id=1, source_target_pairs={{0,16},{4,20},{8,24},{12,28},{16,0},{20,4},{24,8},{28,12},{1,17},{... | collective-permute-start | bytes 393224 | tf_op jit(solution)/shard_map/ppermute | solution.py:194
  8.0 0.1 collective-permute-start.4
  8.1 3.6 %collective-permute-start.5 = (bf16[8,16,512]{2,1,0:T(8,128)(2,1)S(1)}, bf16[8,16,512]{2,1,0:T(8,128)(2,1)S(1)}, u32[]{:S(2)}, u32[]{:S(2)}) collective-permute-start(bf16[8,16,512]{2,1,0:T(8,128)(2,1)S(1)} %pad_maximum_fusion.6), channel_id=1, source_target_pairs={{0,24},{4,28},{8,16},{12,20},{16,8},{20,12},{24,0},{28,4},{1,25},{... | collective-permute-start | bytes 393224 | tf_op jit(solution)/shard_map/ppermute | solution.py:194
  11.7 2.1 %collective-permute-done.1.refs_2_ = bf16[8,16,512]{2,1,0:T(8,128)(2,1)S(1)} collective-permute-done((bf16[8,16,512]{2,1,0:T(8,128)(2,1)S(1)}, bf16[8,16,512]{2,1,0:T(8,128)(2,1)S(1)}, u32[]{:S(2)}, u32[]{:S(2)}) %collective-permute-start.1) | collective-permute-done | bytes 131104 | tf_op jit(solution)/shard_map/ppermute | solution.py:194
  13.9 0.0 collective-permute-start.6
  14.0 0.7 slice.176.refs_0_
  14.7 0.7 pad_maximum_fusion.refs_0_
  15.3 1.4 %collective-permute-done.2.refs_3_ = bf16[8,16,512]{2,1,0:T(8,128)(2,1)S(1)} collective-permute-done((bf16[8,16,512]{2,1,0:T(8,128)(2,1)S(1)}, bf16[8,16,512]{2,1,0:T(8,128)(2,1)S(1)}, u32[]{:S(2)}, u32[]{:S(2)}) %collective-permute-start.2) | collective-permute-done | bytes 131104 | tf_op jit(solution)/shard_map/ppermute | solution.py:194
  16.7 0.8 collective-permute-start.14
  17.5 0.0 collective-permute-done.3.refs_4_
  17.5 7.0 %collective-permute-start.15 = (bf16[8,16,512]{2,1,0:T(8,128)(2,1)S(1)}, bf16[8,16,512]{2,1,0:T(8,128)(2,1)S(1)}, u32[]{:S(2)}, u32[]{:S(2)}) collective-permute-start(bf16[8,16,512]{2,1,0:T(8,128)(2,1)S(1)} %slice.178), channel_id=1, source_target_pairs={{0,8},{4,12},{8,0},{12,4},{16,24},{20,28},{24,16},{28,20},{1,9},{5... | collective-permute-start | bytes 393224 | tf_op jit(solution)/shard_map/ppermute | solution.py:194
  24.6 1.4 %collective-permute-done.4.refs_5_ = bf16[8,16,512]{2,1,0:T(8,128)(2,1)S(1)} collective-permute-done((bf16[8,16,512]{2,1,0:T(8,128)(2,1)S(1)}, bf16[8,16,512]{2,1,0:T(8,128)(2,1)S(1)}, u32[]{:S(2)}, u32[]{:S(2)}) %collective-permute-start.4) | collective-permute-done | bytes 131104 | tf_op jit(solution)/shard_map/ppermute | solution.py:194
  25.9 0.0 collective-permute-start.16
  26.0 6.2 %collective-permute-start.17 = (bf16[8,16,512]{2,1,0:T(8,128)(2,1)S(1)}, bf16[8,16,512]{2,1,0:T(8,128)(2,1)S(1)}, u32[]{:S(2)}, u32[]{:S(2)}) collective-permute-start(bf16[8,16,512]{2,1,0:T(8,128)(2,1)S(1)} %slice.180), channel_id=1, source_target_pairs={{0,16},{4,20},{8,24},{12,28},{16,0},{20,4},{24,8},{28,12},{1,17},{... | collective-permute-start | bytes 393224 | tf_op jit(solution)/shard_map/ppermute | solution.py:194
  32.2 0.0 collective-permute-done.6.refs_7_
  32.2 3.6 %collective-permute-start.18 = (bf16[8,16,512]{2,1,0:T(8,128)(2,1)S(1)}, bf16[8,16,512]{2,1,0:T(8,128)(2,1)S(1)}, u32[]{:S(2)}, u32[]{:S(2)}) collective-permute-start(bf16[8,16,512]{2,1,0:T(8,128)(2,1)S(1)} %slice.181), channel_id=1, source_target_pairs={{0,20},{4,16},{8,28},{12,24},{16,4},{20,0},{24,12},{28,8},{1,21},{... | collective-permute-start | bytes 393224 | tf_op jit(solution)/shard_map/ppermute | solution.py:194
  35.9 10.1 %attend.2 = (bf16[4,16,512]{2,1,0:T(8,128)(2,1)}, bf16[4,16,512]{2,1,0:T(8,128)(2,1)}, bf16[4,16,512]{2,1,0:T(8,128)(2,1)}, bf16[4,16,512]{2,1,0:T(8,128)(2,1)},...) custom-call(bf16[8,16,512]{2,1,0:T(8,128)(2,1)} %pad_maximum_fusion., ...), custom_call_target="tpu_custom_call" | custom-call | flops 4026531840 | bytes 5242880 | tf_op jit(solution)/shard_map/attend/pallas_call | solution.py:97
  46.0 0.9 copy.9
  46.9 0.9 copy.12
  47.8 0.9 copy.13
  48.7 0.9 copy.14
  49.6 0.9 copy.15
  50.5 0.9 copy.16
  51.4 0.0 collective-permute-done.14.refs_1_
  51.4 0.0 copy-start.12
  51.4 0.1 collective-permute-start.19
  51.5 0.0 collective-permute-done.15.refs_2_
  51.5 1.2 %collective-permute-start.20 = (bf16[8,16,512]{2,1,0:T(8,128)(2,1)S(1)}, bf16[8,16,512]{2,1,0:T(8,128)(2,1)S(1)}, u32[]{:S(2)}, u32[]{:S(2)}) collective-permute-start(bf16[8,16,512]{2,1,0:T(8,128)(2,1)S(1)} %slice.183), channel_id=1, source_target_pairs={{0,28},{4,24},{8,20},{12,16},{16,12},{20,8},{24,4},{28,0},{1,29},{... | collective-permute-start | bytes 393224 | tf_op jit(solution)/shard_map/ppermute | solution.py:194
  52.7 2.5 %collective-permute-start.13 = (bf16[4,16,512]{2,0,1:T(4,128)(2,1)S(1)}, bf16[4,16,512]{2,0,1:T(4,128)(2,1)S(1)}, u32[]{:S(2)}, u32[]{:S(2)}) collective-permute-start(bf16[4,16,512]{2,0,1:T(4,128)(2,1)S(1)} %copy.15), channel_id=1, source_target_pairs={{0,28},{4,24},{8,20},{12,16},{16,12},{20,8},{24,4},{28,0},{1,29},{... | collective-permute-start | bytes 196616 | tf_op jit(solution)/shard_map/ppermute | solution.py:194
  55.3 3.7 %collective-permute-start.12 = (bf16[4,16,512]{2,0,1:T(4,128)(2,1)S(1)}, bf16[4,16,512]{2,0,1:T(4,128)(2,1)S(1)}, u32[]{:S(2)}, u32[]{:S(2)}) collective-permute-start(bf16[4,16,512]{2,0,1:T(4,128)(2,1)S(1)} %copy.14), channel_id=1, source_target_pairs={{0,24},{4,28},{8,16},{12,20},{16,8},{20,12},{24,0},{28,4},{1,25},{... | collective-permute-start | bytes 196616 | tf_op jit(solution)/shard_map/ppermute | solution.py:194
  59.0 0.7 collective-permute-done.19.refs_6_
  59.7 5.4 %collective-permute-start.10 = (bf16[4,16,512]{2,0,1:T(4,128)(2,1)S(1)}, bf16[4,16,512]{2,0,1:T(4,128)(2,1)S(1)}, u32[]{:S(2)}, u32[]{:S(2)}) collective-permute-start(bf16[4,16,512]{2,0,1:T(4,128)(2,1)S(1)} %copy.12), channel_id=1, source_target_pairs={{0,16},{4,20},{8,24},{12,28},{16,0},{20,4},{24,8},{28,12},{1,17},{... | collective-permute-start | bytes 196616 | tf_op jit(solution)/shard_map/ppermute | solution.py:194
  65.1 1.9 %collective-permute-start.7 = (bf16[4,16,512]{2,0,1:T(4,128)(2,1)S(1)}, bf16[4,16,512]{2,0,1:T(4,128)(2,1)S(1)}, u32[]{:S(2)}, u32[]{:S(2)}) collective-permute-start(bf16[4,16,512]{2,0,1:T(4,128)(2,1)S(1)} %copy.9), channel_id=1, source_target_pairs={{0,4},{4,0},{8,12},{12,8},{16,20},{20,16},{24,28},{28,24},{1,5},{5... | collective-permute-start | bytes 196616 | tf_op jit(solution)/shard_map/ppermute | solution.py:194
  67.0 10.1 %attend.3 = (bf16[4,16,512]{2,1,0:T(8,128)(2,1)}, bf16[4,16,512]{2,1,0:T(8,128)(2,1)}, bf16[4,16,512]{2,1,0:T(8,128)(2,1)}, bf16[4,16,512]{2,1,0:T(8,128)(2,1)},...) custom-call(bf16[8,16,512]{2,1,0:T(8,128)(2,1)} %slice.176.refs_0_, ...), custom_call_target="tpu_custom_call" | custom-call | flops 4026531840 | bytes 5242880 | tf_op jit(solution)/shard_map/attend/pallas_call | solution.py:97
  77.1 0.1 copy.10
  77.2 0.1 copy.11
  77.3 3.6 %collective-permute-start.8 = (bf16[4,16,512]{2,0,1:T(4,128)(2,1)S(1)}, bf16[4,16,512]{2,0,1:T(4,128)(2,1)S(1)}, u32[]{:S(2)}, u32[]{:S(2)}) collective-permute-start(bf16[4,16,512]{2,0,1:T(4,128)(2,1)S(1)} %copy.10), channel_id=1, source_target_pairs={{0,8},{4,12},{8,0},{12,4},{16,24},{20,28},{24,16},{28,20},{1,9},{5... | collective-permute-start | bytes 196616 | tf_op jit(solution)/shard_map/ppermute | solution.py:194
  80.8 2.2 %collective-permute-done.8 = bf16[4,16,512]{2,0,1:T(4,128)(2,1)S(1)} collective-permute-done((bf16[4,16,512]{2,0,1:T(4,128)(2,1)S(1)}, bf16[4,16,512]{2,0,1:T(4,128)(2,1)S(1)}, u32[]{:S(2)}, u32[]{:S(2)}) %collective-permute-start.8) | collective-permute-done | bytes 65568 | tf_op jit(solution)/shard_map/ppermute | solution.py:194
  83.1 0.4 collective-permute-start.9
  83.5 3.5 %collective-permute-done.9 = bf16[4,16,512]{2,0,1:T(4,128)(2,1)S(1)} collective-permute-done((bf16[4,16,512]{2,0,1:T(4,128)(2,1)S(1)}, bf16[4,16,512]{2,0,1:T(4,128)(2,1)S(1)}, u32[]{:S(2)}, u32[]{:S(2)}) %collective-permute-start.9) | collective-permute-done | bytes 65568 | tf_op jit(solution)/shard_map/ppermute | solution.py:194
  86.9 0.3 collective-permute-start.21
  87.3 1.6 %collective-permute-start.22 = (bf16[4,16,512]{2,1,0:T(8,128)(2,1)}, bf16[4,16,512]{2,1,0:T(8,128)(2,1)S(1)}, u32[]{:S(2)}, u32[]{:S(2)}) collective-permute-start(bf16[4,16,512]{2,1,0:T(8,128)(2,1)} %get-tuple-element.31), channel_id=1, source_target_pairs={{0,8},{4,12},{8,0},{12,4},{16,24},{20,28},{24,16},{28,20},{1,9},{5... | collective-permute-start | bytes 196616 | tf_op jit(solution)/shard_map/ppermute | solution.py:194
  88.9 0.2 collective-permute-start.23
  89.1 3.6 %collective-permute-start.24 = (bf16[4,16,512]{2,1,0:T(8,128)(2,1)}, bf16[4,16,512]{2,1,0:T(8,128)(2,1)S(1)}, u32[]{:S(2)}, u32[]{:S(2)}) collective-permute-start(bf16[4,16,512]{2,1,0:T(8,128)(2,1)} %get-tuple-element.33), channel_id=1, source_target_pairs={{0,16},{4,20},{8,24},{12,28},{16,0},{20,4},{24,8},{28,12},{1,17},{... | collective-permute-start | bytes 196616 | tf_op jit(solution)/shard_map/ppermute | solution.py:194
  92.7 0.1 collective-permute-start.25
  92.8 2.5 %collective-permute-start.26 = (bf16[4,16,512]{2,1,0:T(8,128)(2,1)}, bf16[4,16,512]{2,1,0:T(8,128)(2,1)S(1)}, u32[]{:S(2)}, u32[]{:S(2)}) collective-permute-start(bf16[4,16,512]{2,1,0:T(8,128)(2,1)} %get-tuple-element.35), channel_id=1, source_target_pairs={{0,24},{4,28},{8,16},{12,20},{16,8},{20,12},{24,0},{28,4},{1,25},{... | collective-permute-start | bytes 196616 | tf_op jit(solution)/shard_map/ppermute | solution.py:194
  95.2 0.8 collective-permute-start.27
  96.1 1.3 %collective-permute-start.29 = (bf16[8,4,512]{2,1,0:T(4,128)(2,1)S(1)}, bf16[8,4,512]{2,1,0:T(4,128)(2,1)S(1)}, u32[]{:S(2)}, u32[]{:S(2)}) collective-permute-start(bf16[8,4,512]{2,1,0:T(4,128)(2,1)S(1)} %get-tuple-element.61), channel_id=1, source_target_pairs={{1,0},{2,1},{3,2},{5,4},{6,5},{7,6},{9,8},{10,9},{11,10},{13,12},{... | collective-permute-start | bytes 98312 | tf_op jit(solution)/shard_map/ppermute | solution.py:220
  97.4 4.5 %collective-permute-start.28 = (bf16[8,4,512]{2,1,0:T(4,128)(2,1)S(1)}, bf16[8,4,512]{2,1,0:T(4,128)(2,1)S(1)}, u32[]{:S(2)}, u32[]{:S(2)}) collective-permute-start(bf16[8,4,512]{2,1,0:T(4,128)(2,1)S(1)} %get-tuple-element.62), channel_id=1, source_target_pairs={{0,1},{1,2},{2,3},{4,5},{5,6},{6,7},{8,9},{9,10},{10,11},{12,13},{... | collective-permute-start | bytes 98312 | tf_op jit(solution)/shard_map/ppermute | solution.py:219
  101.9 0.6 copy.24.refs_7_
  102.6 0.6 copy.23.refs_6_
  103.2 0.6 copy.22.refs_5_
  103.8 0.6 copy.21.refs_4_
  104.5 0.6 copy.20.refs_3_
  105.1 0.6 copy.19.refs_2_
  105.7 0.6 copy.18.refs_1_
  106.5 0.5 copy-done.4
  107.0 0.0 copy-done.5
  107.0 0.0 copy-done.6
  107.1 4.7 %depth_filter.1 = bf16[4,8,32,512]{3,2,1,0:T(8,128)(2,1)} custom-call(bf16[4,16,512]{2,1,0:T(8,128)(2,1)} %get-tuple-element.21.refs_0_, bf16[4,16,512]{2,1,0:T(8,128)(2,1)} %copy.18.refs_1_, bf16[4,16,512]{2,1,0:T(8,128)(2,1)} %copy.19.refs_2_, bf16[4,16,512]{2,1,0:T(8,128)(2,1)} %copy.20.refs_3_, bf16[4,16,512]{2,1,0:T(8,128)(2,1)} %copy.21.refs_4_, ...), custom_call_target="tpu_custom_call" | custom-call | flops 9437184 | bytes 2097152 | tf_op jit(solution)/shard_map/depth_filter/pallas_call | solution.py:175
  (93 shorter events, 0.5 us)
Async XLA Ops:
  1.7 6.4 %collective-permute-start = (bf16[8,16,512]{2,1,0:T(8,128)(2,1)S(1)}, bf16[8,16,512]{2,1,0:T(8,128)(2,1)S(1)}, u32[]{:S(2)}, u32[]{:S(2)}) collective-permute-start(bf16[8,16,512]{2,1,0:T(8,128)(2,1)S(1)} %pad_maximum_fusion.1), channel_id=1, source_target_pairs={{0,4},{4,0},{8,12},{12,8},{16,20},{20,16},{24,28},{28,24},{1,5},{5... | collective-permute-start | bytes 393224 | tf_op jit(solution)/shard_map/ppermute | solution.py:194
  2.3 11.6 %collective-permute-start.1 = (bf16[8,16,512]{2,1,0:T(8,128)(2,1)S(1)}, bf16[8,16,512]{2,1,0:T(8,128)(2,1)S(1)}, u32[]{:S(2)}, u32[]{:S(2)}) collective-permute-start(bf16[8,16,512]{2,1,0:T(8,128)(2,1)S(1)} %pad_maximum_fusion.2), channel_id=1, source_target_pairs={{0,8},{4,12},{8,0},{12,4},{16,24},{20,28},{24,16},{28,20},{1,9},{5... | collective-permute-start | bytes 393224 | tf_op jit(solution)/shard_map/ppermute | solution.py:194
  4.9 11.8 %collective-permute-start.2 = (bf16[8,16,512]{2,1,0:T(8,128)(2,1)S(1)}, bf16[8,16,512]{2,1,0:T(8,128)(2,1)S(1)}, u32[]{:S(2)}, u32[]{:S(2)}) collective-permute-start(bf16[8,16,512]{2,1,0:T(8,128)(2,1)S(1)} %pad_maximum_fusion.3), channel_id=1, source_target_pairs={{0,12},{4,8},{8,4},{12,0},{16,28},{20,24},{24,20},{28,16},{1,13},{... | collective-permute-start | bytes 393224 | tf_op jit(solution)/shard_map/ppermute | solution.py:194
  5.2 12.4 %collective-permute-start.3 = (bf16[8,16,512]{2,1,0:T(8,128)(2,1)S(1)}, bf16[8,16,512]{2,1,0:T(8,128)(2,1)S(1)}, u32[]{:S(2)}, u32[]{:S(2)}) collective-permute-start(bf16[8,16,512]{2,1,0:T(8,128)(2,1)S(1)} %pad_maximum_fusion.4), channel_id=1, source_target_pairs={{0,16},{4,20},{8,24},{12,28},{16,0},{20,4},{24,8},{28,12},{1,17},{... | collective-permute-start | bytes 393224 | tf_op jit(solution)/shard_map/ppermute | solution.py:194
  8.0 18.0 %collective-permute-start.4 = (bf16[8,16,512]{2,1,0:T(8,128)(2,1)S(1)}, bf16[8,16,512]{2,1,0:T(8,128)(2,1)S(1)}, u32[]{:S(2)}, u32[]{:S(2)}) collective-permute-start(bf16[8,16,512]{2,1,0:T(8,128)(2,1)S(1)} %pad_maximum_fusion.5), channel_id=1, source_target_pairs={{0,20},{4,16},{8,28},{12,24},{16,4},{20,0},{24,12},{28,8},{1,21},{... | collective-permute-start | bytes 393224 | tf_op jit(solution)/shard_map/ppermute | solution.py:194
  8.1 27.8 %copy-start.11 = (bf16[8,16,512]{2,1,0:T(8,128)(2,1)}, bf16[8,16,512]{2,1,0:T(8,128)(2,1)S(1)}, u32[]{:S(2)}) copy-start(bf16[8,16,512]{2,1,0:T(8,128)(2,1)S(1)} %collective-permute-done.refs_1_) | copy-start | bytes 393220
  8.1 17.9 %collective-permute-start.5 = (bf16[8,16,512]{2,1,0:T(8,128)(2,1)S(1)}, bf16[8,16,512]{2,1,0:T(8,128)(2,1)S(1)}, u32[]{:S(2)}, u32[]{:S(2)}) collective-permute-start(bf16[8,16,512]{2,1,0:T(8,128)(2,1)S(1)} %pad_maximum_fusion.6), channel_id=1, source_target_pairs={{0,24},{4,28},{8,16},{12,20},{16,8},{20,12},{24,0},{28,4},{1,25},{... | collective-permute-start | bytes 393224 | tf_op jit(solution)/shard_map/ppermute | solution.py:194
  13.9 22.0 %copy-start.13 = (bf16[8,16,512]{2,1,0:T(8,128)(2,1)}, bf16[8,16,512]{2,1,0:T(8,128)(2,1)S(1)}, u32[]{:S(2)}) copy-start(bf16[8,16,512]{2,1,0:T(8,128)(2,1)S(1)} %collective-permute-done.1.refs_2_) | copy-start | bytes 393220
  13.9 18.4 %collective-permute-start.6 = (bf16[8,16,512]{2,1,0:T(8,128)(2,1)S(1)}, bf16[8,16,512]{2,1,0:T(8,128)(2,1)S(1)}, u32[]{:S(2)}, u32[]{:S(2)}) collective-permute-start(bf16[8,16,512]{2,1,0:T(8,128)(2,1)S(1)} %pad_maximum_fusion.7), channel_id=1, source_target_pairs={{0,28},{4,24},{8,20},{12,16},{16,12},{20,8},{24,4},{28,0},{1,29},{... | collective-permute-start | bytes 393224 | tf_op jit(solution)/shard_map/ppermute | solution.py:194
  16.7 19.2 %copy-start.15 = (bf16[8,16,512]{2,1,0:T(8,128)(2,1)}, bf16[8,16,512]{2,1,0:T(8,128)(2,1)S(1)}, u32[]{:S(2)}) copy-start(bf16[8,16,512]{2,1,0:T(8,128)(2,1)S(1)} %collective-permute-done.2.refs_3_) | copy-start | bytes 393220
  16.7 34.7 %collective-permute-start.14 = (bf16[8,16,512]{2,1,0:T(8,128)(2,1)S(1)}, bf16[8,16,512]{2,1,0:T(8,128)(2,1)S(1)}, u32[]{:S(2)}, u32[]{:S(2)}) collective-permute-start(bf16[8,16,512]{2,1,0:T(8,128)(2,1)S(1)} %slice.177), channel_id=1, source_target_pairs={{0,4},{4,0},{8,12},{12,8},{16,20},{20,16},{24,28},{28,24},{1,5},{5... | collective-permute-start | bytes 393224 | tf_op jit(solution)/shard_map/ppermute | solution.py:194
  17.5 18.4 %copy-start.17 = (bf16[8,16,512]{2,1,0:T(8,128)(2,1)}, bf16[8,16,512]{2,1,0:T(8,128)(2,1)S(1)}, u32[]{:S(2)}) copy-start(bf16[8,16,512]{2,1,0:T(8,128)(2,1)S(1)} %collective-permute-done.3.refs_4_) | copy-start | bytes 393220
  17.5 34.0 %collective-permute-start.15 = (bf16[8,16,512]{2,1,0:T(8,128)(2,1)S(1)}, bf16[8,16,512]{2,1,0:T(8,128)(2,1)S(1)}, u32[]{:S(2)}, u32[]{:S(2)}) collective-permute-start(bf16[8,16,512]{2,1,0:T(8,128)(2,1)S(1)} %slice.178), channel_id=1, source_target_pairs={{0,8},{4,12},{8,0},{12,4},{16,24},{20,28},{24,16},{28,20},{1,9},{5... | collective-permute-start | bytes 393224 | tf_op jit(solution)/shard_map/ppermute | solution.py:194
  25.9 9.9 %copy-start.19 = (bf16[8,16,512]{2,1,0:T(8,128)(2,1)}, bf16[8,16,512]{2,1,0:T(8,128)(2,1)S(1)}, u32[]{:S(2)}) copy-start(bf16[8,16,512]{2,1,0:T(8,128)(2,1)S(1)} %collective-permute-done.4.refs_5_) | copy-start | bytes 393220
  25.9 26.8 %collective-permute-start.16 = (bf16[8,16,512]{2,1,0:T(8,128)(2,1)S(1)}, bf16[8,16,512]{2,1,0:T(8,128)(2,1)S(1)}, u32[]{:S(2)}, u32[]{:S(2)}) collective-permute-start(bf16[8,16,512]{2,1,0:T(8,128)(2,1)S(1)} %slice.179), channel_id=1, source_target_pairs={{0,12},{4,8},{8,4},{12,0},{16,28},{20,24},{24,20},{28,16},{1,13},{... | collective-permute-start | bytes 393224 | tf_op jit(solution)/shard_map/ppermute | solution.py:194
  26.0 9.9 %copy-start.21 = (bf16[8,16,512]{2,1,0:T(8,128)(2,1)}, bf16[8,16,512]{2,1,0:T(8,128)(2,1)S(1)}, u32[]{:S(2)}) copy-start(bf16[8,16,512]{2,1,0:T(8,128)(2,1)S(1)} %collective-permute-done.5.refs_6_) | copy-start | bytes 393220
  26.0 29.3 %collective-permute-start.17 = (bf16[8,16,512]{2,1,0:T(8,128)(2,1)S(1)}, bf16[8,16,512]{2,1,0:T(8,128)(2,1)S(1)}, u32[]{:S(2)}, u32[]{:S(2)}) collective-permute-start(bf16[8,16,512]{2,1,0:T(8,128)(2,1)S(1)} %slice.180), channel_id=1, source_target_pairs={{0,16},{4,20},{8,24},{12,28},{16,0},{20,4},{24,8},{28,12},{1,17},{... | collective-permute-start | bytes 393224 | tf_op jit(solution)/shard_map/ppermute | solution.py:194
  32.2 3.7 %copy-start.22 = (bf16[8,16,512]{2,1,0:T(8,128)(2,1)}, bf16[8,16,512]{2,1,0:T(8,128)(2,1)S(1)}, u32[]{:S(2)}) copy-start(bf16[8,16,512]{2,1,0:T(8,128)(2,1)S(1)} %collective-permute-done.6.refs_7_) | copy-start | bytes 393220
  32.2 26.8 %collective-permute-start.18 = (bf16[8,16,512]{2,1,0:T(8,128)(2,1)S(1)}, bf16[8,16,512]{2,1,0:T(8,128)(2,1)S(1)}, u32[]{:S(2)}, u32[]{:S(2)}) collective-permute-start(bf16[8,16,512]{2,1,0:T(8,128)(2,1)S(1)} %slice.181), channel_id=1, source_target_pairs={{0,20},{4,16},{8,28},{12,24},{16,4},{20,0},{24,12},{28,8},{1,21},{... | collective-permute-start | bytes 393224 | tf_op jit(solution)/shard_map/ppermute | solution.py:194
  51.4 15.5 %copy-start.12 = (bf16[8,16,512]{2,1,0:T(8,128)(2,1)}, bf16[8,16,512]{2,1,0:T(8,128)(2,1)S(1)}, u32[]{:S(2)}) copy-start(bf16[8,16,512]{2,1,0:T(8,128)(2,1)S(1)} %collective-permute-done.14.refs_1_) | copy-start | bytes 393220
  51.4 8.3 %collective-permute-start.19 = (bf16[8,16,512]{2,1,0:T(8,128)(2,1)S(1)}, bf16[8,16,512]{2,1,0:T(8,128)(2,1)S(1)}, u32[]{:S(2)}, u32[]{:S(2)}) collective-permute-start(bf16[8,16,512]{2,1,0:T(8,128)(2,1)S(1)} %slice.182), channel_id=1, source_target_pairs={{0,24},{4,28},{8,16},{12,20},{16,8},{20,12},{24,0},{28,4},{1,25},{... | collective-permute-start | bytes 393224 | tf_op jit(solution)/shard_map/ppermute | solution.py:194
  51.5 15.4 %copy-start.14 = (bf16[8,16,512]{2,1,0:T(8,128)(2,1)}, bf16[8,16,512]{2,1,0:T(8,128)(2,1)S(1)}, u32[]{:S(2)}) copy-start(bf16[8,16,512]{2,1,0:T(8,128)(2,1)S(1)} %collective-permute-done.15.refs_2_) | copy-start | bytes 393220
  51.5 13.5 %collective-permute-start.20 = (bf16[8,16,512]{2,1,0:T(8,128)(2,1)S(1)}, bf16[8,16,512]{2,1,0:T(8,128)(2,1)S(1)}, u32[]{:S(2)}, u32[]{:S(2)}) collective-permute-start(bf16[8,16,512]{2,1,0:T(8,128)(2,1)S(1)} %slice.183), channel_id=1, source_target_pairs={{0,28},{4,24},{8,20},{12,16},{16,12},{20,8},{24,4},{28,0},{1,29},{... | collective-permute-start | bytes 393224 | tf_op jit(solution)/shard_map/ppermute | solution.py:194
  52.7 24.4 %copy-start.8 = (bf16[4,16,512]{2,1,0:T(8,128)(2,1)S(1)}, bf16[4,16,512]{2,1,0:T(8,128)(2,1)}, u32[]{:S(2)}) copy-start(bf16[4,16,512]{2,1,0:T(8,128)(2,1)} %get-tuple-element.23) | copy-start | bytes 196612
  52.7 24.5 %copy-start.7 = (bf16[4,16,512]{2,1,0:T(8,128)(2,1)S(1)}, bf16[4,16,512]{2,1,0:T(8,128)(2,1)}, u32[]{:S(2)}) copy-start(bf16[4,16,512]{2,1,0:T(8,128)(2,1)} %get-tuple-element.24) | copy-start | bytes 196612
  52.7 14.2 %copy-start.16 = (bf16[8,16,512]{2,1,0:T(8,128)(2,1)}, bf16[8,16,512]{2,1,0:T(8,128)(2,1)S(1)}, u32[]{:S(2)}) copy-start(bf16[8,16,512]{2,1,0:T(8,128)(2,1)S(1)} %collective-permute-done.16.refs_3_) | copy-start | bytes 393220
  52.7 39.9 %collective-permute-start.13 = (bf16[4,16,512]{2,0,1:T(4,128)(2,1)S(1)}, bf16[4,16,512]{2,0,1:T(4,128)(2,1)S(1)}, u32[]{:S(2)}, u32[]{:S(2)}) collective-permute-start(bf16[4,16,512]{2,0,1:T(4,128)(2,1)S(1)} %copy.15), channel_id=1, source_target_pairs={{0,28},{4,24},{8,20},{12,16},{16,12},{20,8},{24,4},{28,0},{1,29},{... | collective-permute-start | bytes 196616 | tf_op jit(solution)/shard_map/ppermute | solution.py:194
  55.3 11.7 %copy-start.18 = (bf16[8,16,512]{2,1,0:T(8,128)(2,1)}, bf16[8,16,512]{2,1,0:T(8,128)(2,1)S(1)}, u32[]{:S(2)}) copy-start(bf16[8,16,512]{2,1,0:T(8,128)(2,1)S(1)} %collective-permute-done.17.refs_4_) | copy-start | bytes 393220
  55.3 33.8 %collective-permute-start.12 = (bf16[4,16,512]{2,0,1:T(4,128)(2,1)S(1)}, bf16[4,16,512]{2,0,1:T(4,128)(2,1)S(1)}, u32[]{:S(2)}, u32[]{:S(2)}) collective-permute-start(bf16[4,16,512]{2,0,1:T(4,128)(2,1)S(1)} %copy.14), channel_id=1, source_target_pairs={{0,24},{4,28},{8,16},{12,20},{16,8},{20,12},{24,0},{28,4},{1,25},{... | collective-permute-start | bytes 196616 | tf_op jit(solution)/shard_map/ppermute | solution.py:194
  59.0 8.0 %copy-start.20 = (bf16[8,16,512]{2,1,0:T(8,128)(2,1)}, bf16[8,16,512]{2,1,0:T(8,128)(2,1)S(1)}, u32[]{:S(2)}) copy-start(bf16[8,16,512]{2,1,0:T(8,128)(2,1)S(1)} %collective-permute-done.18.refs_5_) | copy-start | bytes 393220
  59.0 29.9 %collective-permute-start.11 = (bf16[4,16,512]{2,0,1:T(4,128)(2,1)S(1)}, bf16[4,16,512]{2,0,1:T(4,128)(2,1)S(1)}, u32[]{:S(2)}, u32[]{:S(2)}) collective-permute-start(bf16[4,16,512]{2,0,1:T(4,128)(2,1)S(1)} %copy.13), channel_id=1, source_target_pairs={{0,20},{4,16},{8,28},{12,24},{16,4},{20,0},{24,12},{28,8},{1,21},{... | collective-permute-start | bytes 196616 | tf_op jit(solution)/shard_map/ppermute | solution.py:194
  59.7 7.3 %copy-start.23 = (bf16[8,16,512]{2,1,0:T(8,128)(2,1)}, bf16[8,16,512]{2,1,0:T(8,128)(2,1)S(1)}, u32[]{:S(2)}) copy-start(bf16[8,16,512]{2,1,0:T(8,128)(2,1)S(1)} %collective-permute-done.19.refs_6_) | copy-start | bytes 393220
  59.7 27.6 %collective-permute-start.10 = (bf16[4,16,512]{2,0,1:T(4,128)(2,1)S(1)}, bf16[4,16,512]{2,0,1:T(4,128)(2,1)S(1)}, u32[]{:S(2)}, u32[]{:S(2)}) collective-permute-start(bf16[4,16,512]{2,0,1:T(4,128)(2,1)S(1)} %copy.12), channel_id=1, source_target_pairs={{0,16},{4,20},{8,24},{12,28},{16,0},{20,4},{24,8},{28,12},{1,17},{... | collective-permute-start | bytes 196616 | tf_op jit(solution)/shard_map/ppermute | solution.py:194
  65.1 1.9 %copy-start.24 = (bf16[8,16,512]{2,1,0:T(8,128)(2,1)}, bf16[8,16,512]{2,1,0:T(8,128)(2,1)S(1)}, u32[]{:S(2)}) copy-start(bf16[8,16,512]{2,1,0:T(8,128)(2,1)S(1)} %collective-permute-done.20.refs_7_) | copy-start | bytes 393220
  65.1 12.2 %collective-permute-start.7 = (bf16[4,16,512]{2,0,1:T(4,128)(2,1)S(1)}, bf16[4,16,512]{2,0,1:T(4,128)(2,1)S(1)}, u32[]{:S(2)}, u32[]{:S(2)}) collective-permute-start(bf16[4,16,512]{2,0,1:T(4,128)(2,1)S(1)} %copy.9), channel_id=1, source_target_pairs={{0,4},{4,0},{8,12},{12,8},{16,20},{20,16},{24,28},{28,24},{1,5},{5... | collective-permute-start | bytes 196616 | tf_op jit(solution)/shard_map/ppermute | solution.py:194
  77.3 5.8 %collective-permute-start.8 = (bf16[4,16,512]{2,0,1:T(4,128)(2,1)S(1)}, bf16[4,16,512]{2,0,1:T(4,128)(2,1)S(1)}, u32[]{:S(2)}, u32[]{:S(2)}) collective-permute-start(bf16[4,16,512]{2,0,1:T(4,128)(2,1)S(1)} %copy.10), channel_id=1, source_target_pairs={{0,8},{4,12},{8,0},{12,4},{16,24},{20,28},{24,16},{28,20},{1,9},{5... | collective-permute-start | bytes 196616 | tf_op jit(solution)/shard_map/ppermute | solution.py:194
  83.1 3.9 %collective-permute-start.9 = (bf16[4,16,512]{2,0,1:T(4,128)(2,1)S(1)}, bf16[4,16,512]{2,0,1:T(4,128)(2,1)S(1)}, u32[]{:S(2)}, u32[]{:S(2)}) collective-permute-start(bf16[4,16,512]{2,0,1:T(4,128)(2,1)S(1)} %copy.11), channel_id=1, source_target_pairs={{0,12},{4,8},{8,4},{12,0},{16,28},{20,24},{24,20},{28,16},{1,13},{... | collective-permute-start | bytes 196616 | tf_op jit(solution)/shard_map/ppermute | solution.py:194
  86.9 5.8 %collective-permute-start.21 = (bf16[4,16,512]{2,1,0:T(8,128)(2,1)}, bf16[4,16,512]{2,1,0:T(8,128)(2,1)S(1)}, u32[]{:S(2)}, u32[]{:S(2)}) collective-permute-start(bf16[4,16,512]{2,1,0:T(8,128)(2,1)} %get-tuple-element.30), channel_id=1, source_target_pairs={{0,4},{4,0},{8,12},{12,8},{16,20},{20,16},{24,28},{28,24},{1,5},{5... | collective-permute-start | bytes 196616 | tf_op jit(solution)/shard_map/ppermute | solution.py:194
  87.3 7.9 %collective-permute-start.22 = (bf16[4,16,512]{2,1,0:T(8,128)(2,1)}, bf16[4,16,512]{2,1,0:T(8,128)(2,1)S(1)}, u32[]{:S(2)}, u32[]{:S(2)}) collective-permute-start(bf16[4,16,512]{2,1,0:T(8,128)(2,1)} %get-tuple-element.31), channel_id=1, source_target_pairs={{0,8},{4,12},{8,0},{12,4},{16,24},{20,28},{24,16},{28,20},{1,9},{5... | collective-permute-start | bytes 196616 | tf_op jit(solution)/shard_map/ppermute | solution.py:194
  88.9 7.2 %collective-permute-start.23 = (bf16[4,16,512]{2,1,0:T(8,128)(2,1)}, bf16[4,16,512]{2,1,0:T(8,128)(2,1)S(1)}, u32[]{:S(2)}, u32[]{:S(2)}) collective-permute-start(bf16[4,16,512]{2,1,0:T(8,128)(2,1)} %get-tuple-element.32), channel_id=1, source_target_pairs={{0,12},{4,8},{8,4},{12,0},{16,28},{20,24},{24,20},{28,16},{1,13},{... | collective-permute-start | bytes 196616 | tf_op jit(solution)/shard_map/ppermute | solution.py:194
  89.1 8.3 %collective-permute-start.24 = (bf16[4,16,512]{2,1,0:T(8,128)(2,1)}, bf16[4,16,512]{2,1,0:T(8,128)(2,1)S(1)}, u32[]{:S(2)}, u32[]{:S(2)}) collective-permute-start(bf16[4,16,512]{2,1,0:T(8,128)(2,1)} %get-tuple-element.33), channel_id=1, source_target_pairs={{0,16},{4,20},{8,24},{12,28},{16,0},{20,4},{24,8},{28,12},{1,17},{... | collective-permute-start | bytes 196616 | tf_op jit(solution)/shard_map/ppermute | solution.py:194
  92.7 13.7 %collective-permute-start.25 = (bf16[4,16,512]{2,1,0:T(8,128)(2,1)}, bf16[4,16,512]{2,1,0:T(8,128)(2,1)S(1)}, u32[]{:S(2)}, u32[]{:S(2)}) collective-permute-start(bf16[4,16,512]{2,1,0:T(8,128)(2,1)} %get-tuple-element.34), channel_id=1, source_target_pairs={{0,20},{4,16},{8,28},{12,24},{16,4},{20,0},{24,12},{28,8},{1,21},{... | collective-permute-start | bytes 196616 | tf_op jit(solution)/shard_map/ppermute | solution.py:194
  92.8 13.7 %copy-start = (bf16[4,16,512]{2,1,0:T(8,128)(2,1)}, bf16[4,16,512]{2,1,0:T(8,128)(2,1)S(1)}, u32[]{:S(2)}) copy-start(bf16[4,16,512]{2,1,0:T(8,128)(2,1)S(1)} %collective-permute-done.21.refs_9_) | copy-start | bytes 196612
  92.8 13.6 %collective-permute-start.26 = (bf16[4,16,512]{2,1,0:T(8,128)(2,1)}, bf16[4,16,512]{2,1,0:T(8,128)(2,1)S(1)}, u32[]{:S(2)}, u32[]{:S(2)}) collective-permute-start(bf16[4,16,512]{2,1,0:T(8,128)(2,1)} %get-tuple-element.35), channel_id=1, source_target_pairs={{0,24},{4,28},{8,16},{12,20},{16,8},{20,12},{24,0},{28,4},{1,25},{... | collective-permute-start | bytes 196616 | tf_op jit(solution)/shard_map/ppermute | solution.py:194
  95.2 11.2 %copy-start.1 = (bf16[4,16,512]{2,1,0:T(8,128)(2,1)}, bf16[4,16,512]{2,1,0:T(8,128)(2,1)S(1)}, u32[]{:S(2)}) copy-start(bf16[4,16,512]{2,1,0:T(8,128)(2,1)S(1)} %collective-permute-done.22.refs_10_) | copy-start | bytes 196612
  95.2 11.2 %collective-permute-start.27 = (bf16[4,16,512]{2,1,0:T(8,128)(2,1)}, bf16[4,16,512]{2,1,0:T(8,128)(2,1)S(1)}, u32[]{:S(2)}, u32[]{:S(2)}) collective-permute-start(bf16[4,16,512]{2,1,0:T(8,128)(2,1)} %get-tuple-element.36), channel_id=1, source_target_pairs={{0,28},{4,24},{8,20},{12,16},{16,12},{20,8},{24,4},{28,0},{1,29},{... | collective-permute-start | bytes 196616 | tf_op jit(solution)/shard_map/ppermute | solution.py:194
  96.0 10.4 %copy-start.2 = (bf16[4,16,512]{2,1,0:T(8,128)(2,1)}, bf16[4,16,512]{2,1,0:T(8,128)(2,1)S(1)}, u32[]{:S(2)}) copy-start(bf16[4,16,512]{2,1,0:T(8,128)(2,1)S(1)} %collective-permute-done.23.refs_11_) | copy-start | bytes 196612
  96.1 10.4 %collective-permute-start.29 = (bf16[8,4,512]{2,1,0:T(4,128)(2,1)S(1)}, bf16[8,4,512]{2,1,0:T(4,128)(2,1)S(1)}, u32[]{:S(2)}, u32[]{:S(2)}) collective-permute-start(bf16[8,4,512]{2,1,0:T(4,128)(2,1)S(1)} %get-tuple-element.61), channel_id=1, source_target_pairs={{1,0},{2,1},{3,2},{5,4},{6,5},{7,6},{9,8},{10,9},{11,10},{13,12},{... | collective-permute-start | bytes 98312 | tf_op jit(solution)/shard_map/ppermute | solution.py:220
  97.4 9.1 %copy-start.3 = (bf16[4,16,512]{2,1,0:T(8,128)(2,1)}, bf16[4,16,512]{2,1,0:T(8,128)(2,1)S(1)}, u32[]{:S(2)}) copy-start(bf16[4,16,512]{2,1,0:T(8,128)(2,1)S(1)} %collective-permute-done.24.refs_12_) | copy-start | bytes 196612
  97.4 9.1 %collective-permute-start.28 = (bf16[8,4,512]{2,1,0:T(4,128)(2,1)S(1)}, bf16[8,4,512]{2,1,0:T(4,128)(2,1)S(1)}, u32[]{:S(2)}, u32[]{:S(2)}) collective-permute-start(bf16[8,4,512]{2,1,0:T(4,128)(2,1)S(1)} %get-tuple-element.62), channel_id=1, source_target_pairs={{0,1},{1,2},{2,3},{4,5},{5,6},{6,7},{8,9},{9,10},{10,11},{12,13},{... | collective-permute-start | bytes 98312 | tf_op jit(solution)/shard_map/ppermute | solution.py:219
  106.4 0.6 copy-start.4
  106.4 0.6 copy-start.5
  106.4 0.7 copy-start.6
  106.4 0.6 copy-start.9
  106.4 0.6 copy-start.10

commit v2 on v1

v2 whole, which is shorter than its diff:
```python
import functools
import math

import jax
import jax.numpy as jnp
from jax import lax
from jax.experimental import pallas as pl
from jax.experimental.pallas import tpu as pltpu
from jax.sharding import PartitionSpec as P

epsilon = 1e-06
GROUP = 8
BLOCKS = 2
MIB = 1024 * 1024
ANYWHERE = pl.BlockSpec(memory_space=pl.ANY)
INSIDE = pl.BlockSpec(memory_space=pltpu.VMEM)


def place():
    me = lax.axis_index("frm")
    return me // 2, me % 2


def gather_kernel(pairs_of, n_in, *refs):
    *arrays, sems = refs
    pairs = pairs_of(arrays[:n_in], arrays[n_in:])
    copies = [pltpu.make_async_copy(source, target, sems.at[i]) for i, (source, target) in enumerate(pairs)]
    for copy in copies:
        copy.start()
    for copy in copies:
        copy.wait()


def gather(pairs_of, n_pairs, arrays, shapes, name):
    size = sum(math.prod(shape) for shape in shapes)
    return pl.pallas_call(
        functools.partial(gather_kernel, pairs_of, len(arrays)),
        out_shape=[jax.ShapeDtypeStruct(shape, jnp.bfloat16) for shape in shapes],
        in_specs=[ANYWHERE] * len(arrays),
        out_specs=[INSIDE] * len(shapes),
        scratch_shapes=[pltpu.SemaphoreType.DMA((n_pairs,))],
        compiler_params=pltpu.CompilerParams(vmem_limit_bytes=4 * MIB),
        cost_estimate=pl.CostEstimate(flops=0, bytes_accessed=4 * size, transcendentals=0),
        name=name,
    )(*arrays)


def cut_kernel(order, rim, video, *refs):
    *results, held, sems = refs
    if not rim:
        results = results[:-1] + [results[-1].at[k] for k in range(len(results) - 1)]
    row_of = order(lax.axis_index("frm"))
    edge = held.shape[2] // 4
    copies = [pltpu.make_async_copy(video.at[:, row], held.at[i], sems.at[i]) for i, row in enumerate(row_of)]
    for copy in copies:
        copy.start()
    for i, (copy, result) in enumerate(zip(copies, results)):
        copy.wait()
        row = held[i].astype(jnp.float32)
        if rim:
            row = jnp.concatenate([row[:, :edge], row[:, 3 * edge :]], axis=1)
        else:
            row = row[:, edge : 3 * edge]
        result[...] = row.astype(jnp.bfloat16)


def cut(order, rim, video, name):
    span, height, cols, channels = video.shape
    shape = (span, cols // 2, channels)
    shapes = [shape] * height if rim else [shape] * (height // 2) + [(height // 2, *shape)]
    return pl.pallas_call(
        functools.partial(cut_kernel, order, rim),
        out_shape=[jax.ShapeDtypeStruct(shape, jnp.bfloat16) for shape in shapes],
        in_specs=[ANYWHERE],
        out_specs=[INSIDE] * len(shapes),
        scratch_shapes=[
            pltpu.VMEM((height, span, cols, channels), jnp.bfloat16),
            pltpu.SemaphoreType.DMA((height,)),
        ],
        compiler_params=pltpu.CompilerParams(vmem_limit_bytes=10 * MIB),
        cost_estimate=pl.CostEstimate(flops=0, bytes_accessed=3 * video.size, transcendentals=0),
        name=name,
    )(video)


def stacked(x):
    return jnp.stack([x[:, g : g + GROUP] for g in range(0, x.shape[1], GROUP)])


def attend_frames(x, gain, bias, weights, ready):
    w_query, w_key, w_value, w_out, w_time = weights
    groups, frames, _, channels = x.shape
    rows = frames * GROUP
    x = x.reshape(groups * rows, channels)
    normed = (x * lax.rsqrt(jnp.mean(x * x, axis=-1, keepdims=True) + epsilon) * gain).astype(jnp.bfloat16)

    def project(index):
        ready(index)
        return jnp.dot(normed, weights[index][...], preferred_element_type=jnp.float32).astype(jnp.bfloat16)

    queries, key_proj, values = project(0), project(1), project(2)
    height = rows // BLOCKS
    attended = []
    for group in range(groups):
        first = group * rows
        for block in range(BLOCKS):
            begin = block * height
            span = begin + height
            scores = lax.dot_general(
                queries[first + begin : first + span],
                key_proj[first : first + span],
                (((1,), (1,)), ((), ())),
                preferred_element_type=jnp.float32,
            )
            scores = scores * (1.0 / math.sqrt(channels)) + bias[begin:span, :span]
            raised = jnp.exp(scores - jnp.max(scores, axis=-1, keepdims=True))
            shares = (raised * (1.0 / jnp.sum(raised, axis=-1, keepdims=True))).astype(jnp.bfloat16)
            attended.append(
                jnp.dot(shares, values[first : first + span], preferred_element_type=jnp.float32).astype(jnp.bfloat16)
            )
    ready(3)
    mixed = x + jnp.dot(jnp.concatenate(attended, axis=0), w_out[...], preferred_element_type=jnp.float32)
    mixed = mixed.reshape(groups, frames // 2, 2, GROUP, channels)
    even = mixed[:, :, 0]
    odd = mixed[:, :, 1]
    prior = jnp.concatenate([even[:, :1], odd[:, :-1]], axis=1)
    ready(4)
    summed = None
    for tap, part in enumerate((prior, even, odd)):
        part = part.reshape(groups * rows // 2, channels).astype(jnp.bfloat16)
        term = jnp.dot(part, w_time[tap], preferred_element_type=jnp.float32)
        summed = term if summed is None else summed + term
    return (summed / (1.0 + jnp.exp(-summed))).reshape(groups, frames // 2, GROUP, channels)


def attend_kernel(inward, n_in, chips, with_tail, *refs):
    pieces = refs[:n_in]
    gain = refs[n_in]
    sources = refs[n_in + 1 : n_in + 6]
    rest = refs[n_in + 6 :]
    if with_tail:
        tail, out, band, bias, *held, sems, weight_sems, tail_sem = rest
    else:
        results = rest[:chips]
        low, high, band, out, bias, *held, sems, weight_sems = rest[chips:]
    fetches = [pltpu.make_async_copy(s, h, weight_sems.at[i]) for i, (s, h) in enumerate(zip(sources, held))]
    waited = set()

    def ready(index):
        if index not in waited:
            waited.add(index)
            fetches[index].wait()

    copies = [
        pltpu.make_async_copy(piece, band.at[pl.ds(first, piece.shape[0])], sems.at[i])
        for i, (piece, first) in enumerate(inward(pieces))
    ]
    for copy in copies + fetches:
        copy.start()
    count, block, _ = out.shape
    frames, cols, channels = band.shape
    body = frames * cols // (2 * count)
    if with_tail:
        tail_copy = pltpu.make_async_copy(tail, out.at[:, pl.ds(body, block - body)], tail_sem)
        tail_copy.start()
    to_row = lax.broadcasted_iota(jnp.int32, bias.shape, 0)
    from_row = lax.broadcasted_iota(jnp.int32, bias.shape, 1)
    allowed = (from_row <= to_row) & (lax.rem(from_row, GROUP) == lax.rem(to_row, GROUP))
    bias[...] = jnp.where(allowed, 0.0, -1e30)
    for copy in copies:
        copy.wait()
    made = attend_frames(stacked(band[...].astype(jnp.float32)), gain[...], bias, held, ready)
    made = jnp.concatenate([made[g] for g in range(cols // GROUP)], axis=1)
    out[:, :body] = made.astype(jnp.bfloat16).reshape(count, body, channels)
    if with_tail:
        tail_copy.wait()
    else:
        chip = lax.axis_index("frm") // 2
        copies = [
            pltpu.make_async_copy(out.at[pl.ds(2 * (chip ^ k), 2)], result, sems.at[k])
            for k, result in enumerate(results)
        ]
        for copy in copies:
            copy.start()
        low[...] = made[:, 0].astype(jnp.bfloat16)
        high[...] = made[:, cols - 1].astype(jnp.bfloat16)
        for copy in copies:
            copy.wait()


def attend(inward, n_copies, pieces, weights, count, frames, name, tail=None):
    cols, channels = pieces[0].shape[-2:]
    rows = frames * cols
    body = rows // (2 * count)
    norm_gain, *matrices = weights
    with_tail = tail is not None
    chips = count // 2
    shapes = (
        [(count, body + tail.shape[1], channels)]
        if with_tail
        else [(2, body, channels)] * chips + [(frames // 2, channels)] * 2
    )
    return pl.pallas_call(
        functools.partial(attend_kernel, inward, len(pieces), chips, with_tail),
        out_shape=[jax.ShapeDtypeStruct(shape, jnp.bfloat16) for shape in shapes],
        in_specs=[ANYWHERE] * len(pieces) + [INSIDE] + [ANYWHERE] * (5 + with_tail),
        out_specs=[INSIDE] if with_tail else [ANYWHERE] * chips + [INSIDE] * 2,
        scratch_shapes=[
            pltpu.VMEM((frames, cols, channels), jnp.bfloat16),
            *([] if with_tail else [pltpu.VMEM((count, body, channels), jnp.bfloat16)]),
            pltpu.VMEM((frames * GROUP, frames * GROUP), jnp.float32),
            *[pltpu.VMEM(matrix.shape, jnp.bfloat16) for matrix in matrices],
            pltpu.SemaphoreType.DMA((n_copies,)),
            pltpu.SemaphoreType.DMA((5,)),
            *([pltpu.SemaphoreType.DMA(())] if with_tail else []),
        ],
        compiler_params=pltpu.CompilerParams(vmem_limit_bytes=20 * MIB),
        cost_estimate=pl.CostEstimate(
            flops=rows * channels * (channels * 11 + GROUP * frames * 4),
            bytes_accessed=rows * channels * 3 + channels * channels * 14,
            transcendentals=rows * frames,
        ),
        name=name,
    )(*pieces, norm_gain[None], *matrices, *([tail] if with_tail else []))


def filter_kernel(chips, *refs):
    pieces = refs[:chips]
    other, inner, w_depth, out, outer, sems = refs[chips:]
    me = lax.axis_index("frm")
    chip, core = me // 2, me % 2
    copies = []
    for k in range(chips):
        row = 2 * (chip ^ k)
        copies.append(pltpu.make_async_copy(pieces[k].at[core], outer.at[row + core], sems.at[2 * k]))
        copies.append(pltpu.make_async_copy(other.at[k], outer.at[row + 1 - core], sems.at[2 * k + 1]))
    for copy in copies:
        copy.start()
    for copy in copies:
        copy.wait()
    frames, height, cols, channels = out.shape
    width = cols // 2
    edge = width // 2
    body = frames * width
    lanes = 128

    def one_part(step, carry):
        part = pl.ds(pl.multiple_of(step * lanes, lanes), lanes)
        taps = [[w_depth[a, b, part] for b in range(3)] for a in range(3)]
        for frame in range(frames):
            begin = frame * width

            def filtered(row):
                rim = outer[row, begin : begin + width, part].astype(jnp.float32)
                core = inner[row, begin : begin + width, part].astype(jnp.float32)
                mid = jnp.concatenate([rim[:edge], core, rim[edge:]], axis=0)
                spot = lax.broadcasted_iota(jnp.int32, mid.shape, 0)
                low = inner[row, body + frame, part].astype(jnp.float32)[None]
                high = inner[row, body + frames + frame, part].astype(jnp.float32)[None]
                before = jnp.where(spot == 0, low, pltpu.roll(mid, 1, 0))
                after = jnp.where(spot == cols - 1, high, pltpu.roll(mid, cols - 1, 0))
                return [
                    before * taps[a][0][None] + mid * taps[a][1][None] + after * taps[a][2][None] for a in range(3)
                ]

            above = None
            here = filtered(0)
            for row in range(height):
                below = filtered(row + 1) if row + 1 < height else None
                total = here[1]
                if above is not None:
                    total = total + above[0]
                if below is not None:
                    total = total + below[2]
                out[frame, row, :, part] = total.astype(jnp.bfloat16)
                above, here = here, below
        return carry

    lax.fori_loop(0, channels // lanes, one_part, 0)


def depth_filter(outer, other, inner, w_depth, frames, cols):
    chips, body, channels = other.shape
    height = 2 * chips
    size = frames * height * cols * channels
    return pl.pallas_call(
        functools.partial(filter_kernel, chips),
        out_shape=jax.ShapeDtypeStruct((frames, height, cols, channels), jnp.bfloat16),
        in_specs=[ANYWHERE] * (chips + 1) + [INSIDE] * 2,
        out_specs=INSIDE,
        scratch_shapes=[
            pltpu.VMEM((height, body, channels), jnp.bfloat16),
            pltpu.SemaphoreType.DMA((height,)),
        ],
        compiler_params=pltpu.CompilerParams(vmem_limit_bytes=8 * MIB),
        cost_estimate=pl.CostEstimate(flops=18 * size, bytes_accessed=4 * size, transcendentals=0),
        name="depth_filter",
    )(*outer, other, inner, w_depth)


def local(video, norm_gain, w_query, w_key, w_value, w_out, w_time, w_depth):
    count = lax.axis_size("frm")
    chips = count // 2
    span, height, cols, channels = video.shape
    assert height == count and count & (count - 1) == 0
    made = span // 2
    frames = span * count
    edge = cols // 4
    width = 2 * edge
    weights = (norm_gain, w_query, w_key, w_value, w_out, w_time)

    def swap(block, k):
        return lax.ppermute(block, "frm", [(i, i ^ k) for i in range(count)]) if k else block

    early = [k for k in (1, 3) if k < count]
    late = [k for k in (2,) if k < count]
    order = early + [k for k in range(count - 1, 0, -1) if k not in early + late] + late + [0]
    outer = [swap(piece, k) for k, piece in zip(order, cut(lambda me: [me ^ k for k in order], True, video, "cut_outer"))]

    video, outer[0] = lax.optimization_barrier((video, outer[0]))
    far = list(range(chips - 1, 0, -1))
    nearest = list(range(chips))
    *own, other = cut(
        lambda me: [me ^ (2 * k) for k in nearest] + [me ^ (2 * k) ^ 1 for k in nearest], False, video, "cut_inner"
    )
    other = swap(other, 1)

    def pack_inner(ins, outs):
        pairs = []
        for i, k in enumerate(far):
            pairs.append((ins[i], outs[i].at[pl.ds(0, span)]))
            pairs.append((ins[-1].at[k], outs[i].at[pl.ds(span, span)]))
        return pairs

    packed = gather(
        pack_inner,
        2 * len(far),
        [*[own[k] for k in far], other],
        [(2 * span, width, channels)] * len(far),
        "pack_inner",
    )
    outer, packed = lax.optimization_barrier((outer, packed))
    inner = [swap(piece, 2 * k) for k, piece in zip(far, packed)]

    def outer_in(pieces):
        me = lax.axis_index("frm")
        return [(piece, (me ^ k) * span) for k, piece in zip(order, pieces)]

    def inner_in(pieces):
        me = lax.axis_index("frm")
        chip, core = me // 2, me % 2
        pairs = []
        for k, piece in zip(far, pieces):
            pairs.append((piece.at[pl.ds(0, span)], (2 * (chip ^ k) + core) * span))
            pairs.append((piece.at[pl.ds(span, span)], (2 * (chip ^ k) + 1 - core) * span))
        pairs.append((pieces[-2], me * span))
        pairs.append((pieces[-1].at[0], (me ^ 1) * span))
        return pairs

    *outer, low, high = attend(outer_in, count, outer, weights, count, frames, "attend_outer")
    outer = [swap(piece, 2 * k) for k, piece in enumerate(outer)]
    line = lax.axis_size("col")
    upward = [(i, i + 1) for i in range(line - 1)]
    left = lax.ppermute(high, "col", upward).reshape(count, made, channels)
    right = lax.ppermute(low, "col", [(b, a) for a, b in upward]).reshape(count, made, channels)
    spare = -2 * made % 16
    tail = jnp.concatenate([left, right, jnp.zeros((count, spare, channels), jnp.bfloat16)], axis=1)
    (inner,) = attend(inner_in, count, [*inner, own[0], other], weights, count, frames, "attend_inner", tail)
    *outer, inner = lax.optimization_barrier((*outer, inner))

    def pack_back(ins, outs):
        chip, core = place()
        return [(piece.at[1 - core], outs[0].at[k]) for k, piece in enumerate(ins)]

    outer_other = swap(gather(pack_back, chips, outer, [(chips, *outer[0].shape[1:])], "pack_back")[0], 1)
    inner = lax.all_to_all(inner, "frm", split_axis=0, concat_axis=0, tiled=True)
    return depth_filter(outer, outer_other, inner, w_depth, made, cols)


def solution(mesh):
    return jax.shard_map(
        local,
        mesh=mesh,
        in_specs=(P("frm", None, "col", None), P(), P(), P(), P(), P(), P(), P()),
        out_specs=P("frm", None, "col", None),
        check_vma=False,
    )
```

time: 113 us -> 100 us (0.88)
  starting transfers between devices: 61.1 us -> 31.1 us
  waiting for transfers between devices: 11.3 us -> 38.3 us
  local copies, waits for them, and re-layouts: 13.1 us -> 5.52 us
    ppermute x30 -> x17, starting transfers between devices: 61.1 us -> 27.5 us  [the longest x15 22.9 us: swap(): lax.ppermute(block, 'frm', [(i, i ^ k) for i in range(count)])]
    all_to_all x0 -> x1, waiting for transfers between devices: none -> 16.1 us  [local(): lax.all_to_all(inner, 'frm', split_axis=0, concat_axis=0, tiled=True)]
    ppermute x30 -> x17, waiting for transfers between devices: 11.3 us -> 22.2 us  [the longest x15 20.7 us: swap(): lax.ppermute(block, 'frm', [(i, i ^ k) for i in range(count)])]
    pallas_call x8 -> x0, local copies, waits for them, and re-layouts: 5.47 us -> none  [attend(): pl.pallas_call(functools.partial(attend_kernel, count), out_shape=[jax.Sh...]
    unnamed x57 -> x28, local copies, waits for them, and re-layouts: 0.74 us -> 5.41 us
    ppermute x7 -> x0, local copies, waits for them, and re-layouts: 4.43 us -> none  [swap(): return lax.ppermute(block, 'frm', [(i, i ^ k) for i in range(count)])]
    all_to_all x0 -> x1, starting transfers between devices: none -> 3.55 us  [local(): lax.all_to_all(inner, 'frm', split_axis=0, concat_axis=0, tiled=True)]
    squeeze x1 -> x0, local copies, waits for them, and re-layouts: 1.64 us -> none  [forward(): lax.dynamic_index_in_dim(video, me ^ k, 1, keepdims=False)]
  transfers between devices with their start and end apart: 30 -> 18, of which waited for: 6 -> 9; matrix products, arithmetic and copies ran while one was open for 10% -> 0% of each run, Pallas kernels for 18% -> 21%
where the time goes in v2:
time: 100 us; the launch traced here: 99.6 us
  waiting for transfers between devices  38.3 us (38%)
  starting transfers between devices  31.1 us (31%)
  Pallas kernels  24.4 us (24%)
  local copies, waits for them, and re-layouts  5.52 us (6%)
    ppermute x15, starting transfers between devices, swap(): lax.ppermute(block, 'frm', [(i, i ^ k) for i in range(count)])  22.9 us
    ppermute x15, waiting for transfers between devices, swap(): lax.ppermute(block, 'frm', [(i, i ^ k) for i in range(count)])  20.7 us
    pallas_call x2, Pallas kernels, attend(): pl.pallas_call(functools.partial(attend_kernel, inward, len(pieces), chip...  18.3 us
    all_to_all x1, waiting for transfers between devices, local(): lax.all_to_all(inner, 'frm', split_axis=0, concat_axis=0, tiled=True)  16.1 us
    unnamed x28, local copies, waits for them, and re-layouts  5.41 us
    all_to_all x1, starting transfers between devices, local(): lax.all_to_all(inner, 'frm', split_axis=0, concat_axis=0, tiled=True)  3.55 us
    ppermute x1, starting transfers between devices, local(): left = lax.ppermute(high, 'col', upward).reshape(count, made, channels)  3.39 us
    pallas_call x1, Pallas kernels, depth_filter(): pl.pallas_call(functools.partial(filter_kernel, chips), out_shape=jax.Sha...  3.29 us
  transfers between devices with their start and end apart: 18, of which 9 were waited for; matrix products, arithmetic and copies ran while one was open for 0% of the time, Pallas kernels for 21%

profile of v2, /device:TPU:0, one launch (start us, length us, event | category | flops | bytes accessed | tf_op | source)
XLA Modules:
  0.0 99.6 jit_solution(13401934608207795447)
XLA Ops:
  0.0 1.6 %copy-done = bf16[8,8,32,512]{3,2,1,0:T(8,128)(2,1)S(1)} copy-done((bf16[8,8,32,512]{3,2,1,0:T(8,128)(2,1)S(1)}, bf16[8,8,32,512]{3,2,1,0:T(8,128)(2,1)}, u32[]{:S(2)}) %copy-start) | copy-done | bytes 2097176
  1.6 0.0 copy-start.8
  1.6 0.0 copy-start.13
  1.6 0.3 cut_outer.1
  2.0 0.5 collective-permute-start
  2.5 1.0 collective-permute-done.refs_0_
  3.5 0.3 cut_inner.1
  3.8 0.0 copy-start.10
  3.8 0.4 collective-permute-start.7
  4.2 2.7 %collective-permute-start.1 = (bf16[8,16,512]{2,1,0:T(8,128)(2,1)S(1)}, bf16[8,16,512]{2,1,0:T(8,128)(2,1)S(1)}, u32[]{:S(2)}, u32[]{:S(2)}) collective-permute-start(bf16[8,16,512]{2,1,0:T(8,128)(2,1)S(1)} %get-tuple-element.47), channel_id=1, source_target_pairs={{0,12},{4,8},{8,4},{12,0},{16,28},{20,24},{24,20},{28,16},{1,13},{... | collective-permute-start | bytes 393224 | tf_op jit(solution)/shard_map/ppermute | solution.py:313
  6.9 2.2 %collective-permute-start.2 = (bf16[8,16,512]{2,1,0:T(8,128)(2,1)S(1)}, bf16[8,16,512]{2,1,0:T(8,128)(2,1)S(1)}, u32[]{:S(2)}, u32[]{:S(2)}) collective-permute-start(bf16[8,16,512]{2,1,0:T(8,128)(2,1)S(1)} %get-tuple-element.48), channel_id=1, source_target_pairs={{0,28},{4,24},{8,20},{12,16},{16,12},{20,8},{24,4},{28,0},{1,29},{... | collective-permute-start | bytes 393224 | tf_op jit(solution)/shard_map/ppermute | solution.py:313
  9.1 1.3 %collective-permute-start.3 = (bf16[8,16,512]{2,1,0:T(8,128)(2,1)S(1)}, bf16[8,16,512]{2,1,0:T(8,128)(2,1)S(1)}, u32[]{:S(2)}, u32[]{:S(2)}) collective-permute-start(bf16[8,16,512]{2,1,0:T(8,128)(2,1)S(1)} %get-tuple-element.49), channel_id=1, source_target_pairs={{0,24},{4,28},{8,16},{12,20},{16,8},{20,12},{24,0},{28,4},{1,25},{... | collective-permute-start | bytes 393224 | tf_op jit(solution)/shard_map/ppermute | solution.py:313
  10.5 0.5 collective-permute-start.4
  10.9 0.0 collective-permute-done.1.refs_1_
  10.9 2.3 %collective-permute-start.5 = (bf16[8,16,512]{2,1,0:T(8,128)(2,1)S(1)}, bf16[8,16,512]{2,1,0:T(8,128)(2,1)S(1)}, u32[]{:S(2)}, u32[]{:S(2)}) collective-permute-start(bf16[8,16,512]{2,1,0:T(8,128)(2,1)S(1)} %get-tuple-element.51), channel_id=1, source_target_pairs={{0,16},{4,20},{8,24},{12,28},{16,0},{20,4},{24,8},{28,12},{1,17},{... | collective-permute-start | bytes 393224 | tf_op jit(solution)/shard_map/ppermute | solution.py:313
  13.3 0.0 collective-permute-done.7.refs_3_.refs_4_
  13.3 1.6 %collective-permute-start.6 = (bf16[8,16,512]{2,1,0:T(8,128)(2,1)S(1)}, bf16[8,16,512]{2,1,0:T(8,128)(2,1)S(1)}, u32[]{:S(2)}, u32[]{:S(2)}) collective-permute-start(bf16[8,16,512]{2,1,0:T(8,128)(2,1)S(1)} %get-tuple-element.52), channel_id=1, source_target_pairs={{0,8},{4,12},{8,0},{12,4},{16,24},{20,28},{24,16},{28,20},{1,9},{5... | collective-permute-start | bytes 393224 | tf_op jit(solution)/shard_map/ppermute | solution.py:313
  14.9 1.8 %pack_inner.1 = (bf16[16,16,512]{2,1,0:T(8,128)(2,1)}, bf16[16,16,512]{2,1,0:T(8,128)(2,1)}, bf16[16,16,512]{2,1,0:T(8,128)(2,1)S(1)}) custom-call(bf16[8,16,512]{2,1,0:T(8,128)(2,1)S(1)} %get-tuple-element.55.refs_0_, bf16[8,16,512]{2,1,0:T(8,128)(2,1)S(1)} %get-tuple-element.56.refs_1_, bf16[8,16,512]{2,1,0:T(8,128)(2,1)S(1)} %get-tuple-element.57.refs_2_, ...), custom_call_target="tpu_custom_call" | custom-call | bytes 1572864 | tf_op jit(solution)/shard_map/pack_inner/pallas_call | solution.py:36
  16.8 0.0 collective-permute-done.2.refs_2_
  16.8 2.6 %collective-permute-done.3.refs_3_ = bf16[8,16,512]{2,1,0:T(8,128)(2,1)S(1)} collective-permute-done((bf16[8,16,512]{2,1,0:T(8,128)(2,1)S(1)}, bf16[8,16,512]{2,1,0:T(8,128)(2,1)S(1)}, u32[]{:S(2)}, u32[]{:S(2)}) %collective-permute-start.3) | collective-permute-done | bytes 131104 | tf_op jit(solution)/shard_map/ppermute | solution.py:313
  19.4 10.3 %collective-permute-done.4.refs_4_ = bf16[8,16,512]{2,1,0:T(8,128)(2,1)S(1)} collective-permute-done((bf16[8,16,512]{2,1,0:T(8,128)(2,1)S(1)}, bf16[8,16,512]{2,1,0:T(8,128)(2,1)S(1)}, u32[]{:S(2)}, u32[]{:S(2)}) %collective-permute-start.4) | collective-permute-done | bytes 131104 | tf_op jit(solution)/shard_map/ppermute | solution.py:313
  29.7 3.3 %collective-permute-done.5.refs_5_ = bf16[8,16,512]{2,1,0:T(8,128)(2,1)S(1)} collective-permute-done((bf16[8,16,512]{2,1,0:T(8,128)(2,1)S(1)}, bf16[8,16,512]{2,1,0:T(8,128)(2,1)S(1)}, u32[]{:S(2)}, u32[]{:S(2)}) %collective-permute-start.5) | collective-permute-done | bytes 131104 | tf_op jit(solution)/shard_map/ppermute | solution.py:313
  33.0 0.0 collective-permute-done.6.refs_6_
  33.0 2.9 %collective-permute-start.11 = (bf16[16,16,512]{2,1,0:T(8,128)(2,1)}, bf16[16,16,512]{2,1,0:T(8,128)(2,1)}, u32[]{:S(2)}, u32[]{:S(2)}) collective-permute-start(bf16[16,16,512]{2,1,0:T(8,128)(2,1)} %get-tuple-element.74), channel_id=1, source_target_pairs={{0,24},{4,28},{8,16},{12,20},{16,8},{20,12},{24,0},{28,4},{1,25},{... | collective-permute-start | bytes 786440 | tf_op jit(solution)/shard_map/ppermute | solution.py:313
  35.8 0.0 collective-permute-start.12
  35.8 1.5 %collective-permute-start.13 = (bf16[16,16,512]{2,1,0:T(8,128)(2,1)S(1)}, bf16[16,16,512]{2,1,0:T(8,128)(2,1)}, u32[]{:S(2)}, u32[]{:S(2)}) collective-permute-start(bf16[16,16,512]{2,1,0:T(8,128)(2,1)S(1)} %get-tuple-element.76), channel_id=1, source_target_pairs={{0,8},{4,12},{8,0},{12,4},{16,24},{20,28},{24,16},{28,20},{1,9},{5... | collective-permute-start | bytes 786440 | tf_op jit(solution)/shard_map/ppermute | solution.py:313
  37.4 0.0 copy-done.10
  37.4 0.0 copy-done.2
  37.4 0.0 copy-done.3
  37.4 0.0 copy-done.4
  37.4 0.0 copy-done.6
  37.4 0.0 copy-done.8
  37.4 0.0 copy-done.13
  37.4 0.0 copy-start.11
  37.4 9.5 %attend_outer.1 = (bf16[2,64,512]{2,1,0:T(8,128)(2,1)S(1)}, bf16[2,64,512]{2,1,0:T(8,128)(2,1)}, bf16[2,64,512]{2,1,0:T(8,128)(2,1)S(1)}, bf16[2,64,512]{2,1,0:T...) custom-call(bf16[8,16,512]{2,1,0:T(8,128)(2,1)S(1)} %collective-permute-done.refs_0_, ...), custom_call_target="tpu_custom_call" | custom-call | flops 4026531840 | bytes 5242880 | tf_op jit(solution)/shard_map/attend_outer/pallas_call | solution.py:203
  47.0 0.0 copy-start.12
  47.0 0.7 copy-done.12
  47.6 3.4 %collective-permute-start.14 = (bf16[32,512]{1,0:T(8,128)(2,1)S(1)}, bf16[32,512]{1,0:T(8,128)(2,1)S(1)}, u32[]{:S(2)}, u32[]{:S(2)}) collective-permute-start(bf16[32,512]{1,0:T(8,128)(2,1)S(1)} %get-tuple-element.78), channel_id=1, source_target_pairs={{0,1},{1,2},{2,3},{4,5},{5,6},{6,7},{8,9},{9,10},{10,11},{12,13},{... | collective-permute-start | bytes 98312 | tf_op jit(solution)/shard_map/ppermute | solution.py:364
  51.0 1.3 %collective-permute-start.15 = (bf16[32,512]{1,0:T(8,128)(2,1)S(1)}, bf16[32,512]{1,0:T(8,128)(2,1)S(1)}, u32[]{:S(2)}, u32[]{:S(2)}) collective-permute-start(bf16[32,512]{1,0:T(8,128)(2,1)S(1)} %get-tuple-element.79), channel_id=1, source_target_pairs={{1,0},{2,1},{3,2},{5,4},{6,5},{7,6},{9,8},{10,9},{11,10},{13,12},{... | collective-permute-start | bytes 98312 | tf_op jit(solution)/shard_map/ppermute | solution.py:365
  52.3 0.1 pad.2.clone
  52.4 0.2 collective-permute-done.14
  52.6 2.9 %collective-permute-start.10 = (bf16[2,64,512]{2,1,0:T(8,128)(2,1)}, bf16[2,64,512]{2,1,0:T(8,128)(2,1)S(1)}, u32[]{:S(2)}, u32[]{:S(2)}) collective-permute-start(bf16[2,64,512]{2,1,0:T(8,128)(2,1)} %get-tuple-element.73), channel_id=1, source_target_pairs={{0,24},{4,28},{8,16},{12,20},{16,8},{20,12},{24,0},{28,4},{1,25},{... | collective-permute-start | bytes 393224 | tf_op jit(solution)/shard_map/ppermute | solution.py:313
  55.5 1.3 %collective-permute-done.15 = bf16[32,512]{1,0:T(8,128)(2,1)S(1)} collective-permute-done((bf16[32,512]{1,0:T(8,128)(2,1)S(1)}, bf16[32,512]{1,0:T(8,128)(2,1)S(1)}, u32[]{:S(2)}, u32[]{:S(2)}) %collective-permute-start.15) | collective-permute-done | bytes 32800 | tf_op jit(solution)/shard_map/ppermute | solution.py:365
  56.8 0.5 collective-permute-start.8
  57.3 0.1 maximum_maximum_fusion.refs_11_
  57.4 0.0 collective-permute-done.11.refs_0_
  57.5 3.0 %collective-permute-start.9 = (bf16[2,64,512]{2,1,0:T(8,128)(2,1)}, bf16[2,64,512]{2,1,0:T(8,128)(2,1)S(1)}, u32[]{:S(2)}, u32[]{:S(2)}) collective-permute-start(bf16[2,64,512]{2,1,0:T(8,128)(2,1)} %copy-done.12), channel_id=1, source_target_pairs={{0,16},{4,20},{8,24},{12,28},{16,0},{20,4},{24,8},{28,12},{1,17},{... | collective-permute-start | bytes 393224 | tf_op jit(solution)/shard_map/ppermute | solution.py:313
  60.4 2.3 %collective-permute-done.12.refs_1_ = bf16[16,16,512]{2,1,0:T(8,128)(2,1)} collective-permute-done((bf16[16,16,512]{2,1,0:T(8,128)(2,1)}, bf16[16,16,512]{2,1,0:T(8,128)(2,1)}, u32[]{:S(2)}, u32[]{:S(2)}) %collective-permute-start.12) | collective-permute-done | bytes 262176 | tf_op jit(solution)/shard_map/ppermute | solution.py:313
  62.8 0.0 collective-permute-done.13.refs_2_
  62.8 0.0 copy-done.11
  62.8 1.0 %copy-done.5 = bf16[512,512]{1,0:T(8,128)(2,1)S(1)} copy-done((bf16[512,512]{1,0:T(8,128)(2,1)S(1)}, bf16[512,512]{1,0:T(8,128)(2,1)}, u32[]{:S(2)}) %copy-start.5) | copy-done | bytes 524312
  63.8 1.0 %copy-done.7 = bf16[512,512]{1,0:T(8,128)(2,1)S(1)} copy-done((bf16[512,512]{1,0:T(8,128)(2,1)S(1)}, bf16[512,512]{1,0:T(8,128)(2,1)}, u32[]{:S(2)}) %copy-start.7) | copy-done | bytes 524312
  64.9 1.0 %copy-done.9 = bf16[512,512]{1,0:T(8,128)(2,1)S(1)} copy-done((bf16[512,512]{1,0:T(8,128)(2,1)S(1)}, bf16[512,512]{1,0:T(8,128)(2,1)}, u32[]{:S(2)}) %copy-start.9) | copy-done | bytes 524312
  65.9 8.7 %attend_inner.1 = bf16[8,80,512]{2,1,0:T(8,128)(2,1)} custom-call(bf16[16,16,512]{2,1,0:T(8,128)(2,1)} %collective-permute-done.11.refs_0_, bf16[16,16,512]{2,1,0:T(8,128)(2,1)} %collective-permute-done.12.refs_1_, bf16[16,16,512]{2,1,0:T(8,128)(2,1)} %collective-permute-done.13.refs_2_, bf16[8,16,512]{2,1,0:T(8,128)(2,1)S(1)} %copy-done.11, ...), custom_call_target="tpu_custom_call" | custom-call | flops 4026531840 | bytes 5242880 | tf_op jit(solution)/shard_map/attend_inner/pallas_call | solution.py:203
  74.6 0.0 copy-start.1
  74.6 0.0 collective-permute-done.10.refs_3_
  74.6 0.0 collective-permute-done.8.refs_1_
  74.7 0.0 collective-permute-done.9.refs_2_
  74.7 3.6 %all-to-all-start = ((bf16[8,80,512]{2,1,0:T(8,128)(2,1)}), bf16[8,80,512]{2,1,0:T(8,128)(2,1)S(1)}, u32[]{:S(2)}, u32[]{:S(2)}) async-start(bf16[8,80,512]{2,1,0:T(8,128)(2,1)} %attend_inner.1), calls=%async_computation | async-start | bytes 1310720 | tf_op jit(solution)/shard_map/all_to_all | solution.py:376
  78.2 0.4 pack_back.1
  78.6 0.4 collective-permute-start.16
  79.1 1.2 %collective-permute-done.16.refs_4_ = bf16[4,64,512]{2,1,0:T(8,128)(2,1)S(1)} collective-permute-done((bf16[4,64,512]{2,1,0:T(8,128)(2,1)S(1)}, bf16[4,64,512]{2,1,0:T(8,128)(2,1)S(1)}, u32[]{:S(2)}, u32[]{:S(2)}) %collective-permute-start.16) | collective-permute-done | bytes 262176 | tf_op jit(solution)/shard_map/ppermute | solution.py:313
  80.2 16.1 %all-to-all-done.refs_5_ = bf16[8,80,512]{2,1,0:T(8,128)(2,1)S(1)} async-done(((bf16[8,80,512]{2,1,0:T(8,128)(2,1)}), bf16[8,80,512]{2,1,0:T(8,128)(2,1)S(1)}, u32[]{:S(2)}, u32[]{:S(2)}) %all-to-all-start) | async-done | bytes 655392 | tf_op jit(solution)/shard_map/all_to_all | solution.py:376
  96.3 3.3 %depth_filter.1 = bf16[4,8,32,512]{3,2,1,0:T(8,128)(2,1)} custom-call(bf16[2,64,512]{2,1,0:T(8,128)(2,1)S(1)} %get-tuple-element.80.refs_0_, bf16[2,64,512]{2,1,0:T(8,128)(2,1)S(1)} %collective-permute-done.8.refs_1_, bf16[2,64,512]{2,1,0:T(8,128)(2,1)S(1)} %collective-permute-done.9.refs_2_, bf16[2,64,512]{2,1,0:T(8,128)(2,1)S(1)} %collective-permute-done.10.refs_3_, ...), custom_call_target="tpu_custom_call" | custom-call | flops 9437184 | bytes 2097152 | tf_op jit(solution)/shard_map/depth_filter/pallas_call | solution.py:286
  (12 shorter events, 0.0 us)
Async XLA Ops:
  0.0 1.6 %copy-start = (bf16[8,8,32,512]{3,2,1,0:T(8,128)(2,1)S(1)}, bf16[8,8,32,512]{3,2,1,0:T(8,128)(2,1)}, u32[]{:S(2)}) copy-start(bf16[8,8,32,512]{3,2,1,0:T(8,128)(2,1)} %video.2) | copy-start | bytes 6291460
  1.6 35.8 %copy-start.2 = (bf16[3,512,512]{2,1,0:T(8,128)(2,1)S(1)}, bf16[3,512,512]{2,1,0:T(8,128)(2,1)}, u32[]{:S(2)}) copy-start(bf16[3,512,512]{2,1,0:T(8,128)(2,1)} %refs_10_.3) | copy-start | bytes 4718596
  1.6 35.8 %copy-start.3 = (bf16[512,512]{1,0:T(8,128)(2,1)S(1)}, bf16[512,512]{1,0:T(8,128)(2,1)}, u32[]{:S(2)}) copy-start(bf16[512,512]{1,0:T(8,128)(2,1)} %refs_6_.2) | copy-start | bytes 1572868
  1.6 35.8 %copy-start.4 = (bf16[512,512]{1,0:T(8,128)(2,1)S(1)}, bf16[512,512]{1,0:T(8,128)(2,1)}, u32[]{:S(2)}) copy-start(bf16[512,512]{1,0:T(8,128)(2,1)} %refs_7_.1) | copy-start | bytes 1572868
  1.6 35.8 %copy-start.6 = (bf16[512,512]{1,0:T(8,128)(2,1)S(1)}, bf16[512,512]{1,0:T(8,128)(2,1)}, u32[]{:S(2)}) copy-start(bf16[512,512]{1,0:T(8,128)(2,1)} %refs_8_.1) | copy-start | bytes 1572868
  1.6 35.8 %copy-start.8 = (bf16[512,512]{1,0:T(8,128)(2,1)S(1)}, bf16[512,512]{1,0:T(8,128)(2,1)}, u32[]{:S(2)}) copy-start(bf16[512,512]{1,0:T(8,128)(2,1)} %refs_9_.3) | copy-start | bytes 1572868
  1.6 35.8 %copy-start.13 = (f32[512]{0:T(512)S(1)}, f32[512]{0:T(512)}, u32[]{:S(2)}) copy-start(f32[512]{0:T(512)} %param.9) | copy-start | bytes 6148
  2.0 1.5 %collective-permute-start = (bf16[8,16,512]{2,1,0:T(8,128)(2,1)S(1)}, bf16[8,16,512]{2,1,0:T(8,128)(2,1)S(1)}, u32[]{:S(2)}, u32[]{:S(2)}) collective-permute-start(bf16[8,16,512]{2,1,0:T(8,128)(2,1)S(1)} %get-tuple-element.45), channel_id=1, source_target_pairs={{0,4},{4,0},{8,12},{12,8},{16,20},{20,16},{24,28},{28,24},{1,5},{5... | collective-permute-start | bytes 393224 | tf_op jit(solution)/shard_map/ppermute | solution.py:313
  3.8 33.6 %copy-start.10 = (bf16[8,16,512]{2,1,0:T(8,128)(2,1)}, bf16[8,16,512]{2,1,0:T(8,128)(2,1)S(1)}, u32[]{:S(2)}) copy-start(bf16[8,16,512]{2,1,0:T(8,128)(2,1)S(1)} %get-tuple-element.77.refs_3_) | copy-start | bytes 393220
  3.8 9.5 %collective-permute-start.7 = (bf16[4,8,16,512]{3,2,1,0:T(8,128)(2,1)S(1)}, bf16[4,8,16,512]{3,2,1,0:T(8,128)(2,1)S(1)}, u32[]{:S(2)}, u32[]{:S(2)}) collective-permute-start(bf16[4,8,16,512]{3,2,1,0:T(8,128)(2,1)S(1)} %get-tuple-element.58), channel_id=1, source_target_pairs={{0,4},{4,0},{8,12},{12,8},{16,20},{20,16},{24,28},{28,24},{1,5},{5... | collective-permute-start | bytes 1572872 | tf_op jit(solution)/shard_map/ppermute | solution.py:313
  4.2 6.7 %collective-permute-start.1 = (bf16[8,16,512]{2,1,0:T(8,128)(2,1)S(1)}, bf16[8,16,512]{2,1,0:T(8,128)(2,1)S(1)}, u32[]{:S(2)}, u32[]{:S(2)}) collective-permute-start(bf16[8,16,512]{2,1,0:T(8,128)(2,1)S(1)} %get-tuple-element.47), channel_id=1, source_target_pairs={{0,12},{4,8},{8,4},{12,0},{16,28},{20,24},{24,20},{28,16},{1,13},{... | collective-permute-start | bytes 393224 | tf_op jit(solution)/shard_map/ppermute | solution.py:313
  6.9 9.9 %collective-permute-start.2 = (bf16[8,16,512]{2,1,0:T(8,128)(2,1)S(1)}, bf16[8,16,512]{2,1,0:T(8,128)(2,1)S(1)}, u32[]{:S(2)}, u32[]{:S(2)}) collective-permute-start(bf16[8,16,512]{2,1,0:T(8,128)(2,1)S(1)} %get-tuple-element.48), channel_id=1, source_target_pairs={{0,28},{4,24},{8,20},{12,16},{16,12},{20,8},{24,4},{28,0},{1,29},{... | collective-permute-start | bytes 393224 | tf_op jit(solution)/shard_map/ppermute | solution.py:313
  9.1 10.2 %collective-permute-start.3 = (bf16[8,16,512]{2,1,0:T(8,128)(2,1)S(1)}, bf16[8,16,512]{2,1,0:T(8,128)(2,1)S(1)}, u32[]{:S(2)}, u32[]{:S(2)}) collective-permute-start(bf16[8,16,512]{2,1,0:T(8,128)(2,1)S(1)} %get-tuple-element.49), channel_id=1, source_target_pairs={{0,24},{4,28},{8,16},{12,20},{16,8},{20,12},{24,0},{28,4},{1,25},{... | collective-permute-start | bytes 393224 | tf_op jit(solution)/shard_map/ppermute | solution.py:313
  10.5 19.2 %collective-permute-start.4 = (bf16[8,16,512]{2,1,0:T(8,128)(2,1)S(1)}, bf16[8,16,512]{2,1,0:T(8,128)(2,1)S(1)}, u32[]{:S(2)}, u32[]{:S(2)}) collective-permute-start(bf16[8,16,512]{2,1,0:T(8,128)(2,1)S(1)} %get-tuple-element.50), channel_id=1, source_target_pairs={{0,20},{4,16},{8,28},{12,24},{16,4},{20,0},{24,12},{28,8},{1,21},{... | collective-permute-start | bytes 393224 | tf_op jit(solution)/shard_map/ppermute | solution.py:313
  10.9 22.0 %collective-permute-start.5 = (bf16[8,16,512]{2,1,0:T(8,128)(2,1)S(1)}, bf16[8,16,512]{2,1,0:T(8,128)(2,1)S(1)}, u32[]{:S(2)}, u32[]{:S(2)}) collective-permute-start(bf16[8,16,512]{2,1,0:T(8,128)(2,1)S(1)} %get-tuple-element.51), channel_id=1, source_target_pairs={{0,16},{4,20},{8,24},{12,28},{16,0},{20,4},{24,8},{28,12},{1,17},{... | collective-permute-start | bytes 393224 | tf_op jit(solution)/shard_map/ppermute | solution.py:313
  13.3 19.7 %collective-permute-start.6 = (bf16[8,16,512]{2,1,0:T(8,128)(2,1)S(1)}, bf16[8,16,512]{2,1,0:T(8,128)(2,1)S(1)}, u32[]{:S(2)}, u32[]{:S(2)}) collective-permute-start(bf16[8,16,512]{2,1,0:T(8,128)(2,1)S(1)} %get-tuple-element.52), channel_id=1, source_target_pairs={{0,8},{4,12},{8,0},{12,4},{16,24},{20,28},{24,16},{28,20},{1,9},{5... | collective-permute-start | bytes 393224 | tf_op jit(solution)/shard_map/ppermute | solution.py:313
  33.0 24.5 %collective-permute-start.11 = (bf16[16,16,512]{2,1,0:T(8,128)(2,1)}, bf16[16,16,512]{2,1,0:T(8,128)(2,1)}, u32[]{:S(2)}, u32[]{:S(2)}) collective-permute-start(bf16[16,16,512]{2,1,0:T(8,128)(2,1)} %get-tuple-element.74), channel_id=1, source_target_pairs={{0,24},{4,28},{8,16},{12,20},{16,8},{20,12},{24,0},{28,4},{1,25},{... | collective-permute-start | bytes 786440 | tf_op jit(solution)/shard_map/ppermute | solution.py:313
  35.8 26.9 %collective-permute-start.12 = (bf16[16,16,512]{2,1,0:T(8,128)(2,1)}, bf16[16,16,512]{2,1,0:T(8,128)(2,1)}, u32[]{:S(2)}, u32[]{:S(2)}) collective-permute-start(bf16[16,16,512]{2,1,0:T(8,128)(2,1)} %get-tuple-element.75), channel_id=1, source_target_pairs={{0,16},{4,20},{8,24},{12,28},{16,0},{20,4},{24,8},{28,12},{1,17},{... | collective-permute-start | bytes 786440 | tf_op jit(solution)/shard_map/ppermute | solution.py:313
  35.8 26.9 %collective-permute-start.13 = (bf16[16,16,512]{2,1,0:T(8,128)(2,1)S(1)}, bf16[16,16,512]{2,1,0:T(8,128)(2,1)}, u32[]{:S(2)}, u32[]{:S(2)}) collective-permute-start(bf16[16,16,512]{2,1,0:T(8,128)(2,1)S(1)} %get-tuple-element.76), channel_id=1, source_target_pairs={{0,8},{4,12},{8,0},{12,4},{16,24},{20,28},{24,16},{28,20},{1,9},{5... | collective-permute-start | bytes 786440 | tf_op jit(solution)/shard_map/ppermute | solution.py:313
  37.4 25.4 %copy-start.11 = (bf16[8,16,512]{2,1,0:T(8,128)(2,1)S(1)}, bf16[8,16,512]{2,1,0:T(8,128)(2,1)}, u32[]{:S(2)}) copy-start(bf16[8,16,512]{2,1,0:T(8,128)(2,1)} %copy-done.10) | copy-start | bytes 393220
  47.0 0.7 copy-start.12
  47.6 5.0 %collective-permute-start.14 = (bf16[32,512]{1,0:T(8,128)(2,1)S(1)}, bf16[32,512]{1,0:T(8,128)(2,1)S(1)}, u32[]{:S(2)}, u32[]{:S(2)}) collective-permute-start(bf16[32,512]{1,0:T(8,128)(2,1)S(1)} %get-tuple-element.78), channel_id=1, source_target_pairs={{0,1},{1,2},{2,3},{4,5},{5,6},{6,7},{8,9},{9,10},{10,11},{12,13},{... | collective-permute-start | bytes 98312 | tf_op jit(solution)/shard_map/ppermute | solution.py:364
  51.0 5.8 %collective-permute-start.15 = (bf16[32,512]{1,0:T(8,128)(2,1)S(1)}, bf16[32,512]{1,0:T(8,128)(2,1)S(1)}, u32[]{:S(2)}, u32[]{:S(2)}) collective-permute-start(bf16[32,512]{1,0:T(8,128)(2,1)S(1)} %get-tuple-element.79), channel_id=1, source_target_pairs={{1,0},{2,1},{3,2},{5,4},{6,5},{7,6},{9,8},{10,9},{11,10},{13,12},{... | collective-permute-start | bytes 98312 | tf_op jit(solution)/shard_map/ppermute | solution.py:365
  52.6 22.0 %collective-permute-start.10 = (bf16[2,64,512]{2,1,0:T(8,128)(2,1)}, bf16[2,64,512]{2,1,0:T(8,128)(2,1)S(1)}, u32[]{:S(2)}, u32[]{:S(2)}) collective-permute-start(bf16[2,64,512]{2,1,0:T(8,128)(2,1)} %get-tuple-element.73), channel_id=1, source_target_pairs={{0,24},{4,28},{8,16},{12,20},{16,8},{20,12},{24,0},{28,4},{1,25},{... | collective-permute-start | bytes 393224 | tf_op jit(solution)/shard_map/ppermute | solution.py:313
  56.8 17.8 %collective-permute-start.8 = (bf16[2,64,512]{2,1,0:T(8,128)(2,1)}, bf16[2,64,512]{2,1,0:T(8,128)(2,1)S(1)}, u32[]{:S(2)}, u32[]{:S(2)}) collective-permute-start(bf16[2,64,512]{2,1,0:T(8,128)(2,1)} %get-tuple-element.71), channel_id=1, source_target_pairs={{0,8},{4,12},{8,0},{12,4},{16,24},{20,28},{24,16},{28,20},{1,9},{5... | collective-permute-start | bytes 393224 | tf_op jit(solution)/shard_map/ppermute | solution.py:313
  57.5 17.2 %collective-permute-start.9 = (bf16[2,64,512]{2,1,0:T(8,128)(2,1)}, bf16[2,64,512]{2,1,0:T(8,128)(2,1)S(1)}, u32[]{:S(2)}, u32[]{:S(2)}) collective-permute-start(bf16[2,64,512]{2,1,0:T(8,128)(2,1)} %copy-done.12), channel_id=1, source_target_pairs={{0,16},{4,20},{8,24},{12,28},{16,0},{20,4},{24,8},{28,12},{1,17},{... | collective-permute-start | bytes 393224 | tf_op jit(solution)/shard_map/ppermute | solution.py:313
  62.8 1.0 %copy-start.5 = (bf16[512,512]{1,0:T(8,128)(2,1)S(1)}, bf16[512,512]{1,0:T(8,128)(2,1)}, u32[]{:S(2)}) copy-start(bf16[512,512]{1,0:T(8,128)(2,1)} %refs_7_.1) | copy-start | bytes 1572868
  63.8 1.0 %copy-start.7 = (bf16[512,512]{1,0:T(8,128)(2,1)S(1)}, bf16[512,512]{1,0:T(8,128)(2,1)}, u32[]{:S(2)}) copy-start(bf16[512,512]{1,0:T(8,128)(2,1)} %refs_8_.1) | copy-start | bytes 1572868
  64.9 1.0 %copy-start.9 = (bf16[512,512]{1,0:T(8,128)(2,1)S(1)}, bf16[512,512]{1,0:T(8,128)(2,1)}, u32[]{:S(2)}) copy-start(bf16[512,512]{1,0:T(8,128)(2,1)} %refs_9_.3) | copy-start | bytes 1572868
  74.6 21.7 %copy-start.1 = (f32[3,3,512]{2,1,0:T(4,128)S(1)}, f32[3,3,512]{2,1,0:T(4,128)}, u32[]{:S(2)}) copy-start(f32[3,3,512]{2,1,0:T(4,128)} %refs_6_.3) | copy-start | bytes 55300
  74.7 21.6 %all-to-all-start = ((bf16[8,80,512]{2,1,0:T(8,128)(2,1)}), bf16[8,80,512]{2,1,0:T(8,128)(2,1)S(1)}, u32[]{:S(2)}, u32[]{:S(2)}) async-start(bf16[8,80,512]{2,1,0:T(8,128)(2,1)} %attend_inner.1), calls=%async_computation | async-start | bytes 1310720 | tf_op jit(solution)/shard_map/all_to_all | solution.py:376
  78.6 1.6 %collective-permute-start.16 = (bf16[4,64,512]{2,1,0:T(8,128)(2,1)S(1)}, bf16[4,64,512]{2,1,0:T(8,128)(2,1)S(1)}, u32[]{:S(2)}, u32[]{:S(2)}) collective-permute-start(bf16[4,64,512]{2,1,0:T(8,128)(2,1)S(1)} %pack_back.1), channel_id=1, source_target_pairs={{0,4},{4,0},{8,12},{12,8},{16,20},{20,16},{24,28},{28,24},{1,5},{5... | collective-permute-start | bytes 786440 | tf_op jit(solution)/shard_map/ppermute | solution.py:313

commit v3 on v2

v3 whole, which is shorter than its diff:
```python
import functools
import math

import jax
import jax.numpy as jnp
from jax import lax
from jax.experimental import pallas as pl
from jax.experimental.pallas import tpu as pltpu
from jax.sharding import PartitionSpec as P

epsilon = 1e-06
GROUP = 8
BLOCKS = 2
MIB = 1024 * 1024
ANYWHERE = pl.BlockSpec(memory_space=pl.ANY)
INSIDE = pl.BlockSpec(memory_space=pltpu.VMEM)


def place():
    me = lax.axis_index("frm")
    return me // 2, me % 2


def gather_kernel(pairs_of, n_in, *refs):
    *arrays, sems = refs
    pairs = pairs_of(arrays[:n_in], arrays[n_in:])
    copies = [pltpu.make_async_copy(source, target, sems.at[i]) for i, (source, target) in enumerate(pairs)]
    for copy in copies:
        copy.start()
    for copy in copies:
        copy.wait()


def gather(pairs_of, n_pairs, arrays, shapes, name):
    size = sum(math.prod(shape) for shape in shapes)
    return pl.pallas_call(
        functools.partial(gather_kernel, pairs_of, len(arrays)),
        out_shape=[jax.ShapeDtypeStruct(shape, jnp.bfloat16) for shape in shapes],
        in_specs=[ANYWHERE] * len(arrays),
        out_specs=[INSIDE] * len(shapes),
        scratch_shapes=[pltpu.SemaphoreType.DMA((n_pairs,))],
        compiler_params=pltpu.CompilerParams(vmem_limit_bytes=4 * MIB),
        cost_estimate=pl.CostEstimate(flops=0, bytes_accessed=4 * size, transcendentals=0),
        name=name,
    )(*arrays)


def cut_kernel(rows_of, video, *refs):
    *results, held, sems = refs
    span, height, cols = held.shape[1], held.shape[0], held.shape[2]
    edge = cols // 4
    copies = [pltpu.make_async_copy(video.at[:, row], held.at[row], sems.at[row]) for row in range(height)]
    for copy in copies:
        copy.start()
    for copy in copies:
        copy.wait()
    half = len(results) // 2
    own, other = rows_of(lax.axis_index("frm"))
    for rim in (True, False):
        *singles, stack = results[:half] if rim else results[half:]
        targets = singles + [stack.at[k] for k in range(stack.shape[0])]
        for row, target in zip(own + other, targets):
            values = held[row].astype(jnp.float32)
            if rim:
                values = jnp.concatenate([values[:, :edge], values[:, 3 * edge :]], axis=1)
            else:
                values = values[:, edge : 3 * edge]
            target[...] = values.astype(jnp.bfloat16)


def cut(rows_of, chips, video):
    span, height, cols, channels = video.shape
    shape = (span, cols // 2, channels)
    shapes = ([shape] * chips + [(chips, *shape)]) * 2
    return pl.pallas_call(
        functools.partial(cut_kernel, rows_of),
        out_shape=[jax.ShapeDtypeStruct(shape, jnp.bfloat16) for shape in shapes],
        in_specs=[ANYWHERE],
        out_specs=[INSIDE] * len(shapes),
        scratch_shapes=[
            pltpu.VMEM((height, span, cols, channels), jnp.bfloat16),
            pltpu.SemaphoreType.DMA((height,)),
        ],
        compiler_params=pltpu.CompilerParams(vmem_limit_bytes=12 * MIB),
        cost_estimate=pl.CostEstimate(flops=0, bytes_accessed=3 * video.size, transcendentals=0),
        name="cut",
    )(video)


def stacked(x):
    return jnp.stack([x[:, g : g + GROUP] for g in range(0, x.shape[1], GROUP)])


def attend_frames(x, gain, bias, weights, ready):
    w_query, w_key, w_value, w_out, w_time = weights
    groups, frames, _, channels = x.shape
    rows = frames * GROUP
    x = x.reshape(groups * rows, channels)
    normed = (x * lax.rsqrt(jnp.mean(x * x, axis=-1, keepdims=True) + epsilon) * gain).astype(jnp.bfloat16)

    def project(index):
        ready(index)
        return jnp.dot(normed, weights[index][...], preferred_element_type=jnp.float32).astype(jnp.bfloat16)

    queries, key_proj, values = project(0), project(1), project(2)
    height = rows // BLOCKS
    attended = []
    for group in range(groups):
        first = group * rows
        for block in range(BLOCKS):
            begin = block * height
            span = begin + height
            scores = lax.dot_general(
                queries[first + begin : first + span],
                key_proj[first : first + span],
                (((1,), (1,)), ((), ())),
                preferred_element_type=jnp.float32,
            )
            scores = scores * (1.0 / math.sqrt(channels)) + bias[begin:span, :span]
            raised = jnp.exp(scores - jnp.max(scores, axis=-1, keepdims=True))
            shares = (raised * (1.0 / jnp.sum(raised, axis=-1, keepdims=True))).astype(jnp.bfloat16)
            attended.append(
                jnp.dot(shares, values[first : first + span], preferred_element_type=jnp.float32).astype(jnp.bfloat16)
            )
    ready(3)
    mixed = x + jnp.dot(jnp.concatenate(attended, axis=0), w_out[...], preferred_element_type=jnp.float32)
    mixed = mixed.reshape(groups, frames // 2, 2, GROUP, channels)
    even = mixed[:, :, 0]
    odd = mixed[:, :, 1]
    prior = jnp.concatenate([even[:, :1], odd[:, :-1]], axis=1)
    ready(4)
    summed = None
    for tap, part in enumerate((prior, even, odd)):
        part = part.reshape(groups * rows // 2, channels).astype(jnp.bfloat16)
        term = jnp.dot(part, w_time[tap], preferred_element_type=jnp.float32)
        summed = term if summed is None else summed + term
    return (summed / (1.0 + jnp.exp(-summed))).reshape(groups, frames // 2, GROUP, channels)


def attend_kernel(inward, n_in, n_out, *refs):
    pieces = refs[:n_in]
    gain = refs[n_in]
    sources = refs[n_in + 1 : n_in + 6]
    results = refs[n_in + 6 : n_in + 6 + n_out]
    band, done, bias, *held, sems, weight_sems = refs[n_in + 6 + n_out :]
    fetches = [pltpu.make_async_copy(s, h, weight_sems.at[i]) for i, (s, h) in enumerate(zip(sources, held))]
    waited = set()

    def ready(index):
        if index not in waited:
            waited.add(index)
            fetches[index].wait()

    copies = [
        pltpu.make_async_copy(piece, band.at[pl.ds(first, piece.shape[0])], sems.at[i])
        for i, (piece, first) in enumerate(inward(pieces))
    ]
    for copy in copies + fetches:
        copy.start()
    to_row = lax.broadcasted_iota(jnp.int32, bias.shape, 0)
    from_row = lax.broadcasted_iota(jnp.int32, bias.shape, 1)
    allowed = (from_row <= to_row) & (lax.rem(from_row, GROUP) == lax.rem(to_row, GROUP))
    bias[...] = jnp.where(allowed, 0.0, -1e30)
    for copy in copies:
        copy.wait()
    made = attend_frames(stacked(band[...].astype(jnp.float32)), gain[...], bias, held, ready)
    done[...] = jnp.concatenate([made[g] for g in range(made.shape[0])], axis=1).astype(jnp.bfloat16)
    chip, _ = place()
    copies = [
        pltpu.make_async_copy(
            done if n_out == 1 else done.at[pl.ds((chip ^ k) * result.shape[0], result.shape[0])], result, sems.at[k]
        )
        for k, result in enumerate(results)
    ]
    for copy in copies:
        copy.start()
    for copy in copies:
        copy.wait()


def attend(inward, n_copies, pieces, weights, frames, n_out, name):
    cols, channels = pieces[0].shape[-2:]
    rows = frames * cols
    made = frames // 2
    norm_gain, *matrices = weights
    return pl.pallas_call(
        functools.partial(attend_kernel, inward, len(pieces), n_out),
        out_shape=[jax.ShapeDtypeStruct((made // n_out, cols, channels), jnp.bfloat16)] * n_out,
        in_specs=[ANYWHERE] * len(pieces) + [INSIDE] + [ANYWHERE] * 5,
        out_specs=[ANYWHERE] * n_out,
        scratch_shapes=[
            pltpu.VMEM((frames, cols, channels), jnp.bfloat16),
            pltpu.VMEM((made, cols, channels), jnp.bfloat16),
            pltpu.VMEM((frames * GROUP, frames * GROUP), jnp.float32),
            *[pltpu.VMEM(matrix.shape, jnp.bfloat16) for matrix in matrices],
            pltpu.SemaphoreType.DMA((n_copies,)),
            pltpu.SemaphoreType.DMA((5,)),
        ],
        compiler_params=pltpu.CompilerParams(vmem_limit_bytes=20 * MIB),
        cost_estimate=pl.CostEstimate(
            flops=rows * channels * (channels * 11 + GROUP * frames * 4),
            bytes_accessed=rows * channels * 3 + channels * channels * 14,
            transcendentals=rows * frames,
        ),
        name=name,
    )(*pieces, norm_gain[None], *matrices)


def rim_kernel(chips, *refs):
    mine = refs[:chips]
    other, left, right = refs[chips:]
    _, core = place()
    made, cols, _ = other.shape[1:]
    for k in range(chips):
        own = mine[k][pl.ds(core * made, made)]
        for slot, part in ((2 * k, own), (2 * k + 1, other[k])):
            left[slot] = part[:, 0]
            right[slot] = part[:, cols - 1]


def rim(mine, other):
    chips, made, _, channels = other.shape
    return pl.pallas_call(
        functools.partial(rim_kernel, chips),
        out_shape=[jax.ShapeDtypeStruct((2 * chips, made, channels), jnp.bfloat16)] * 2,
        in_specs=[INSIDE] * (chips + 1),
        out_specs=[INSIDE] * 2,
        compiler_params=pltpu.CompilerParams(vmem_limit_bytes=4 * MIB),
        name="rim",
    )(*mine, other)


def filter_kernel(chips, *refs):
    pieces = refs[:chips]
    other, inner, left, right, w_depth, out, outer, sems = refs[chips:]
    chip, core = place()
    made = other.shape[1]
    copies = []
    for k in range(chips):
        row = 2 * (chip ^ k)
        copies.append(
            pltpu.make_async_copy(pieces[k].at[pl.ds(core * made, made)], outer.at[row + core], sems.at[2 * k])
        )
        copies.append(pltpu.make_async_copy(other.at[k], outer.at[row + 1 - core], sems.at[2 * k + 1]))
    for copy in copies:
        copy.start()
    for copy in copies:
        copy.wait()
    frames, height, cols, channels = out.shape
    edge = cols // 4
    lanes = 128

    def one_part(step, carry):
        part = pl.ds(pl.multiple_of(step * lanes, lanes), lanes)
        taps = [[w_depth[a, b, part] for b in range(3)] for a in range(3)]
        for frame in range(frames):

            def filtered(row):
                sides = outer[row, frame, :, part].astype(jnp.float32)
                between = inner[row, frame, :, part].astype(jnp.float32)
                mid = jnp.concatenate([sides[:edge], between, sides[edge:]], axis=0)
                spot = lax.broadcasted_iota(jnp.int32, mid.shape, 0)
                slot = 2 * (chip ^ (row // 2)) + (core ^ (row % 2))
                low = left[slot, frame, part].astype(jnp.float32)[None]
                high = right[slot, frame, part].astype(jnp.float32)[None]
                before = jnp.where(spot == 0, low, pltpu.roll(mid, 1, 0))
                after = jnp.where(spot == cols - 1, high, pltpu.roll(mid, cols - 1, 0))
                return [
                    before * taps[a][0][None] + mid * taps[a][1][None] + after * taps[a][2][None] for a in range(3)
                ]

            above = None
            here = filtered(0)
            for row in range(height):
                below = filtered(row + 1) if row + 1 < height else None
                total = here[1]
                if above is not None:
                    total = total + above[0]
                if below is not None:
                    total = total + below[2]
                out[frame, row, :, part] = total.astype(jnp.bfloat16)
                above, here = here, below
        return carry

    lax.fori_loop(0, channels // lanes, one_part, 0)


def depth_filter(outer, other, inner, left, right, w_depth):
    height, frames, width, channels = inner.shape
    cols = 2 * width
    size = frames * height * cols * channels
    return pl.pallas_call(
        functools.partial(filter_kernel, len(outer)),
        out_shape=jax.ShapeDtypeStruct((frames, height, cols, channels), jnp.bfloat16),
        in_specs=[ANYWHERE] * (len(outer) + 1) + [INSIDE] * 4,
        out_specs=INSIDE,
        scratch_shapes=[
            pltpu.VMEM((height, frames, width, channels), jnp.bfloat16),
            pltpu.SemaphoreType.DMA((height,)),
        ],
        compiler_params=pltpu.CompilerParams(vmem_limit_bytes=8 * MIB),
        cost_estimate=pl.CostEstimate(flops=18 * size, bytes_accessed=4 * size, transcendentals=0),
        name="depth_filter",
    )(*outer, other, inner, left, right, w_depth)


def local(video, norm_gain, w_query, w_key, w_value, w_out, w_time, w_depth):
    count = lax.axis_size("frm")
    chips = count // 2
    span, height, cols, channels = video.shape
    assert height == count and chips & (chips - 1) == 0 and chips > 1
    made = span // 2
    frames = span * count
    width = cols // 2
    weights = (norm_gain, w_query, w_key, w_value, w_out, w_time)

    def swap(block, k):
        return lax.ppermute(block, "frm", [(i, i ^ k) for i in range(count)]) if k else block

    far = list(range(chips - 1, 0, -1))
    hops = [2 * k for k in [*far, 0]]
    pieces = cut(lambda me: ([me ^ k for k in hops], [me ^ k ^ 1 for k in hops]), chips, video)
    *outer, outer_stack = pieces[: chips + 1]
    *inner, inner_stack = pieces[chips + 1 :]

    def joined(ins, outs):
        *owns, other = ins
        pairs = []
        for i, own in enumerate(owns):
            pairs.append((own, outs[i].at[pl.ds(0, span)]))
            pairs.append((other.at[i], outs[i].at[pl.ds(span, span)]))
        return pairs

    def join(owns, other, name):
        return gather(joined, 2 * len(far), [*owns[:-1], other], [(2 * span, width, channels)] * len(far), name)

    outer_other = swap(outer_stack, 1)
    outer_far = join(outer, outer_other, "join_outer")
    *outer_far, inner_stack = lax.optimization_barrier((*outer_far, inner_stack))
    outer_far = [swap(piece, k) for k, piece in zip(hops, outer_far)]
    inner_other = swap(inner_stack, 1)
    inner_far = join(inner, inner_other, "join_inner")
    outer_far[0], *inner_far = lax.optimization_barrier((outer_far[0], *inner_far))
    inner_far = [swap(piece, k) for k, piece in zip(hops, inner_far)]

    def inward(pieces):
        me = lax.axis_index("frm")
        *pieces, own, other = pieces
        pairs = []
        for k, piece in zip(hops, pieces):
            pairs.append((piece.at[pl.ds(0, span)], (me ^ k) * span))
            pairs.append((piece.at[pl.ds(span, span)], (me ^ k ^ 1) * span))
        return pairs + [(own, me * span), (other.at[len(far)], (me ^ 1) * span)]

    outer = attend(inward, count, [*outer_far, outer[-1], outer_other], weights, frames, chips, "attend_outer")
    outer = [swap(piece, 2 * k) for k, piece in enumerate(outer)]
    (inner,) = attend(inward, count, [*inner_far, inner[-1], inner_other], weights, frames, 1, "attend_inner")
    *outer, inner = lax.optimization_barrier((*outer, inner))

    def halves(ins, outs):
        _, core = place()
        return [(piece.at[pl.ds((1 - core) * made, made)], outs[0].at[k]) for k, piece in enumerate(ins)]

    outer_other = swap(gather(halves, chips, outer, [(chips, made, width, channels)], "halves")[0], 1)
    inner = lax.all_to_all(
        inner.reshape(count, made, width, channels), "frm", split_axis=0, concat_axis=0, tiled=True
    )
    low_side, high_side = rim(outer, outer_other)
    line = lax.axis_size("col")
    upward = [(i, i + 1) for i in range(line - 1)]
    left = lax.ppermute(high_side, "col", upward)
    right = lax.ppermute(low_side, "col", [(b, a) for a, b in upward])
    return depth_filter(outer, outer_other, inner, left, right, w_depth)


def solution(mesh):
    return jax.shard_map(
        local,
        mesh=mesh,
        in_specs=(P("frm", None, "col", None), P(), P(), P(), P(), P(), P(), P()),
        out_specs=P("frm", None, "col", None),
        check_vma=False,
    )
```

time: 100 us -> 90.5 us (0.905)
  waiting for transfers between devices: 38.3 us -> 31.5 us
  local copies, waits for them, and re-layouts: 5.52 us -> 1.62 us
  starting transfers between devices: 31.1 us -> 32.4 us
    all_to_all x1, waiting for transfers between devices: 16.1 us -> 3.91 us  [local(): lax.all_to_all(inner.reshape(count, made, width, channels), 'frm', split_...]
    unnamed x28 -> x16, local copies, waits for them, and re-layouts: 5.41 us -> 1.62 us
    ppermute x2, waiting for transfers between devices: 1.53 us -> 4.51 us  [the longest x1 4.23 us: local(): right = lax.ppermute(low_side, 'col', [(b, a) for a, b in upward])]
    ppermute x15 -> x12, waiting for transfers between devices: 20.7 us -> 23.1 us  [swap(): lax.ppermute(block, 'frm', [(i, i ^ k) for i in range(count)])]
    ppermute x15 -> x12, starting transfers between devices: 22.9 us -> 23.9 us  [swap(): lax.ppermute(block, 'frm', [(i, i ^ k) for i in range(count)])]
    pallas_call x2 -> x3, Pallas kernels: 2.25 us -> 2.47 us  [gather(): pl.pallas_call(functools.partial(gather_kernel, pairs_of, len(arrays)), o...]
  transfers between devices with their start and end apart: 18 -> 15, of which waited for: 9 -> 7; matrix products, arithmetic and copies ran while one was open for 0% -> 0% of each run, Pallas kernels for 21% -> 22%
where the time goes in v3:
time: 90.5 us; the launch traced here: 90.2 us
  starting transfers between devices  32.4 us (36%)
  waiting for transfers between devices  31.5 us (35%)
  Pallas kernels  24.5 us (27%)
  local copies, waits for them, and re-layouts  1.62 us (2%)
    ppermute x12, starting transfers between devices, swap(): lax.ppermute(block, 'frm', [(i, i ^ k) for i in range(count)])  23.9 us
    ppermute x12, waiting for transfers between devices, swap(): lax.ppermute(block, 'frm', [(i, i ^ k) for i in range(count)])  23.1 us
    pallas_call x2, Pallas kernels, attend(): pl.pallas_call(functools.partial(attend_kernel, inward, len(pieces), n_ou...  18.3 us
    ppermute x1, waiting for transfers between devices, local(): right = lax.ppermute(low_side, 'col', [(b, a) for a, b in upward])  4.23 us
    all_to_all x1, waiting for transfers between devices, local(): lax.all_to_all(inner.reshape(count, made, width, channels), 'frm', split_...  3.91 us
    all_to_all x1, starting transfers between devices, local(): lax.all_to_all(inner.reshape(count, made, width, channels), 'frm', split_...  3.76 us
    ppermute x1, starting transfers between devices, local(): left = lax.ppermute(high_side, 'col', upward)  3.42 us
    pallas_call x1, Pallas kernels, depth_filter(): pl.pallas_call(functools.partial(filter_kernel, len(outer)), out_shape=ja...  3.3 us
  transfers between devices with their start and end apart: 15, of which 7 were waited for; matrix products, arithmetic and copies ran while one was open for 0% of the time, Pallas kernels for 22%

profile of v3, /device:TPU:0, one launch (start us, length us, event | category | flops | bytes accessed | tf_op | source)
XLA Modules:
  0.0 90.2 jit_solution(11815560162819264594)
XLA Ops:
  0.0 0.0 copy-start
  0.0 1.6 %copy-done = bf16[8,8,32,512]{3,2,1,0:T(8,128)(2,1)S(1)} copy-done((bf16[8,8,32,512]{3,2,1,0:T(8,128)(2,1)S(1)}, bf16[8,8,32,512]{3,2,1,0:T(8,128)(2,1)}, u32[]{:S(2)}) %copy-start) | copy-done | bytes 2097176
  1.6 0.0 copy-start.2
  1.6 0.0 copy-start.3
  1.6 0.0 copy-start.4
  1.6 0.0 copy-start.5
  1.6 0.0 copy-start.6
  1.6 0.0 copy-start.7
  1.6 0.4 cut.1
  2.0 0.5 collective-permute-start
  2.5 1.5 %collective-permute-done.refs_3_.refs_4_ = bf16[4,8,16,512]{3,2,1,0:T(8,128)(2,1)S(1)} collective-permute-done((bf16[4,8,16,512]{3,2,1,0:T(8,128)(2,1)S(1)}, bf16[4,8,16,512]{3,2,1,0:T(8,128)(2,1)S(1)}, u32[]{:S(2)}, u32[]{:S(2)}) %collective-permute-start) | collective-permute-done | bytes 524320 | tf_op jit(solution)/shard_map/ppermute | solution.py:318
  4.1 1.0 %join_outer.1 = (bf16[16,16,512]{2,1,0:T(8,128)(2,1)S(1)}, bf16[16,16,512]{2,1,0:T(8,128)(2,1)S(1)}, bf16[16,16,512]{2,1,0:T(8,128)(2,1)S(1)}) custom-call(bf16[8,16,512]{2,1,0:T(8,128)(2,1)S(1)} %get-tuple-element.40.refs_0_, bf16[8,16,512]{2,1,0:T(8,128)(2,1)S(1)} %get-tuple-element.41.refs_1_, bf16[8,16,512]{2,1,0:T(8,128)(2,1)S(1)} %get-tuple-element.42.refs_2_, ...), custom_call_target="tpu_custom_call" | custom-call | bytes 1572864 | tf_op jit(solution)/shard_map/join_outer/pallas_call | solution.py:36
  5.1 0.4 collective-permute-start.2
  5.6 4.7 %collective-permute-start.1 = (bf16[16,16,512]{2,1,0:T(8,128)(2,1)S(1)}, bf16[16,16,512]{2,1,0:T(8,128)(2,1)S(1)}, u32[]{:S(2)}, u32[]{:S(2)}) collective-permute-start(bf16[16,16,512]{2,1,0:T(8,128)(2,1)S(1)} %get-tuple-element.48), channel_id=1, source_target_pairs={{0,24},{4,28},{8,16},{12,20},{16,8},{20,12},{24,0},{28,4},{1,25},{... | collective-permute-start | bytes 786440 | tf_op jit(solution)/shard_map/ppermute | solution.py:318
  10.3 0.0 collective-permute-start.3
  10.3 0.6 collective-permute-start.4
  10.9 0.0 collective-permute-done.2.refs_3_.refs_4_
  10.9 1.1 %join_inner.1 = (bf16[16,16,512]{2,1,0:T(8,128)(2,1)S(1)}, bf16[16,16,512]{2,1,0:T(8,128)(2,1)S(1)}, bf16[16,16,512]{2,1,0:T(8,128)(2,1)S(1)}) custom-call(bf16[8,16,512]{2,1,0:T(8,128)(2,1)S(1)} %get-tuple-element.49.refs_0_, bf16[8,16,512]{2,1,0:T(8,128)(2,1)S(1)} %get-tuple-element.50.refs_1_, bf16[8,16,512]{2,1,0:T(8,128)(2,1)S(1)} %get-tuple-element.51.refs_2_, ...), custom_call_target="tpu_custom_call" | custom-call | bytes 1572864 | tf_op jit(solution)/shard_map/join_inner/pallas_call | solution.py:36
  11.9 5.6 %collective-permute-done.1.refs_0_ = bf16[16,16,512]{2,1,0:T(8,128)(2,1)S(1)} collective-permute-done((bf16[16,16,512]{2,1,0:T(8,128)(2,1)S(1)}, bf16[16,16,512]{2,1,0:T(8,128)(2,1)S(1)}, u32[]{:S(2)}, u32[]{:S(2)}) %collective-permute-start.1) | collective-permute-done | bytes 262176 | tf_op jit(solution)/shard_map/ppermute | solution.py:318
  17.6 3.8 %collective-permute-start.8 = (bf16[16,16,512]{2,1,0:T(8,128)(2,1)S(1)}, bf16[16,16,512]{2,1,0:T(8,128)(2,1)S(1)}, u32[]{:S(2)}, u32[]{:S(2)}) collective-permute-start(bf16[16,16,512]{2,1,0:T(8,128)(2,1)S(1)} %get-tuple-element.64), channel_id=1, source_target_pairs={{0,24},{4,28},{8,16},{12,20},{16,8},{20,12},{24,0},{28,4},{1,25},{... | collective-permute-start | bytes 786440 | tf_op jit(solution)/shard_map/ppermute | solution.py:318
  21.4 8.7 %collective-permute-start.9 = (bf16[16,16,512]{2,1,0:T(8,128)(2,1)S(1)}, bf16[16,16,512]{2,1,0:T(8,128)(2,1)S(1)}, u32[]{:S(2)}, u32[]{:S(2)}) collective-permute-start(bf16[16,16,512]{2,1,0:T(8,128)(2,1)S(1)} %get-tuple-element.65), channel_id=1, source_target_pairs={{0,16},{4,20},{8,24},{12,28},{16,0},{20,4},{24,8},{28,12},{1,17},{... | collective-permute-start | bytes 786440 | tf_op jit(solution)/shard_map/ppermute | solution.py:318
  30.1 0.1 collective-permute-start.10
  30.2 14.8 %collective-permute-done.3.refs_1_ = bf16[16,16,512]{2,1,0:T(8,128)(2,1)S(1)} collective-permute-done((bf16[16,16,512]{2,1,0:T(8,128)(2,1)S(1)}, bf16[16,16,512]{2,1,0:T(8,128)(2,1)S(1)}, u32[]{:S(2)}, u32[]{:S(2)}) %collective-permute-start.3) | collective-permute-done | bytes 262176 | tf_op jit(solution)/shard_map/ppermute | solution.py:318
  45.0 0.0 collective-permute-done.4.refs_2_
  45.0 0.0 copy-done.2
  45.0 0.0 copy-done.3
  45.0 0.0 copy-done.4
  45.0 0.0 copy-done.5
  45.0 0.0 copy-done.6
  45.0 0.0 copy-done.7
  45.0 9.1 %attend_outer.1 = (bf16[8,16,512]{2,1,0:T(8,128)(2,1)S(1)}, bf16[8,16,512]{2,1,0:T(8,128)(2,1)S(1)}, bf16[8,16,512]{2,1,0:T(8,128)(2,1)S(1)}, bf16[8,16,512]{2,1,0:T(8,128)(2,1)S(1)}) custom-call(bf16[16,16,512]{2,1,0:T(8,128)(2,1)S(1)} %collective-permute-done.1.refs_0_, bf16[16,16,512]{2,1,0:T(8,128)(2,1)S(1)} %collective-permute-done.3.refs_1_, ...), custom_call_target="tpu_custom_call" | custom-call | flops 4026531840 | bytes 5242880 | tf_op jit(solution)/shard_map/attend_outer/pallas_call | solution.py:186
  54.1 0.1 collective-permute-start.5
  54.2 3.0 %collective-permute-start.6 = (bf16[8,16,512]{2,1,0:T(8,128)(2,1)S(1)}, bf16[8,16,512]{2,1,0:T(8,128)(2,1)S(1)}, u32[]{:S(2)}, u32[]{:S(2)}) collective-permute-start(bf16[8,16,512]{2,1,0:T(8,128)(2,1)S(1)} %get-tuple-element.62), channel_id=1, source_target_pairs={{0,16},{4,20},{8,24},{12,28},{16,0},{20,4},{24,8},{28,12},{1,17},{... | collective-permute-start | bytes 393224 | tf_op jit(solution)/shard_map/ppermute | solution.py:318
  57.2 0.0 collective-permute-done.8.refs_0_
  57.2 1.4 %collective-permute-start.7 = (bf16[8,16,512]{2,1,0:T(8,128)(2,1)S(1)}, bf16[8,16,512]{2,1,0:T(8,128)(2,1)S(1)}, u32[]{:S(2)}, u32[]{:S(2)}) collective-permute-start(bf16[8,16,512]{2,1,0:T(8,128)(2,1)S(1)} %get-tuple-element.63), channel_id=1, source_target_pairs={{0,24},{4,28},{8,16},{12,20},{16,8},{20,12},{24,0},{28,4},{1,25},{... | collective-permute-start | bytes 393224 | tf_op jit(solution)/shard_map/ppermute | solution.py:318
  58.6 0.0 collective-permute-done.9.refs_1_
  58.6 0.0 collective-permute-done.10.refs_2_
  58.6 9.2 %attend_inner.1 = bf16[32,16,512]{2,1,0:T(8,128)(2,1)} custom-call(bf16[16,16,512]{2,1,0:T(8,128)(2,1)S(1)} %collective-permute-done.8.refs_0_, bf16[16,16,512]{2,1,0:T(8,128)(2,1)S(1)} %collective-permute-done.9.refs_1_, bf16[16,16,512]{2,1,0:T(8,128)(2,1)S(1)} %collective-permute-done.10.refs_2_, bf16[8,16,512]{2,1,0:T(8,128)(2,1)S(1)} %get-tuple-element.67.refs_3_, ...), custom_call_target="tpu_custom_call" | custom-call | flops 4026531840 | bytes 5242880 | tf_op jit(solution)/shard_map/attend_inner/pallas_call | solution.py:186
  67.7 0.0 copy-start.1
  67.8 0.0 collective-permute-done.5.refs_1_
  67.8 0.0 collective-permute-done.6.refs_2_
  67.8 0.0 collective-permute-done.7.refs_3_
  67.8 3.8 %all-to-all-start = ((bf16[8,4,16,512]{3,2,1,0:T(8,128)(2,1)}), bf16[8,4,16,512]{3,2,1,0:T(8,128)(2,1)S(1)}, u32[]{:S(2)}, u32[]{:S(2)}) async-start(bf16[8,4,16,512]{3,2,1,0:T(8,128)(2,1)} %bitcast.1), calls=%async_computation | async-start | bytes 1048576 | tf_op jit(solution)/shard_map/all_to_all | solution.py:365
  71.5 0.4 halves.1
  71.9 0.6 collective-permute-start.11
  72.5 1.2 %collective-permute-done.11.refs_4_ = bf16[4,4,16,512]{3,2,1,0:T(8,128)(2,1)S(1)} collective-permute-done((bf16[4,4,16,512]{3,2,1,0:T(8,128)(2,1)S(1)}, bf16[4,4,16,512]{3,2,1,0:T(8,128)(2,1)S(1)}, u32[]{:S(2)}, u32[]{:S(2)}) %collective-permute-start.11) | collective-permute-done | bytes 262176 | tf_op jit(solution)/shard_map/ppermute | solution.py:318
  73.6 0.1 rim.1
  73.8 3.4 %collective-permute-start.12 = (bf16[8,4,512]{2,1,0:T(4,128)(2,1)S(1)}, bf16[8,4,512]{2,1,0:T(4,128)(2,1)S(1)}, u32[]{:S(2)}, u32[]{:S(2)}) collective-permute-start(bf16[8,4,512]{2,1,0:T(4,128)(2,1)S(1)} %get-tuple-element.73), channel_id=1, source_target_pairs={{0,1},{1,2},{2,3},{4,5},{5,6},{6,7},{8,9},{9,10},{10,11},{12,13},{... | collective-permute-start | bytes 98312 | tf_op jit(solution)/shard_map/ppermute | solution.py:371
  77.2 1.3 %collective-permute-start.13 = (bf16[8,4,512]{2,1,0:T(4,128)(2,1)S(1)}, bf16[8,4,512]{2,1,0:T(4,128)(2,1)S(1)}, u32[]{:S(2)}, u32[]{:S(2)}) collective-permute-start(bf16[8,4,512]{2,1,0:T(4,128)(2,1)S(1)} %get-tuple-element.74), channel_id=1, source_target_pairs={{1,0},{2,1},{3,2},{5,4},{6,5},{7,6},{9,8},{10,9},{11,10},{13,12},{... | collective-permute-start | bytes 98312 | tf_op jit(solution)/shard_map/ppermute | solution.py:372
  78.5 0.3 collective-permute-done.12.refs_6_
  78.8 4.2 %collective-permute-done.13.refs_7_ = bf16[8,4,512]{2,1,0:T(4,128)(2,1)S(1)} collective-permute-done((bf16[8,4,512]{2,1,0:T(4,128)(2,1)S(1)}, bf16[8,4,512]{2,1,0:T(4,128)(2,1)S(1)}, u32[]{:S(2)}, u32[]{:S(2)}) %collective-permute-start.13) | collective-permute-done | bytes 32800 | tf_op jit(solution)/shard_map/ppermute | solution.py:372
  83.0 3.9 %all-to-all-done.refs_5_ = bf16[8,4,16,512]{3,2,1,0:T(8,128)(2,1)S(1)} async-done(((bf16[8,4,16,512]{3,2,1,0:T(8,128)(2,1)}), bf16[8,4,16,512]{3,2,1,0:T(8,128)(2,1)S(1)}, u32[]{:S(2)}, u32[]{:S(2)}) %all-to-all-start) | async-done | bytes 524320 | tf_op jit(solution)/shard_map/all_to_all | solution.py:365
  86.9 0.0 copy-done.1
  86.9 3.3 %depth_filter.1 = bf16[4,8,32,512]{3,2,1,0:T(8,128)(2,1)} custom-call(bf16[8,16,512]{2,1,0:T(8,128)(2,1)S(1)} %get-tuple-element.68.refs_0_, bf16[8,16,512]{2,1,0:T(8,128)(2,1)S(1)} %collective-permute-done.5.refs_1_, bf16[8,16,512]{2,1,0:T(8,128)(2,1)S(1)} %collective-permute-done.6.refs_2_, bf16[8,16,512]{2,1,0:T(8,128)(2,1)S(1)} %collective-permute-done.7.refs_3_, ...), custom_call_target="tpu_custom_call" | custom-call | flops 9437184 | bytes 2097152 | tf_op jit(solution)/shard_map/depth_filter/pallas_call | solution.py:292
Async XLA Ops:
  0.0 1.6 %copy-start = (bf16[8,8,32,512]{3,2,1,0:T(8,128)(2,1)S(1)}, bf16[8,8,32,512]{3,2,1,0:T(8,128)(2,1)}, u32[]{:S(2)}) copy-start(bf16[8,8,32,512]{3,2,1,0:T(8,128)(2,1)} %video.1) | copy-start | bytes 6291460
  1.6 43.4 %copy-start.2 = (bf16[3,512,512]{2,1,0:T(8,128)(2,1)S(1)}, bf16[3,512,512]{2,1,0:T(8,128)(2,1)}, u32[]{:S(2)}) copy-start(bf16[3,512,512]{2,1,0:T(8,128)(2,1)} %refs_10_.3) | copy-start | bytes 4718596
  1.6 43.4 %copy-start.3 = (bf16[512,512]{1,0:T(8,128)(2,1)S(1)}, bf16[512,512]{1,0:T(8,128)(2,1)}, u32[]{:S(2)}) copy-start(bf16[512,512]{1,0:T(8,128)(2,1)} %refs_6_.3) | copy-start | bytes 1572868
  1.6 43.4 %copy-start.4 = (bf16[512,512]{1,0:T(8,128)(2,1)S(1)}, bf16[512,512]{1,0:T(8,128)(2,1)}, u32[]{:S(2)}) copy-start(bf16[512,512]{1,0:T(8,128)(2,1)} %refs_7_.3) | copy-start | bytes 1572868
  1.6 43.4 %copy-start.5 = (bf16[512,512]{1,0:T(8,128)(2,1)S(1)}, bf16[512,512]{1,0:T(8,128)(2,1)}, u32[]{:S(2)}) copy-start(bf16[512,512]{1,0:T(8,128)(2,1)} %refs_8_.4) | copy-start | bytes 1572868
  1.6 43.4 %copy-start.6 = (bf16[512,512]{1,0:T(8,128)(2,1)S(1)}, bf16[512,512]{1,0:T(8,128)(2,1)}, u32[]{:S(2)}) copy-start(bf16[512,512]{1,0:T(8,128)(2,1)} %refs_9_.3) | copy-start | bytes 1572868
  1.6 43.4 %copy-start.7 = (f32[512]{0:T(512)S(1)}, f32[512]{0:T(512)}, u32[]{:S(2)}) copy-start(f32[512]{0:T(512)} %param.9) | copy-start | bytes 6148
  2.0 2.1 %collective-permute-start = (bf16[4,8,16,512]{3,2,1,0:T(8,128)(2,1)S(1)}, bf16[4,8,16,512]{3,2,1,0:T(8,128)(2,1)S(1)}, u32[]{:S(2)}, u32[]{:S(2)}) collective-permute-start(bf16[4,8,16,512]{3,2,1,0:T(8,128)(2,1)S(1)} %get-tuple-element.43), channel_id=1, source_target_pairs={{0,4},{4,0},{8,12},{12,8},{16,20},{20,16},{24,28},{28,24},{1,5},{5... | collective-permute-start | bytes 1572872 | tf_op jit(solution)/shard_map/ppermute | solution.py:318
  5.1 5.8 %collective-permute-start.2 = (bf16[4,8,16,512]{3,2,1,0:T(8,128)(2,1)S(1)}, bf16[4,8,16,512]{3,2,1,0:T(8,128)(2,1)S(1)}, u32[]{:S(2)}, u32[]{:S(2)}) collective-permute-start(bf16[4,8,16,512]{3,2,1,0:T(8,128)(2,1)S(1)} %get-tuple-element.52), channel_id=1, source_target_pairs={{0,4},{4,0},{8,12},{12,8},{16,20},{20,16},{24,28},{28,24},{1,5},{5... | collective-permute-start | bytes 1572872 | tf_op jit(solution)/shard_map/ppermute | solution.py:318
  5.6 12.0 %collective-permute-start.1 = (bf16[16,16,512]{2,1,0:T(8,128)(2,1)S(1)}, bf16[16,16,512]{2,1,0:T(8,128)(2,1)S(1)}, u32[]{:S(2)}, u32[]{:S(2)}) collective-permute-start(bf16[16,16,512]{2,1,0:T(8,128)(2,1)S(1)} %get-tuple-element.48), channel_id=1, source_target_pairs={{0,24},{4,28},{8,16},{12,20},{16,8},{20,12},{24,0},{28,4},{1,25},{... | collective-permute-start | bytes 786440 | tf_op jit(solution)/shard_map/ppermute | solution.py:318
  10.3 34.7 %collective-permute-start.3 = (bf16[16,16,512]{2,1,0:T(8,128)(2,1)S(1)}, bf16[16,16,512]{2,1,0:T(8,128)(2,1)S(1)}, u32[]{:S(2)}, u32[]{:S(2)}) collective-permute-start(bf16[16,16,512]{2,1,0:T(8,128)(2,1)S(1)} %get-tuple-element.57), channel_id=1, source_target_pairs={{0,16},{4,20},{8,24},{12,28},{16,0},{20,4},{24,8},{28,12},{1,17},{... | collective-permute-start | bytes 786440 | tf_op jit(solution)/shard_map/ppermute | solution.py:318
  10.3 34.7 %collective-permute-start.4 = (bf16[16,16,512]{2,1,0:T(8,128)(2,1)S(1)}, bf16[16,16,512]{2,1,0:T(8,128)(2,1)S(1)}, u32[]{:S(2)}, u32[]{:S(2)}) collective-permute-start(bf16[16,16,512]{2,1,0:T(8,128)(2,1)S(1)} %get-tuple-element.58), channel_id=1, source_target_pairs={{0,8},{4,12},{8,0},{12,4},{16,24},{20,28},{24,16},{28,20},{1,9},{5... | collective-permute-start | bytes 786440 | tf_op jit(solution)/shard_map/ppermute | solution.py:318
  17.6 39.6 %collective-permute-start.8 = (bf16[16,16,512]{2,1,0:T(8,128)(2,1)S(1)}, bf16[16,16,512]{2,1,0:T(8,128)(2,1)S(1)}, u32[]{:S(2)}, u32[]{:S(2)}) collective-permute-start(bf16[16,16,512]{2,1,0:T(8,128)(2,1)S(1)} %get-tuple-element.64), channel_id=1, source_target_pairs={{0,24},{4,28},{8,16},{12,20},{16,8},{20,12},{24,0},{28,4},{1,25},{... | collective-permute-start | bytes 786440 | tf_op jit(solution)/shard_map/ppermute | solution.py:318
  21.4 37.2 %collective-permute-start.9 = (bf16[16,16,512]{2,1,0:T(8,128)(2,1)S(1)}, bf16[16,16,512]{2,1,0:T(8,128)(2,1)S(1)}, u32[]{:S(2)}, u32[]{:S(2)}) collective-permute-start(bf16[16,16,512]{2,1,0:T(8,128)(2,1)S(1)} %get-tuple-element.65), channel_id=1, source_target_pairs={{0,16},{4,20},{8,24},{12,28},{16,0},{20,4},{24,8},{28,12},{1,17},{... | collective-permute-start | bytes 786440 | tf_op jit(solution)/shard_map/ppermute | solution.py:318
  30.1 28.5 %collective-permute-start.10 = (bf16[16,16,512]{2,1,0:T(8,128)(2,1)S(1)}, bf16[16,16,512]{2,1,0:T(8,128)(2,1)S(1)}, u32[]{:S(2)}, u32[]{:S(2)}) collective-permute-start(bf16[16,16,512]{2,1,0:T(8,128)(2,1)S(1)} %get-tuple-element.66), channel_id=1, source_target_pairs={{0,8},{4,12},{8,0},{12,4},{16,24},{20,28},{24,16},{28,20},{1,9},{5... | collective-permute-start | bytes 786440 | tf_op jit(solution)/shard_map/ppermute | solution.py:318
  54.1 13.7 %collective-permute-start.5 = (bf16[8,16,512]{2,1,0:T(8,128)(2,1)S(1)}, bf16[8,16,512]{2,1,0:T(8,128)(2,1)S(1)}, u32[]{:S(2)}, u32[]{:S(2)}) collective-permute-start(bf16[8,16,512]{2,1,0:T(8,128)(2,1)S(1)} %get-tuple-element.61), channel_id=1, source_target_pairs={{0,8},{4,12},{8,0},{12,4},{16,24},{20,28},{24,16},{28,20},{1,9},{5... | collective-permute-start | bytes 393224 | tf_op jit(solution)/shard_map/ppermute | solution.py:318
  54.2 13.6 %collective-permute-start.6 = (bf16[8,16,512]{2,1,0:T(8,128)(2,1)S(1)}, bf16[8,16,512]{2,1,0:T(8,128)(2,1)S(1)}, u32[]{:S(2)}, u32[]{:S(2)}) collective-permute-start(bf16[8,16,512]{2,1,0:T(8,128)(2,1)S(1)} %get-tuple-element.62), channel_id=1, source_target_pairs={{0,16},{4,20},{8,24},{12,28},{16,0},{20,4},{24,8},{28,12},{1,17},{... | collective-permute-start | bytes 393224 | tf_op jit(solution)/shard_map/ppermute | solution.py:318
  57.2 10.6 %collective-permute-start.7 = (bf16[8,16,512]{2,1,0:T(8,128)(2,1)S(1)}, bf16[8,16,512]{2,1,0:T(8,128)(2,1)S(1)}, u32[]{:S(2)}, u32[]{:S(2)}) collective-permute-start(bf16[8,16,512]{2,1,0:T(8,128)(2,1)S(1)} %get-tuple-element.63), channel_id=1, source_target_pairs={{0,24},{4,28},{8,16},{12,20},{16,8},{20,12},{24,0},{28,4},{1,25},{... | collective-permute-start | bytes 393224 | tf_op jit(solution)/shard_map/ppermute | solution.py:318
  67.7 19.2 %copy-start.1 = (f32[3,3,512]{2,1,0:T(4,128)S(1)}, f32[3,3,512]{2,1,0:T(4,128)}, u32[]{:S(2)}) copy-start(f32[3,3,512]{2,1,0:T(4,128)} %refs_8_.5) | copy-start | bytes 55300
  67.8 19.1 %all-to-all-start = ((bf16[8,4,16,512]{3,2,1,0:T(8,128)(2,1)}), bf16[8,4,16,512]{3,2,1,0:T(8,128)(2,1)S(1)}, u32[]{:S(2)}, u32[]{:S(2)}) async-start(bf16[8,4,16,512]{3,2,1,0:T(8,128)(2,1)} %bitcast.1), calls=%async_computation | async-start | bytes 1048576 | tf_op jit(solution)/shard_map/all_to_all | solution.py:365
  71.9 1.7 %collective-permute-start.11 = (bf16[4,4,16,512]{3,2,1,0:T(8,128)(2,1)S(1)}, bf16[4,4,16,512]{3,2,1,0:T(8,128)(2,1)S(1)}, u32[]{:S(2)}, u32[]{:S(2)}) collective-permute-start(bf16[4,4,16,512]{3,2,1,0:T(8,128)(2,1)S(1)} %halves.1), channel_id=1, source_target_pairs={{0,4},{4,0},{8,12},{12,8},{16,20},{20,16},{24,28},{28,24},{1,5},{5... | collective-permute-start | bytes 786440 | tf_op jit(solution)/shard_map/ppermute | solution.py:318
  73.8 5.0 %collective-permute-start.12 = (bf16[8,4,512]{2,1,0:T(4,128)(2,1)S(1)}, bf16[8,4,512]{2,1,0:T(4,128)(2,1)S(1)}, u32[]{:S(2)}, u32[]{:S(2)}) collective-permute-start(bf16[8,4,512]{2,1,0:T(4,128)(2,1)S(1)} %get-tuple-element.73), channel_id=1, source_target_pairs={{0,1},{1,2},{2,3},{4,5},{5,6},{6,7},{8,9},{9,10},{10,11},{12,13},{... | collective-permute-start | bytes 98312 | tf_op jit(solution)/shard_map/ppermute | solution.py:371
  77.2 5.8 %collective-permute-start.13 = (bf16[8,4,512]{2,1,0:T(4,128)(2,1)S(1)}, bf16[8,4,512]{2,1,0:T(4,128)(2,1)S(1)}, u32[]{:S(2)}, u32[]{:S(2)}) collective-permute-start(bf16[8,4,512]{2,1,0:T(4,128)(2,1)S(1)} %get-tuple-element.74), channel_id=1, source_target_pairs={{1,0},{2,1},{3,2},{5,4},{6,5},{7,6},{9,8},{10,9},{11,10},{13,12},{... | collective-permute-start | bytes 98312 | tf_op jit(solution)/shard_map/ppermute | solution.py:372

commit v4 on v3

--- a/solution.py
+++ b/solution.py
@@ -11,6 +11,8 @@
 epsilon = 1e-06
 GROUP = 8
 BLOCKS = 2
+NORM_ROWS = 64
+SOFT_ROWS = 32
 MIB = 1024 * 1024
 ANYWHERE = pl.BlockSpec(memory_space=pl.ANY)
 INSIDE = pl.BlockSpec(memory_space=pltpu.VMEM)
@@ -87,24 +89,27 @@
     )(video)
 
 
-def stacked(x):
-    return jnp.stack([x[:, g : g + GROUP] for g in range(0, x.shape[1], GROUP)])
-
-
-def attend_frames(x, gain, bias, weights, ready):
-    w_query, w_key, w_value, w_out, w_time = weights
-    groups, frames, _, channels = x.shape
+def attend_frames(band, gain, bias, weights, ready, normed, projected, attended, mixed):
+    w_out, w_time = weights[3:]
+    frames, cols, channels = band.shape
+    groups = cols // GROUP
     rows = frames * GROUP
-    x = x.reshape(groups * rows, channels)
-    normed = (x * lax.rsqrt(jnp.mean(x * x, axis=-1, keepdims=True) + epsilon) * gain).astype(jnp.bfloat16)
-
-    def project(index):
+    tile = NORM_ROWS // GROUP
+    for first in range(0, frames, tile):
+        wide = band[first : first + tile].astype(jnp.float32)
+        for group in range(groups):
+            x = wide[:, group * GROUP : (group + 1) * GROUP].reshape(NORM_ROWS, channels)
+            x = x * lax.rsqrt(jnp.mean(x * x, axis=-1, keepdims=True) + epsilon) * gain
+            begin = group * rows + first * GROUP
+            normed[begin : begin + NORM_ROWS] = x.astype(jnp.bfloat16)
+    for index in range(3):
         ready(index)
-        return jnp.dot(normed, weights[index][...], preferred_element_type=jnp.float32).astype(jnp.bfloat16)
-
-    queries, key_proj, values = project(0), project(1), project(2)
+        projected[index] = jnp.dot(normed[...], weights[index][...], preferred_element_type=jnp.float32).astype(
+            jnp.bfloat16
+        )
+    queries, key_proj, values = projected.at[0], projected.at[1], projected.at[2]
     height = rows // BLOCKS
-    attended = []
+    power = math.log2(math.e) / math.sqrt(channels)
     for group in range(groups):
         first = group * rows
         for block in range(BLOCKS):
@@ -116,24 +121,35 @@
                 (((1,), (1,)), ((), ())),
                 preferred_element_type=jnp.float32,
             )
-            scores = scores * (1.0 / math.sqrt(channels)) + bias[begin:span, :span]
-            raised = jnp.exp(scores - jnp.max(scores, axis=-1, keepdims=True))
-            shares = (raised * (1.0 / jnp.sum(raised, axis=-1, keepdims=True))).astype(jnp.bfloat16)
-            attended.append(
-                jnp.dot(shares, values[first : first + span], preferred_element_type=jnp.float32).astype(jnp.bfloat16)
-            )
+            shares = []
+            for low in range(0, height, SOFT_ROWS):
+                part = scores[low : low + SOFT_ROWS] + bias[begin + low : begin + low + SOFT_ROWS, :span]
+                raised = jnp.exp2((part - jnp.max(part, axis=-1, keepdims=True)) * power)
+                scale = 1.0 / jnp.sum(raised, axis=-1, keepdims=True)
+                shares.append((raised * scale).astype(jnp.bfloat16))
+            attended[first + begin : first + span] = jnp.dot(
+                jnp.concatenate(shares, axis=0), values[first : first + span], preferred_element_type=jnp.float32
+            ).astype(jnp.bfloat16)
     ready(3)
-    mixed = x + jnp.dot(jnp.concatenate(attended, axis=0), w_out[...], preferred_element_type=jnp.float32)
-    mixed = mixed.reshape(groups, frames // 2, 2, GROUP, channels)
-    even = mixed[:, :, 0]
-    odd = mixed[:, :, 1]
-    prior = jnp.concatenate([even[:, :1], odd[:, :-1]], axis=1)
+    out = jnp.dot(attended[...], w_out[...], preferred_element_type=jnp.float32).reshape(
+        groups, frames, GROUP, channels
+    )
+    for group in range(groups):
+        for first in range(0, frames, tile):
+            x = band[first : first + tile, group * GROUP : (group + 1) * GROUP].astype(jnp.float32)
+            x = x + out[group, first : first + tile]
+            mixed[group, first + 1 : first + 1 + tile] = x
+            if first == 0:
+                mixed[group, 0] = x[0]
     ready(4)
-    summed = None
-    for tap, part in enumerate((prior, even, odd)):
-        part = part.reshape(groups * rows // 2, channels).astype(jnp.bfloat16)
-        term = jnp.dot(part, w_time[tap], preferred_element_type=jnp.float32)
-        summed = term if summed is None else summed + term
+    taps = []
+    for tap in range(3):
+        parts = []
+        for group in range(groups):
+            view = mixed[group, tap - tap % 2 : tap - tap % 2 + frames].reshape(frames // 2, 2, GROUP, channels)
+            parts.append(view[:, tap % 2].reshape(rows // 2, channels).astype(jnp.bfloat16))
+        taps.append(jnp.dot(jnp.concatenate(parts, axis=0), w_time[tap], preferred_element_type=jnp.float32))
+    summed = (taps[0] + taps[1]) + taps[2]
     return (summed / (1.0 + jnp.exp(-summed))).reshape(groups, frames // 2, GROUP, channels)
 
 
@@ -142,7 +158,7 @@
     gain = refs[n_in]
     sources = refs[n_in + 1 : n_in + 6]
     results = refs[n_in + 6 : n_in + 6 + n_out]
-    band, done, bias, *held, sems, weight_sems = refs[n_in + 6 + n_out :]
+    band, done, bias, normed, projected, attended, mixed, *held, sems, weight_sems = refs[n_in + 6 + n_out :]
     fetches = [pltpu.make_async_copy(s, h, weight_sems.at[i]) for i, (s, h) in enumerate(zip(sources, held))]
     waited = set()
 
@@ -159,11 +175,11 @@
         copy.start()
     to_row = lax.broadcasted_iota(jnp.int32, bias.shape, 0)
     from_row = lax.broadcasted_iota(jnp.int32, bias.shape, 1)
-    allowed = (from_row <= to_row) & (lax.rem(from_row, GROUP) == lax.rem(to_row, GROUP))
+    allowed = (from_row <= to_row) & (((from_row ^ to_row) & (GROUP - 1)) == 0)
     bias[...] = jnp.where(allowed, 0.0, -1e30)
     for copy in copies:
         copy.wait()
-    made = attend_frames(stacked(band[...].astype(jnp.float32)), gain[...], bias, held, ready)
+    made = attend_frames(band, gain[...], bias, held, ready, normed, projected, attended, mixed)
     done[...] = jnp.concatenate([made[g] for g in range(made.shape[0])], axis=1).astype(jnp.bfloat16)
     chip, _ = place()
     copies = [
@@ -192,6 +208,10 @@
             pltpu.VMEM((frames, cols, channels), jnp.bfloat16),
             pltpu.VMEM((made, cols, channels), jnp.bfloat16),
             pltpu.VMEM((frames * GROUP, frames * GROUP), jnp.float32),
+            pltpu.VMEM((rows, channels), jnp.bfloat16),
+            pltpu.VMEM((3, rows, channels), jnp.bfloat16),
+            pltpu.VMEM((rows, channels), jnp.bfloat16),
+            pltpu.VMEM((cols // GROUP, frames + 2, GROUP, channels), jnp.float32),
             *[pltpu.VMEM(matrix.shape, jnp.bfloat16) for matrix in matrices],
             pltpu.SemaphoreType.DMA((n_copies,)),
             pltpu.SemaphoreType.DMA((5,)),

time: 90.5 us -> 90.7 us (level)
  no operation moved by 1% of the time
where the time goes in v4:
time: 90.7 us; the launch traced here: 90.4 us
  starting transfers between devices  32.4 us (36%)
  waiting for transfers between devices  31.5 us (35%)
  Pallas kernels  24.7 us (27%)
  local copies, waits for them, and re-layouts  1.62 us (2%)
    ppermute x12, starting transfers between devices, swap(): lax.ppermute(block, 'frm', [(i, i ^ k) for i in range(count)])  23.9 us
    ppermute x12, waiting for transfers between devices, swap(): lax.ppermute(block, 'frm', [(i, i ^ k) for i in range(count)])  23.1 us
    pallas_call x2, Pallas kernels, attend(): pl.pallas_call(functools.partial(attend_kernel, inward, len(pieces), n_ou...  18.4 us
    ppermute x1, waiting for transfers between devices, local(): right = lax.ppermute(low_side, 'col', [(b, a) for a, b in upward])  4.23 us
    all_to_all x1, waiting for transfers between devices, local(): lax.all_to_all(inner.reshape(count, made, width, channels), 'frm', split_...  3.92 us
    all_to_all x1, starting transfers between devices, local(): lax.all_to_all(inner.reshape(count, made, width, channels), 'frm', split_...  3.76 us
    ppermute x1, starting transfers between devices, local(): left = lax.ppermute(high_side, 'col', upward)  3.41 us
    pallas_call x1, Pallas kernels, depth_filter(): pl.pallas_call(functools.partial(filter_kernel, len(outer)), out_shape=ja...  3.3 us
  transfers between devices with their start and end apart: 15, of which 7 were waited for; matrix products, arithmetic and copies ran while one was open for 0% of the time, Pallas kernels for 22%

profile of v4, /device:TPU:0, one launch (start us, length us, event | category | flops | bytes accessed | tf_op | source)
XLA Modules:
  0.0 90.4 jit_solution(6286220710791326553)
XLA Ops:
  0.0 0.0 copy-start
  0.0 1.6 %copy-done = bf16[8,8,32,512]{3,2,1,0:T(8,128)(2,1)S(1)} copy-done((bf16[8,8,32,512]{3,2,1,0:T(8,128)(2,1)S(1)}, bf16[8,8,32,512]{3,2,1,0:T(8,128)(2,1)}, u32[]{:S(2)}) %copy-start) | copy-done | bytes 2097176
  1.6 0.0 copy-start.2
  1.6 0.0 copy-start.3
  1.6 0.0 copy-start.4
  1.6 0.0 copy-start.5
  1.6 0.0 copy-start.6
  1.6 0.0 copy-start.7
  1.6 0.4 cut.1
  2.0 0.5 collective-permute-start
  2.5 1.5 %collective-permute-done.refs_3_.refs_4_ = bf16[4,8,16,512]{3,2,1,0:T(8,128)(2,1)S(1)} collective-permute-done((bf16[4,8,16,512]{3,2,1,0:T(8,128)(2,1)S(1)}, bf16[4,8,16,512]{3,2,1,0:T(8,128)(2,1)S(1)}, u32[]{:S(2)}, u32[]{:S(2)}) %collective-permute-start) | collective-permute-done | bytes 524320 | tf_op jit(solution)/shard_map/ppermute | solution.py:338
  4.1 1.0 %join_outer.1 = (bf16[16,16,512]{2,1,0:T(8,128)(2,1)S(1)}, bf16[16,16,512]{2,1,0:T(8,128)(2,1)S(1)}, bf16[16,16,512]{2,1,0:T(8,128)(2,1)S(1)}) custom-call(bf16[8,16,512]{2,1,0:T(8,128)(2,1)S(1)} %get-tuple-element.40.refs_0_, bf16[8,16,512]{2,1,0:T(8,128)(2,1)S(1)} %get-tuple-element.41.refs_1_, bf16[8,16,512]{2,1,0:T(8,128)(2,1)S(1)} %get-tuple-element.42.refs_2_, ...), custom_call_target="tpu_custom_call" | custom-call | bytes 1572864 | tf_op jit(solution)/shard_map/join_outer/pallas_call | solution.py:38
  5.1 0.4 collective-permute-start.2
  5.6 4.7 %collective-permute-start.1 = (bf16[16,16,512]{2,1,0:T(8,128)(2,1)S(1)}, bf16[16,16,512]{2,1,0:T(8,128)(2,1)S(1)}, u32[]{:S(2)}, u32[]{:S(2)}) collective-permute-start(bf16[16,16,512]{2,1,0:T(8,128)(2,1)S(1)} %get-tuple-element.48), channel_id=1, source_target_pairs={{0,24},{4,28},{8,16},{12,20},{16,8},{20,12},{24,0},{28,4},{1,25},{... | collective-permute-start | bytes 786440 | tf_op jit(solution)/shard_map/ppermute | solution.py:338
  10.3 0.0 collective-permute-start.3
  10.3 0.6 collective-permute-start.4
  10.9 0.0 collective-permute-done.2.refs_3_.refs_4_
  10.9 1.1 %join_inner.1 = (bf16[16,16,512]{2,1,0:T(8,128)(2,1)S(1)}, bf16[16,16,512]{2,1,0:T(8,128)(2,1)S(1)}, bf16[16,16,512]{2,1,0:T(8,128)(2,1)S(1)}) custom-call(bf16[8,16,512]{2,1,0:T(8,128)(2,1)S(1)} %get-tuple-element.49.refs_0_, bf16[8,16,512]{2,1,0:T(8,128)(2,1)S(1)} %get-tuple-element.50.refs_1_, bf16[8,16,512]{2,1,0:T(8,128)(2,1)S(1)} %get-tuple-element.51.refs_2_, ...), custom_call_target="tpu_custom_call" | custom-call | bytes 1572864 | tf_op jit(solution)/shard_map/join_inner/pallas_call | solution.py:38
  11.9 5.6 %collective-permute-done.1.refs_0_ = bf16[16,16,512]{2,1,0:T(8,128)(2,1)S(1)} collective-permute-done((bf16[16,16,512]{2,1,0:T(8,128)(2,1)S(1)}, bf16[16,16,512]{2,1,0:T(8,128)(2,1)S(1)}, u32[]{:S(2)}, u32[]{:S(2)}) %collective-permute-start.1) | collective-permute-done | bytes 262176 | tf_op jit(solution)/shard_map/ppermute | solution.py:338
  17.6 3.8 %collective-permute-start.8 = (bf16[16,16,512]{2,1,0:T(8,128)(2,1)S(1)}, bf16[16,16,512]{2,1,0:T(8,128)(2,1)S(1)}, u32[]{:S(2)}, u32[]{:S(2)}) collective-permute-start(bf16[16,16,512]{2,1,0:T(8,128)(2,1)S(1)} %get-tuple-element.64), channel_id=1, source_target_pairs={{0,24},{4,28},{8,16},{12,20},{16,8},{20,12},{24,0},{28,4},{1,25},{... | collective-permute-start | bytes 786440 | tf_op jit(solution)/shard_map/ppermute | solution.py:338
  21.4 8.7 %collective-permute-start.9 = (bf16[16,16,512]{2,1,0:T(8,128)(2,1)S(1)}, bf16[16,16,512]{2,1,0:T(8,128)(2,1)S(1)}, u32[]{:S(2)}, u32[]{:S(2)}) collective-permute-start(bf16[16,16,512]{2,1,0:T(8,128)(2,1)S(1)} %get-tuple-element.65), channel_id=1, source_target_pairs={{0,16},{4,20},{8,24},{12,28},{16,0},{20,4},{24,8},{28,12},{1,17},{... | collective-permute-start | bytes 786440 | tf_op jit(solution)/shard_map/ppermute | solution.py:338
  30.1 0.1 collective-permute-start.10
  30.2 14.8 %collective-permute-done.3.refs_1_ = bf16[16,16,512]{2,1,0:T(8,128)(2,1)S(1)} collective-permute-done((bf16[16,16,512]{2,1,0:T(8,128)(2,1)S(1)}, bf16[16,16,512]{2,1,0:T(8,128)(2,1)S(1)}, u32[]{:S(2)}, u32[]{:S(2)}) %collective-permute-start.3) | collective-permute-done | bytes 262176 | tf_op jit(solution)/shard_map/ppermute | solution.py:338
  45.0 0.0 collective-permute-done.4.refs_2_
  45.0 0.0 copy-done.2
  45.0 0.0 copy-done.3
  45.0 0.0 copy-done.4
  45.0 0.0 copy-done.5
  45.0 0.0 copy-done.6
  45.0 0.0 copy-done.7
  45.0 9.2 %attend_outer.1 = (bf16[8,16,512]{2,1,0:T(8,128)(2,1)S(1)}, bf16[8,16,512]{2,1,0:T(8,128)(2,1)S(1)}, bf16[8,16,512]{2,1,0:T(8,128)(2,1)S(1)}, bf16[8,16,512]{2,1,0:T(8,128)(2,1)S(1)}) custom-call(bf16[16,16,512]{2,1,0:T(8,128)(2,1)S(1)} %collective-permute-done.1.refs_0_, bf16[16,16,512]{2,1,0:T(8,128)(2,1)S(1)} %collective-permute-done.3.refs_1_, ...), custom_call_target="tpu_custom_call" | custom-call | flops 4026531840 | bytes 5242880 | tf_op jit(solution)/shard_map/attend_outer/pallas_call | solution.py:202
  54.2 0.1 collective-permute-start.5
  54.3 3.0 %collective-permute-start.6 = (bf16[8,16,512]{2,1,0:T(8,128)(2,1)S(1)}, bf16[8,16,512]{2,1,0:T(8,128)(2,1)S(1)}, u32[]{:S(2)}, u32[]{:S(2)}) collective-permute-start(bf16[8,16,512]{2,1,0:T(8,128)(2,1)S(1)} %get-tuple-element.62), channel_id=1, source_target_pairs={{0,16},{4,20},{8,24},{12,28},{16,0},{20,4},{24,8},{28,12},{1,17},{... | collective-permute-start | bytes 393224 | tf_op jit(solution)/shard_map/ppermute | solution.py:338
  57.3 0.0 collective-permute-done.8.refs_0_
  57.3 1.3 %collective-permute-start.7 = (bf16[8,16,512]{2,1,0:T(8,128)(2,1)S(1)}, bf16[8,16,512]{2,1,0:T(8,128)(2,1)S(1)}, u32[]{:S(2)}, u32[]{:S(2)}) collective-permute-start(bf16[8,16,512]{2,1,0:T(8,128)(2,1)S(1)} %get-tuple-element.63), channel_id=1, source_target_pairs={{0,24},{4,28},{8,16},{12,20},{16,8},{20,12},{24,0},{28,4},{1,25},{... | collective-permute-start | bytes 393224 | tf_op jit(solution)/shard_map/ppermute | solution.py:338
  58.6 0.0 collective-permute-done.9.refs_1_
  58.6 0.0 collective-permute-done.10.refs_2_
  58.7 9.3 %attend_inner.1 = bf16[32,16,512]{2,1,0:T(8,128)(2,1)} custom-call(bf16[16,16,512]{2,1,0:T(8,128)(2,1)S(1)} %collective-permute-done.8.refs_0_, bf16[16,16,512]{2,1,0:T(8,128)(2,1)S(1)} %collective-permute-done.9.refs_1_, bf16[16,16,512]{2,1,0:T(8,128)(2,1)S(1)} %collective-permute-done.10.refs_2_, bf16[8,16,512]{2,1,0:T(8,128)(2,1)S(1)} %get-tuple-element.67.refs_3_, ...), custom_call_target="tpu_custom_call" | custom-call | flops 4026531840 | bytes 5242880 | tf_op jit(solution)/shard_map/attend_inner/pallas_call | solution.py:202
  67.9 0.0 copy-start.1
  67.9 0.0 collective-permute-done.5.refs_1_
  67.9 0.0 collective-permute-done.6.refs_2_
  67.9 0.0 collective-permute-done.7.refs_3_
  68.0 3.8 %all-to-all-start = ((bf16[8,4,16,512]{3,2,1,0:T(8,128)(2,1)}), bf16[8,4,16,512]{3,2,1,0:T(8,128)(2,1)S(1)}, u32[]{:S(2)}, u32[]{:S(2)}) async-start(bf16[8,4,16,512]{3,2,1,0:T(8,128)(2,1)} %bitcast.1), calls=%async_computation | async-start | bytes 1048576 | tf_op jit(solution)/shard_map/all_to_all | solution.py:385
  71.7 0.4 halves.1
  72.1 0.6 collective-permute-start.11
  72.7 1.2 %collective-permute-done.11.refs_4_ = bf16[4,4,16,512]{3,2,1,0:T(8,128)(2,1)S(1)} collective-permute-done((bf16[4,4,16,512]{3,2,1,0:T(8,128)(2,1)S(1)}, bf16[4,4,16,512]{3,2,1,0:T(8,128)(2,1)S(1)}, u32[]{:S(2)}, u32[]{:S(2)}) %collective-permute-start.11) | collective-permute-done | bytes 262176 | tf_op jit(solution)/shard_map/ppermute | solution.py:338
  73.8 0.1 rim.1
  73.9 3.4 %collective-permute-start.12 = (bf16[8,4,512]{2,1,0:T(4,128)(2,1)S(1)}, bf16[8,4,512]{2,1,0:T(4,128)(2,1)S(1)}, u32[]{:S(2)}, u32[]{:S(2)}) collective-permute-start(bf16[8,4,512]{2,1,0:T(4,128)(2,1)S(1)} %get-tuple-element.73), channel_id=1, source_target_pairs={{0,1},{1,2},{2,3},{4,5},{5,6},{6,7},{8,9},{9,10},{10,11},{12,13},{... | collective-permute-start | bytes 98312 | tf_op jit(solution)/shard_map/ppermute | solution.py:391
  77.4 1.3 %collective-permute-start.13 = (bf16[8,4,512]{2,1,0:T(4,128)(2,1)S(1)}, bf16[8,4,512]{2,1,0:T(4,128)(2,1)S(1)}, u32[]{:S(2)}, u32[]{:S(2)}) collective-permute-start(bf16[8,4,512]{2,1,0:T(4,128)(2,1)S(1)} %get-tuple-element.74), channel_id=1, source_target_pairs={{1,0},{2,1},{3,2},{5,4},{6,5},{7,6},{9,8},{10,9},{11,10},{13,12},{... | collective-permute-start | bytes 98312 | tf_op jit(solution)/shard_map/ppermute | solution.py:392
  78.7 0.3 collective-permute-done.12.refs_6_
  78.9 4.2 %collective-permute-done.13.refs_7_ = bf16[8,4,512]{2,1,0:T(4,128)(2,1)S(1)} collective-permute-done((bf16[8,4,512]{2,1,0:T(4,128)(2,1)S(1)}, bf16[8,4,512]{2,1,0:T(4,128)(2,1)S(1)}, u32[]{:S(2)}, u32[]{:S(2)}) %collective-permute-start.13) | collective-permute-done | bytes 32800 | tf_op jit(solution)/shard_map/ppermute | solution.py:392
  83.2 3.9 %all-to-all-done.refs_5_ = bf16[8,4,16,512]{3,2,1,0:T(8,128)(2,1)S(1)} async-done(((bf16[8,4,16,512]{3,2,1,0:T(8,128)(2,1)}), bf16[8,4,16,512]{3,2,1,0:T(8,128)(2,1)S(1)}, u32[]{:S(2)}, u32[]{:S(2)}) %all-to-all-start) | async-done | bytes 524320 | tf_op jit(solution)/shard_map/all_to_all | solution.py:385
  87.1 0.0 copy-done.1
  87.1 3.3 %depth_filter.1 = bf16[4,8,32,512]{3,2,1,0:T(8,128)(2,1)} custom-call(bf16[8,16,512]{2,1,0:T(8,128)(2,1)S(1)} %get-tuple-element.68.refs_0_, bf16[8,16,512]{2,1,0:T(8,128)(2,1)S(1)} %collective-permute-done.5.refs_1_, bf16[8,16,512]{2,1,0:T(8,128)(2,1)S(1)} %collective-permute-done.6.refs_2_, bf16[8,16,512]{2,1,0:T(8,128)(2,1)S(1)} %collective-permute-done.7.refs_3_, ...), custom_call_target="tpu_custom_call" | custom-call | flops 9437184 | bytes 2097152 | tf_op jit(solution)/shard_map/depth_filter/pallas_call | solution.py:312
Async XLA Ops:
  0.0 1.6 %copy-start = (bf16[8,8,32,512]{3,2,1,0:T(8,128)(2,1)S(1)}, bf16[8,8,32,512]{3,2,1,0:T(8,128)(2,1)}, u32[]{:S(2)}) copy-start(bf16[8,8,32,512]{3,2,1,0:T(8,128)(2,1)} %video.1) | copy-start | bytes 6291460
  1.6 43.4 %copy-start.2 = (bf16[3,512,512]{2,1,0:T(8,128)(2,1)S(1)}, bf16[3,512,512]{2,1,0:T(8,128)(2,1)}, u32[]{:S(2)}) copy-start(bf16[3,512,512]{2,1,0:T(8,128)(2,1)} %refs_10_.3) | copy-start | bytes 4718596
  1.6 43.4 %copy-start.3 = (bf16[512,512]{1,0:T(8,128)(2,1)S(1)}, bf16[512,512]{1,0:T(8,128)(2,1)}, u32[]{:S(2)}) copy-start(bf16[512,512]{1,0:T(8,128)(2,1)} %refs_6_.3) | copy-start | bytes 1572868
  1.6 43.4 %copy-start.4 = (bf16[512,512]{1,0:T(8,128)(2,1)S(1)}, bf16[512,512]{1,0:T(8,128)(2,1)}, u32[]{:S(2)}) copy-start(bf16[512,512]{1,0:T(8,128)(2,1)} %refs_7_.3) | copy-start | bytes 1572868
  1.6 43.4 %copy-start.5 = (bf16[512,512]{1,0:T(8,128)(2,1)S(1)}, bf16[512,512]{1,0:T(8,128)(2,1)}, u32[]{:S(2)}) copy-start(bf16[512,512]{1,0:T(8,128)(2,1)} %refs_8_.4) | copy-start | bytes 1572868
  1.6 43.4 %copy-start.6 = (bf16[512,512]{1,0:T(8,128)(2,1)S(1)}, bf16[512,512]{1,0:T(8,128)(2,1)}, u32[]{:S(2)}) copy-start(bf16[512,512]{1,0:T(8,128)(2,1)} %refs_9_.3) | copy-start | bytes 1572868
  1.6 43.4 %copy-start.7 = (f32[512]{0:T(512)S(1)}, f32[512]{0:T(512)}, u32[]{:S(2)}) copy-start(f32[512]{0:T(512)} %param.9) | copy-start | bytes 6148
  2.0 2.1 %collective-permute-start = (bf16[4,8,16,512]{3,2,1,0:T(8,128)(2,1)S(1)}, bf16[4,8,16,512]{3,2,1,0:T(8,128)(2,1)S(1)}, u32[]{:S(2)}, u32[]{:S(2)}) collective-permute-start(bf16[4,8,16,512]{3,2,1,0:T(8,128)(2,1)S(1)} %get-tuple-element.43), channel_id=1, source_target_pairs={{0,4},{4,0},{8,12},{12,8},{16,20},{20,16},{24,28},{28,24},{1,5},{5... | collective-permute-start | bytes 1572872 | tf_op jit(solution)/shard_map/ppermute | solution.py:338
  5.1 5.8 %collective-permute-start.2 = (bf16[4,8,16,512]{3,2,1,0:T(8,128)(2,1)S(1)}, bf16[4,8,16,512]{3,2,1,0:T(8,128)(2,1)S(1)}, u32[]{:S(2)}, u32[]{:S(2)}) collective-permute-start(bf16[4,8,16,512]{3,2,1,0:T(8,128)(2,1)S(1)} %get-tuple-element.52), channel_id=1, source_target_pairs={{0,4},{4,0},{8,12},{12,8},{16,20},{20,16},{24,28},{28,24},{1,5},{5... | collective-permute-start | bytes 1572872 | tf_op jit(solution)/shard_map/ppermute | solution.py:338
  5.6 12.0 %collective-permute-start.1 = (bf16[16,16,512]{2,1,0:T(8,128)(2,1)S(1)}, bf16[16,16,512]{2,1,0:T(8,128)(2,1)S(1)}, u32[]{:S(2)}, u32[]{:S(2)}) collective-permute-start(bf16[16,16,512]{2,1,0:T(8,128)(2,1)S(1)} %get-tuple-element.48), channel_id=1, source_target_pairs={{0,24},{4,28},{8,16},{12,20},{16,8},{20,12},{24,0},{28,4},{1,25},{... | collective-permute-start | bytes 786440 | tf_op jit(solution)/shard_map/ppermute | solution.py:338
  10.3 34.7 %collective-permute-start.3 = (bf16[16,16,512]{2,1,0:T(8,128)(2,1)S(1)}, bf16[16,16,512]{2,1,0:T(8,128)(2,1)S(1)}, u32[]{:S(2)}, u32[]{:S(2)}) collective-permute-start(bf16[16,16,512]{2,1,0:T(8,128)(2,1)S(1)} %get-tuple-element.57), channel_id=1, source_target_pairs={{0,16},{4,20},{8,24},{12,28},{16,0},{20,4},{24,8},{28,12},{1,17},{... | collective-permute-start | bytes 786440 | tf_op jit(solution)/shard_map/ppermute | solution.py:338
  10.3 34.7 %collective-permute-start.4 = (bf16[16,16,512]{2,1,0:T(8,128)(2,1)S(1)}, bf16[16,16,512]{2,1,0:T(8,128)(2,1)S(1)}, u32[]{:S(2)}, u32[]{:S(2)}) collective-permute-start(bf16[16,16,512]{2,1,0:T(8,128)(2,1)S(1)} %get-tuple-element.58), channel_id=1, source_target_pairs={{0,8},{4,12},{8,0},{12,4},{16,24},{20,28},{24,16},{28,20},{1,9},{5... | collective-permute-start | bytes 786440 | tf_op jit(solution)/shard_map/ppermute | solution.py:338
  17.6 39.7 %collective-permute-start.8 = (bf16[16,16,512]{2,1,0:T(8,128)(2,1)S(1)}, bf16[16,16,512]{2,1,0:T(8,128)(2,1)S(1)}, u32[]{:S(2)}, u32[]{:S(2)}) collective-permute-start(bf16[16,16,512]{2,1,0:T(8,128)(2,1)S(1)} %get-tuple-element.64), channel_id=1, source_target_pairs={{0,24},{4,28},{8,16},{12,20},{16,8},{20,12},{24,0},{28,4},{1,25},{... | collective-permute-start | bytes 786440 | tf_op jit(solution)/shard_map/ppermute | solution.py:338
  21.4 37.3 %collective-permute-start.9 = (bf16[16,16,512]{2,1,0:T(8,128)(2,1)S(1)}, bf16[16,16,512]{2,1,0:T(8,128)(2,1)S(1)}, u32[]{:S(2)}, u32[]{:S(2)}) collective-permute-start(bf16[16,16,512]{2,1,0:T(8,128)(2,1)S(1)} %get-tuple-element.65), channel_id=1, source_target_pairs={{0,16},{4,20},{8,24},{12,28},{16,0},{20,4},{24,8},{28,12},{1,17},{... | collective-permute-start | bytes 786440 | tf_op jit(solution)/shard_map/ppermute | solution.py:338
  30.1 28.6 %collective-permute-start.10 = (bf16[16,16,512]{2,1,0:T(8,128)(2,1)S(1)}, bf16[16,16,512]{2,1,0:T(8,128)(2,1)S(1)}, u32[]{:S(2)}, u32[]{:S(2)}) collective-permute-start(bf16[16,16,512]{2,1,0:T(8,128)(2,1)S(1)} %get-tuple-element.66), channel_id=1, source_target_pairs={{0,8},{4,12},{8,0},{12,4},{16,24},{20,28},{24,16},{28,20},{1,9},{5... | collective-permute-start | bytes 786440 | tf_op jit(solution)/shard_map/ppermute | solution.py:338
  54.2 13.7 %collective-permute-start.5 = (bf16[8,16,512]{2,1,0:T(8,128)(2,1)S(1)}, bf16[8,16,512]{2,1,0:T(8,128)(2,1)S(1)}, u32[]{:S(2)}, u32[]{:S(2)}) collective-permute-start(bf16[8,16,512]{2,1,0:T(8,128)(2,1)S(1)} %get-tuple-element.61), channel_id=1, source_target_pairs={{0,8},{4,12},{8,0},{12,4},{16,24},{20,28},{24,16},{28,20},{1,9},{5... | collective-permute-start | bytes 393224 | tf_op jit(solution)/shard_map/ppermute | solution.py:338
  54.3 13.7 %collective-permute-start.6 = (bf16[8,16,512]{2,1,0:T(8,128)(2,1)S(1)}, bf16[8,16,512]{2,1,0:T(8,128)(2,1)S(1)}, u32[]{:S(2)}, u32[]{:S(2)}) collective-permute-start(bf16[8,16,512]{2,1,0:T(8,128)(2,1)S(1)} %get-tuple-element.62), channel_id=1, source_target_pairs={{0,16},{4,20},{8,24},{12,28},{16,0},{20,4},{24,8},{28,12},{1,17},{... | collective-permute-start | bytes 393224 | tf_op jit(solution)/shard_map/ppermute | solution.py:338
  57.3 10.7 %collective-permute-start.7 = (bf16[8,16,512]{2,1,0:T(8,128)(2,1)S(1)}, bf16[8,16,512]{2,1,0:T(8,128)(2,1)S(1)}, u32[]{:S(2)}, u32[]{:S(2)}) collective-permute-start(bf16[8,16,512]{2,1,0:T(8,128)(2,1)S(1)} %get-tuple-element.63), channel_id=1, source_target_pairs={{0,24},{4,28},{8,16},{12,20},{16,8},{20,12},{24,0},{28,4},{1,25},{... | collective-permute-start | bytes 393224 | tf_op jit(solution)/shard_map/ppermute | solution.py:338
  67.9 19.2 %copy-start.1 = (f32[3,3,512]{2,1,0:T(4,128)S(1)}, f32[3,3,512]{2,1,0:T(4,128)}, u32[]{:S(2)}) copy-start(f32[3,3,512]{2,1,0:T(4,128)} %refs_8_.5) | copy-start | bytes 55300
  68.0 19.1 %all-to-all-start = ((bf16[8,4,16,512]{3,2,1,0:T(8,128)(2,1)}), bf16[8,4,16,512]{3,2,1,0:T(8,128)(2,1)S(1)}, u32[]{:S(2)}, u32[]{:S(2)}) async-start(bf16[8,4,16,512]{3,2,1,0:T(8,128)(2,1)} %bitcast.1), calls=%async_computation | async-start | bytes 1048576 | tf_op jit(solution)/shard_map/all_to_all | solution.py:385
  72.1 1.7 %collective-permute-start.11 = (bf16[4,4,16,512]{3,2,1,0:T(8,128)(2,1)S(1)}, bf16[4,4,16,512]{3,2,1,0:T(8,128)(2,1)S(1)}, u32[]{:S(2)}, u32[]{:S(2)}) collective-permute-start(bf16[4,4,16,512]{3,2,1,0:T(8,128)(2,1)S(1)} %halves.1), channel_id=1, source_target_pairs={{0,4},{4,0},{8,12},{12,8},{16,20},{20,16},{24,28},{28,24},{1,5},{5... | collective-permute-start | bytes 786440 | tf_op jit(solution)/shard_map/ppermute | solution.py:338
  73.9 5.0 %collective-permute-start.12 = (bf16[8,4,512]{2,1,0:T(4,128)(2,1)S(1)}, bf16[8,4,512]{2,1,0:T(4,128)(2,1)S(1)}, u32[]{:S(2)}, u32[]{:S(2)}) collective-permute-start(bf16[8,4,512]{2,1,0:T(4,128)(2,1)S(1)} %get-tuple-element.73), channel_id=1, source_target_pairs={{0,1},{1,2},{2,3},{4,5},{5,6},{6,7},{8,9},{9,10},{10,11},{12,13},{... | collective-permute-start | bytes 98312 | tf_op jit(solution)/shard_map/ppermute | solution.py:391
  77.4 5.8 %collective-permute-start.13 = (bf16[8,4,512]{2,1,0:T(4,128)(2,1)S(1)}, bf16[8,4,512]{2,1,0:T(4,128)(2,1)S(1)}, u32[]{:S(2)}, u32[]{:S(2)}) collective-permute-start(bf16[8,4,512]{2,1,0:T(4,128)(2,1)S(1)} %get-tuple-element.74), channel_id=1, source_target_pairs={{1,0},{2,1},{3,2},{5,4},{6,5},{7,6},{9,8},{10,9},{11,10},{13,12},{... | collective-permute-start | bytes 98312 | tf_op jit(solution)/shard_map/ppermute | solution.py:392

commit v5 on v4

--- a/solution.py
+++ b/solution.py
@@ -11,10 +11,9 @@
 epsilon = 1e-06
 GROUP = 8
 BLOCKS = 2
-NORM_ROWS = 64
+TILE = 8
 SOFT_ROWS = 32
 MIB = 1024 * 1024
-ANYWHERE = pl.BlockSpec(memory_space=pl.ANY)
 INSIDE = pl.BlockSpec(memory_space=pltpu.VMEM)
 
 
@@ -24,45 +23,32 @@
 
 
 def gather_kernel(pairs_of, n_in, *refs):
-    *arrays, sems = refs
-    pairs = pairs_of(arrays[:n_in], arrays[n_in:])
-    copies = [pltpu.make_async_copy(source, target, sems.at[i]) for i, (source, target) in enumerate(pairs)]
-    for copy in copies:
-        copy.start()
-    for copy in copies:
-        copy.wait()
-
-
-def gather(pairs_of, n_pairs, arrays, shapes, name):
+    for source, target in pairs_of(refs[:n_in], refs[n_in:]):
+        target[...] = source[...]
+
+
+def gather(pairs_of, arrays, shapes, name):
     size = sum(math.prod(shape) for shape in shapes)
     return pl.pallas_call(
         functools.partial(gather_kernel, pairs_of, len(arrays)),
         out_shape=[jax.ShapeDtypeStruct(shape, jnp.bfloat16) for shape in shapes],
-        in_specs=[ANYWHERE] * len(arrays),
+        in_specs=[INSIDE] * len(arrays),
         out_specs=[INSIDE] * len(shapes),
-        scratch_shapes=[pltpu.SemaphoreType.DMA((n_pairs,))],
-        compiler_params=pltpu.CompilerParams(vmem_limit_bytes=4 * MIB),
+        compiler_params=pltpu.CompilerParams(vmem_limit_bytes=6 * MIB),
         cost_estimate=pl.CostEstimate(flops=0, bytes_accessed=4 * size, transcendentals=0),
         name=name,
     )(*arrays)
 
 
-def cut_kernel(rows_of, video, *refs):
-    *results, held, sems = refs
-    span, height, cols = held.shape[1], held.shape[0], held.shape[2]
-    edge = cols // 4
-    copies = [pltpu.make_async_copy(video.at[:, row], held.at[row], sems.at[row]) for row in range(height)]
-    for copy in copies:
-        copy.start()
-    for copy in copies:
-        copy.wait()
+def cut_kernel(rows_of, video, *results):
+    edge = video.shape[2] // 4
     half = len(results) // 2
     own, other = rows_of(lax.axis_index("frm"))
     for rim in (True, False):
         *singles, stack = results[:half] if rim else results[half:]
-        targets = singles + [stack.at[k] for k in range(stack.shape[0])]
+        targets = list(singles) + [stack.at[k] for k in range(stack.shape[0])]
         for row, target in zip(own + other, targets):
-            values = held[row].astype(jnp.float32)
+            values = video[:, row].astype(jnp.float32)
             if rim:
                 values = jnp.concatenate([values[:, :edge], values[:, 3 * edge :]], axis=1)
             else:
@@ -77,36 +63,31 @@
     return pl.pallas_call(
         functools.partial(cut_kernel, rows_of),
         out_shape=[jax.ShapeDtypeStruct(shape, jnp.bfloat16) for shape in shapes],
-        in_specs=[ANYWHERE],
+        in_specs=[INSIDE],
         out_specs=[INSIDE] * len(shapes),
-        scratch_shapes=[
-            pltpu.VMEM((height, span, cols, channels), jnp.bfloat16),
-            pltpu.SemaphoreType.DMA((height,)),
-        ],
         compiler_params=pltpu.CompilerParams(vmem_limit_bytes=12 * MIB),
         cost_estimate=pl.CostEstimate(flops=0, bytes_accessed=3 * video.size, transcendentals=0),
         name="cut",
     )(video)
 
 
-def attend_frames(band, gain, bias, weights, ready, normed, projected, attended, mixed):
-    w_out, w_time = weights[3:]
-    frames, cols, channels = band.shape
-    groups = cols // GROUP
+def attend_frames(pieces, gain, bias, weights, normed, projected, attended, mixed):
+    w_query, w_key, w_value, w_out, w_time = weights
+    groups, frames, _, channels = mixed.shape
+    frames = frames - 2
     rows = frames * GROUP
-    tile = NORM_ROWS // GROUP
-    for first in range(0, frames, tile):
-        wide = band[first : first + tile].astype(jnp.float32)
+    for piece, first in pieces:
+        wide = piece[...].astype(jnp.float32)
+        span = wide.shape[0]
         for group in range(groups):
-            x = wide[:, group * GROUP : (group + 1) * GROUP].reshape(NORM_ROWS, channels)
+            x = wide[:, group * GROUP : (group + 1) * GROUP]
+            mixed[group, pl.ds(first + 1, span)] = x
+            x = x.reshape(span * GROUP, channels)
             x = x * lax.rsqrt(jnp.mean(x * x, axis=-1, keepdims=True) + epsilon) * gain
-            begin = group * rows + first * GROUP
-            normed[begin : begin + NORM_ROWS] = x.astype(jnp.bfloat16)
-    for index in range(3):
-        ready(index)
-        projected[index] = jnp.dot(normed[...], weights[index][...], preferred_element_type=jnp.float32).astype(
-            jnp.bfloat16
-        )
+            begin = pl.multiple_of(group * rows + first * GROUP, span * GROUP)
+            normed[pl.ds(begin, span * GROUP)] = x.astype(jnp.bfloat16)
+    for index, weight in enumerate((w_query, w_key, w_value)):
+        projected[index] = jnp.dot(normed[...], weight[...], preferred_element_type=jnp.float32).astype(jnp.bfloat16)
     queries, key_proj, values = projected.at[0], projected.at[1], projected.at[2]
     height = rows // BLOCKS
     power = math.log2(math.e) / math.sqrt(channels)
@@ -130,18 +111,15 @@
             attended[first + begin : first + span] = jnp.dot(
                 jnp.concatenate(shares, axis=0), values[first : first + span], preferred_element_type=jnp.float32
             ).astype(jnp.bfloat16)
-    ready(3)
     out = jnp.dot(attended[...], w_out[...], preferred_element_type=jnp.float32).reshape(
         groups, frames, GROUP, channels
     )
     for group in range(groups):
-        for first in range(0, frames, tile):
-            x = band[first : first + tile, group * GROUP : (group + 1) * GROUP].astype(jnp.float32)
-            x = x + out[group, first : first + tile]
-            mixed[group, first + 1 : first + 1 + tile] = x
+        for first in range(0, frames, TILE):
+            x = mixed[group, first + 1 : first + 1 + TILE] + out[group, first : first + TILE]
+            mixed[group, first + 1 : first + 1 + TILE] = x
             if first == 0:
                 mixed[group, 0] = x[0]
-    ready(4)
     taps = []
     for tap in range(3):
         parts = []
@@ -154,47 +132,25 @@
 
 
 def attend_kernel(inward, n_in, n_out, *refs):
-    pieces = refs[:n_in]
-    gain = refs[n_in]
-    sources = refs[n_in + 1 : n_in + 6]
+    gain, *weights = refs[n_in : n_in + 6]
     results = refs[n_in + 6 : n_in + 6 + n_out]
-    band, done, bias, normed, projected, attended, mixed, *held, sems, weight_sems = refs[n_in + 6 + n_out :]
-    fetches = [pltpu.make_async_copy(s, h, weight_sems.at[i]) for i, (s, h) in enumerate(zip(sources, held))]
-    waited = set()
-
-    def ready(index):
-        if index not in waited:
-            waited.add(index)
-            fetches[index].wait()
-
-    copies = [
-        pltpu.make_async_copy(piece, band.at[pl.ds(first, piece.shape[0])], sems.at[i])
-        for i, (piece, first) in enumerate(inward(pieces))
-    ]
-    for copy in copies + fetches:
-        copy.start()
+    bias, normed, projected, attended, mixed, *done = refs[n_in + 6 + n_out :]
     to_row = lax.broadcasted_iota(jnp.int32, bias.shape, 0)
     from_row = lax.broadcasted_iota(jnp.int32, bias.shape, 1)
     allowed = (from_row <= to_row) & (((from_row ^ to_row) & (GROUP - 1)) == 0)
     bias[...] = jnp.where(allowed, 0.0, -1e30)
-    for copy in copies:
-        copy.wait()
-    made = attend_frames(band, gain[...], bias, held, ready, normed, projected, attended, mixed)
-    done[...] = jnp.concatenate([made[g] for g in range(made.shape[0])], axis=1).astype(jnp.bfloat16)
-    chip, _ = place()
-    copies = [
-        pltpu.make_async_copy(
-            done if n_out == 1 else done.at[pl.ds((chip ^ k) * result.shape[0], result.shape[0])], result, sems.at[k]
-        )
-        for k, result in enumerate(results)
-    ]
-    for copy in copies:
-        copy.start()
-    for copy in copies:
-        copy.wait()
-
-
-def attend(inward, n_copies, pieces, weights, frames, n_out, name):
+    made = attend_frames(inward(refs[:n_in]), gain[...], bias, weights, normed, projected, attended, mixed)
+    made = jnp.concatenate([made[g] for g in range(made.shape[0])], axis=1).astype(jnp.bfloat16)
+    if n_out == 1:
+        results[0][...] = made
+    else:
+        done[0][...] = made
+        chip, _ = place()
+        for k, result in enumerate(results):
+            result[...] = done[0][pl.ds((chip ^ k) * result.shape[0], result.shape[0])]
+
+
+def attend(inward, pieces, weights, frames, n_out, name):
     cols, channels = pieces[0].shape[-2:]
     rows = frames * cols
     made = frames // 2
@@ -202,21 +158,17 @@
     return pl.pallas_call(
         functools.partial(attend_kernel, inward, len(pieces), n_out),
         out_shape=[jax.ShapeDtypeStruct((made // n_out, cols, channels), jnp.bfloat16)] * n_out,
-        in_specs=[ANYWHERE] * len(pieces) + [INSIDE] + [ANYWHERE] * 5,
-        out_specs=[ANYWHERE] * n_out,
+        in_specs=[INSIDE] * (len(pieces) + 6),
+        out_specs=[INSIDE] * n_out,
         scratch_shapes=[
-            pltpu.VMEM((frames, cols, channels), jnp.bfloat16),
-            pltpu.VMEM((made, cols, channels), jnp.bfloat16),
             pltpu.VMEM((frames * GROUP, frames * GROUP), jnp.float32),
             pltpu.VMEM((rows, channels), jnp.bfloat16),
             pltpu.VMEM((3, rows, channels), jnp.bfloat16),
             pltpu.VMEM((rows, channels), jnp.bfloat16),
             pltpu.VMEM((cols // GROUP, frames + 2, GROUP, channels), jnp.float32),
-            *[pltpu.VMEM(matrix.shape, jnp.bfloat16) for matrix in matrices],
-            pltpu.SemaphoreType.DMA((n_copies,)),
-            pltpu.SemaphoreType.DMA((5,)),
+            *([pltpu.VMEM((made, cols, channels), jnp.bfloat16)] if n_out > 1 else []),
         ],
-        compiler_params=pltpu.CompilerParams(vmem_limit_bytes=20 * MIB),
+        compiler_params=pltpu.CompilerParams(vmem_limit_bytes=24 * MIB),
         cost_estimate=pl.CostEstimate(
             flops=rows * channels * (channels * 11 + GROUP * frames * 4),
             bytes_accessed=rows * channels * 3 + channels * channels * 14,
@@ -252,20 +204,13 @@
 
 def filter_kernel(chips, *refs):
     pieces = refs[:chips]
-    other, inner, left, right, w_depth, out, outer, sems = refs[chips:]
+    other, inner, left, right, w_depth, out, outer = refs[chips:]
     chip, core = place()
     made = other.shape[1]
-    copies = []
     for k in range(chips):
         row = 2 * (chip ^ k)
-        copies.append(
-            pltpu.make_async_copy(pieces[k].at[pl.ds(core * made, made)], outer.at[row + core], sems.at[2 * k])
-        )
-        copies.append(pltpu.make_async_copy(other.at[k], outer.at[row + 1 - core], sems.at[2 * k + 1]))
-    for copy in copies:
-        copy.start()
-    for copy in copies:
-        copy.wait()
+        outer[row + core] = pieces[k][pl.ds(core * made, made)]
+        outer[row + 1 - core] = other[k]
     frames, height, cols, channels = out.shape
     edge = cols // 4
     lanes = 128
@@ -312,12 +257,9 @@
     return pl.pallas_call(
         functools.partial(filter_kernel, len(outer)),
         out_shape=jax.ShapeDtypeStruct((frames, height, cols, channels), jnp.bfloat16),
-        in_specs=[ANYWHERE] * (len(outer) + 1) + [INSIDE] * 4,
+        in_specs=[INSIDE] * (len(outer) + 5),
         out_specs=INSIDE,
-        scratch_shapes=[
-            pltpu.VMEM((height, frames, width, channels), jnp.bfloat16),
-            pltpu.SemaphoreType.DMA((height,)),
-        ],
+        scratch_shapes=[pltpu.VMEM((height, frames, width, channels), jnp.bfloat16)],
         compiler_params=pltpu.CompilerParams(vmem_limit_bytes=8 * MIB),
         cost_estimate=pl.CostEstimate(flops=18 * size, bytes_accessed=4 * size, transcendentals=0),
         name="depth_filter",
@@ -352,7 +294,7 @@
         return pairs
 
     def join(owns, other, name):
-        return gather(joined, 2 * len(far), [*owns[:-1], other], [(2 * span, width, channels)] * len(far), name)
+        return gather(joined, [*owns[:-1], other], [(2 * span, width, channels)] * len(far), name)
 
     outer_other = swap(outer_stack, 1)
     outer_far = join(outer, outer_other, "join_outer")
@@ -372,16 +314,16 @@
             pairs.append((piece.at[pl.ds(span, span)], (me ^ k ^ 1) * span))
         return pairs + [(own, me * span), (other.at[len(far)], (me ^ 1) * span)]
 
-    outer = attend(inward, count, [*outer_far, outer[-1], outer_other], weights, frames, chips, "attend_outer")
+    outer = attend(inward, [*outer_far, outer[-1], outer_other], weights, frames, chips, "attend_outer")
     outer = [swap(piece, 2 * k) for k, piece in enumerate(outer)]
-    (inner,) = attend(inward, count, [*inner_far, inner[-1], inner_other], weights, frames, 1, "attend_inner")
+    (inner,) = attend(inward, [*inner_far, inner[-1], inner_other], weights, frames, 1, "attend_inner")
     *outer, inner = lax.optimization_barrier((*outer, inner))
 
     def halves(ins, outs):
         _, core = place()
         return [(piece.at[pl.ds((1 - core) * made, made)], outs[0].at[k]) for k, piece in enumerate(ins)]
 
-    outer_other = swap(gather(halves, chips, outer, [(chips, made, width, channels)], "halves")[0], 1)
+    outer_other = swap(gather(halves, outer, [(chips, made, width, channels)], "halves")[0], 1)
     inner = lax.all_to_all(
         inner.reshape(count, made, width, channels), "frm", split_axis=0, concat_axis=0, tiled=True
     )

time: 90.7 us -> 89.7 us (0.989)
  Pallas kernels: 24.7 us -> 16.1 us
  starting transfers between devices: 32.4 us -> 36.4 us
  waiting for transfers between devices: 31.5 us -> 35.1 us
    pallas_call x2, Pallas kernels: 18.4 us -> 13.1 us  [attend(): pl.pallas_call(functools.partial(attend_kernel, inward, len(pieces), n_ou...]
    all_to_all x1, starting transfers between devices: 3.76 us -> 7.74 us  [local(): lax.all_to_all(inner.reshape(count, made, width, channels), 'frm', split_...]
    ppermute x12, waiting for transfers between devices: 23.1 us -> 26.4 us  [swap(): lax.ppermute(block, 'frm', [(i, i ^ k) for i in range(count)])]
    pallas_call x3, Pallas kernels: 2.47 us -> 0.12 us  [gather(): pl.pallas_call(functools.partial(gather_kernel, pairs_of, len(arrays)), o...]
  transfers between devices with their start and end apart: 15 -> 15, of which waited for: 7 -> 8; matrix products, arithmetic and copies ran while one was open for 0% -> 0% of each run, Pallas kernels for 22% -> 15%
where the time goes in v5:
time: 89.7 us; the launch traced here: 89.4 us
  starting transfers between devices  36.4 us (41%)
  waiting for transfers between devices  35.1 us (39%)
  Pallas kernels  16.1 us (18%)
  local copies, waits for them, and re-layouts  1.62 us (2%)
    ppermute x12, waiting for transfers between devices, swap(): lax.ppermute(block, 'frm', [(i, i ^ k) for i in range(count)])  26.4 us
    ppermute x12, starting transfers between devices, swap(): lax.ppermute(block, 'frm', [(i, i ^ k) for i in range(count)])  23.9 us
    pallas_call x2, Pallas kernels, attend(): pl.pallas_call(functools.partial(attend_kernel, inward, len(pieces), n_ou...  13.1 us
    all_to_all x1, starting transfers between devices, local(): lax.all_to_all(inner.reshape(count, made, width, channels), 'frm', split_...  7.74 us
    all_to_all x1, waiting for transfers between devices, local(): lax.all_to_all(inner.reshape(count, made, width, channels), 'frm', split_...  4.26 us
    ppermute x1, waiting for transfers between devices, local(): right = lax.ppermute(low_side, 'col', [(b, a) for a, b in upward])  4.23 us
    ppermute x1, starting transfers between devices, local(): left = lax.ppermute(high_side, 'col', upward)  3.41 us
    pallas_call x1, Pallas kernels, depth_filter(): pl.pallas_call(functools.partial(filter_kernel, len(outer)), out_shape=ja...  2.61 us
  transfers between devices with their start and end apart: 15, of which 8 were waited for; matrix products, arithmetic and copies ran while one was open for 0% of the time, Pallas kernels for 15%

profile of v5, /device:TPU:0, one launch (start us, length us, event | category | flops | bytes accessed | tf_op | source)
XLA Modules:
  0.0 89.4 jit_solution(12224201825209011236)
XLA Ops:
  0.0 0.0 copy-start
  0.0 1.6 %copy-done = bf16[8,8,32,512]{3,2,1,0:T(8,128)(2,1)S(1)} copy-done((bf16[8,8,32,512]{3,2,1,0:T(8,128)(2,1)S(1)}, bf16[8,8,32,512]{3,2,1,0:T(8,128)(2,1)}, u32[]{:S(2)}) %copy-start) | copy-done | bytes 2097176
  1.6 0.0 copy-start.2
  1.6 0.0 copy-start.3
  1.6 0.0 copy-start.4
  1.6 0.0 copy-start.5
  1.6 0.0 copy-start.6
  1.6 0.0 copy-start.7
  1.6 0.1 cut.1
  1.8 0.5 collective-permute-start
  2.3 1.5 %collective-permute-done.refs_3_.refs_4_ = bf16[4,8,16,512]{3,2,1,0:T(8,128)(2,1)S(1)} collective-permute-done((bf16[4,8,16,512]{3,2,1,0:T(8,128)(2,1)S(1)}, bf16[4,8,16,512]{3,2,1,0:T(8,128)(2,1)S(1)}, u32[]{:S(2)}, u32[]{:S(2)}) %collective-permute-start) | collective-permute-done | bytes 524320 | tf_op jit(solution)/shard_map/ppermute | solution.py:280
  3.8 0.1 join_outer.1
  3.9 0.4 collective-permute-start.2
  4.3 4.7 %collective-permute-start.1 = (bf16[16,16,512]{2,1,0:T(8,128)(2,1)S(1)}, bf16[16,16,512]{2,1,0:T(8,128)(2,1)S(1)}, u32[]{:S(2)}, u32[]{:S(2)}) collective-permute-start(bf16[16,16,512]{2,1,0:T(8,128)(2,1)S(1)} %get-tuple-element.48), channel_id=1, source_target_pairs={{0,24},{4,28},{8,16},{12,20},{16,8},{20,12},{24,0},{28,4},{1,25},{... | collective-permute-start | bytes 786440 | tf_op jit(solution)/shard_map/ppermute | solution.py:280
  9.1 0.0 collective-permute-start.3
  9.1 0.6 collective-permute-start.4
  9.7 0.0 collective-permute-done.2.refs_3_.refs_4_
  9.7 0.1 join_inner.1
  9.7 6.7 %collective-permute-done.1.refs_0_ = bf16[16,16,512]{2,1,0:T(8,128)(2,1)S(1)} collective-permute-done((bf16[16,16,512]{2,1,0:T(8,128)(2,1)S(1)}, bf16[16,16,512]{2,1,0:T(8,128)(2,1)S(1)}, u32[]{:S(2)}, u32[]{:S(2)}) %collective-permute-start.1) | collective-permute-done | bytes 262176 | tf_op jit(solution)/shard_map/ppermute | solution.py:280
  16.4 3.8 %collective-permute-start.8 = (bf16[16,16,512]{2,1,0:T(8,128)(2,1)S(1)}, bf16[16,16,512]{2,1,0:T(8,128)(2,1)S(1)}, u32[]{:S(2)}, u32[]{:S(2)}) collective-permute-start(bf16[16,16,512]{2,1,0:T(8,128)(2,1)S(1)} %get-tuple-element.64), channel_id=1, source_target_pairs={{0,24},{4,28},{8,16},{12,20},{16,8},{20,12},{24,0},{28,4},{1,25},{... | collective-permute-start | bytes 786440 | tf_op jit(solution)/shard_map/ppermute | solution.py:280
  20.1 8.7 %collective-permute-start.9 = (bf16[16,16,512]{2,1,0:T(8,128)(2,1)S(1)}, bf16[16,16,512]{2,1,0:T(8,128)(2,1)S(1)}, u32[]{:S(2)}, u32[]{:S(2)}) collective-permute-start(bf16[16,16,512]{2,1,0:T(8,128)(2,1)S(1)} %get-tuple-element.65), channel_id=1, source_target_pairs={{0,16},{4,20},{8,24},{12,28},{16,0},{20,4},{24,8},{28,12},{1,17},{... | collective-permute-start | bytes 786440 | tf_op jit(solution)/shard_map/ppermute | solution.py:280
  28.9 0.1 collective-permute-start.10
  29.0 14.8 %collective-permute-done.3.refs_1_ = bf16[16,16,512]{2,1,0:T(8,128)(2,1)S(1)} collective-permute-done((bf16[16,16,512]{2,1,0:T(8,128)(2,1)S(1)}, bf16[16,16,512]{2,1,0:T(8,128)(2,1)S(1)}, u32[]{:S(2)}, u32[]{:S(2)}) %collective-permute-start.3) | collective-permute-done | bytes 262176 | tf_op jit(solution)/shard_map/ppermute | solution.py:280
  43.7 0.0 collective-permute-done.4.refs_2_
  43.8 0.0 copy-done.2
  43.8 0.0 copy-done.3
  43.8 0.0 copy-done.4
  43.8 0.0 copy-done.5
  43.8 0.0 copy-done.6
  43.8 0.0 copy-done.7
  43.8 6.2 %attend_outer.1 = (bf16[8,16,512]{2,1,0:T(8,128)(2,1)S(1)}, bf16[8,16,512]{2,1,0:T(8,128)(2,1)S(1)}, bf16[8,16,512]{2,1,0:T(8,128)(2,1)S(1)}, bf16[8,16,512]{2,1,0:T(8,128)(2,1)S(1)}) custom-call(bf16[16,16,512]{2,1,0:T(8,128)(2,1)S(1)} %collective-permute-done.1.refs_0_, bf16[16,16,512]{2,1,0:T(8,128)(2,1)S(1)} %collective-permute-done.3.refs_1_, ...), custom_call_target="tpu_custom_call" | custom-call | flops 4026531840 | bytes 5242880 | tf_op jit(solution)/shard_map/attend_outer/pallas_call | solution.py:158
  50.0 0.1 collective-permute-start.5
  50.1 3.0 %collective-permute-start.6 = (bf16[8,16,512]{2,1,0:T(8,128)(2,1)S(1)}, bf16[8,16,512]{2,1,0:T(8,128)(2,1)S(1)}, u32[]{:S(2)}, u32[]{:S(2)}) collective-permute-start(bf16[8,16,512]{2,1,0:T(8,128)(2,1)S(1)} %get-tuple-element.62), channel_id=1, source_target_pairs={{0,16},{4,20},{8,24},{12,28},{16,0},{20,4},{24,8},{28,12},{1,17},{... | collective-permute-start | bytes 393224 | tf_op jit(solution)/shard_map/ppermute | solution.py:280
  53.1 0.0 collective-permute-done.8.refs_0_
  53.1 1.3 %collective-permute-start.7 = (bf16[8,16,512]{2,1,0:T(8,128)(2,1)S(1)}, bf16[8,16,512]{2,1,0:T(8,128)(2,1)S(1)}, u32[]{:S(2)}, u32[]{:S(2)}) collective-permute-start(bf16[8,16,512]{2,1,0:T(8,128)(2,1)S(1)} %get-tuple-element.63), channel_id=1, source_target_pairs={{0,24},{4,28},{8,16},{12,20},{16,8},{20,12},{24,0},{28,4},{1,25},{... | collective-permute-start | bytes 393224 | tf_op jit(solution)/shard_map/ppermute | solution.py:280
  54.4 2.2 %collective-permute-done.9.refs_1_ = bf16[16,16,512]{2,1,0:T(8,128)(2,1)S(1)} collective-permute-done((bf16[16,16,512]{2,1,0:T(8,128)(2,1)S(1)}, bf16[16,16,512]{2,1,0:T(8,128)(2,1)S(1)}, u32[]{:S(2)}, u32[]{:S(2)}) %collective-permute-start.9) | collective-permute-done | bytes 262176 | tf_op jit(solution)/shard_map/ppermute | solution.py:280
  56.7 0.0 collective-permute-done.10.refs_2_
  56.7 6.9 %attend_inner.1 = bf16[32,16,512]{2,1,0:T(8,128)(2,1)} custom-call(bf16[16,16,512]{2,1,0:T(8,128)(2,1)S(1)} %collective-permute-done.8.refs_0_, bf16[16,16,512]{2,1,0:T(8,128)(2,1)S(1)} %collective-permute-done.9.refs_1_, bf16[16,16,512]{2,1,0:T(8,128)(2,1)S(1)} %collective-permute-done.10.refs_2_, bf16[8,16,512]{2,1,0:T(8,128)(2,1)S(1)} %get-tuple-element.67.refs_3_, ...), custom_call_target="tpu_custom_call" | custom-call | flops 4026531840 | bytes 5242880 | tf_op jit(solution)/shard_map/attend_inner/pallas_call | solution.py:158
  63.6 0.0 copy-start.1
  63.6 0.0 collective-permute-done.5.refs_1_
  63.6 0.0 collective-permute-done.6.refs_2_
  63.6 0.0 collective-permute-done.7.refs_3_
  63.6 7.7 %all-to-all-start = ((bf16[8,4,16,512]{3,2,1,0:T(8,128)(2,1)}), bf16[8,4,16,512]{3,2,1,0:T(8,128)(2,1)S(1)}, u32[]{:S(2)}, u32[]{:S(2)}) async-start(bf16[8,4,16,512]{3,2,1,0:T(8,128)(2,1)} %bitcast.1), calls=%async_computation | async-start | bytes 1048576 | tf_op jit(solution)/shard_map/all_to_all | solution.py:327
  71.4 0.6 collective-permute-start.11
  72.0 1.2 %collective-permute-done.11.refs_4_ = bf16[4,4,16,512]{3,2,1,0:T(8,128)(2,1)S(1)} collective-permute-done((bf16[4,4,16,512]{3,2,1,0:T(8,128)(2,1)S(1)}, bf16[4,4,16,512]{3,2,1,0:T(8,128)(2,1)S(1)}, u32[]{:S(2)}, u32[]{:S(2)}) %collective-permute-start.11) | collective-permute-done | bytes 262176 | tf_op jit(solution)/shard_map/ppermute | solution.py:280
  73.1 0.1 rim.1
  73.3 3.4 %collective-permute-start.12 = (bf16[8,4,512]{2,1,0:T(4,128)(2,1)S(1)}, bf16[8,4,512]{2,1,0:T(4,128)(2,1)S(1)}, u32[]{:S(2)}, u32[]{:S(2)}) collective-permute-start(bf16[8,4,512]{2,1,0:T(4,128)(2,1)S(1)} %get-tuple-element.73), channel_id=1, source_target_pairs={{0,1},{1,2},{2,3},{4,5},{5,6},{6,7},{8,9},{9,10},{10,11},{12,13},{... | collective-permute-start | bytes 98312 | tf_op jit(solution)/shard_map/ppermute | solution.py:333
  76.7 1.3 %collective-permute-start.13 = (bf16[8,4,512]{2,1,0:T(4,128)(2,1)S(1)}, bf16[8,4,512]{2,1,0:T(4,128)(2,1)S(1)}, u32[]{:S(2)}, u32[]{:S(2)}) collective-permute-start(bf16[8,4,512]{2,1,0:T(4,128)(2,1)S(1)} %get-tuple-element.74), channel_id=1, source_target_pairs={{1,0},{2,1},{3,2},{5,4},{6,5},{7,6},{9,8},{10,9},{11,10},{13,12},{... | collective-permute-start | bytes 98312 | tf_op jit(solution)/shard_map/ppermute | solution.py:334
  78.0 0.3 collective-permute-done.12.refs_6_
  78.3 4.2 %collective-permute-done.13.refs_7_ = bf16[8,4,512]{2,1,0:T(4,128)(2,1)S(1)} collective-permute-done((bf16[8,4,512]{2,1,0:T(4,128)(2,1)S(1)}, bf16[8,4,512]{2,1,0:T(4,128)(2,1)S(1)}, u32[]{:S(2)}, u32[]{:S(2)}) %collective-permute-start.13) | collective-permute-done | bytes 32800 | tf_op jit(solution)/shard_map/ppermute | solution.py:334
  82.5 4.3 %all-to-all-done.refs_5_ = bf16[8,4,16,512]{3,2,1,0:T(8,128)(2,1)S(1)} async-done(((bf16[8,4,16,512]{3,2,1,0:T(8,128)(2,1)}), bf16[8,4,16,512]{3,2,1,0:T(8,128)(2,1)S(1)}, u32[]{:S(2)}, u32[]{:S(2)}) %all-to-all-start) | async-done | bytes 524320 | tf_op jit(solution)/shard_map/all_to_all | solution.py:327
  86.7 0.0 copy-done.1
  86.7 2.6 %depth_filter.1 = bf16[4,8,32,512]{3,2,1,0:T(8,128)(2,1)} custom-call(bf16[8,16,512]{2,1,0:T(8,128)(2,1)S(1)} %get-tuple-element.68.refs_0_, bf16[8,16,512]{2,1,0:T(8,128)(2,1)S(1)} %collective-permute-done.5.refs_1_, bf16[8,16,512]{2,1,0:T(8,128)(2,1)S(1)} %collective-permute-done.6.refs_2_, bf16[8,16,512]{2,1,0:T(8,128)(2,1)S(1)} %collective-permute-done.7.refs_3_, ...), custom_call_target="tpu_custom_call" | custom-call | flops 9437184 | bytes 2097152 | tf_op jit(solution)/shard_map/depth_filter/pallas_call | solution.py:257
  (1 shorter events, 0.0 us)
Async XLA Ops:
  0.0 1.6 %copy-start = (bf16[8,8,32,512]{3,2,1,0:T(8,128)(2,1)S(1)}, bf16[8,8,32,512]{3,2,1,0:T(8,128)(2,1)}, u32[]{:S(2)}) copy-start(bf16[8,8,32,512]{3,2,1,0:T(8,128)(2,1)} %video.1) | copy-start | bytes 6291460
  1.6 42.2 %copy-start.2 = (bf16[3,512,512]{2,1,0:T(8,128)(2,1)S(1)}, bf16[3,512,512]{2,1,0:T(8,128)(2,1)}, u32[]{:S(2)}) copy-start(bf16[3,512,512]{2,1,0:T(8,128)(2,1)} %refs_10_.3) | copy-start | bytes 4718596
  1.6 42.2 %copy-start.3 = (bf16[512,512]{1,0:T(8,128)(2,1)S(1)}, bf16[512,512]{1,0:T(8,128)(2,1)}, u32[]{:S(2)}) copy-start(bf16[512,512]{1,0:T(8,128)(2,1)} %refs_6_.3) | copy-start | bytes 1572868
  1.6 42.2 %copy-start.4 = (bf16[512,512]{1,0:T(8,128)(2,1)S(1)}, bf16[512,512]{1,0:T(8,128)(2,1)}, u32[]{:S(2)}) copy-start(bf16[512,512]{1,0:T(8,128)(2,1)} %refs_7_.3) | copy-start | bytes 1572868
  1.6 42.2 %copy-start.5 = (bf16[512,512]{1,0:T(8,128)(2,1)S(1)}, bf16[512,512]{1,0:T(8,128)(2,1)}, u32[]{:S(2)}) copy-start(bf16[512,512]{1,0:T(8,128)(2,1)} %refs_8_.4) | copy-start | bytes 1572868
  1.6 42.2 %copy-start.6 = (bf16[512,512]{1,0:T(8,128)(2,1)S(1)}, bf16[512,512]{1,0:T(8,128)(2,1)}, u32[]{:S(2)}) copy-start(bf16[512,512]{1,0:T(8,128)(2,1)} %refs_9_.3) | copy-start | bytes 1572868
  1.6 42.2 %copy-start.7 = (f32[512]{0:T(512)S(1)}, f32[512]{0:T(512)}, u32[]{:S(2)}) copy-start(f32[512]{0:T(512)} %param.9) | copy-start | bytes 6148
  1.8 2.1 %collective-permute-start = (bf16[4,8,16,512]{3,2,1,0:T(8,128)(2,1)S(1)}, bf16[4,8,16,512]{3,2,1,0:T(8,128)(2,1)S(1)}, u32[]{:S(2)}, u32[]{:S(2)}) collective-permute-start(bf16[4,8,16,512]{3,2,1,0:T(8,128)(2,1)S(1)} %get-tuple-element.43), channel_id=1, source_target_pairs={{0,4},{4,0},{8,12},{12,8},{16,20},{20,16},{24,28},{28,24},{1,5},{5... | collective-permute-start | bytes 1572872 | tf_op jit(solution)/shard_map/ppermute | solution.py:280
  3.9 5.8 %collective-permute-start.2 = (bf16[4,8,16,512]{3,2,1,0:T(8,128)(2,1)S(1)}, bf16[4,8,16,512]{3,2,1,0:T(8,128)(2,1)S(1)}, u32[]{:S(2)}, u32[]{:S(2)}) collective-permute-start(bf16[4,8,16,512]{3,2,1,0:T(8,128)(2,1)S(1)} %get-tuple-element.52), channel_id=1, source_target_pairs={{0,4},{4,0},{8,12},{12,8},{16,20},{20,16},{24,28},{28,24},{1,5},{5... | collective-permute-start | bytes 1572872 | tf_op jit(solution)/shard_map/ppermute | solution.py:280
  4.3 12.0 %collective-permute-start.1 = (bf16[16,16,512]{2,1,0:T(8,128)(2,1)S(1)}, bf16[16,16,512]{2,1,0:T(8,128)(2,1)S(1)}, u32[]{:S(2)}, u32[]{:S(2)}) collective-permute-start(bf16[16,16,512]{2,1,0:T(8,128)(2,1)S(1)} %get-tuple-element.48), channel_id=1, source_target_pairs={{0,24},{4,28},{8,16},{12,20},{16,8},{20,12},{24,0},{28,4},{1,25},{... | collective-permute-start | bytes 786440 | tf_op jit(solution)/shard_map/ppermute | solution.py:280
  9.1 34.7 %collective-permute-start.3 = (bf16[16,16,512]{2,1,0:T(8,128)(2,1)S(1)}, bf16[16,16,512]{2,1,0:T(8,128)(2,1)S(1)}, u32[]{:S(2)}, u32[]{:S(2)}) collective-permute-start(bf16[16,16,512]{2,1,0:T(8,128)(2,1)S(1)} %get-tuple-element.57), channel_id=1, source_target_pairs={{0,16},{4,20},{8,24},{12,28},{16,0},{20,4},{24,8},{28,12},{1,17},{... | collective-permute-start | bytes 786440 | tf_op jit(solution)/shard_map/ppermute | solution.py:280
  9.1 34.7 %collective-permute-start.4 = (bf16[16,16,512]{2,1,0:T(8,128)(2,1)S(1)}, bf16[16,16,512]{2,1,0:T(8,128)(2,1)S(1)}, u32[]{:S(2)}, u32[]{:S(2)}) collective-permute-start(bf16[16,16,512]{2,1,0:T(8,128)(2,1)S(1)} %get-tuple-element.58), channel_id=1, source_target_pairs={{0,8},{4,12},{8,0},{12,4},{16,24},{20,28},{24,16},{28,20},{1,9},{5... | collective-permute-start | bytes 786440 | tf_op jit(solution)/shard_map/ppermute | solution.py:280
  16.4 36.7 %collective-permute-start.8 = (bf16[16,16,512]{2,1,0:T(8,128)(2,1)S(1)}, bf16[16,16,512]{2,1,0:T(8,128)(2,1)S(1)}, u32[]{:S(2)}, u32[]{:S(2)}) collective-permute-start(bf16[16,16,512]{2,1,0:T(8,128)(2,1)S(1)} %get-tuple-element.64), channel_id=1, source_target_pairs={{0,24},{4,28},{8,16},{12,20},{16,8},{20,12},{24,0},{28,4},{1,25},{... | collective-permute-start | bytes 786440 | tf_op jit(solution)/shard_map/ppermute | solution.py:280
  20.1 36.5 %collective-permute-start.9 = (bf16[16,16,512]{2,1,0:T(8,128)(2,1)S(1)}, bf16[16,16,512]{2,1,0:T(8,128)(2,1)S(1)}, u32[]{:S(2)}, u32[]{:S(2)}) collective-permute-start(bf16[16,16,512]{2,1,0:T(8,128)(2,1)S(1)} %get-tuple-element.65), channel_id=1, source_target_pairs={{0,16},{4,20},{8,24},{12,28},{16,0},{20,4},{24,8},{28,12},{1,17},{... | collective-permute-start | bytes 786440 | tf_op jit(solution)/shard_map/ppermute | solution.py:280
  28.9 27.8 %collective-permute-start.10 = (bf16[16,16,512]{2,1,0:T(8,128)(2,1)S(1)}, bf16[16,16,512]{2,1,0:T(8,128)(2,1)S(1)}, u32[]{:S(2)}, u32[]{:S(2)}) collective-permute-start(bf16[16,16,512]{2,1,0:T(8,128)(2,1)S(1)} %get-tuple-element.66), channel_id=1, source_target_pairs={{0,8},{4,12},{8,0},{12,4},{16,24},{20,28},{24,16},{28,20},{1,9},{5... | collective-permute-start | bytes 786440 | tf_op jit(solution)/shard_map/ppermute | solution.py:280
  50.0 13.6 %collective-permute-start.5 = (bf16[8,16,512]{2,1,0:T(8,128)(2,1)S(1)}, bf16[8,16,512]{2,1,0:T(8,128)(2,1)S(1)}, u32[]{:S(2)}, u32[]{:S(2)}) collective-permute-start(bf16[8,16,512]{2,1,0:T(8,128)(2,1)S(1)} %get-tuple-element.61), channel_id=1, source_target_pairs={{0,8},{4,12},{8,0},{12,4},{16,24},{20,28},{24,16},{28,20},{1,9},{5... | collective-permute-start | bytes 393224 | tf_op jit(solution)/shard_map/ppermute | solution.py:280
  50.1 13.6 %collective-permute-start.6 = (bf16[8,16,512]{2,1,0:T(8,128)(2,1)S(1)}, bf16[8,16,512]{2,1,0:T(8,128)(2,1)S(1)}, u32[]{:S(2)}, u32[]{:S(2)}) collective-permute-start(bf16[8,16,512]{2,1,0:T(8,128)(2,1)S(1)} %get-tuple-element.62), channel_id=1, source_target_pairs={{0,16},{4,20},{8,24},{12,28},{16,0},{20,4},{24,8},{28,12},{1,17},{... | collective-permute-start | bytes 393224 | tf_op jit(solution)/shard_map/ppermute | solution.py:280
  53.1 10.5 %collective-permute-start.7 = (bf16[8,16,512]{2,1,0:T(8,128)(2,1)S(1)}, bf16[8,16,512]{2,1,0:T(8,128)(2,1)S(1)}, u32[]{:S(2)}, u32[]{:S(2)}) collective-permute-start(bf16[8,16,512]{2,1,0:T(8,128)(2,1)S(1)} %get-tuple-element.63), channel_id=1, source_target_pairs={{0,24},{4,28},{8,16},{12,20},{16,8},{20,12},{24,0},{28,4},{1,25},{... | collective-permute-start | bytes 393224 | tf_op jit(solution)/shard_map/ppermute | solution.py:280
  63.6 23.1 %copy-start.1 = (f32[3,3,512]{2,1,0:T(4,128)S(1)}, f32[3,3,512]{2,1,0:T(4,128)}, u32[]{:S(2)}) copy-start(f32[3,3,512]{2,1,0:T(4,128)} %refs_8_.5) | copy-start | bytes 55300
  63.6 23.1 %all-to-all-start = ((bf16[8,4,16,512]{3,2,1,0:T(8,128)(2,1)}), bf16[8,4,16,512]{3,2,1,0:T(8,128)(2,1)S(1)}, u32[]{:S(2)}, u32[]{:S(2)}) async-start(bf16[8,4,16,512]{3,2,1,0:T(8,128)(2,1)} %bitcast.1), calls=%async_computation | async-start | bytes 1048576 | tf_op jit(solution)/shard_map/all_to_all | solution.py:327
  71.4 1.7 %collective-permute-start.11 = (bf16[4,4,16,512]{3,2,1,0:T(8,128)(2,1)S(1)}, bf16[4,4,16,512]{3,2,1,0:T(8,128)(2,1)S(1)}, u32[]{:S(2)}, u32[]{:S(2)}) collective-permute-start(bf16[4,4,16,512]{3,2,1,0:T(8,128)(2,1)S(1)} %halves.1), channel_id=1, source_target_pairs={{0,4},{4,0},{8,12},{12,8},{16,20},{20,16},{24,28},{28,24},{1,5},{5... | collective-permute-start | bytes 786440 | tf_op jit(solution)/shard_map/ppermute | solution.py:280
  73.3 5.0 %collective-permute-start.12 = (bf16[8,4,512]{2,1,0:T(4,128)(2,1)S(1)}, bf16[8,4,512]{2,1,0:T(4,128)(2,1)S(1)}, u32[]{:S(2)}, u32[]{:S(2)}) collective-permute-start(bf16[8,4,512]{2,1,0:T(4,128)(2,1)S(1)} %get-tuple-element.73), channel_id=1, source_target_pairs={{0,1},{1,2},{2,3},{4,5},{5,6},{6,7},{8,9},{9,10},{10,11},{12,13},{... | collective-permute-start | bytes 98312 | tf_op jit(solution)/shard_map/ppermute | solution.py:333
  76.7 5.8 %collective-permute-start.13 = (bf16[8,4,512]{2,1,0:T(4,128)(2,1)S(1)}, bf16[8,4,512]{2,1,0:T(4,128)(2,1)S(1)}, u32[]{:S(2)}, u32[]{:S(2)}) collective-permute-start(bf16[8,4,512]{2,1,0:T(4,128)(2,1)S(1)} %get-tuple-element.74), channel_id=1, source_target_pairs={{1,0},{2,1},{3,2},{5,4},{6,5},{7,6},{9,8},{10,9},{11,10},{13,12},{... | collective-permute-start | bytes 98312 | tf_op jit(solution)/shard_map/ppermute | solution.py:334

commit v6 on v5

--- a/solution.py
+++ b/solution.py
@@ -131,42 +131,46 @@
     return (summed / (1.0 + jnp.exp(-summed))).reshape(groups, frames // 2, GROUP, channels)
 
 
-def attend_kernel(inward, n_in, n_out, *refs):
+def attend_kernel(inward, hops, paired, n_in, *refs):
     gain, *weights = refs[n_in : n_in + 6]
-    results = refs[n_in + 6 : n_in + 6 + n_out]
-    bias, normed, projected, attended, mixed, *done = refs[n_in + 6 + n_out :]
+    *results, done, bias, normed, projected, attended, mixed = refs[n_in + 6 :]
     to_row = lax.broadcasted_iota(jnp.int32, bias.shape, 0)
     from_row = lax.broadcasted_iota(jnp.int32, bias.shape, 1)
     allowed = (from_row <= to_row) & (((from_row ^ to_row) & (GROUP - 1)) == 0)
     bias[...] = jnp.where(allowed, 0.0, -1e30)
     made = attend_frames(inward(refs[:n_in]), gain[...], bias, weights, normed, projected, attended, mixed)
-    made = jnp.concatenate([made[g] for g in range(made.shape[0])], axis=1).astype(jnp.bfloat16)
-    if n_out == 1:
-        results[0][...] = made
-    else:
-        done[0][...] = made
-        chip, _ = place()
-        for k, result in enumerate(results):
-            result[...] = done[0][pl.ds((chip ^ k) * result.shape[0], result.shape[0])]
-
-
-def attend(inward, pieces, weights, frames, n_out, name):
+    done[...] = jnp.concatenate([made[g] for g in range(made.shape[0])], axis=1).astype(jnp.bfloat16)
+    me = lax.axis_index("frm")
+    for i, (hop, result) in enumerate(zip(hops, results)):
+        span = result.shape[0]
+        if paired:
+            result[...] = done[pl.ds((me ^ hop) // 2 * span, span)]
+        else:
+            result[...] = done[pl.ds((me ^ hop) * span, span)]
+            results[-1][i] = done[pl.ds((me ^ hop ^ 1) * span, span)]
+
+
+def attend(inward, hops, paired, pieces, weights, frames, name):
     cols, channels = pieces[0].shape[-2:]
     rows = frames * cols
     made = frames // 2
+    size = made // (2 * len(hops))
+    shapes = [(2 * size if paired else size, cols, channels)] * len(hops)
+    if not paired:
+        shapes.append((len(hops), size, cols, channels))
     norm_gain, *matrices = weights
     return pl.pallas_call(
-        functools.partial(attend_kernel, inward, len(pieces), n_out),
-        out_shape=[jax.ShapeDtypeStruct((made // n_out, cols, channels), jnp.bfloat16)] * n_out,
+        functools.partial(attend_kernel, inward, hops, paired, len(pieces)),
+        out_shape=[jax.ShapeDtypeStruct(shape, jnp.bfloat16) for shape in shapes],
         in_specs=[INSIDE] * (len(pieces) + 6),
-        out_specs=[INSIDE] * n_out,
+        out_specs=[INSIDE] * len(shapes),
         scratch_shapes=[
+            pltpu.VMEM((made, cols, channels), jnp.bfloat16),
             pltpu.VMEM((frames * GROUP, frames * GROUP), jnp.float32),
             pltpu.VMEM((rows, channels), jnp.bfloat16),
             pltpu.VMEM((3, rows, channels), jnp.bfloat16),
             pltpu.VMEM((rows, channels), jnp.bfloat16),
             pltpu.VMEM((cols // GROUP, frames + 2, GROUP, channels), jnp.float32),
-            *([pltpu.VMEM((made, cols, channels), jnp.bfloat16)] if n_out > 1 else []),
         ],
         compiler_params=pltpu.CompilerParams(vmem_limit_bytes=24 * MIB),
         cost_estimate=pl.CostEstimate(
@@ -178,39 +182,49 @@
     )(*pieces, norm_gain[None], *matrices)
 
 
-def rim_kernel(chips, *refs):
-    mine = refs[:chips]
-    other, left, right = refs[chips:]
+def outer_rows(hops, pieces, taken):
     _, core = place()
-    made, cols, _ = other.shape[1:]
-    for k in range(chips):
-        own = mine[k][pl.ds(core * made, made)]
-        for slot, part in ((2 * k, own), (2 * k + 1, other[k])):
-            left[slot] = part[:, 0]
-            right[slot] = part[:, cols - 1]
-
-
-def rim(mine, other):
-    chips, made, _, channels = other.shape
-    return pl.pallas_call(
-        functools.partial(rim_kernel, chips),
-        out_shape=[jax.ShapeDtypeStruct((2 * chips, made, channels), jnp.bfloat16)] * 2,
-        in_specs=[INSIDE] * (chips + 1),
+    made = taken.shape[1]
+    pairs = []
+    for i, (hop, piece) in enumerate(zip(hops, pieces)):
+        pairs += [(hop, piece.at[pl.ds(core * made, made)]), (hop + 1, taken.at[i])]
+    return pairs
+
+
+def inner_rows(hops, pieces, taken):
+    *far, own = pieces
+    pairs = [(hop + j, piece.at[j]) for hop, piece in zip(hops, far) for j in range(2)]
+    return pairs + [(0, own), (1, taken.at[2 * len(hops) - 1])]
+
+
+def rim_kernel(hops, *refs):
+    *pieces, taken, left, right = refs
+    for k, piece in outer_rows(hops, pieces, taken):
+        part = piece[...]
+        left[k] = part[:, 0]
+        right[k] = part[:, part.shape[1] - 1]
+
+
+def rim(hops, pieces, taken):
+    _, made, _, channels = taken.shape
+    return pl.pallas_call(
+        functools.partial(rim_kernel, hops),
+        out_shape=[jax.ShapeDtypeStruct((2 * len(hops), made, channels), jnp.bfloat16)] * 2,
+        in_specs=[INSIDE] * (len(pieces) + 1),
         out_specs=[INSIDE] * 2,
         compiler_params=pltpu.CompilerParams(vmem_limit_bytes=4 * MIB),
         name="rim",
-    )(*mine, other)
-
-
-def filter_kernel(chips, *refs):
-    pieces = refs[:chips]
-    other, inner, left, right, w_depth, out, outer = refs[chips:]
-    chip, core = place()
-    made = other.shape[1]
-    for k in range(chips):
-        row = 2 * (chip ^ k)
-        outer[row + core] = pieces[k][pl.ds(core * made, made)]
-        outer[row + 1 - core] = other[k]
+    )(*pieces, taken)
+
+
+def filter_kernel(hops, *refs):
+    count = len(hops)
+    taken, left, right, w_depth, out, outer, inner = refs[2 * count :]
+    me = lax.axis_index("frm")
+    for k, piece in outer_rows(hops, refs[:count], taken):
+        outer[me ^ k] = piece[...]
+    for k, piece in inner_rows(hops, refs[count : 2 * count], taken):
+        inner[me ^ k] = piece[...]
     frames, height, cols, channels = out.shape
     edge = cols // 4
     lanes = 128
@@ -225,9 +239,8 @@
                 between = inner[row, frame, :, part].astype(jnp.float32)
                 mid = jnp.concatenate([sides[:edge], between, sides[edge:]], axis=0)
                 spot = lax.broadcasted_iota(jnp.int32, mid.shape, 0)
-                slot = 2 * (chip ^ (row // 2)) + (core ^ (row % 2))
-                low = left[slot, frame, part].astype(jnp.float32)[None]
-                high = right[slot, frame, part].astype(jnp.float32)[None]
+                low = left[me ^ row, frame, part].astype(jnp.float32)[None]
+                high = right[me ^ row, frame, part].astype(jnp.float32)[None]
                 before = jnp.where(spot == 0, low, pltpu.roll(mid, 1, 0))
                 after = jnp.where(spot == cols - 1, high, pltpu.roll(mid, cols - 1, 0))
                 return [
@@ -250,20 +263,21 @@
     lax.fori_loop(0, channels // lanes, one_part, 0)
 
 
-def depth_filter(outer, other, inner, left, right, w_depth):
-    height, frames, width, channels = inner.shape
+def depth_filter(hops, outer, inner, taken, left, right, w_depth):
+    height, frames, channels = left.shape
+    width = taken.shape[2]
     cols = 2 * width
     size = frames * height * cols * channels
     return pl.pallas_call(
-        functools.partial(filter_kernel, len(outer)),
+        functools.partial(filter_kernel, hops),
         out_shape=jax.ShapeDtypeStruct((frames, height, cols, channels), jnp.bfloat16),
-        in_specs=[INSIDE] * (len(outer) + 5),
+        in_specs=[INSIDE] * (2 * len(hops) + 4),
         out_specs=INSIDE,
-        scratch_shapes=[pltpu.VMEM((height, frames, width, channels), jnp.bfloat16)],
-        compiler_params=pltpu.CompilerParams(vmem_limit_bytes=8 * MIB),
+        scratch_shapes=[pltpu.VMEM((height, frames, width, channels), jnp.bfloat16)] * 2,
+        compiler_params=pltpu.CompilerParams(vmem_limit_bytes=10 * MIB),
         cost_estimate=pl.CostEstimate(flops=18 * size, bytes_accessed=4 * size, transcendentals=0),
         name="depth_filter",
-    )(*outer, other, inner, left, right, w_depth)
+    )(*outer, *inner, taken, left, right, w_depth)
 
 
 def local(video, norm_gain, w_query, w_key, w_value, w_out, w_time, w_depth):
@@ -279,7 +293,7 @@
     def swap(block, k):
         return lax.ppermute(block, "frm", [(i, i ^ k) for i in range(count)]) if k else block
 
-    far = list(range(chips - 1, 0, -1))
+    far = [chips - 1, *([1] if chips > 2 else []), *range(chips - 2, 1, -1)]
     hops = [2 * k for k in [*far, 0]]
     pieces = cut(lambda me: ([me ^ k for k in hops], [me ^ k ^ 1 for k in hops]), chips, video)
     *outer, outer_stack = pieces[: chips + 1]
@@ -314,25 +328,36 @@
             pairs.append((piece.at[pl.ds(span, span)], (me ^ k ^ 1) * span))
         return pairs + [(own, me * span), (other.at[len(far)], (me ^ 1) * span)]
 
-    outer = attend(inward, [*outer_far, outer[-1], outer_other], weights, frames, chips, "attend_outer")
-    outer = [swap(piece, 2 * k) for k, piece in enumerate(outer)]
-    (inner,) = attend(inward, [*inner_far, inner[-1], inner_other], weights, frames, 1, "attend_inner")
-    *outer, inner = lax.optimization_barrier((*outer, inner))
-
-    def halves(ins, outs):
+    outer = attend(inward, hops, True, [*outer_far, outer[-1], outer_other], weights, frames, "attend_outer")
+    outer = [swap(piece, k) for k, piece in zip(hops, outer)]
+    *keep, give = attend(inward, hops, False, [*inner_far, inner[-1], inner_other], weights, frames, "attend_inner")
+
+    def for_mate(ins, outs):
         _, core = place()
-        return [(piece.at[pl.ds((1 - core) * made, made)], outs[0].at[k]) for k, piece in enumerate(ins)]
-
-    outer_other = swap(gather(halves, outer, [(chips, made, width, channels)], "halves")[0], 1)
-    inner = lax.all_to_all(
-        inner.reshape(count, made, width, channels), "frm", split_axis=0, concat_axis=0, tiled=True
-    )
-    low_side, high_side = rim(outer, outer_other)
+        *pieces, give = ins
+        pairs = [(piece.at[pl.ds((1 - core) * made, made)], outs[0].at[i]) for i, piece in enumerate(pieces)]
+        return pairs + [(give, outs[0].at[pl.ds(chips, chips)])]
+
+    (stack,) = gather(for_mate, [*outer, give], [(2 * chips, made, width, channels)], "stack_back")
+    taken = swap(stack, 1)
+
+    def joined_back(ins, outs):
+        *keep, taken = ins
+        pairs = []
+        for i, own in enumerate(keep):
+            pairs += [(own, outs[i].at[0]), (taken.at[chips + i], outs[i].at[1])]
+        return pairs
+
+    inner = gather(joined_back, [*keep[:-1], taken], [(2, made, width, channels)] * len(far), "join_back")
+    inner = [swap(piece, k) for k, piece in zip(hops, inner)]
+    low_side, high_side = rim(hops, outer, taken)
+    nearest = far.index(1)
+    low_side, high_side, inner[nearest] = lax.optimization_barrier((low_side, high_side, inner[nearest]))
     line = lax.axis_size("col")
     upward = [(i, i + 1) for i in range(line - 1)]
     left = lax.ppermute(high_side, "col", upward)
     right = lax.ppermute(low_side, "col", [(b, a) for a, b in upward])
-    return depth_filter(outer, outer_other, inner, left, right, w_depth)
+    return depth_filter(hops, outer, [*inner, keep[-1]], taken, left, right, w_depth)
 
 
 def solution(mesh):

time: 89.7 us -> 87.4 us (0.974)
  starting transfers between devices: 36.4 us -> 31 us
  waiting for transfers between devices: 35.1 us -> 38.5 us
    ppermute x12 -> x15, waiting for transfers between devices: 26.4 us -> 38.5 us  [swap(): lax.ppermute(block, 'frm', [(i, i ^ k) for i in range(count)])]
    all_to_all x1 -> x0, starting transfers between devices: 7.74 us -> none  [local(): lax.all_to_all(inner.reshape(count, made, width, channels), 'frm', split_...]
    all_to_all x1 -> x0, waiting for transfers between devices: 4.26 us -> none  [local(): lax.all_to_all(inner.reshape(count, made, width, channels), 'frm', split_...]
    ppermute x1, waiting for transfers between devices: 4.23 us -> 0.01 us  [local(): right = lax.ppermute(low_side, 'col', [(b, a) for a, b in upward])]
    ppermute x12 -> x15, starting transfers between devices: 23.9 us -> 26.3 us  [swap(): lax.ppermute(block, 'frm', [(i, i ^ k) for i in range(count)])]
  transfers between devices with their start and end apart: 15 -> 17, of which waited for: 8 -> 7; matrix products, arithmetic and copies ran while one was open for 0% -> 0% of each run, Pallas kernels for 15% -> 14%
where the time goes in v6:
time: 87.4 us; the launch traced here: 86.8 us
  waiting for transfers between devices  38.5 us (44%)
  starting transfers between devices  31 us (35%)
  Pallas kernels  15.4 us (18%)
  local copies, waits for them, and re-layouts  1.62 us (2%)
    ppermute x15, waiting for transfers between devices, swap(): lax.ppermute(block, 'frm', [(i, i ^ k) for i in range(count)])  38.5 us
    ppermute x15, starting transfers between devices, swap(): lax.ppermute(block, 'frm', [(i, i ^ k) for i in range(count)])  26.3 us
    pallas_call x2, Pallas kernels, attend(): pl.pallas_call(functools.partial(attend_kernel, inward, hops, paired, len...  12.3 us
    ppermute x1, starting transfers between devices, local(): left = lax.ppermute(high_side, 'col', upward)  3.39 us
    pallas_call x1, Pallas kernels, depth_filter(): pl.pallas_call(functools.partial(filter_kernel, hops), out_shape=jax.Shap...  2.64 us
  transfers between devices with their start and end apart: 17, of which 7 were waited for; matrix products, arithmetic and copies ran while one was open for 0% of the time, Pallas kernels for 14%

profile of v6, /device:TPU:0, one launch (start us, length us, event | category | flops | bytes accessed | tf_op | source)
XLA Modules:
  0.0 86.8 jit_solution(5036337121493306625)
XLA Ops:
  0.0 0.0 copy-start
  0.0 1.6 %copy-done = bf16[8,8,32,512]{3,2,1,0:T(8,128)(2,1)S(1)} copy-done((bf16[8,8,32,512]{3,2,1,0:T(8,128)(2,1)S(1)}, bf16[8,8,32,512]{3,2,1,0:T(8,128)(2,1)}, u32[]{:S(2)}) %copy-start) | copy-done | bytes 2097176
  1.6 0.0 copy-start.2
  1.6 0.0 copy-start.3
  1.6 0.0 copy-start.4
  1.6 0.0 copy-start.5
  1.6 0.0 copy-start.6
  1.6 0.0 copy-start.7
  1.6 0.1 cut.1
  1.8 0.5 collective-permute-start
  2.3 1.5 %collective-permute-done.refs_3_.refs_4_ = bf16[4,8,16,512]{3,2,1,0:T(8,128)(2,1)S(1)} collective-permute-done((bf16[4,8,16,512]{3,2,1,0:T(8,128)(2,1)S(1)}, bf16[4,8,16,512]{3,2,1,0:T(8,128)(2,1)S(1)}, u32[]{:S(2)}, u32[]{:S(2)}) %collective-permute-start) | collective-permute-done | bytes 524320 | tf_op jit(solution)/shard_map/ppermute | solution.py:294
  3.8 0.1 join_outer.1
  3.9 0.4 collective-permute-start.2
  4.3 4.7 %collective-permute-start.1 = (bf16[16,16,512]{2,1,0:T(8,128)(2,1)S(1)}, bf16[16,16,512]{2,1,0:T(8,128)(2,1)S(1)}, u32[]{:S(2)}, u32[]{:S(2)}) collective-permute-start(bf16[16,16,512]{2,1,0:T(8,128)(2,1)S(1)} %get-tuple-element.54), channel_id=1, source_target_pairs={{0,24},{4,28},{8,16},{12,20},{16,8},{20,12},{24,0},{28,4},{1,25},{... | collective-permute-start | bytes 786440 | tf_op jit(solution)/shard_map/ppermute | solution.py:294
  9.1 0.0 collective-permute-start.3
  9.1 0.6 collective-permute-start.4
  9.7 0.0 collective-permute-done.2.refs_3_.refs_4_
  9.7 0.1 join_inner.1
  9.7 6.6 %collective-permute-done.1.refs_0_ = bf16[16,16,512]{2,1,0:T(8,128)(2,1)S(1)} collective-permute-done((bf16[16,16,512]{2,1,0:T(8,128)(2,1)S(1)}, bf16[16,16,512]{2,1,0:T(8,128)(2,1)S(1)}, u32[]{:S(2)}, u32[]{:S(2)}) %collective-permute-start.1) | collective-permute-done | bytes 262176 | tf_op jit(solution)/shard_map/ppermute | solution.py:294
  16.3 3.7 %collective-permute-start.8 = (bf16[16,16,512]{2,1,0:T(8,128)(2,1)S(1)}, bf16[16,16,512]{2,1,0:T(8,128)(2,1)S(1)}, u32[]{:S(2)}, u32[]{:S(2)}) collective-permute-start(bf16[16,16,512]{2,1,0:T(8,128)(2,1)S(1)} %get-tuple-element.70), channel_id=1, source_target_pairs={{0,24},{4,28},{8,16},{12,20},{16,8},{20,12},{24,0},{28,4},{1,25},{... | collective-permute-start | bytes 786440 | tf_op jit(solution)/shard_map/ppermute | solution.py:294
  20.1 3.3 %collective-permute-start.9 = (bf16[16,16,512]{2,1,0:T(8,128)(2,1)S(1)}, bf16[16,16,512]{2,1,0:T(8,128)(2,1)S(1)}, u32[]{:S(2)}, u32[]{:S(2)}) collective-permute-start(bf16[16,16,512]{2,1,0:T(8,128)(2,1)S(1)} %get-tuple-element.71), channel_id=1, source_target_pairs={{0,8},{4,12},{8,0},{12,4},{16,24},{20,28},{24,16},{28,20},{1,9},{5... | collective-permute-start | bytes 786440 | tf_op jit(solution)/shard_map/ppermute | solution.py:294
  23.4 0.0 collective-permute-start.10
  23.4 0.0 collective-permute-done.3.refs_1_
  23.4 14.8 %collective-permute-done.4.refs_2_ = bf16[16,16,512]{2,1,0:T(8,128)(2,1)S(1)} collective-permute-done((bf16[16,16,512]{2,1,0:T(8,128)(2,1)S(1)}, bf16[16,16,512]{2,1,0:T(8,128)(2,1)S(1)}, u32[]{:S(2)}, u32[]{:S(2)}) %collective-permute-start.4) | collective-permute-done | bytes 262176 | tf_op jit(solution)/shard_map/ppermute | solution.py:294
  38.1 0.0 copy-done.2
  38.1 0.0 copy-done.3
  38.1 0.0 copy-done.4
  38.1 0.0 copy-done.5
  38.2 0.0 copy-done.6
  38.2 0.0 copy-done.7
  38.2 6.2 %attend_outer.1 = (bf16[8,16,512]{2,1,0:T(8,128)(2,1)S(1)}, bf16[8,16,512]{2,1,0:T(8,128)(2,1)S(1)}, bf16[8,16,512]{2,1,0:T(8,128)(2,1)S(1)}, bf16[8,16,512]{2,1,0:T(8,128)(2,1)S(1)}) custom-call(bf16[16,16,512]{2,1,0:T(8,128)(2,1)S(1)} %collective-permute-done.1.refs_0_, bf16[16,16,512]{2,1,0:T(8,128)(2,1)S(1)} %collective-permute-done.3.refs_1_, ...), custom_call_target="tpu_custom_call" | custom-call | flops 4026531840 | bytes 5242880 | tf_op jit(solution)/shard_map/attend_outer/pallas_call | solution.py:162
  44.4 2.5 %collective-permute-start.5 = (bf16[8,16,512]{2,1,0:T(8,128)(2,1)S(1)}, bf16[8,16,512]{2,1,0:T(8,128)(2,1)S(1)}, u32[]{:S(2)}, u32[]{:S(2)}) collective-permute-start(bf16[8,16,512]{2,1,0:T(8,128)(2,1)S(1)} %get-tuple-element.66), channel_id=1, source_target_pairs={{0,24},{4,28},{8,16},{12,20},{16,8},{20,12},{24,0},{28,4},{1,25},{... | collective-permute-start | bytes 393224 | tf_op jit(solution)/shard_map/ppermute | solution.py:294
  46.9 0.0 collective-permute-start.6
  46.9 0.0 collective-permute-done.8.refs_0_
  46.9 6.9 %collective-permute-start.7 = (bf16[8,16,512]{2,1,0:T(8,128)(2,1)S(1)}, bf16[8,16,512]{2,1,0:T(8,128)(2,1)S(1)}, u32[]{:S(2)}, u32[]{:S(2)}) collective-permute-start(bf16[8,16,512]{2,1,0:T(8,128)(2,1)S(1)} %get-tuple-element.68), channel_id=1, source_target_pairs={{0,16},{4,20},{8,24},{12,28},{16,0},{20,4},{24,8},{28,12},{1,17},{... | collective-permute-start | bytes 393224 | tf_op jit(solution)/shard_map/ppermute | solution.py:294
  53.8 0.0 collective-permute-done.9.refs_1_
  53.8 6.9 %collective-permute-done.10.refs_2_ = bf16[16,16,512]{2,1,0:T(8,128)(2,1)S(1)} collective-permute-done((bf16[16,16,512]{2,1,0:T(8,128)(2,1)S(1)}, bf16[16,16,512]{2,1,0:T(8,128)(2,1)S(1)}, u32[]{:S(2)}, u32[]{:S(2)}) %collective-permute-start.10) | collective-permute-done | bytes 262176 | tf_op jit(solution)/shard_map/ppermute | solution.py:294
  60.6 6.2 %attend_inner.1 = (bf16[4,16,512]{2,1,0:T(8,128)(2,1)S(1)}, bf16[4,16,512]{2,1,0:T(8,128)(2,1)S(1)}, bf16[4,16,512]{2,1,0:T(8,128)(2,1)S(1)}, bf16[4,16,512]{2,1,0:T(8,128)(2,1)S(1)}, bf16[4,4,16,512]{3,2,1,0:T(8,128)(2,1)S(1)}) custom-call(bf16[16,16,512]{2,1,0:T(8,128)(2,1)S(1)} %collective-permute-done.8.refs_0_, ...), custom_call_target="tpu_custom_call" | custom-call | flops 4026531840 | bytes 5242880 | tf_op jit(solution)/shard_map/attend_inner/pallas_call | solution.py:162
  66.8 0.0 copy-start.1
  66.8 0.0 collective-permute-done.5.refs_0_
  66.8 0.0 collective-permute-done.6.refs_1_
  66.8 0.0 collective-permute-done.7.refs_2_
  66.9 0.1 collective-permute-start.11
  67.0 1.9 %collective-permute-done.11.refs_3_.refs_4_.refs_8_ = bf16[8,4,16,512]{3,2,1,0:T(8,128)(2,1)S(1)} collective-permute-done((bf16[8,4,16,512]{3,2,1,0:T(8,128)(2,1)S(1)}, bf16[8,4,16,512]{3,2,1,0:T(8,128)(2,1)S(1)}, u32[]{:S(2)}, u32[]{:S(2)}) %collective-permute-start.11) | collective-permute-done | bytes 524320 | tf_op jit(solution)/shard_map/ppermute | solution.py:294
  68.9 0.1 collective-permute-start.13
  69.0 2.5 %collective-permute-start.12 = (bf16[2,4,16,512]{3,2,1,0:T(8,128)(2,1)S(1)}, bf16[2,4,16,512]{3,2,1,0:T(8,128)(2,1)S(1)}, u32[]{:S(2)}, u32[]{:S(2)}) collective-permute-start(bf16[2,4,16,512]{3,2,1,0:T(8,128)(2,1)S(1)} %get-tuple-element.78), channel_id=1, source_target_pairs={{0,24},{4,28},{8,16},{12,20},{16,8},{20,12},{24,0},{28,4},{1,25},{... | collective-permute-start | bytes 393224 | tf_op jit(solution)/shard_map/ppermute | solution.py:294
  71.5 1.0 %collective-permute-start.14 = (bf16[2,4,16,512]{3,2,1,0:T(8,128)(2,1)S(1)}, bf16[2,4,16,512]{3,2,1,0:T(8,128)(2,1)S(1)}, u32[]{:S(2)}, u32[]{:S(2)}) collective-permute-start(bf16[2,4,16,512]{3,2,1,0:T(8,128)(2,1)S(1)} %get-tuple-element.83), channel_id=1, source_target_pairs={{0,16},{4,20},{8,24},{12,28},{16,0},{20,4},{24,8},{28,12},{1,17},{... | collective-permute-start | bytes 393224 | tf_op jit(solution)/shard_map/ppermute | solution.py:294
  72.5 0.1 rim.1
  72.6 1.9 %collective-permute-done.13.refs_5_ = bf16[2,4,16,512]{3,2,1,0:T(8,128)(2,1)S(1)} collective-permute-done((bf16[2,4,16,512]{3,2,1,0:T(8,128)(2,1)S(1)}, bf16[2,4,16,512]{3,2,1,0:T(8,128)(2,1)S(1)}, u32[]{:S(2)}, u32[]{:S(2)}) %collective-permute-start.13) | collective-permute-done | bytes 131104 | tf_op jit(solution)/shard_map/ppermute | solution.py:294
  74.5 3.4 %collective-permute-start.15 = (bf16[8,4,512]{2,1,0:T(4,128)(2,1)S(1)}, bf16[8,4,512]{2,1,0:T(4,128)(2,1)S(1)}, u32[]{:S(2)}, u32[]{:S(2)}) collective-permute-start(bf16[8,4,512]{2,1,0:T(4,128)(2,1)S(1)} %get-tuple-element.85), channel_id=1, source_target_pairs={{0,1},{1,2},{2,3},{4,5},{5,6},{6,7},{8,9},{9,10},{10,11},{12,13},{... | collective-permute-start | bytes 98312 | tf_op jit(solution)/shard_map/ppermute | solution.py:358
  77.9 1.3 %collective-permute-start.16 = (bf16[8,4,512]{2,1,0:T(4,128)(2,1)S(1)}, bf16[8,4,512]{2,1,0:T(4,128)(2,1)S(1)}, u32[]{:S(2)}, u32[]{:S(2)}) collective-permute-start(bf16[8,4,512]{2,1,0:T(4,128)(2,1)S(1)} %get-tuple-element.86), channel_id=1, source_target_pairs={{1,0},{2,1},{3,2},{5,4},{6,5},{7,6},{9,8},{10,9},{11,10},{13,12},{... | collective-permute-start | bytes 98312 | tf_op jit(solution)/shard_map/ppermute | solution.py:359
  79.2 0.0 collective-permute-done.12.refs_4_
  79.2 4.9 %collective-permute-done.14.refs_6_ = bf16[2,4,16,512]{3,2,1,0:T(8,128)(2,1)S(1)} collective-permute-done((bf16[2,4,16,512]{3,2,1,0:T(8,128)(2,1)S(1)}, bf16[2,4,16,512]{3,2,1,0:T(8,128)(2,1)S(1)}, u32[]{:S(2)}, u32[]{:S(2)}) %collective-permute-start.14) | collective-permute-done | bytes 131104 | tf_op jit(solution)/shard_map/ppermute | solution.py:294
  84.1 0.0 collective-permute-done.15.refs_9_
  84.1 0.0 collective-permute-done.16.refs_10_
  84.1 0.0 copy-done.1
  84.1 2.6 %depth_filter.1 = bf16[4,8,32,512]{3,2,1,0:T(8,128)(2,1)} custom-call(bf16[8,16,512]{2,1,0:T(8,128)(2,1)S(1)} %collective-permute-done.5.refs_0_, bf16[8,16,512]{2,1,0:T(8,128)(2,1)S(1)} %collective-permute-done.6.refs_1_, bf16[8,16,512]{2,1,0:T(8,128)(2,1)S(1)} %collective-permute-done.7.refs_2_, bf16[8,16,512]{2,1,0:T(8,128)(2,1)S(1)} %get-tuple-element.69.refs_3_, ...), custom_call_target="tpu_custom_call" | custom-call | flops 9437184 | bytes 2097152 | tf_op jit(solution)/shard_map/depth_filter/pallas_call | solution.py:271
  (2 shorter events, 0.1 us)
Async XLA Ops:
  0.0 1.6 %copy-start = (bf16[8,8,32,512]{3,2,1,0:T(8,128)(2,1)S(1)}, bf16[8,8,32,512]{3,2,1,0:T(8,128)(2,1)}, u32[]{:S(2)}) copy-start(bf16[8,8,32,512]{3,2,1,0:T(8,128)(2,1)} %video.1) | copy-start | bytes 6291460
  1.6 36.5 %copy-start.2 = (bf16[3,512,512]{2,1,0:T(8,128)(2,1)S(1)}, bf16[3,512,512]{2,1,0:T(8,128)(2,1)}, u32[]{:S(2)}) copy-start(bf16[3,512,512]{2,1,0:T(8,128)(2,1)} %refs_10_.3) | copy-start | bytes 4718596
  1.6 36.5 %copy-start.3 = (bf16[512,512]{1,0:T(8,128)(2,1)S(1)}, bf16[512,512]{1,0:T(8,128)(2,1)}, u32[]{:S(2)}) copy-start(bf16[512,512]{1,0:T(8,128)(2,1)} %refs_6_.3) | copy-start | bytes 1572868
  1.6 36.5 %copy-start.4 = (bf16[512,512]{1,0:T(8,128)(2,1)S(1)}, bf16[512,512]{1,0:T(8,128)(2,1)}, u32[]{:S(2)}) copy-start(bf16[512,512]{1,0:T(8,128)(2,1)} %refs_7_.3) | copy-start | bytes 1572868
  1.6 36.5 %copy-start.5 = (bf16[512,512]{1,0:T(8,128)(2,1)S(1)}, bf16[512,512]{1,0:T(8,128)(2,1)}, u32[]{:S(2)}) copy-start(bf16[512,512]{1,0:T(8,128)(2,1)} %refs_8_.3) | copy-start | bytes 1572868
  1.6 36.6 %copy-start.6 = (bf16[512,512]{1,0:T(8,128)(2,1)S(1)}, bf16[512,512]{1,0:T(8,128)(2,1)}, u32[]{:S(2)}) copy-start(bf16[512,512]{1,0:T(8,128)(2,1)} %refs_9_.3) | copy-start | bytes 1572868
  1.6 36.6 %copy-start.7 = (f32[512]{0:T(512)S(1)}, f32[512]{0:T(512)}, u32[]{:S(2)}) copy-start(f32[512]{0:T(512)} %param.9) | copy-start | bytes 6148
  1.8 2.1 %collective-permute-start = (bf16[4,8,16,512]{3,2,1,0:T(8,128)(2,1)S(1)}, bf16[4,8,16,512]{3,2,1,0:T(8,128)(2,1)S(1)}, u32[]{:S(2)}, u32[]{:S(2)}) collective-permute-start(bf16[4,8,16,512]{3,2,1,0:T(8,128)(2,1)S(1)} %get-tuple-element.49), channel_id=1, source_target_pairs={{0,4},{4,0},{8,12},{12,8},{16,20},{20,16},{24,28},{28,24},{1,5},{5... | collective-permute-start | bytes 1572872 | tf_op jit(solution)/shard_map/ppermute | solution.py:294
  3.9 5.8 %collective-permute-start.2 = (bf16[4,8,16,512]{3,2,1,0:T(8,128)(2,1)S(1)}, bf16[4,8,16,512]{3,2,1,0:T(8,128)(2,1)S(1)}, u32[]{:S(2)}, u32[]{:S(2)}) collective-permute-start(bf16[4,8,16,512]{3,2,1,0:T(8,128)(2,1)S(1)} %get-tuple-element.58), channel_id=1, source_target_pairs={{0,4},{4,0},{8,12},{12,8},{16,20},{20,16},{24,28},{28,24},{1,5},{5... | collective-permute-start | bytes 1572872 | tf_op jit(solution)/shard_map/ppermute | solution.py:294
  4.3 12.0 %collective-permute-start.1 = (bf16[16,16,512]{2,1,0:T(8,128)(2,1)S(1)}, bf16[16,16,512]{2,1,0:T(8,128)(2,1)S(1)}, u32[]{:S(2)}, u32[]{:S(2)}) collective-permute-start(bf16[16,16,512]{2,1,0:T(8,128)(2,1)S(1)} %get-tuple-element.54), channel_id=1, source_target_pairs={{0,24},{4,28},{8,16},{12,20},{16,8},{20,12},{24,0},{28,4},{1,25},{... | collective-permute-start | bytes 786440 | tf_op jit(solution)/shard_map/ppermute | solution.py:294
  9.1 14.3 %collective-permute-start.3 = (bf16[16,16,512]{2,1,0:T(8,128)(2,1)S(1)}, bf16[16,16,512]{2,1,0:T(8,128)(2,1)S(1)}, u32[]{:S(2)}, u32[]{:S(2)}) collective-permute-start(bf16[16,16,512]{2,1,0:T(8,128)(2,1)S(1)} %get-tuple-element.63), channel_id=1, source_target_pairs={{0,8},{4,12},{8,0},{12,4},{16,24},{20,28},{24,16},{28,20},{1,9},{5... | collective-permute-start | bytes 786440 | tf_op jit(solution)/shard_map/ppermute | solution.py:294
  9.1 29.0 %collective-permute-start.4 = (bf16[16,16,512]{2,1,0:T(8,128)(2,1)S(1)}, bf16[16,16,512]{2,1,0:T(8,128)(2,1)S(1)}, u32[]{:S(2)}, u32[]{:S(2)}) collective-permute-start(bf16[16,16,512]{2,1,0:T(8,128)(2,1)S(1)} %get-tuple-element.64), channel_id=1, source_target_pairs={{0,16},{4,20},{8,24},{12,28},{16,0},{20,4},{24,8},{28,12},{1,17},{... | collective-permute-start | bytes 786440 | tf_op jit(solution)/shard_map/ppermute | solution.py:294
  16.3 30.6 %collective-permute-start.8 = (bf16[16,16,512]{2,1,0:T(8,128)(2,1)S(1)}, bf16[16,16,512]{2,1,0:T(8,128)(2,1)S(1)}, u32[]{:S(2)}, u32[]{:S(2)}) collective-permute-start(bf16[16,16,512]{2,1,0:T(8,128)(2,1)S(1)} %get-tuple-element.70), channel_id=1, source_target_pairs={{0,24},{4,28},{8,16},{12,20},{16,8},{20,12},{24,0},{28,4},{1,25},{... | collective-permute-start | bytes 786440 | tf_op jit(solution)/shard_map/ppermute | solution.py:294
  20.1 33.7 %collective-permute-start.9 = (bf16[16,16,512]{2,1,0:T(8,128)(2,1)S(1)}, bf16[16,16,512]{2,1,0:T(8,128)(2,1)S(1)}, u32[]{:S(2)}, u32[]{:S(2)}) collective-permute-start(bf16[16,16,512]{2,1,0:T(8,128)(2,1)S(1)} %get-tuple-element.71), channel_id=1, source_target_pairs={{0,8},{4,12},{8,0},{12,4},{16,24},{20,28},{24,16},{28,20},{1,9},{5... | collective-permute-start | bytes 786440 | tf_op jit(solution)/shard_map/ppermute | solution.py:294
  23.4 37.3 %collective-permute-start.10 = (bf16[16,16,512]{2,1,0:T(8,128)(2,1)S(1)}, bf16[16,16,512]{2,1,0:T(8,128)(2,1)S(1)}, u32[]{:S(2)}, u32[]{:S(2)}) collective-permute-start(bf16[16,16,512]{2,1,0:T(8,128)(2,1)S(1)} %get-tuple-element.72), channel_id=1, source_target_pairs={{0,16},{4,20},{8,24},{12,28},{16,0},{20,4},{24,8},{28,12},{1,17},{... | collective-permute-start | bytes 786440 | tf_op jit(solution)/shard_map/ppermute | solution.py:294
  44.4 22.5 %collective-permute-start.5 = (bf16[8,16,512]{2,1,0:T(8,128)(2,1)S(1)}, bf16[8,16,512]{2,1,0:T(8,128)(2,1)S(1)}, u32[]{:S(2)}, u32[]{:S(2)}) collective-permute-start(bf16[8,16,512]{2,1,0:T(8,128)(2,1)S(1)} %get-tuple-element.66), channel_id=1, source_target_pairs={{0,24},{4,28},{8,16},{12,20},{16,8},{20,12},{24,0},{28,4},{1,25},{... | collective-permute-start | bytes 393224 | tf_op jit(solution)/shard_map/ppermute | solution.py:294
  46.9 19.9 %collective-permute-start.6 = (bf16[8,16,512]{2,1,0:T(8,128)(2,1)S(1)}, bf16[8,16,512]{2,1,0:T(8,128)(2,1)S(1)}, u32[]{:S(2)}, u32[]{:S(2)}) collective-permute-start(bf16[8,16,512]{2,1,0:T(8,128)(2,1)S(1)} %get-tuple-element.67), channel_id=1, source_target_pairs={{0,8},{4,12},{8,0},{12,4},{16,24},{20,28},{24,16},{28,20},{1,9},{5... | collective-permute-start | bytes 393224 | tf_op jit(solution)/shard_map/ppermute | solution.py:294
  46.9 20.0 %collective-permute-start.7 = (bf16[8,16,512]{2,1,0:T(8,128)(2,1)S(1)}, bf16[8,16,512]{2,1,0:T(8,128)(2,1)S(1)}, u32[]{:S(2)}, u32[]{:S(2)}) collective-permute-start(bf16[8,16,512]{2,1,0:T(8,128)(2,1)S(1)} %get-tuple-element.68), channel_id=1, source_target_pairs={{0,16},{4,20},{8,24},{12,28},{16,0},{20,4},{24,8},{28,12},{1,17},{... | collective-permute-start | bytes 393224 | tf_op jit(solution)/shard_map/ppermute | solution.py:294
  66.8 17.3 %copy-start.1 = (f32[3,3,512]{2,1,0:T(4,128)S(1)}, f32[3,3,512]{2,1,0:T(4,128)}, u32[]{:S(2)}) copy-start(f32[3,3,512]{2,1,0:T(4,128)} %refs_11_.1) | copy-start | bytes 55300
  66.9 2.0 %collective-permute-start.11 = (bf16[8,4,16,512]{3,2,1,0:T(8,128)(2,1)S(1)}, bf16[8,4,16,512]{3,2,1,0:T(8,128)(2,1)S(1)}, u32[]{:S(2)}, u32[]{:S(2)}) collective-permute-start(bf16[8,4,16,512]{3,2,1,0:T(8,128)(2,1)S(1)} %stack_back.1), channel_id=1, source_target_pairs={{0,4},{4,0},{8,12},{12,8},{16,20},{20,16},{24,28},{28,24},{1,5},{5... | collective-permute-start | bytes 1572872 | tf_op jit(solution)/shard_map/ppermute | solution.py:294
  68.9 5.6 %collective-permute-start.13 = (bf16[2,4,16,512]{3,2,1,0:T(8,128)(2,1)S(1)}, bf16[2,4,16,512]{3,2,1,0:T(8,128)(2,1)S(1)}, u32[]{:S(2)}, u32[]{:S(2)}) collective-permute-start(bf16[2,4,16,512]{3,2,1,0:T(8,128)(2,1)S(1)} %get-tuple-element.81), channel_id=1, source_target_pairs={{0,8},{4,12},{8,0},{12,4},{16,24},{20,28},{24,16},{28,20},{1,9},{5... | collective-permute-start | bytes 393224 | tf_op jit(solution)/shard_map/ppermute | solution.py:294
  69.0 10.2 %collective-permute-start.12 = (bf16[2,4,16,512]{3,2,1,0:T(8,128)(2,1)S(1)}, bf16[2,4,16,512]{3,2,1,0:T(8,128)(2,1)S(1)}, u32[]{:S(2)}, u32[]{:S(2)}) collective-permute-start(bf16[2,4,16,512]{3,2,1,0:T(8,128)(2,1)S(1)} %get-tuple-element.78), channel_id=1, source_target_pairs={{0,24},{4,28},{8,16},{12,20},{16,8},{20,12},{24,0},{28,4},{1,25},{... | collective-permute-start | bytes 393224 | tf_op jit(solution)/shard_map/ppermute | solution.py:294
  71.5 12.6 %collective-permute-start.14 = (bf16[2,4,16,512]{3,2,1,0:T(8,128)(2,1)S(1)}, bf16[2,4,16,512]{3,2,1,0:T(8,128)(2,1)S(1)}, u32[]{:S(2)}, u32[]{:S(2)}) collective-permute-start(bf16[2,4,16,512]{3,2,1,0:T(8,128)(2,1)S(1)} %get-tuple-element.83), channel_id=1, source_target_pairs={{0,16},{4,20},{8,24},{12,28},{16,0},{20,4},{24,8},{28,12},{1,17},{... | collective-permute-start | bytes 393224 | tf_op jit(solution)/shard_map/ppermute | solution.py:294
  74.5 9.6 %collective-permute-start.15 = (bf16[8,4,512]{2,1,0:T(4,128)(2,1)S(1)}, bf16[8,4,512]{2,1,0:T(4,128)(2,1)S(1)}, u32[]{:S(2)}, u32[]{:S(2)}) collective-permute-start(bf16[8,4,512]{2,1,0:T(4,128)(2,1)S(1)} %get-tuple-element.85), channel_id=1, source_target_pairs={{0,1},{1,2},{2,3},{4,5},{5,6},{6,7},{8,9},{9,10},{10,11},{12,13},{... | collective-permute-start | bytes 98312 | tf_op jit(solution)/shard_map/ppermute | solution.py:358
  77.9 6.2 %collective-permute-start.16 = (bf16[8,4,512]{2,1,0:T(4,128)(2,1)S(1)}, bf16[8,4,512]{2,1,0:T(4,128)(2,1)S(1)}, u32[]{:S(2)}, u32[]{:S(2)}) collective-permute-start(bf16[8,4,512]{2,1,0:T(4,128)(2,1)S(1)} %get-tuple-element.86), channel_id=1, source_target_pairs={{1,0},{2,1},{3,2},{5,4},{6,5},{7,6},{9,8},{10,9},{11,10},{13,12},{... | collective-permute-start | bytes 98312 | tf_op jit(solution)/shard_map/ppermute | solution.py:359

commit v7 on v6

--- a/solution.py
+++ b/solution.py
@@ -328,7 +328,10 @@
             pairs.append((piece.at[pl.ds(span, span)], (me ^ k ^ 1) * span))
         return pairs + [(own, me * span), (other.at[len(far)], (me ^ 1) * span)]
 
-    outer = attend(inward, hops, True, [*outer_far, outer[-1], outer_other], weights, frames, "attend_outer")
+    outer = list(attend(inward, hops, True, [*outer_far, outer[-1], outer_other], weights, frames, "attend_outer"))
+    outer[:2], inner_far[0] = lax.optimization_barrier((outer[:2], inner_far[0]))
+    for i in range(2, len(far)):
+        outer[i], inner_far[i] = lax.optimization_barrier((outer[i], inner_far[i]))
     outer = [swap(piece, k) for k, piece in zip(hops, outer)]
     *keep, give = attend(inward, hops, False, [*inner_far, inner[-1], inner_other], weights, frames, "attend_inner")
 

time: 87.4 us -> 85.8 us (0.982)
  starting transfers between devices: 31 us -> 24.2 us
  waiting for transfers between devices: 38.5 us -> 44.2 us
    ppermute x15, starting transfers between devices: 26.3 us -> 19.5 us  [swap(): lax.ppermute(block, 'frm', [(i, i ^ k) for i in range(count)])]
    ppermute x15, waiting for transfers between devices: 38.5 us -> 44.2 us  [swap(): lax.ppermute(block, 'frm', [(i, i ^ k) for i in range(count)])]
  transfers between devices with their start and end apart: 17 -> 17, of which waited for: 7 -> 8; matrix products, arithmetic and copies ran while one was open for 0% -> 0% of each run, Pallas kernels for 14% -> 15%
where the time goes in v7:
time: 85.8 us; the launch traced here: 85.6 us
  waiting for transfers between devices  44.2 us (52%)
  starting transfers between devices  24.2 us (28%)
  Pallas kernels  15.4 us (18%)
  local copies, waits for them, and re-layouts  1.62 us (2%)
    ppermute x15, waiting for transfers between devices, swap(): lax.ppermute(block, 'frm', [(i, i ^ k) for i in range(count)])  44.2 us
    ppermute x15, starting transfers between devices, swap(): lax.ppermute(block, 'frm', [(i, i ^ k) for i in range(count)])  19.5 us
    pallas_call x2, Pallas kernels, attend(): pl.pallas_call(functools.partial(attend_kernel, inward, hops, paired, len...  12.3 us
    ppermute x1, starting transfers between devices, local(): left = lax.ppermute(high_side, 'col', upward)  3.39 us
    pallas_call x1, Pallas kernels, depth_filter(): pl.pallas_call(functools.partial(filter_kernel, hops), out_shape=jax.Shap...  2.64 us
  transfers between devices with their start and end apart: 17, of which 8 were waited for; matrix products, arithmetic and copies ran while one was open for 0% of the time, Pallas kernels for 15%

profile of v7, /device:TPU:0, one launch (start us, length us, event | category | flops | bytes accessed | tf_op | source)
XLA Modules:
  0.0 85.6 jit_solution(13954872625205384115)
XLA Ops:
  0.0 0.0 copy-start
  0.0 1.6 %copy-done = bf16[8,8,32,512]{3,2,1,0:T(8,128)(2,1)S(1)} copy-done((bf16[8,8,32,512]{3,2,1,0:T(8,128)(2,1)S(1)}, bf16[8,8,32,512]{3,2,1,0:T(8,128)(2,1)}, u32[]{:S(2)}) %copy-start) | copy-done | bytes 2097176
  1.6 0.0 copy-start.2
  1.6 0.0 copy-start.3
  1.6 0.0 copy-start.4
  1.6 0.0 copy-start.5
  1.6 0.0 copy-start.6
  1.6 0.0 copy-start.7
  1.6 0.1 cut.1
  1.8 0.5 collective-permute-start
  2.3 1.5 %collective-permute-done.refs_3_.refs_4_ = bf16[4,8,16,512]{3,2,1,0:T(8,128)(2,1)S(1)} collective-permute-done((bf16[4,8,16,512]{3,2,1,0:T(8,128)(2,1)S(1)}, bf16[4,8,16,512]{3,2,1,0:T(8,128)(2,1)S(1)}, u32[]{:S(2)}, u32[]{:S(2)}) %collective-permute-start) | collective-permute-done | bytes 524320 | tf_op jit(solution)/shard_map/ppermute | solution.py:294
  3.8 0.1 join_outer.1
  3.9 0.4 collective-permute-start.2
  4.3 4.7 %collective-permute-start.1 = (bf16[16,16,512]{2,1,0:T(8,128)(2,1)S(1)}, bf16[16,16,512]{2,1,0:T(8,128)(2,1)S(1)}, u32[]{:S(2)}, u32[]{:S(2)}) collective-permute-start(bf16[16,16,512]{2,1,0:T(8,128)(2,1)S(1)} %get-tuple-element.59), channel_id=1, source_target_pairs={{0,24},{4,28},{8,16},{12,20},{16,8},{20,12},{24,0},{28,4},{1,25},{... | collective-permute-start | bytes 786440 | tf_op jit(solution)/shard_map/ppermute | solution.py:294
  9.1 0.0 collective-permute-start.3
  9.1 0.6 collective-permute-start.4
  9.7 0.0 collective-permute-done.2.refs_3_.refs_4_
  9.7 0.1 join_inner.1
  9.7 6.6 %collective-permute-done.1.refs_0_ = bf16[16,16,512]{2,1,0:T(8,128)(2,1)S(1)} collective-permute-done((bf16[16,16,512]{2,1,0:T(8,128)(2,1)S(1)}, bf16[16,16,512]{2,1,0:T(8,128)(2,1)S(1)}, u32[]{:S(2)}, u32[]{:S(2)}) %collective-permute-start.1) | collective-permute-done | bytes 262176 | tf_op jit(solution)/shard_map/ppermute | solution.py:294
  16.3 3.7 %collective-permute-start.5 = (bf16[16,16,512]{2,1,0:T(8,128)(2,1)S(1)}, bf16[16,16,512]{2,1,0:T(8,128)(2,1)S(1)}, u32[]{:S(2)}, u32[]{:S(2)}) collective-permute-start(bf16[16,16,512]{2,1,0:T(8,128)(2,1)S(1)} %get-tuple-element.73), channel_id=1, source_target_pairs={{0,24},{4,28},{8,16},{12,20},{16,8},{20,12},{24,0},{28,4},{1,25},{... | collective-permute-start | bytes 786440 | tf_op jit(solution)/shard_map/ppermute | solution.py:294
  20.1 3.2 %collective-permute-start.8 = (bf16[16,16,512]{2,1,0:T(8,128)(2,1)S(1)}, bf16[16,16,512]{2,1,0:T(8,128)(2,1)S(1)}, u32[]{:S(2)}, u32[]{:S(2)}) collective-permute-start(bf16[16,16,512]{2,1,0:T(8,128)(2,1)S(1)} %get-tuple-element.77), channel_id=1, source_target_pairs={{0,16},{4,20},{8,24},{12,28},{16,0},{20,4},{24,8},{28,12},{1,17},{... | collective-permute-start | bytes 786440 | tf_op jit(solution)/shard_map/ppermute | solution.py:294
  23.3 0.1 collective-permute-start.10
  23.4 0.0 collective-permute-done.3.refs_1_
  23.4 20.4 %collective-permute-done.4.refs_2_ = bf16[16,16,512]{2,1,0:T(8,128)(2,1)S(1)} collective-permute-done((bf16[16,16,512]{2,1,0:T(8,128)(2,1)S(1)}, bf16[16,16,512]{2,1,0:T(8,128)(2,1)S(1)}, u32[]{:S(2)}, u32[]{:S(2)}) %collective-permute-start.4) | collective-permute-done | bytes 262176 | tf_op jit(solution)/shard_map/ppermute | solution.py:294
  43.7 0.0 copy-done.2
  43.8 0.0 copy-done.3
  43.8 0.0 copy-done.4
  43.8 0.0 copy-done.5
  43.8 0.0 copy-done.6
  43.8 0.0 copy-done.7
  43.8 6.2 %attend_outer.1 = (bf16[8,16,512]{2,1,0:T(8,128)(2,1)S(1)}, bf16[8,16,512]{2,1,0:T(8,128)(2,1)S(1)}, bf16[8,16,512]{2,1,0:T(8,128)(2,1)S(1)}, bf16[8,16,512]{2,1,0:T(8,128)(2,1)S(1)}) custom-call(bf16[16,16,512]{2,1,0:T(8,128)(2,1)S(1)} %collective-permute-done.1.refs_0_, bf16[16,16,512]{2,1,0:T(8,128)(2,1)S(1)} %collective-permute-done.3.refs_1_, ...), custom_call_target="tpu_custom_call" | custom-call | flops 4026531840 | bytes 5242880 | tf_op jit(solution)/shard_map/attend_outer/pallas_call | solution.py:162
  50.0 0.0 collective-permute-done.5.refs_0_
  50.0 2.5 %collective-permute-start.6 = (bf16[8,16,512]{2,1,0:T(8,128)(2,1)S(1)}, bf16[8,16,512]{2,1,0:T(8,128)(2,1)S(1)}, u32[]{:S(2)}, u32[]{:S(2)}) collective-permute-start(bf16[8,16,512]{2,1,0:T(8,128)(2,1)S(1)} %get-tuple-element.74), channel_id=1, source_target_pairs={{0,24},{4,28},{8,16},{12,20},{16,8},{20,12},{24,0},{28,4},{1,25},{... | collective-permute-start | bytes 393224 | tf_op jit(solution)/shard_map/ppermute | solution.py:294
  52.5 0.0 collective-permute-start.7
  52.5 4.7 %collective-permute-done.8.refs_2_ = bf16[16,16,512]{2,1,0:T(8,128)(2,1)S(1)} collective-permute-done((bf16[16,16,512]{2,1,0:T(8,128)(2,1)S(1)}, bf16[16,16,512]{2,1,0:T(8,128)(2,1)S(1)}, u32[]{:S(2)}, u32[]{:S(2)}) %collective-permute-start.8) | collective-permute-done | bytes 262176 | tf_op jit(solution)/shard_map/ppermute | solution.py:294
  57.2 0.0 collective-permute-start.9
  57.2 0.0 collective-permute-done.10.refs_1_
  57.2 6.2 %attend_inner.1 = (bf16[4,16,512]{2,1,0:T(8,128)(2,1)S(1)}, bf16[4,16,512]{2,1,0:T(8,128)(2,1)S(1)}, bf16[4,16,512]{2,1,0:T(8,128)(2,1)S(1)}, bf16[4,16,512]{2,1,0:T(8,128)(2,1)S(1)}, bf16[4,4,16,512]{3,2,1,0:T(8,128)(2,1)S(1)}) custom-call(bf16[16,16,512]{2,1,0:T(8,128)(2,1)S(1)} %collective-permute-done.5.refs_0_, ...), custom_call_target="tpu_custom_call" | custom-call | flops 4026531840 | bytes 5242880 | tf_op jit(solution)/shard_map/attend_inner/pallas_call | solution.py:162
  63.4 0.0 copy-start.1
  63.4 0.0 collective-permute-done.6.refs_0_
  63.4 0.0 collective-permute-done.7.refs_1_
  63.4 2.2 %collective-permute-done.9.refs_2_ = bf16[8,16,512]{2,1,0:T(8,128)(2,1)S(1)} collective-permute-done((bf16[8,16,512]{2,1,0:T(8,128)(2,1)S(1)}, bf16[8,16,512]{2,1,0:T(8,128)(2,1)S(1)}, u32[]{:S(2)}, u32[]{:S(2)}) %collective-permute-start.9) | collective-permute-done | bytes 131104 | tf_op jit(solution)/shard_map/ppermute | solution.py:294
  65.7 0.1 collective-permute-start.11
  65.8 1.9 %collective-permute-done.11.refs_3_.refs_4_.refs_8_ = bf16[8,4,16,512]{3,2,1,0:T(8,128)(2,1)S(1)} collective-permute-done((bf16[8,4,16,512]{3,2,1,0:T(8,128)(2,1)S(1)}, bf16[8,4,16,512]{3,2,1,0:T(8,128)(2,1)S(1)}, u32[]{:S(2)}, u32[]{:S(2)}) %collective-permute-start.11) | collective-permute-done | bytes 524320 | tf_op jit(solution)/shard_map/ppermute | solution.py:294
  67.7 1.7 %collective-permute-start.13 = (bf16[2,4,16,512]{3,2,1,0:T(8,128)(2,1)S(1)}, bf16[2,4,16,512]{3,2,1,0:T(8,128)(2,1)S(1)}, u32[]{:S(2)}, u32[]{:S(2)}) collective-permute-start(bf16[2,4,16,512]{3,2,1,0:T(8,128)(2,1)S(1)} %get-tuple-element.91), channel_id=1, source_target_pairs={{0,8},{4,12},{8,0},{12,4},{16,24},{20,28},{24,16},{28,20},{1,9},{5... | collective-permute-start | bytes 393224 | tf_op jit(solution)/shard_map/ppermute | solution.py:294
  69.4 1.0 %collective-permute-start.12 = (bf16[2,4,16,512]{3,2,1,0:T(8,128)(2,1)S(1)}, bf16[2,4,16,512]{3,2,1,0:T(8,128)(2,1)S(1)}, u32[]{:S(2)}, u32[]{:S(2)}) collective-permute-start(bf16[2,4,16,512]{3,2,1,0:T(8,128)(2,1)S(1)} %get-tuple-element.88), channel_id=1, source_target_pairs={{0,24},{4,28},{8,16},{12,20},{16,8},{20,12},{24,0},{28,4},{1,25},{... | collective-permute-start | bytes 393224 | tf_op jit(solution)/shard_map/ppermute | solution.py:294
  70.4 0.9 %collective-permute-start.14 = (bf16[2,4,16,512]{3,2,1,0:T(8,128)(2,1)S(1)}, bf16[2,4,16,512]{3,2,1,0:T(8,128)(2,1)S(1)}, u32[]{:S(2)}, u32[]{:S(2)}) collective-permute-start(bf16[2,4,16,512]{3,2,1,0:T(8,128)(2,1)S(1)} %get-tuple-element.93), channel_id=1, source_target_pairs={{0,16},{4,20},{8,24},{12,28},{16,0},{20,4},{24,8},{28,12},{1,17},{... | collective-permute-start | bytes 393224 | tf_op jit(solution)/shard_map/ppermute | solution.py:294
  71.3 0.1 rim.1
  71.4 1.9 %collective-permute-done.13.refs_5_ = bf16[2,4,16,512]{3,2,1,0:T(8,128)(2,1)S(1)} collective-permute-done((bf16[2,4,16,512]{3,2,1,0:T(8,128)(2,1)S(1)}, bf16[2,4,16,512]{3,2,1,0:T(8,128)(2,1)S(1)}, u32[]{:S(2)}, u32[]{:S(2)}) %collective-permute-start.13) | collective-permute-done | bytes 131104 | tf_op jit(solution)/shard_map/ppermute | solution.py:294
  73.3 3.4 %collective-permute-start.15 = (bf16[8,4,512]{2,1,0:T(4,128)(2,1)S(1)}, bf16[8,4,512]{2,1,0:T(4,128)(2,1)S(1)}, u32[]{:S(2)}, u32[]{:S(2)}) collective-permute-start(bf16[8,4,512]{2,1,0:T(4,128)(2,1)S(1)} %get-tuple-element.95), channel_id=1, source_target_pairs={{0,1},{1,2},{2,3},{4,5},{5,6},{6,7},{8,9},{9,10},{10,11},{12,13},{... | collective-permute-start | bytes 98312 | tf_op jit(solution)/shard_map/ppermute | solution.py:361
  76.7 1.3 %collective-permute-start.16 = (bf16[8,4,512]{2,1,0:T(4,128)(2,1)S(1)}, bf16[8,4,512]{2,1,0:T(4,128)(2,1)S(1)}, u32[]{:S(2)}, u32[]{:S(2)}) collective-permute-start(bf16[8,4,512]{2,1,0:T(4,128)(2,1)S(1)} %get-tuple-element.96), channel_id=1, source_target_pairs={{1,0},{2,1},{3,2},{5,4},{6,5},{7,6},{9,8},{10,9},{11,10},{13,12},{... | collective-permute-start | bytes 98312 | tf_op jit(solution)/shard_map/ppermute | solution.py:362
  78.0 0.0 collective-permute-done.12.refs_4_
  78.0 4.9 %collective-permute-done.14.refs_6_ = bf16[2,4,16,512]{3,2,1,0:T(8,128)(2,1)S(1)} collective-permute-done((bf16[2,4,16,512]{3,2,1,0:T(8,128)(2,1)S(1)}, bf16[2,4,16,512]{3,2,1,0:T(8,128)(2,1)S(1)}, u32[]{:S(2)}, u32[]{:S(2)}) %collective-permute-start.14) | collective-permute-done | bytes 131104 | tf_op jit(solution)/shard_map/ppermute | solution.py:294
  82.9 0.0 collective-permute-done.15.refs_9_
  82.9 0.0 collective-permute-done.16.refs_10_
  82.9 0.0 copy-done.1
  82.9 2.6 %depth_filter.1 = bf16[4,8,32,512]{3,2,1,0:T(8,128)(2,1)} custom-call(bf16[8,16,512]{2,1,0:T(8,128)(2,1)S(1)} %collective-permute-done.6.refs_0_, bf16[8,16,512]{2,1,0:T(8,128)(2,1)S(1)} %collective-permute-done.7.refs_1_, bf16[8,16,512]{2,1,0:T(8,128)(2,1)S(1)} %collective-permute-done.9.refs_2_, bf16[8,16,512]{2,1,0:T(8,128)(2,1)S(1)} %get-tuple-element.79.refs_3_, ...), custom_call_target="tpu_custom_call" | custom-call | flops 9437184 | bytes 2097152 | tf_op jit(solution)/shard_map/depth_filter/pallas_call | solution.py:271
  (2 shorter events, 0.1 us)
Async XLA Ops:
  0.0 1.6 %copy-start = (bf16[8,8,32,512]{3,2,1,0:T(8,128)(2,1)S(1)}, bf16[8,8,32,512]{3,2,1,0:T(8,128)(2,1)}, u32[]{:S(2)}) copy-start(bf16[8,8,32,512]{3,2,1,0:T(8,128)(2,1)} %video.1) | copy-start | bytes 6291460
  1.6 42.2 %copy-start.2 = (bf16[3,512,512]{2,1,0:T(8,128)(2,1)S(1)}, bf16[3,512,512]{2,1,0:T(8,128)(2,1)}, u32[]{:S(2)}) copy-start(bf16[3,512,512]{2,1,0:T(8,128)(2,1)} %refs_10_.3) | copy-start | bytes 4718596
  1.6 42.2 %copy-start.3 = (bf16[512,512]{1,0:T(8,128)(2,1)S(1)}, bf16[512,512]{1,0:T(8,128)(2,1)}, u32[]{:S(2)}) copy-start(bf16[512,512]{1,0:T(8,128)(2,1)} %refs_6_.3) | copy-start | bytes 1572868
  1.6 42.2 %copy-start.4 = (bf16[512,512]{1,0:T(8,128)(2,1)S(1)}, bf16[512,512]{1,0:T(8,128)(2,1)}, u32[]{:S(2)}) copy-start(bf16[512,512]{1,0:T(8,128)(2,1)} %refs_7_.3) | copy-start | bytes 1572868
  1.6 42.2 %copy-start.5 = (bf16[512,512]{1,0:T(8,128)(2,1)S(1)}, bf16[512,512]{1,0:T(8,128)(2,1)}, u32[]{:S(2)}) copy-start(bf16[512,512]{1,0:T(8,128)(2,1)} %refs_8_.3) | copy-start | bytes 1572868
  1.6 42.2 %copy-start.6 = (bf16[512,512]{1,0:T(8,128)(2,1)S(1)}, bf16[512,512]{1,0:T(8,128)(2,1)}, u32[]{:S(2)}) copy-start(bf16[512,512]{1,0:T(8,128)(2,1)} %refs_9_.3) | copy-start | bytes 1572868
  1.6 42.2 %copy-start.7 = (f32[512]{0:T(512)S(1)}, f32[512]{0:T(512)}, u32[]{:S(2)}) copy-start(f32[512]{0:T(512)} %param.9) | copy-start | bytes 6148
  1.8 2.1 %collective-permute-start = (bf16[4,8,16,512]{3,2,1,0:T(8,128)(2,1)S(1)}, bf16[4,8,16,512]{3,2,1,0:T(8,128)(2,1)S(1)}, u32[]{:S(2)}, u32[]{:S(2)}) collective-permute-start(bf16[4,8,16,512]{3,2,1,0:T(8,128)(2,1)S(1)} %get-tuple-element.54), channel_id=1, source_target_pairs={{0,4},{4,0},{8,12},{12,8},{16,20},{20,16},{24,28},{28,24},{1,5},{5... | collective-permute-start | bytes 1572872 | tf_op jit(solution)/shard_map/ppermute | solution.py:294
  3.9 5.8 %collective-permute-start.2 = (bf16[4,8,16,512]{3,2,1,0:T(8,128)(2,1)S(1)}, bf16[4,8,16,512]{3,2,1,0:T(8,128)(2,1)S(1)}, u32[]{:S(2)}, u32[]{:S(2)}) collective-permute-start(bf16[4,8,16,512]{3,2,1,0:T(8,128)(2,1)S(1)} %get-tuple-element.63), channel_id=1, source_target_pairs={{0,4},{4,0},{8,12},{12,8},{16,20},{20,16},{24,28},{28,24},{1,5},{5... | collective-permute-start | bytes 1572872 | tf_op jit(solution)/shard_map/ppermute | solution.py:294
  4.3 12.0 %collective-permute-start.1 = (bf16[16,16,512]{2,1,0:T(8,128)(2,1)S(1)}, bf16[16,16,512]{2,1,0:T(8,128)(2,1)S(1)}, u32[]{:S(2)}, u32[]{:S(2)}) collective-permute-start(bf16[16,16,512]{2,1,0:T(8,128)(2,1)S(1)} %get-tuple-element.59), channel_id=1, source_target_pairs={{0,24},{4,28},{8,16},{12,20},{16,8},{20,12},{24,0},{28,4},{1,25},{... | collective-permute-start | bytes 786440 | tf_op jit(solution)/shard_map/ppermute | solution.py:294
  9.1 14.3 %collective-permute-start.3 = (bf16[16,16,512]{2,1,0:T(8,128)(2,1)S(1)}, bf16[16,16,512]{2,1,0:T(8,128)(2,1)S(1)}, u32[]{:S(2)}, u32[]{:S(2)}) collective-permute-start(bf16[16,16,512]{2,1,0:T(8,128)(2,1)S(1)} %get-tuple-element.68), channel_id=1, source_target_pairs={{0,8},{4,12},{8,0},{12,4},{16,24},{20,28},{24,16},{28,20},{1,9},{5... | collective-permute-start | bytes 786440 | tf_op jit(solution)/shard_map/ppermute | solution.py:294
  9.1 34.7 %collective-permute-start.4 = (bf16[16,16,512]{2,1,0:T(8,128)(2,1)S(1)}, bf16[16,16,512]{2,1,0:T(8,128)(2,1)S(1)}, u32[]{:S(2)}, u32[]{:S(2)}) collective-permute-start(bf16[16,16,512]{2,1,0:T(8,128)(2,1)S(1)} %get-tuple-element.69), channel_id=1, source_target_pairs={{0,16},{4,20},{8,24},{12,28},{16,0},{20,4},{24,8},{28,12},{1,17},{... | collective-permute-start | bytes 786440 | tf_op jit(solution)/shard_map/ppermute | solution.py:294
  16.3 33.7 %collective-permute-start.5 = (bf16[16,16,512]{2,1,0:T(8,128)(2,1)S(1)}, bf16[16,16,512]{2,1,0:T(8,128)(2,1)S(1)}, u32[]{:S(2)}, u32[]{:S(2)}) collective-permute-start(bf16[16,16,512]{2,1,0:T(8,128)(2,1)S(1)} %get-tuple-element.73), channel_id=1, source_target_pairs={{0,24},{4,28},{8,16},{12,20},{16,8},{20,12},{24,0},{28,4},{1,25},{... | collective-permute-start | bytes 786440 | tf_op jit(solution)/shard_map/ppermute | solution.py:294
  20.1 37.2 %collective-permute-start.8 = (bf16[16,16,512]{2,1,0:T(8,128)(2,1)S(1)}, bf16[16,16,512]{2,1,0:T(8,128)(2,1)S(1)}, u32[]{:S(2)}, u32[]{:S(2)}) collective-permute-start(bf16[16,16,512]{2,1,0:T(8,128)(2,1)S(1)} %get-tuple-element.77), channel_id=1, source_target_pairs={{0,16},{4,20},{8,24},{12,28},{16,0},{20,4},{24,8},{28,12},{1,17},{... | collective-permute-start | bytes 786440 | tf_op jit(solution)/shard_map/ppermute | solution.py:294
  23.3 34.0 %collective-permute-start.10 = (bf16[16,16,512]{2,1,0:T(8,128)(2,1)S(1)}, bf16[16,16,512]{2,1,0:T(8,128)(2,1)S(1)}, u32[]{:S(2)}, u32[]{:S(2)}) collective-permute-start(bf16[16,16,512]{2,1,0:T(8,128)(2,1)S(1)} %get-tuple-element.81), channel_id=1, source_target_pairs={{0,8},{4,12},{8,0},{12,4},{16,24},{20,28},{24,16},{28,20},{1,9},{5... | collective-permute-start | bytes 786440 | tf_op jit(solution)/shard_map/ppermute | solution.py:294
  50.0 13.4 %collective-permute-start.6 = (bf16[8,16,512]{2,1,0:T(8,128)(2,1)S(1)}, bf16[8,16,512]{2,1,0:T(8,128)(2,1)S(1)}, u32[]{:S(2)}, u32[]{:S(2)}) collective-permute-start(bf16[8,16,512]{2,1,0:T(8,128)(2,1)S(1)} %get-tuple-element.74), channel_id=1, source_target_pairs={{0,24},{4,28},{8,16},{12,20},{16,8},{20,12},{24,0},{28,4},{1,25},{... | collective-permute-start | bytes 393224 | tf_op jit(solution)/shard_map/ppermute | solution.py:294
  52.5 10.9 %collective-permute-start.7 = (bf16[8,16,512]{2,1,0:T(8,128)(2,1)S(1)}, bf16[8,16,512]{2,1,0:T(8,128)(2,1)S(1)}, u32[]{:S(2)}, u32[]{:S(2)}) collective-permute-start(bf16[8,16,512]{2,1,0:T(8,128)(2,1)S(1)} %get-tuple-element.75), channel_id=1, source_target_pairs={{0,8},{4,12},{8,0},{12,4},{16,24},{20,28},{24,16},{28,20},{1,9},{5... | collective-permute-start | bytes 393224 | tf_op jit(solution)/shard_map/ppermute | solution.py:294
  57.2 8.4 %collective-permute-start.9 = (bf16[8,16,512]{2,1,0:T(8,128)(2,1)S(1)}, bf16[8,16,512]{2,1,0:T(8,128)(2,1)S(1)}, u32[]{:S(2)}, u32[]{:S(2)}) collective-permute-start(bf16[8,16,512]{2,1,0:T(8,128)(2,1)S(1)} %get-tuple-element.78), channel_id=1, source_target_pairs={{0,16},{4,20},{8,24},{12,28},{16,0},{20,4},{24,8},{28,12},{1,17},{... | collective-permute-start | bytes 393224 | tf_op jit(solution)/shard_map/ppermute | solution.py:294
  63.4 19.5 %copy-start.1 = (f32[3,3,512]{2,1,0:T(4,128)S(1)}, f32[3,3,512]{2,1,0:T(4,128)}, u32[]{:S(2)}) copy-start(f32[3,3,512]{2,1,0:T(4,128)} %refs_11_.1) | copy-start | bytes 55300
  65.7 2.0 %collective-permute-start.11 = (bf16[8,4,16,512]{3,2,1,0:T(8,128)(2,1)S(1)}, bf16[8,4,16,512]{3,2,1,0:T(8,128)(2,1)S(1)}, u32[]{:S(2)}, u32[]{:S(2)}) collective-permute-start(bf16[8,4,16,512]{3,2,1,0:T(8,128)(2,1)S(1)} %stack_back.1), channel_id=1, source_target_pairs={{0,4},{4,0},{8,12},{12,8},{16,20},{20,16},{24,28},{28,24},{1,5},{5... | collective-permute-start | bytes 1572872 | tf_op jit(solution)/shard_map/ppermute | solution.py:294
  67.7 5.6 %collective-permute-start.13 = (bf16[2,4,16,512]{3,2,1,0:T(8,128)(2,1)S(1)}, bf16[2,4,16,512]{3,2,1,0:T(8,128)(2,1)S(1)}, u32[]{:S(2)}, u32[]{:S(2)}) collective-permute-start(bf16[2,4,16,512]{3,2,1,0:T(8,128)(2,1)S(1)} %get-tuple-element.91), channel_id=1, source_target_pairs={{0,8},{4,12},{8,0},{12,4},{16,24},{20,28},{24,16},{28,20},{1,9},{5... | collective-permute-start | bytes 393224 | tf_op jit(solution)/shard_map/ppermute | solution.py:294
  69.4 8.6 %collective-permute-start.12 = (bf16[2,4,16,512]{3,2,1,0:T(8,128)(2,1)S(1)}, bf16[2,4,16,512]{3,2,1,0:T(8,128)(2,1)S(1)}, u32[]{:S(2)}, u32[]{:S(2)}) collective-permute-start(bf16[2,4,16,512]{3,2,1,0:T(8,128)(2,1)S(1)} %get-tuple-element.88), channel_id=1, source_target_pairs={{0,24},{4,28},{8,16},{12,20},{16,8},{20,12},{24,0},{28,4},{1,25},{... | collective-permute-start | bytes 393224 | tf_op jit(solution)/shard_map/ppermute | solution.py:294
  70.4 12.6 %collective-permute-start.14 = (bf16[2,4,16,512]{3,2,1,0:T(8,128)(2,1)S(1)}, bf16[2,4,16,512]{3,2,1,0:T(8,128)(2,1)S(1)}, u32[]{:S(2)}, u32[]{:S(2)}) collective-permute-start(bf16[2,4,16,512]{3,2,1,0:T(8,128)(2,1)S(1)} %get-tuple-element.93), channel_id=1, source_target_pairs={{0,16},{4,20},{8,24},{12,28},{16,0},{20,4},{24,8},{28,12},{1,17},{... | collective-permute-start | bytes 393224 | tf_op jit(solution)/shard_map/ppermute | solution.py:294
  73.3 9.6 %collective-permute-start.15 = (bf16[8,4,512]{2,1,0:T(4,128)(2,1)S(1)}, bf16[8,4,512]{2,1,0:T(4,128)(2,1)S(1)}, u32[]{:S(2)}, u32[]{:S(2)}) collective-permute-start(bf16[8,4,512]{2,1,0:T(4,128)(2,1)S(1)} %get-tuple-element.95), channel_id=1, source_target_pairs={{0,1},{1,2},{2,3},{4,5},{5,6},{6,7},{8,9},{9,10},{10,11},{12,13},{... | collective-permute-start | bytes 98312 | tf_op jit(solution)/shard_map/ppermute | solution.py:361
  76.7 6.2 %collective-permute-start.16 = (bf16[8,4,512]{2,1,0:T(4,128)(2,1)S(1)}, bf16[8,4,512]{2,1,0:T(4,128)(2,1)S(1)}, u32[]{:S(2)}, u32[]{:S(2)}) collective-permute-start(bf16[8,4,512]{2,1,0:T(4,128)(2,1)S(1)} %get-tuple-element.96), channel_id=1, source_target_pairs={{1,0},{2,1},{3,2},{5,4},{6,5},{7,6},{9,8},{10,9},{11,10},{13,12},{... | collective-permute-start | bytes 98312 | tf_op jit(solution)/shard_map/ppermute | solution.py:362

commit v8 on v7

--- a/solution.py
+++ b/solution.py
@@ -14,6 +14,7 @@
 TILE = 8
 SOFT_ROWS = 32
 MIB = 1024 * 1024
+SMALL = pl.CostEstimate(flops=1, bytes_accessed=1, transcendentals=0)
 INSIDE = pl.BlockSpec(memory_space=pltpu.VMEM)
 
 
@@ -35,7 +36,7 @@
         in_specs=[INSIDE] * len(arrays),
         out_specs=[INSIDE] * len(shapes),
         compiler_params=pltpu.CompilerParams(vmem_limit_bytes=6 * MIB),
-        cost_estimate=pl.CostEstimate(flops=0, bytes_accessed=4 * size, transcendentals=0),
+        cost_estimate=SMALL,
         name=name,
     )(*arrays)
 
@@ -66,7 +67,7 @@
         in_specs=[INSIDE],
         out_specs=[INSIDE] * len(shapes),
         compiler_params=pltpu.CompilerParams(vmem_limit_bytes=12 * MIB),
-        cost_estimate=pl.CostEstimate(flops=0, bytes_accessed=3 * video.size, transcendentals=0),
+        cost_estimate=SMALL,
         name="cut",
     )(video)
 
@@ -173,11 +174,7 @@
             pltpu.VMEM((cols // GROUP, frames + 2, GROUP, channels), jnp.float32),
         ],
         compiler_params=pltpu.CompilerParams(vmem_limit_bytes=24 * MIB),
-        cost_estimate=pl.CostEstimate(
-            flops=rows * channels * (channels * 11 + GROUP * frames * 4),
-            bytes_accessed=rows * channels * 3 + channels * channels * 14,
-            transcendentals=rows * frames,
-        ),
+        cost_estimate=SMALL,
         name=name,
     )(*pieces, norm_gain[None], *matrices)
 
@@ -194,7 +191,7 @@
 def inner_rows(hops, pieces, taken):
     *far, own = pieces
     pairs = [(hop + j, piece.at[j]) for hop, piece in zip(hops, far) for j in range(2)]
-    return pairs + [(0, own), (1, taken.at[2 * len(hops) - 1])]
+    return pairs + [(0, own), (1, taken.at[len(far)])]
 
 
 def rim_kernel(hops, *refs):
@@ -218,21 +215,22 @@
 
 
 def filter_kernel(hops, *refs):
-    count = len(hops)
-    taken, left, right, w_depth, out, outer, inner = refs[2 * count :]
+    count = len(hops) + 1
+    left, right, w_depth, result, outer, inner, out, sems = refs[2 * count :]
     me = lax.axis_index("frm")
-    for k, piece in outer_rows(hops, refs[:count], taken):
+    for k, piece in outer_rows(hops, refs[: count - 1], refs[count - 1]):
         outer[me ^ k] = piece[...]
-    for k, piece in inner_rows(hops, refs[count : 2 * count], taken):
+    for k, piece in inner_rows(hops, refs[count : 2 * count - 1], refs[2 * count - 1]):
         inner[me ^ k] = piece[...]
     frames, height, cols, channels = out.shape
     edge = cols // 4
     lanes = 128
 
-    def one_part(step, carry):
-        part = pl.ds(pl.multiple_of(step * lanes, lanes), lanes)
-        taps = [[w_depth[a, b, part] for b in range(3)] for a in range(3)]
-        for frame in range(frames):
+    copies = [pltpu.make_async_copy(out.at[frame], result.at[frame], sems.at[frame]) for frame in range(frames)]
+    for frame in range(frames):
+        for first in range(0, channels, lanes):
+            part = pl.ds(first, lanes)
+            taps = [[w_depth[a, b, part] for b in range(3)] for a in range(3)]
 
             def filtered(row):
                 sides = outer[row, frame, :, part].astype(jnp.float32)
@@ -258,26 +256,30 @@
                     total = total + below[2]
                 out[frame, row, :, part] = total.astype(jnp.bfloat16)
                 above, here = here, below
-        return carry
-
-    lax.fori_loop(0, channels // lanes, one_part, 0)
-
-
-def depth_filter(hops, outer, inner, taken, left, right, w_depth):
+        copies[frame].start()
+    for copy in copies:
+        copy.wait()
+
+
+def depth_filter(hops, outer, inner, left, right, w_depth):
     height, frames, channels = left.shape
-    width = taken.shape[2]
+    width = inner[-1].shape[2]
     cols = 2 * width
     size = frames * height * cols * channels
     return pl.pallas_call(
         functools.partial(filter_kernel, hops),
         out_shape=jax.ShapeDtypeStruct((frames, height, cols, channels), jnp.bfloat16),
-        in_specs=[INSIDE] * (2 * len(hops) + 4),
-        out_specs=INSIDE,
-        scratch_shapes=[pltpu.VMEM((height, frames, width, channels), jnp.bfloat16)] * 2,
+        in_specs=[INSIDE] * (2 * len(hops) + 5),
+        out_specs=pl.BlockSpec(memory_space=pl.ANY),
+        scratch_shapes=[
+            *[pltpu.VMEM((height, frames, width, channels), jnp.bfloat16)] * 2,
+            pltpu.VMEM((frames, height, cols, channels), jnp.bfloat16),
+            pltpu.SemaphoreType.DMA((frames,)),
+        ],
         compiler_params=pltpu.CompilerParams(vmem_limit_bytes=10 * MIB),
-        cost_estimate=pl.CostEstimate(flops=18 * size, bytes_accessed=4 * size, transcendentals=0),
+        cost_estimate=SMALL,
         name="depth_filter",
-    )(*outer, *inner, taken, left, right, w_depth)
+    )(*outer, *inner, left, right, w_depth)
 
 
 def local(video, norm_gain, w_query, w_key, w_value, w_out, w_time, w_depth):
@@ -314,6 +316,7 @@
     outer_far = join(outer, outer_other, "join_outer")
     *outer_far, inner_stack = lax.optimization_barrier((*outer_far, inner_stack))
     outer_far = [swap(piece, k) for k, piece in zip(hops, outer_far)]
+    nearest = far.index(1)
     inner_other = swap(inner_stack, 1)
     inner_far = join(inner, inner_other, "join_inner")
     outer_far[0], *inner_far = lax.optimization_barrier((outer_far[0], *inner_far))
@@ -335,32 +338,32 @@
     outer = [swap(piece, k) for k, piece in zip(hops, outer)]
     *keep, give = attend(inward, hops, False, [*inner_far, inner[-1], inner_other], weights, frames, "attend_inner")
 
-    def for_mate(ins, outs):
-        _, core = place()
-        *pieces, give = ins
-        pairs = [(piece.at[pl.ds((1 - core) * made, made)], outs[0].at[i]) for i, piece in enumerate(pieces)]
-        return pairs + [(give, outs[0].at[pl.ds(chips, chips)])]
-
-    (stack,) = gather(for_mate, [*outer, give], [(2 * chips, made, width, channels)], "stack_back")
-    taken = swap(stack, 1)
+    outer[:2], give = lax.optimization_barrier((outer[:2], give))
+    taken = swap(give, 1)
 
     def joined_back(ins, outs):
         *keep, taken = ins
         pairs = []
         for i, own in enumerate(keep):
-            pairs += [(own, outs[i].at[0]), (taken.at[chips + i], outs[i].at[1])]
+            pairs += [(own, outs[i].at[0]), (taken.at[i], outs[i].at[1])]
         return pairs
 
     inner = gather(joined_back, [*keep[:-1], taken], [(2, made, width, channels)] * len(far), "join_back")
     inner = [swap(piece, k) for k, piece in zip(hops, inner)]
-    low_side, high_side = rim(hops, outer, taken)
-    nearest = far.index(1)
+
+    def for_mate(ins, outs):
+        _, core = place()
+        return [(piece.at[pl.ds((1 - core) * made, made)], outs[0].at[i]) for i, piece in enumerate(ins)]
+
+    (stack,) = gather(for_mate, outer, [(chips, made, width, channels)], "stack_back")
+    halves = swap(stack, 1)
+    low_side, high_side = rim(hops, outer, halves)
     low_side, high_side, inner[nearest] = lax.optimization_barrier((low_side, high_side, inner[nearest]))
     line = lax.axis_size("col")
     upward = [(i, i + 1) for i in range(line - 1)]
     left = lax.ppermute(high_side, "col", upward)
     right = lax.ppermute(low_side, "col", [(b, a) for a, b in upward])
-    return depth_filter(hops, outer, [*inner, keep[-1]], taken, left, right, w_depth)
+    return depth_filter(hops, [*outer, halves], [*inner, keep[-1], taken], left, right, w_depth)
 
 
 def solution(mesh):

time: 85.8 us -> 85.1 us (level)
  waiting for transfers between devices: 44.2 us -> 42.5 us
  starting transfers between devices: 24.2 us -> 25.4 us
    ppermute x15 -> x16, waiting for transfers between devices: 44.2 us -> 42.5 us  [swap(): lax.ppermute(block, 'frm', [(i, i ^ k) for i in range(count)])]
    ppermute x15 -> x16, starting transfers between devices: 19.5 us -> 20.7 us  [swap(): lax.ppermute(block, 'frm', [(i, i ^ k) for i in range(count)])]
  transfers between devices with their start and end apart: 17 -> 18, of which waited for: 8 -> 7; matrix products, arithmetic and copies ran while one was open for 0% -> 0% of each run, Pallas kernels for 15% -> 15%
where the time goes in v8:
time: 85.1 us; the launch traced here: 85 us
  waiting for transfers between devices  42.5 us (50%)
  starting transfers between devices  25.4 us (30%)
  Pallas kernels  15.1 us (18%)
  local copies, waits for them, and re-layouts  1.76 us (2%)
    ppermute x16, waiting for transfers between devices, swap(): lax.ppermute(block, 'frm', [(i, i ^ k) for i in range(count)])  42.5 us
    ppermute x16, starting transfers between devices, swap(): lax.ppermute(block, 'frm', [(i, i ^ k) for i in range(count)])  20.7 us
    pallas_call x2, Pallas kernels, attend(): pl.pallas_call(functools.partial(attend_kernel, inward, hops, paired, len...  12.3 us
    ppermute x1, starting transfers between devices, local(): left = lax.ppermute(high_side, 'col', upward)  3.39 us
    pallas_call x1, Pallas kernels, depth_filter(): pl.pallas_call(functools.partial(filter_kernel, hops), out_shape=jax.Shap...  2.38 us
    unnamed x16, local copies, waits for them, and re-layouts  1.76 us
  transfers between devices with their start and end apart: 18, of which 7 were waited for; matrix products, arithmetic and copies ran while one was open for 0% of the time, Pallas kernels for 15%

profile of v8, /device:TPU:0, one launch (start us, length us, event | category | flops | bytes accessed | tf_op | source)
XLA Modules:
  0.0 85.0 jit_solution(14661528917333202479)
XLA Ops:
  0.0 0.0 copy-start
  0.0 0.0 copy-start.4
  0.0 0.0 copy-start.3
  0.0 0.0 copy-start.2
  0.0 0.0 copy-start.1
  0.0 0.0 copy-start.5
  0.0 1.7 %copy-done.5 = bf16[8,8,32,512]{3,2,1,0:T(8,128)(2,1)S(1)} copy-done((bf16[8,8,32,512]{3,2,1,0:T(8,128)(2,1)S(1)}, bf16[8,8,32,512]{3,2,1,0:T(8,128)(2,1)}, u32[]{:S(2)}) %copy-start.5) | copy-done | bytes 2097176
  1.8 0.0 copy-start.7
  1.8 0.1 cut.1
  1.9 0.5 collective-permute-start
  2.4 1.5 %collective-permute-done.refs_3_.refs_4_ = bf16[4,8,16,512]{3,2,1,0:T(8,128)(2,1)S(1)} collective-permute-done((bf16[4,8,16,512]{3,2,1,0:T(8,128)(2,1)S(1)}, bf16[4,8,16,512]{3,2,1,0:T(8,128)(2,1)S(1)}, u32[]{:S(2)}, u32[]{:S(2)}) %collective-permute-start) | collective-permute-done | bytes 524320 | tf_op jit(solution)/shard_map/ppermute | solution.py:296
  4.0 0.1 join_outer.1
  4.0 0.4 collective-permute-start.2
  4.5 4.7 %collective-permute-start.1 = (bf16[16,16,512]{2,1,0:T(8,128)(2,1)S(1)}, bf16[16,16,512]{2,1,0:T(8,128)(2,1)S(1)}, u32[]{:S(2)}, u32[]{:S(2)}) collective-permute-start(bf16[16,16,512]{2,1,0:T(8,128)(2,1)S(1)} %get-tuple-element.62), channel_id=1, source_target_pairs={{0,24},{4,28},{8,16},{12,20},{16,8},{20,12},{24,0},{28,4},{1,25},{... | collective-permute-start | bytes 786440 | tf_op jit(solution)/shard_map/ppermute | solution.py:296
  9.2 0.0 collective-permute-start.3
  9.2 0.6 collective-permute-start.4
  9.8 0.0 collective-permute-done.2.refs_3_.refs_4_
  9.8 0.1 join_inner.1
  9.8 6.6 %collective-permute-done.1.refs_0_ = bf16[16,16,512]{2,1,0:T(8,128)(2,1)S(1)} collective-permute-done((bf16[16,16,512]{2,1,0:T(8,128)(2,1)S(1)}, bf16[16,16,512]{2,1,0:T(8,128)(2,1)S(1)}, u32[]{:S(2)}, u32[]{:S(2)}) %collective-permute-start.1) | collective-permute-done | bytes 262176 | tf_op jit(solution)/shard_map/ppermute | solution.py:296
  16.4 3.7 %collective-permute-start.5 = (bf16[16,16,512]{2,1,0:T(8,128)(2,1)S(1)}, bf16[16,16,512]{2,1,0:T(8,128)(2,1)S(1)}, u32[]{:S(2)}, u32[]{:S(2)}) collective-permute-start(bf16[16,16,512]{2,1,0:T(8,128)(2,1)S(1)} %get-tuple-element.76), channel_id=1, source_target_pairs={{0,24},{4,28},{8,16},{12,20},{16,8},{20,12},{24,0},{28,4},{1,25},{... | collective-permute-start | bytes 786440 | tf_op jit(solution)/shard_map/ppermute | solution.py:296
  20.2 3.2 %collective-permute-start.9 = (bf16[16,16,512]{2,1,0:T(8,128)(2,1)S(1)}, bf16[16,16,512]{2,1,0:T(8,128)(2,1)S(1)}, u32[]{:S(2)}, u32[]{:S(2)}) collective-permute-start(bf16[16,16,512]{2,1,0:T(8,128)(2,1)S(1)} %get-tuple-element.82), channel_id=1, source_target_pairs={{0,16},{4,20},{8,24},{12,28},{16,0},{20,4},{24,8},{28,12},{1,17},{... | collective-permute-start | bytes 786440 | tf_op jit(solution)/shard_map/ppermute | solution.py:296
  23.4 0.1 collective-permute-start.8
  23.5 0.0 collective-permute-done.3.refs_1_
  23.5 20.4 %collective-permute-done.4.refs_2_ = bf16[16,16,512]{2,1,0:T(8,128)(2,1)S(1)} collective-permute-done((bf16[16,16,512]{2,1,0:T(8,128)(2,1)S(1)}, bf16[16,16,512]{2,1,0:T(8,128)(2,1)S(1)}, u32[]{:S(2)}, u32[]{:S(2)}) %collective-permute-start.4) | collective-permute-done | bytes 262176 | tf_op jit(solution)/shard_map/ppermute | solution.py:296
  43.9 0.0 copy-done
  43.9 0.0 copy-done.4
  43.9 0.0 copy-done.3
  43.9 0.0 copy-done.2
  43.9 0.0 copy-done.1
  43.9 0.0 copy-done.7
  43.9 6.2 %attend_outer.1 = (bf16[8,16,512]{2,1,0:T(8,128)(2,1)S(1)}, bf16[8,16,512]{2,1,0:T(8,128)(2,1)S(1)}, bf16[8,16,512]{2,1,0:T(8,128)(2,1)S(1)}, bf16[8,16,512]{2,1,0:T(8,128)(2,1)S(1)}) custom-call(bf16[16,16,512]{2,1,0:T(8,128)(2,1)S(1)} %collective-permute-done.1.refs_0_, bf16[16,16,512]{2,1,0:T(8,128)(2,1)S(1)} %collective-permute-done.3.refs_1_, ...), custom_call_target="tpu_custom_call" | custom-call | flops 1 | bytes 1 | tf_op jit(solution)/shard_map/attend_outer/pallas_call | solution.py:163
  50.1 0.0 collective-permute-done.5.refs_0_
  50.1 2.5 %collective-permute-start.6 = (bf16[8,16,512]{2,1,0:T(8,128)(2,1)S(1)}, bf16[8,16,512]{2,1,0:T(8,128)(2,1)S(1)}, u32[]{:S(2)}, u32[]{:S(2)}) collective-permute-start(bf16[8,16,512]{2,1,0:T(8,128)(2,1)S(1)} %get-tuple-element.77), channel_id=1, source_target_pairs={{0,24},{4,28},{8,16},{12,20},{16,8},{20,12},{24,0},{28,4},{1,25},{... | collective-permute-start | bytes 393224 | tf_op jit(solution)/shard_map/ppermute | solution.py:296
  52.7 0.0 collective-permute-start.7
  52.7 4.7 %collective-permute-done.9.refs_2_ = bf16[16,16,512]{2,1,0:T(8,128)(2,1)S(1)} collective-permute-done((bf16[16,16,512]{2,1,0:T(8,128)(2,1)S(1)}, bf16[16,16,512]{2,1,0:T(8,128)(2,1)S(1)}, u32[]{:S(2)}, u32[]{:S(2)}) %collective-permute-start.9) | collective-permute-done | bytes 262176 | tf_op jit(solution)/shard_map/ppermute | solution.py:296
  57.3 0.0 collective-permute-start.10
  57.4 0.0 collective-permute-done.8.refs_1_
  57.4 0.0 copy-start.6
  57.4 6.2 %attend_inner.1 = (bf16[4,16,512]{2,1,0:T(8,128)(2,1)S(1)}, bf16[4,16,512]{2,1,0:T(8,128)(2,1)S(1)}, bf16[4,16,512]{2,1,0:T(8,128)(2,1)S(1)}, bf16[4,16,512]{2,1,0:T(8,128)(2,1)S(1)}, bf16[4,4,16,512]{3,2,1,0:T(8,128)(2,1)S(1)}) custom-call(bf16[16,16,512]{2,1,0:T(8,128)(2,1)S(1)} %collective-permute-done.5.refs_0_, ...), custom_call_target="tpu_custom_call" | custom-call | flops 1 | bytes 1 | tf_op jit(solution)/shard_map/attend_inner/pallas_call | solution.py:163
  63.5 0.0 collective-permute-done.6.refs_0_
  63.5 0.0 collective-permute-done.7.refs_1_
  63.6 0.1 collective-permute-start.12
  63.6 2.2 %collective-permute-done.10.refs_2_ = bf16[8,16,512]{2,1,0:T(8,128)(2,1)S(1)} collective-permute-done((bf16[8,16,512]{2,1,0:T(8,128)(2,1)S(1)}, bf16[8,16,512]{2,1,0:T(8,128)(2,1)S(1)}, u32[]{:S(2)}, u32[]{:S(2)}) %collective-permute-start.10) | collective-permute-done | bytes 131104 | tf_op jit(solution)/shard_map/ppermute | solution.py:296
  65.8 0.1 collective-permute-start.11
  65.9 0.0 collective-permute-done.12.refs_3_.refs_9_
  65.9 3.1 %collective-permute-start.14 = (bf16[2,4,16,512]{3,2,1,0:T(8,128)(2,1)S(1)}, bf16[2,4,16,512]{3,2,1,0:T(8,128)(2,1)S(1)}, u32[]{:S(2)}, u32[]{:S(2)}) collective-permute-start(bf16[2,4,16,512]{3,2,1,0:T(8,128)(2,1)S(1)} %get-tuple-element.97), channel_id=1, source_target_pairs={{0,8},{4,12},{8,0},{12,4},{16,24},{20,28},{24,16},{28,20},{1,9},{5... | collective-permute-start | bytes 393224 | tf_op jit(solution)/shard_map/ppermute | solution.py:296
  69.1 0.6 collective-permute-start.13
  69.6 1.0 %collective-permute-start.15 = (bf16[2,4,16,512]{3,2,1,0:T(8,128)(2,1)S(1)}, bf16[2,4,16,512]{3,2,1,0:T(8,128)(2,1)S(1)}, u32[]{:S(2)}, u32[]{:S(2)}) collective-permute-start(bf16[2,4,16,512]{3,2,1,0:T(8,128)(2,1)S(1)} %get-tuple-element.99), channel_id=1, source_target_pairs={{0,16},{4,20},{8,24},{12,28},{16,0},{20,4},{24,8},{28,12},{1,17},{... | collective-permute-start | bytes 393224 | tf_op jit(solution)/shard_map/ppermute | solution.py:296
  70.6 0.0 collective-permute-done.11.refs_4_
  70.6 0.1 rim.1
  70.7 2.2 %collective-permute-done.14.refs_6_ = bf16[2,4,16,512]{3,2,1,0:T(8,128)(2,1)S(1)} collective-permute-done((bf16[2,4,16,512]{3,2,1,0:T(8,128)(2,1)S(1)}, bf16[2,4,16,512]{3,2,1,0:T(8,128)(2,1)S(1)}, u32[]{:S(2)}, u32[]{:S(2)}) %collective-permute-start.14) | collective-permute-done | bytes 131104 | tf_op jit(solution)/shard_map/ppermute | solution.py:296
  72.9 3.4 %collective-permute-start.16 = (bf16[8,4,512]{2,1,0:T(4,128)(2,1)S(1)}, bf16[8,4,512]{2,1,0:T(4,128)(2,1)S(1)}, u32[]{:S(2)}, u32[]{:S(2)}) collective-permute-start(bf16[8,4,512]{2,1,0:T(4,128)(2,1)S(1)} %get-tuple-element.101), channel_id=1, source_target_pairs={{0,1},{1,2},{2,3},{4,5},{5,6},{6,7},{8,9},{9,10},{10,11},{12,13},{... | collective-permute-start | bytes 98312 | tf_op jit(solution)/shard_map/ppermute | solution.py:364
  76.3 1.3 %collective-permute-start.17 = (bf16[8,4,512]{2,1,0:T(4,128)(2,1)S(1)}, bf16[8,4,512]{2,1,0:T(4,128)(2,1)S(1)}, u32[]{:S(2)}, u32[]{:S(2)}) collective-permute-start(bf16[8,4,512]{2,1,0:T(4,128)(2,1)S(1)} %get-tuple-element.102), channel_id=1, source_target_pairs={{1,0},{2,1},{3,2},{5,4},{6,5},{7,6},{9,8},{10,9},{11,10},{13,12},{... | collective-permute-start | bytes 98312 | tf_op jit(solution)/shard_map/ppermute | solution.py:365
  77.6 0.0 collective-permute-done.13.refs_5_
  77.6 4.9 %collective-permute-done.15.refs_7_ = bf16[2,4,16,512]{3,2,1,0:T(8,128)(2,1)S(1)} collective-permute-done((bf16[2,4,16,512]{3,2,1,0:T(8,128)(2,1)S(1)}, bf16[2,4,16,512]{3,2,1,0:T(8,128)(2,1)S(1)}, u32[]{:S(2)}, u32[]{:S(2)}) %collective-permute-start.15) | collective-permute-done | bytes 131104 | tf_op jit(solution)/shard_map/ppermute | solution.py:296
  82.6 0.0 collective-permute-done.16.refs_10_
  82.6 0.0 collective-permute-done.17.refs_11_
  82.6 0.0 copy-done.6
  82.6 2.4 %depth_filter.1 = bf16[4,8,32,512]{3,2,1,0:T(8,128)(2,1)} custom-call(bf16[8,16,512]{2,1,0:T(8,128)(2,1)S(1)} %collective-permute-done.6.refs_0_, bf16[8,16,512]{2,1,0:T(8,128)(2,1)S(1)} %collective-permute-done.7.refs_1_, bf16[8,16,512]{2,1,0:T(8,128)(2,1)S(1)} %collective-permute-done.10.refs_2_, bf16[8,16,512]{2,1,0:T(8,128)(2,1)S(1)} %get-tuple-element.89.refs_3_, ...), custom_call_target="tpu_custom_call" | custom-call | flops 1 | bytes 1 | tf_op jit(solution)/shard_map/depth_filter/pallas_call | solution.py:269
  (2 shorter events, 0.0 us)
Async XLA Ops:
  0.0 43.9 %copy-start = (bf16[3,512,512]{2,1,0:T(8,128)(2,1)S(1)}, bf16[3,512,512]{2,1,0:T(8,128)(2,1)}, u32[]{:S(2)}) copy-start(bf16[3,512,512]{2,1,0:T(8,128)(2,1)} %refs_10_.3) | copy-start | bytes 4718596
  0.0 43.9 %copy-start.4 = (bf16[512,512]{1,0:T(8,128)(2,1)S(1)}, bf16[512,512]{1,0:T(8,128)(2,1)}, u32[]{:S(2)}) copy-start(bf16[512,512]{1,0:T(8,128)(2,1)} %refs_9_.3) | copy-start | bytes 1572868
  0.0 43.9 %copy-start.3 = (bf16[512,512]{1,0:T(8,128)(2,1)S(1)}, bf16[512,512]{1,0:T(8,128)(2,1)}, u32[]{:S(2)}) copy-start(bf16[512,512]{1,0:T(8,128)(2,1)} %refs_8_.3) | copy-start | bytes 1572868
  0.0 43.9 %copy-start.2 = (bf16[512,512]{1,0:T(8,128)(2,1)S(1)}, bf16[512,512]{1,0:T(8,128)(2,1)}, u32[]{:S(2)}) copy-start(bf16[512,512]{1,0:T(8,128)(2,1)} %refs_7_.3) | copy-start | bytes 1572868
  0.0 43.9 %copy-start.1 = (bf16[512,512]{1,0:T(8,128)(2,1)S(1)}, bf16[512,512]{1,0:T(8,128)(2,1)}, u32[]{:S(2)}) copy-start(bf16[512,512]{1,0:T(8,128)(2,1)} %refs_6_.3) | copy-start | bytes 1572868
  0.0 1.7 %copy-start.5 = (bf16[8,8,32,512]{3,2,1,0:T(8,128)(2,1)S(1)}, bf16[8,8,32,512]{3,2,1,0:T(8,128)(2,1)}, u32[]{:S(2)}) copy-start(bf16[8,8,32,512]{3,2,1,0:T(8,128)(2,1)} %video.1) | copy-start | bytes 6291460
  1.8 42.2 %copy-start.7 = (f32[512]{0:T(512)S(1)}, f32[512]{0:T(512)}, u32[]{:S(2)}) copy-start(f32[512]{0:T(512)} %param.9) | copy-start | bytes 6148
  1.9 2.1 %collective-permute-start = (bf16[4,8,16,512]{3,2,1,0:T(8,128)(2,1)S(1)}, bf16[4,8,16,512]{3,2,1,0:T(8,128)(2,1)S(1)}, u32[]{:S(2)}, u32[]{:S(2)}) collective-permute-start(bf16[4,8,16,512]{3,2,1,0:T(8,128)(2,1)S(1)} %get-tuple-element.57), channel_id=1, source_target_pairs={{0,4},{4,0},{8,12},{12,8},{16,20},{20,16},{24,28},{28,24},{1,5},{5... | collective-permute-start | bytes 1572872 | tf_op jit(solution)/shard_map/ppermute | solution.py:296
  4.0 5.8 %collective-permute-start.2 = (bf16[4,8,16,512]{3,2,1,0:T(8,128)(2,1)S(1)}, bf16[4,8,16,512]{3,2,1,0:T(8,128)(2,1)S(1)}, u32[]{:S(2)}, u32[]{:S(2)}) collective-permute-start(bf16[4,8,16,512]{3,2,1,0:T(8,128)(2,1)S(1)} %get-tuple-element.66), channel_id=1, source_target_pairs={{0,4},{4,0},{8,12},{12,8},{16,20},{20,16},{24,28},{28,24},{1,5},{5... | collective-permute-start | bytes 1572872 | tf_op jit(solution)/shard_map/ppermute | solution.py:296
  4.5 12.0 %collective-permute-start.1 = (bf16[16,16,512]{2,1,0:T(8,128)(2,1)S(1)}, bf16[16,16,512]{2,1,0:T(8,128)(2,1)S(1)}, u32[]{:S(2)}, u32[]{:S(2)}) collective-permute-start(bf16[16,16,512]{2,1,0:T(8,128)(2,1)S(1)} %get-tuple-element.62), channel_id=1, source_target_pairs={{0,24},{4,28},{8,16},{12,20},{16,8},{20,12},{24,0},{28,4},{1,25},{... | collective-permute-start | bytes 786440 | tf_op jit(solution)/shard_map/ppermute | solution.py:296
  9.2 14.3 %collective-permute-start.3 = (bf16[16,16,512]{2,1,0:T(8,128)(2,1)S(1)}, bf16[16,16,512]{2,1,0:T(8,128)(2,1)S(1)}, u32[]{:S(2)}, u32[]{:S(2)}) collective-permute-start(bf16[16,16,512]{2,1,0:T(8,128)(2,1)S(1)} %get-tuple-element.71), channel_id=1, source_target_pairs={{0,8},{4,12},{8,0},{12,4},{16,24},{20,28},{24,16},{28,20},{1,9},{5... | collective-permute-start | bytes 786440 | tf_op jit(solution)/shard_map/ppermute | solution.py:296
  9.2 34.7 %collective-permute-start.4 = (bf16[16,16,512]{2,1,0:T(8,128)(2,1)S(1)}, bf16[16,16,512]{2,1,0:T(8,128)(2,1)S(1)}, u32[]{:S(2)}, u32[]{:S(2)}) collective-permute-start(bf16[16,16,512]{2,1,0:T(8,128)(2,1)S(1)} %get-tuple-element.72), channel_id=1, source_target_pairs={{0,16},{4,20},{8,24},{12,28},{16,0},{20,4},{24,8},{28,12},{1,17},{... | collective-permute-start | bytes 786440 | tf_op jit(solution)/shard_map/ppermute | solution.py:296
  16.4 33.7 %collective-permute-start.5 = (bf16[16,16,512]{2,1,0:T(8,128)(2,1)S(1)}, bf16[16,16,512]{2,1,0:T(8,128)(2,1)S(1)}, u32[]{:S(2)}, u32[]{:S(2)}) collective-permute-start(bf16[16,16,512]{2,1,0:T(8,128)(2,1)S(1)} %get-tuple-element.76), channel_id=1, source_target_pairs={{0,24},{4,28},{8,16},{12,20},{16,8},{20,12},{24,0},{28,4},{1,25},{... | collective-permute-start | bytes 786440 | tf_op jit(solution)/shard_map/ppermute | solution.py:296
  20.2 37.2 %collective-permute-start.9 = (bf16[16,16,512]{2,1,0:T(8,128)(2,1)S(1)}, bf16[16,16,512]{2,1,0:T(8,128)(2,1)S(1)}, u32[]{:S(2)}, u32[]{:S(2)}) collective-permute-start(bf16[16,16,512]{2,1,0:T(8,128)(2,1)S(1)} %get-tuple-element.82), channel_id=1, source_target_pairs={{0,16},{4,20},{8,24},{12,28},{16,0},{20,4},{24,8},{28,12},{1,17},{... | collective-permute-start | bytes 786440 | tf_op jit(solution)/shard_map/ppermute | solution.py:296
  23.4 34.0 %collective-permute-start.8 = (bf16[16,16,512]{2,1,0:T(8,128)(2,1)S(1)}, bf16[16,16,512]{2,1,0:T(8,128)(2,1)S(1)}, u32[]{:S(2)}, u32[]{:S(2)}) collective-permute-start(bf16[16,16,512]{2,1,0:T(8,128)(2,1)S(1)} %get-tuple-element.80), channel_id=1, source_target_pairs={{0,8},{4,12},{8,0},{12,4},{16,24},{20,28},{24,16},{28,20},{1,9},{5... | collective-permute-start | bytes 786440 | tf_op jit(solution)/shard_map/ppermute | solution.py:296
  50.1 13.4 %collective-permute-start.6 = (bf16[8,16,512]{2,1,0:T(8,128)(2,1)S(1)}, bf16[8,16,512]{2,1,0:T(8,128)(2,1)S(1)}, u32[]{:S(2)}, u32[]{:S(2)}) collective-permute-start(bf16[8,16,512]{2,1,0:T(8,128)(2,1)S(1)} %get-tuple-element.77), channel_id=1, source_target_pairs={{0,24},{4,28},{8,16},{12,20},{16,8},{20,12},{24,0},{28,4},{1,25},{... | collective-permute-start | bytes 393224 | tf_op jit(solution)/shard_map/ppermute | solution.py:296
  52.7 10.9 %collective-permute-start.7 = (bf16[8,16,512]{2,1,0:T(8,128)(2,1)S(1)}, bf16[8,16,512]{2,1,0:T(8,128)(2,1)S(1)}, u32[]{:S(2)}, u32[]{:S(2)}) collective-permute-start(bf16[8,16,512]{2,1,0:T(8,128)(2,1)S(1)} %get-tuple-element.78), channel_id=1, source_target_pairs={{0,8},{4,12},{8,0},{12,4},{16,24},{20,28},{24,16},{28,20},{1,9},{5... | collective-permute-start | bytes 393224 | tf_op jit(solution)/shard_map/ppermute | solution.py:296
  57.3 8.4 %collective-permute-start.10 = (bf16[8,16,512]{2,1,0:T(8,128)(2,1)S(1)}, bf16[8,16,512]{2,1,0:T(8,128)(2,1)S(1)}, u32[]{:S(2)}, u32[]{:S(2)}) collective-permute-start(bf16[8,16,512]{2,1,0:T(8,128)(2,1)S(1)} %get-tuple-element.88), channel_id=1, source_target_pairs={{0,16},{4,20},{8,24},{12,28},{16,0},{20,4},{24,8},{28,12},{1,17},{... | collective-permute-start | bytes 393224 | tf_op jit(solution)/shard_map/ppermute | solution.py:296
  57.4 25.2 %copy-start.6 = (f32[3,3,512]{2,1,0:T(4,128)S(1)}, f32[3,3,512]{2,1,0:T(4,128)}, u32[]{:S(2)}) copy-start(f32[3,3,512]{2,1,0:T(4,128)} %refs_12_.1) | copy-start | bytes 55300
  63.6 2.3 %collective-permute-start.12 = (bf16[4,4,16,512]{3,2,1,0:T(8,128)(2,1)S(1)}, bf16[4,4,16,512]{3,2,1,0:T(8,128)(2,1)S(1)}, u32[]{:S(2)}, u32[]{:S(2)}) collective-permute-start(bf16[4,4,16,512]{3,2,1,0:T(8,128)(2,1)S(1)} %get-tuple-element.93), channel_id=1, source_target_pairs={{0,4},{4,0},{8,12},{12,8},{16,20},{20,16},{24,28},{28,24},{1,5},{5... | collective-permute-start | bytes 786440 | tf_op jit(solution)/shard_map/ppermute | solution.py:296
  65.8 4.8 %collective-permute-start.11 = (bf16[4,4,16,512]{3,2,1,0:T(8,128)(2,1)S(1)}, bf16[4,4,16,512]{3,2,1,0:T(8,128)(2,1)S(1)}, u32[]{:S(2)}, u32[]{:S(2)}) collective-permute-start(bf16[4,4,16,512]{3,2,1,0:T(8,128)(2,1)S(1)} %stack_back.1), channel_id=1, source_target_pairs={{0,4},{4,0},{8,12},{12,8},{16,20},{20,16},{24,28},{28,24},{1,5},{5... | collective-permute-start | bytes 786440 | tf_op jit(solution)/shard_map/ppermute | solution.py:296
  65.9 7.0 %collective-permute-start.14 = (bf16[2,4,16,512]{3,2,1,0:T(8,128)(2,1)S(1)}, bf16[2,4,16,512]{3,2,1,0:T(8,128)(2,1)S(1)}, u32[]{:S(2)}, u32[]{:S(2)}) collective-permute-start(bf16[2,4,16,512]{3,2,1,0:T(8,128)(2,1)S(1)} %get-tuple-element.97), channel_id=1, source_target_pairs={{0,8},{4,12},{8,0},{12,4},{16,24},{20,28},{24,16},{28,20},{1,9},{5... | collective-permute-start | bytes 393224 | tf_op jit(solution)/shard_map/ppermute | solution.py:296
  69.1 8.6 %collective-permute-start.13 = (bf16[2,4,16,512]{3,2,1,0:T(8,128)(2,1)S(1)}, bf16[2,4,16,512]{3,2,1,0:T(8,128)(2,1)S(1)}, u32[]{:S(2)}, u32[]{:S(2)}) collective-permute-start(bf16[2,4,16,512]{3,2,1,0:T(8,128)(2,1)S(1)} %get-tuple-element.94), channel_id=1, source_target_pairs={{0,24},{4,28},{8,16},{12,20},{16,8},{20,12},{24,0},{28,4},{1,25},{... | collective-permute-start | bytes 393224 | tf_op jit(solution)/shard_map/ppermute | solution.py:296
  69.6 12.9 %collective-permute-start.15 = (bf16[2,4,16,512]{3,2,1,0:T(8,128)(2,1)S(1)}, bf16[2,4,16,512]{3,2,1,0:T(8,128)(2,1)S(1)}, u32[]{:S(2)}, u32[]{:S(2)}) collective-permute-start(bf16[2,4,16,512]{3,2,1,0:T(8,128)(2,1)S(1)} %get-tuple-element.99), channel_id=1, source_target_pairs={{0,16},{4,20},{8,24},{12,28},{16,0},{20,4},{24,8},{28,12},{1,17},{... | collective-permute-start | bytes 393224 | tf_op jit(solution)/shard_map/ppermute | solution.py:296
  72.9 9.6 %collective-permute-start.16 = (bf16[8,4,512]{2,1,0:T(4,128)(2,1)S(1)}, bf16[8,4,512]{2,1,0:T(4,128)(2,1)S(1)}, u32[]{:S(2)}, u32[]{:S(2)}) collective-permute-start(bf16[8,4,512]{2,1,0:T(4,128)(2,1)S(1)} %get-tuple-element.101), channel_id=1, source_target_pairs={{0,1},{1,2},{2,3},{4,5},{5,6},{6,7},{8,9},{9,10},{10,11},{12,13},{... | collective-permute-start | bytes 98312 | tf_op jit(solution)/shard_map/ppermute | solution.py:364
  76.3 6.2 %collective-permute-start.17 = (bf16[8,4,512]{2,1,0:T(4,128)(2,1)S(1)}, bf16[8,4,512]{2,1,0:T(4,128)(2,1)S(1)}, u32[]{:S(2)}, u32[]{:S(2)}) collective-permute-start(bf16[8,4,512]{2,1,0:T(4,128)(2,1)S(1)} %get-tuple-element.102), channel_id=1, source_target_pairs={{1,0},{2,1},{3,2},{5,4},{6,5},{7,6},{9,8},{10,9},{11,10},{13,12},{... | collective-permute-start | bytes 98312 | tf_op jit(solution)/shard_map/ppermute | solution.py:365

commit v9 on v8

--- a/solution.py
+++ b/solution.py
@@ -51,16 +51,17 @@
         for row, target in zip(own + other, targets):
             values = video[:, row].astype(jnp.float32)
             if rim:
-                values = jnp.concatenate([values[:, :edge], values[:, 3 * edge :]], axis=1)
+                values = jnp.concatenate([values[:, :edge], values[:, 2 * edge :]], axis=1)
             else:
-                values = values[:, edge : 3 * edge]
+                values = values[:, edge : 2 * edge]
             target[...] = values.astype(jnp.bfloat16)
 
 
 def cut(rows_of, chips, video):
     span, height, cols, channels = video.shape
-    shape = (span, cols // 2, channels)
-    shapes = ([shape] * chips + [(chips, *shape)]) * 2
+    shapes = []
+    for width in (cols - cols // 4, cols // 4):
+        shapes += [(span, width, channels)] * chips + [(chips, span, width, channels)]
     return pl.pallas_call(
         functools.partial(cut_kernel, rows_of),
         out_shape=[jax.ShapeDtypeStruct(shape, jnp.bfloat16) for shape in shapes],
@@ -173,7 +174,7 @@
             pltpu.VMEM((rows, channels), jnp.bfloat16),
             pltpu.VMEM((cols // GROUP, frames + 2, GROUP, channels), jnp.float32),
         ],
-        compiler_params=pltpu.CompilerParams(vmem_limit_bytes=24 * MIB),
+        compiler_params=pltpu.CompilerParams(vmem_limit_bytes=32 * MIB),
         cost_estimate=SMALL,
         name=name,
     )(*pieces, norm_gain[None], *matrices)
@@ -263,8 +264,8 @@
 
 def depth_filter(hops, outer, inner, left, right, w_depth):
     height, frames, channels = left.shape
-    width = inner[-1].shape[2]
-    cols = 2 * width
+    widths = [pieces[-1].shape[2] for pieces in (outer, inner)]
+    cols = sum(widths)
     size = frames * height * cols * channels
     return pl.pallas_call(
         functools.partial(filter_kernel, hops),
@@ -272,7 +273,7 @@
         in_specs=[INSIDE] * (2 * len(hops) + 5),
         out_specs=pl.BlockSpec(memory_space=pl.ANY),
         scratch_shapes=[
-            *[pltpu.VMEM((height, frames, width, channels), jnp.bfloat16)] * 2,
+            *[pltpu.VMEM((height, frames, width, channels), jnp.bfloat16) for width in widths],
             pltpu.VMEM((frames, height, cols, channels), jnp.bfloat16),
             pltpu.SemaphoreType.DMA((frames,)),
         ],
@@ -289,7 +290,6 @@
     assert height == count and chips & (chips - 1) == 0 and chips > 1
     made = span // 2
     frames = span * count
-    width = cols // 2
     weights = (norm_gain, w_query, w_key, w_value, w_out, w_time)
 
     def swap(block, k):
@@ -310,7 +310,7 @@
         return pairs
 
     def join(owns, other, name):
-        return gather(joined, [*owns[:-1], other], [(2 * span, width, channels)] * len(far), name)
+        return gather(joined, [*owns[:-1], other], [(2 * span, *other.shape[2:])] * len(far), name)
 
     outer_other = swap(outer_stack, 1)
     outer_far = join(outer, outer_other, "join_outer")
@@ -332,7 +332,7 @@
         return pairs + [(own, me * span), (other.at[len(far)], (me ^ 1) * span)]
 
     outer = list(attend(inward, hops, True, [*outer_far, outer[-1], outer_other], weights, frames, "attend_outer"))
-    outer[:2], inner_far[0] = lax.optimization_barrier((outer[:2], inner_far[0]))
+    outer[:2], inner_far[:2] = lax.optimization_barrier((outer[:2], inner_far[:2]))
     for i in range(2, len(far)):
         outer[i], inner_far[i] = lax.optimization_barrier((outer[i], inner_far[i]))
     outer = [swap(piece, k) for k, piece in zip(hops, outer)]
@@ -348,14 +348,14 @@
             pairs += [(own, outs[i].at[0]), (taken.at[i], outs[i].at[1])]
         return pairs
 
-    inner = gather(joined_back, [*keep[:-1], taken], [(2, made, width, channels)] * len(far), "join_back")
+    inner = gather(joined_back, [*keep[:-1], taken], [(2, *taken.shape[1:])] * len(far), "join_back")
     inner = [swap(piece, k) for k, piece in zip(hops, inner)]
 
     def for_mate(ins, outs):
         _, core = place()
         return [(piece.at[pl.ds((1 - core) * made, made)], outs[0].at[i]) for i, piece in enumerate(ins)]
 
-    (stack,) = gather(for_mate, outer, [(chips, made, width, channels)], "stack_back")
+    (stack,) = gather(for_mate, outer, [(chips, made, *outer[0].shape[1:])], "stack_back")
     halves = swap(stack, 1)
     low_side, high_side = rim(hops, outer, halves)
     low_side, high_side, inner[nearest] = lax.optimization_barrier((low_side, high_side, inner[nearest]))

time: 85.1 us -> 94.6 us (1.11)
  waiting for transfers between devices: 42.5 us -> 47.5 us
  starting transfers between devices: 25.4 us -> 29.8 us
    ppermute x16, starting transfers between devices: 20.7 us -> 25.1 us  [swap(): lax.ppermute(block, 'frm', [(i, i ^ k) for i in range(count)])]
    ppermute x1, waiting for transfers between devices: 0.01 us -> 3.94 us  [local(): right = lax.ppermute(low_side, 'col', [(b, a) for a, b in upward])]
    ppermute x16, waiting for transfers between devices: 42.5 us -> 43.5 us  [swap(): lax.ppermute(block, 'frm', [(i, i ^ k) for i in range(count)])]
  transfers between devices with their start and end apart: 18 -> 18, of which waited for: 7 -> 11; matrix products, arithmetic and copies ran while one was open for 0% -> 0% of each run, Pallas kernels for 15% -> 13%
where the time goes in v9:
time: 94.6 us; the launch traced here: 94.4 us
  waiting for transfers between devices  47.5 us (50%)
  starting transfers between devices  29.8 us (32%)
  Pallas kernels  15.2 us (16%)
  local copies, waits for them, and re-layouts  1.74 us (2%)
    ppermute x16, waiting for transfers between devices, swap(): lax.ppermute(block, 'frm', [(i, i ^ k) for i in range(count)])  43.5 us
    ppermute x16, starting transfers between devices, swap(): lax.ppermute(block, 'frm', [(i, i ^ k) for i in range(count)])  25.1 us
    pallas_call x2, Pallas kernels, attend(): pl.pallas_call(functools.partial(attend_kernel, inward, hops, paired, len...  12.4 us
    ppermute x1, waiting for transfers between devices, local(): right = lax.ppermute(low_side, 'col', [(b, a) for a, b in upward])  3.94 us
    ppermute x1, starting transfers between devices, local(): left = lax.ppermute(high_side, 'col', upward)  3.39 us
    pallas_call x1, Pallas kernels, depth_filter(): pl.pallas_call(functools.partial(filter_kernel, hops), out_shape=jax.Shap...  2.38 us
  transfers between devices with their start and end apart: 18, of which 11 were waited for; matrix products, arithmetic and copies ran while one was open for 0% of the time, Pallas kernels for 13%

profile of v9, /device:TPU:0, one launch (start us, length us, event | category | flops | bytes accessed | tf_op | source)
XLA Modules:
  0.0 94.4 jit_solution(2829678739559622058)
XLA Ops:
  0.0 0.0 copy-start
  0.0 0.0 copy-start.1
  0.0 1.7 %copy-done.1 = bf16[8,8,32,512]{3,2,1,0:T(8,128)(2,1)S(1)} copy-done((bf16[8,8,32,512]{3,2,1,0:T(8,128)(2,1)S(1)}, bf16[8,8,32,512]{3,2,1,0:T(8,128)(2,1)}, u32[]{:S(2)}) %copy-start.1) | copy-done | bytes 2097176
  1.7 0.0 copy-start.2
  1.7 0.0 copy-start.3
  1.7 0.0 copy-start.4
  1.7 0.0 copy-start.5
  1.7 0.0 copy-start.7
  1.7 0.2 cut.1
  1.9 0.5 collective-permute-start
  2.4 1.9 %collective-permute-done.refs_3_.refs_4_ = bf16[4,8,24,512]{3,2,1,0:T(8,128)(2,1)S(1)} collective-permute-done((bf16[4,8,24,512]{3,2,1,0:T(8,128)(2,1)S(1)}, bf16[4,8,24,512]{3,2,1,0:T(8,128)(2,1)S(1)}, u32[]{:S(2)}, u32[]{:S(2)}) %collective-permute-start) | collective-permute-done | bytes 786464 | tf_op jit(solution)/shard_map/ppermute | solution.py:296
  4.3 0.1 join_outer.1
  4.4 5.0 %collective-permute-start.1 = (bf16[16,24,512]{2,1,0:T(8,128)(2,1)S(1)}, bf16[16,24,512]{2,1,0:T(8,128)(2,1)S(1)}, u32[]{:S(2)}, u32[]{:S(2)}) collective-permute-start(bf16[16,24,512]{2,1,0:T(8,128)(2,1)S(1)} %get-tuple-element.63), channel_id=1, source_target_pairs={{0,24},{4,28},{8,16},{12,20},{16,8},{20,12},{24,0},{28,4},{1,25},{... | collective-permute-start | bytes 1179656 | tf_op jit(solution)/shard_map/ppermute | solution.py:296
  9.4 0.0 collective-permute-start.2
  9.4 0.0 collective-permute-start.3
  9.4 0.8 collective-permute-start.4
  10.2 0.7 collective-permute-done.2.refs_3_.refs_4_
  11.0 8.4 %collective-permute-done.1.refs_0_ = bf16[16,24,512]{2,1,0:T(8,128)(2,1)S(1)} collective-permute-done((bf16[16,24,512]{2,1,0:T(8,128)(2,1)S(1)}, bf16[16,24,512]{2,1,0:T(8,128)(2,1)S(1)}, u32[]{:S(2)}, u32[]{:S(2)}) %collective-permute-start.1) | collective-permute-done | bytes 393248 | tf_op jit(solution)/shard_map/ppermute | solution.py:296
  19.4 3.8 %collective-permute-start.5 = (bf16[16,8,512]{2,1,0:T(8,128)(2,1)S(1)}, bf16[16,8,512]{2,1,0:T(8,128)(2,1)S(1)}, u32[]{:S(2)}, u32[]{:S(2)}) collective-permute-start(bf16[16,8,512]{2,1,0:T(8,128)(2,1)S(1)} %get-tuple-element.77), channel_id=1, source_target_pairs={{0,24},{4,28},{8,16},{12,20},{16,8},{20,12},{24,0},{28,4},{1,25},{... | collective-permute-start | bytes 393224 | tf_op jit(solution)/shard_map/ppermute | solution.py:296
  23.2 6.1 %collective-permute-start.6 = (bf16[16,8,512]{2,1,0:T(8,128)(2,1)S(1)}, bf16[16,8,512]{2,1,0:T(8,128)(2,1)S(1)}, u32[]{:S(2)}, u32[]{:S(2)}) collective-permute-start(bf16[16,8,512]{2,1,0:T(8,128)(2,1)S(1)} %get-tuple-element.78), channel_id=1, source_target_pairs={{0,8},{4,12},{8,0},{12,4},{16,24},{20,28},{24,16},{28,20},{1,9},{5... | collective-permute-start | bytes 393224 | tf_op jit(solution)/shard_map/ppermute | solution.py:296
  29.4 0.2 collective-permute-start.9
  29.6 0.0 collective-permute-done.3.refs_1_
  29.6 20.1 %collective-permute-done.4.refs_2_ = bf16[16,24,512]{2,1,0:T(8,128)(2,1)S(1)} collective-permute-done((bf16[16,24,512]{2,1,0:T(8,128)(2,1)S(1)}, bf16[16,24,512]{2,1,0:T(8,128)(2,1)S(1)}, u32[]{:S(2)}, u32[]{:S(2)}) %collective-permute-start.4) | collective-permute-done | bytes 393248 | tf_op jit(solution)/shard_map/ppermute | solution.py:296
  49.7 0.0 copy-done
  49.7 0.0 copy-done.2
  49.7 0.0 copy-done.3
  49.7 0.0 copy-done.4
  49.7 0.0 copy-done.5
  49.7 0.0 copy-done.7
  49.7 9.2 %attend_outer.1 = (bf16[8,24,512]{2,1,0:T(8,128)(2,1)S(1)}, bf16[8,24,512]{2,1,0:T(8,128)(2,1)S(1)}, bf16[8,24,512]{2,1,0:T(8,128)(2,1)S(1)}, bf16[8,24,512]{2,1,0:T(8,128)(2,1)S(1)}) custom-call(bf16[16,24,512]{2,1,0:T(8,128)(2,1)S(1)} %collective-permute-done.1.refs_0_, bf16[16,24,512]{2,1,0:T(8,128)(2,1)S(1)} %collective-permute-done.3.refs_1_, ...), custom_call_target="tpu_custom_call" | custom-call | flops 1 | bytes 1 | tf_op jit(solution)/shard_map/attend_outer/pallas_call | solution.py:164
  58.9 0.0 collective-permute-done.5.refs_0_
  58.9 0.0 collective-permute-done.6.refs_1_
  58.9 2.5 %collective-permute-start.7 = (bf16[8,24,512]{2,1,0:T(8,128)(2,1)S(1)}, bf16[8,24,512]{2,1,0:T(8,128)(2,1)S(1)}, u32[]{:S(2)}, u32[]{:S(2)}) collective-permute-start(bf16[8,24,512]{2,1,0:T(8,128)(2,1)S(1)} %get-tuple-element.79), channel_id=1, source_target_pairs={{0,24},{4,28},{8,16},{12,20},{16,8},{20,12},{24,0},{28,4},{1,25},{... | collective-permute-start | bytes 589832 | tf_op jit(solution)/shard_map/ppermute | solution.py:296
  61.5 0.0 collective-permute-start.8
  61.5 0.0 collective-permute-done.9.refs_2_
  61.5 1.9 %collective-permute-start.10 = (bf16[8,24,512]{2,1,0:T(8,128)(2,1)S(1)}, bf16[8,24,512]{2,1,0:T(8,128)(2,1)S(1)}, u32[]{:S(2)}, u32[]{:S(2)}) collective-permute-start(bf16[8,24,512]{2,1,0:T(8,128)(2,1)S(1)} %get-tuple-element.90), channel_id=1, source_target_pairs={{0,16},{4,20},{8,24},{12,28},{16,0},{20,4},{24,8},{28,12},{1,17},{... | collective-permute-start | bytes 589832 | tf_op jit(solution)/shard_map/ppermute | solution.py:296
  63.4 3.3 %attend_inner.1 = (bf16[4,8,512]{2,1,0:T(8,128)(2,1)S(1)}, bf16[4,8,512]{2,1,0:T(8,128)(2,1)S(1)}, bf16[4,8,512]{2,1,0:T(8,128)(2,1)S(1)}, bf16[4,8,512]{2,1,0:T(8,128)(2,1)S(1)}, bf16[4,4,8,512]{3,2,1,0:T(8,128)(2,1)S(1)}) custom-call(bf16[16,8,512]{2,1,0:T(8,128)(2,1)S(1)} %collective-permute-done.5.refs_0_, ...), custom_call_target="tpu_custom_call" | custom-call | flops 1 | bytes 1 | tf_op jit(solution)/shard_map/attend_inner/pallas_call | solution.py:164
  66.7 0.0 copy-start.6
  66.7 2.0 %collective-permute-done.7.refs_0_ = bf16[8,24,512]{2,1,0:T(8,128)(2,1)S(1)} collective-permute-done((bf16[8,24,512]{2,1,0:T(8,128)(2,1)S(1)}, bf16[8,24,512]{2,1,0:T(8,128)(2,1)S(1)}, u32[]{:S(2)}, u32[]{:S(2)}) %collective-permute-start.7) | collective-permute-done | bytes 196640 | tf_op jit(solution)/shard_map/ppermute | solution.py:296
  68.6 4.1 %collective-permute-done.8.refs_1_ = bf16[8,24,512]{2,1,0:T(8,128)(2,1)S(1)} collective-permute-done((bf16[8,24,512]{2,1,0:T(8,128)(2,1)S(1)}, bf16[8,24,512]{2,1,0:T(8,128)(2,1)S(1)}, u32[]{:S(2)}, u32[]{:S(2)}) %collective-permute-start.8) | collective-permute-done | bytes 196640 | tf_op jit(solution)/shard_map/ppermute | solution.py:296
  72.8 3.7 %collective-permute-done.10.refs_2_ = bf16[8,24,512]{2,1,0:T(8,128)(2,1)S(1)} collective-permute-done((bf16[8,24,512]{2,1,0:T(8,128)(2,1)S(1)}, bf16[8,24,512]{2,1,0:T(8,128)(2,1)S(1)}, u32[]{:S(2)}, u32[]{:S(2)}) %collective-permute-start.10) | collective-permute-done | bytes 196640 | tf_op jit(solution)/shard_map/ppermute | solution.py:296
  76.5 0.1 collective-permute-start.11
  76.6 0.5 collective-permute-start.12
  77.1 1.4 %collective-permute-done.12.refs_3_.refs_9_ = bf16[4,4,8,512]{3,2,1,0:T(8,128)(2,1)S(1)} collective-permute-done((bf16[4,4,8,512]{3,2,1,0:T(8,128)(2,1)S(1)}, bf16[4,4,8,512]{3,2,1,0:T(8,128)(2,1)S(1)}, u32[]{:S(2)}, u32[]{:S(2)}) %collective-permute-start.12) | collective-permute-done | bytes 131104 | tf_op jit(solution)/shard_map/ppermute | solution.py:296
  78.5 0.1 collective-permute-start.14
  78.5 1.4 %collective-permute-start.13 = (bf16[2,4,8,512]{3,2,1,0:T(8,128)(2,1)S(1)}, bf16[2,4,8,512]{3,2,1,0:T(8,128)(2,1)S(1)}, u32[]{:S(2)}, u32[]{:S(2)}) collective-permute-start(bf16[2,4,8,512]{3,2,1,0:T(8,128)(2,1)S(1)} %get-tuple-element.96), channel_id=1, source_target_pairs={{0,24},{4,28},{8,16},{12,20},{16,8},{20,12},{24,0},{28,4},{1,25},{... | collective-permute-start | bytes 196616 | tf_op jit(solution)/shard_map/ppermute | solution.py:296
  79.9 2.1 %collective-permute-start.15 = (bf16[2,4,8,512]{3,2,1,0:T(8,128)(2,1)S(1)}, bf16[2,4,8,512]{3,2,1,0:T(8,128)(2,1)S(1)}, u32[]{:S(2)}, u32[]{:S(2)}) collective-permute-start(bf16[2,4,8,512]{3,2,1,0:T(8,128)(2,1)S(1)} %get-tuple-element.101), channel_id=1, source_target_pairs={{0,16},{4,20},{8,24},{12,28},{16,0},{20,4},{24,8},{28,12},{1,17},{... | collective-permute-start | bytes 196616 | tf_op jit(solution)/shard_map/ppermute | solution.py:296
  82.0 0.0 collective-permute-done.11.refs_4_
  82.0 0.1 rim.1
  82.1 0.7 collective-permute-done.14.refs_6_
  82.8 3.4 %collective-permute-start.16 = (bf16[8,4,512]{2,1,0:T(4,128)(2,1)S(1)}, bf16[8,4,512]{2,1,0:T(4,128)(2,1)S(1)}, u32[]{:S(2)}, u32[]{:S(2)}) collective-permute-start(bf16[8,4,512]{2,1,0:T(4,128)(2,1)S(1)} %get-tuple-element.103), channel_id=1, source_target_pairs={{0,1},{1,2},{2,3},{4,5},{5,6},{6,7},{8,9},{9,10},{10,11},{12,13},{... | collective-permute-start | bytes 98312 | tf_op jit(solution)/shard_map/ppermute | solution.py:364
  86.2 1.3 %collective-permute-start.17 = (bf16[8,4,512]{2,1,0:T(4,128)(2,1)S(1)}, bf16[8,4,512]{2,1,0:T(4,128)(2,1)S(1)}, u32[]{:S(2)}, u32[]{:S(2)}) collective-permute-start(bf16[8,4,512]{2,1,0:T(4,128)(2,1)S(1)} %get-tuple-element.104), channel_id=1, source_target_pairs={{1,0},{2,1},{3,2},{5,4},{6,5},{7,6},{9,8},{10,9},{11,10},{13,12},{... | collective-permute-start | bytes 98312 | tf_op jit(solution)/shard_map/ppermute | solution.py:365
  87.5 0.0 collective-permute-done.13.refs_5_
  87.5 0.6 collective-permute-done.15.refs_7_
  88.1 0.0 collective-permute-done.16.refs_10_
  88.1 3.9 %collective-permute-done.17.refs_11_ = bf16[8,4,512]{2,1,0:T(4,128)(2,1)S(1)} collective-permute-done((bf16[8,4,512]{2,1,0:T(4,128)(2,1)S(1)}, bf16[8,4,512]{2,1,0:T(4,128)(2,1)S(1)}, u32[]{:S(2)}, u32[]{:S(2)}) %collective-permute-start.17) | collective-permute-done | bytes 32800 | tf_op jit(solution)/shard_map/ppermute | solution.py:365
  92.0 0.0 copy-done.6
  92.0 2.4 %depth_filter.1 = bf16[4,8,32,512]{3,2,1,0:T(8,128)(2,1)} custom-call(bf16[8,24,512]{2,1,0:T(8,128)(2,1)S(1)} %collective-permute-done.7.refs_0_, bf16[8,24,512]{2,1,0:T(8,128)(2,1)S(1)} %collective-permute-done.8.refs_1_, bf16[8,24,512]{2,1,0:T(8,128)(2,1)S(1)} %collective-permute-done.10.refs_2_, bf16[8,24,512]{2,1,0:T(8,128)(2,1)S(1)} %get-tuple-element.91.refs_3_, ...), custom_call_target="tpu_custom_call" | custom-call | flops 1 | bytes 1 | tf_op jit(solution)/shard_map/depth_filter/pallas_call | solution.py:270
  (3 shorter events, 0.1 us)
Async XLA Ops:
  0.0 49.7 %copy-start = (bf16[3,512,512]{2,1,0:T(8,128)(2,1)S(1)}, bf16[3,512,512]{2,1,0:T(8,128)(2,1)}, u32[]{:S(2)}) copy-start(bf16[3,512,512]{2,1,0:T(8,128)(2,1)} %refs_10_.3) | copy-start | bytes 4718596
  0.0 1.7 %copy-start.1 = (bf16[8,8,32,512]{3,2,1,0:T(8,128)(2,1)S(1)}, bf16[8,8,32,512]{3,2,1,0:T(8,128)(2,1)}, u32[]{:S(2)}) copy-start(bf16[8,8,32,512]{3,2,1,0:T(8,128)(2,1)} %video.1) | copy-start | bytes 6291460
  1.7 48.0 %copy-start.2 = (bf16[512,512]{1,0:T(8,128)(2,1)S(1)}, bf16[512,512]{1,0:T(8,128)(2,1)}, u32[]{:S(2)}) copy-start(bf16[512,512]{1,0:T(8,128)(2,1)} %refs_6_.3) | copy-start | bytes 1572868
  1.7 48.0 %copy-start.3 = (bf16[512,512]{1,0:T(8,128)(2,1)S(1)}, bf16[512,512]{1,0:T(8,128)(2,1)}, u32[]{:S(2)}) copy-start(bf16[512,512]{1,0:T(8,128)(2,1)} %refs_7_.3) | copy-start | bytes 1572868
  1.7 48.0 %copy-start.4 = (bf16[512,512]{1,0:T(8,128)(2,1)S(1)}, bf16[512,512]{1,0:T(8,128)(2,1)}, u32[]{:S(2)}) copy-start(bf16[512,512]{1,0:T(8,128)(2,1)} %refs_8_.3) | copy-start | bytes 1572868
  1.7 48.0 %copy-start.5 = (bf16[512,512]{1,0:T(8,128)(2,1)S(1)}, bf16[512,512]{1,0:T(8,128)(2,1)}, u32[]{:S(2)}) copy-start(bf16[512,512]{1,0:T(8,128)(2,1)} %refs_9_.3) | copy-start | bytes 1572868
  1.7 48.0 %copy-start.7 = (f32[512]{0:T(512)S(1)}, f32[512]{0:T(512)}, u32[]{:S(2)}) copy-start(f32[512]{0:T(512)} %param.9) | copy-start | bytes 6148
  1.9 2.4 %collective-permute-start = (bf16[4,8,24,512]{3,2,1,0:T(8,128)(2,1)S(1)}, bf16[4,8,24,512]{3,2,1,0:T(8,128)(2,1)S(1)}, u32[]{:S(2)}, u32[]{:S(2)}) collective-permute-start(bf16[4,8,24,512]{3,2,1,0:T(8,128)(2,1)S(1)} %get-tuple-element.58), channel_id=1, source_target_pairs={{0,4},{4,0},{8,12},{12,8},{16,20},{20,16},{24,28},{28,24},{1,5},{5... | collective-permute-start | bytes 2359304 | tf_op jit(solution)/shard_map/ppermute | solution.py:296
  4.4 15.0 %collective-permute-start.1 = (bf16[16,24,512]{2,1,0:T(8,128)(2,1)S(1)}, bf16[16,24,512]{2,1,0:T(8,128)(2,1)S(1)}, u32[]{:S(2)}, u32[]{:S(2)}) collective-permute-start(bf16[16,24,512]{2,1,0:T(8,128)(2,1)S(1)} %get-tuple-element.63), channel_id=1, source_target_pairs={{0,24},{4,28},{8,16},{12,20},{16,8},{20,12},{24,0},{28,4},{1,25},{... | collective-permute-start | bytes 1179656 | tf_op jit(solution)/shard_map/ppermute | solution.py:296
  9.4 1.5 %collective-permute-start.2 = (bf16[4,8,8,512]{3,2,1,0:T(8,128)(2,1)S(1)}, bf16[4,8,8,512]{3,2,1,0:T(8,128)(2,1)S(1)}, u32[]{:S(2)}, u32[]{:S(2)}) collective-permute-start(bf16[4,8,8,512]{3,2,1,0:T(8,128)(2,1)S(1)} %get-tuple-element.67), channel_id=1, source_target_pairs={{0,4},{4,0},{8,12},{12,8},{16,20},{20,16},{24,28},{28,24},{1,5},{5... | collective-permute-start | bytes 786440 | tf_op jit(solution)/shard_map/ppermute | solution.py:296
  9.4 20.2 %collective-permute-start.3 = (bf16[16,24,512]{2,1,0:T(8,128)(2,1)S(1)}, bf16[16,24,512]{2,1,0:T(8,128)(2,1)S(1)}, u32[]{:S(2)}, u32[]{:S(2)}) collective-permute-start(bf16[16,24,512]{2,1,0:T(8,128)(2,1)S(1)} %get-tuple-element.72), channel_id=1, source_target_pairs={{0,8},{4,12},{8,0},{12,4},{16,24},{20,28},{24,16},{28,20},{1,9},{5... | collective-permute-start | bytes 1179656 | tf_op jit(solution)/shard_map/ppermute | solution.py:296
  9.4 40.3 %collective-permute-start.4 = (bf16[16,24,512]{2,1,0:T(8,128)(2,1)S(1)}, bf16[16,24,512]{2,1,0:T(8,128)(2,1)S(1)}, u32[]{:S(2)}, u32[]{:S(2)}) collective-permute-start(bf16[16,24,512]{2,1,0:T(8,128)(2,1)S(1)} %get-tuple-element.73), channel_id=1, source_target_pairs={{0,16},{4,20},{8,24},{12,28},{16,0},{20,4},{24,8},{28,12},{1,17},{... | collective-permute-start | bytes 1179656 | tf_op jit(solution)/shard_map/ppermute | solution.py:296
  19.4 39.5 %collective-permute-start.5 = (bf16[16,8,512]{2,1,0:T(8,128)(2,1)S(1)}, bf16[16,8,512]{2,1,0:T(8,128)(2,1)S(1)}, u32[]{:S(2)}, u32[]{:S(2)}) collective-permute-start(bf16[16,8,512]{2,1,0:T(8,128)(2,1)S(1)} %get-tuple-element.77), channel_id=1, source_target_pairs={{0,24},{4,28},{8,16},{12,20},{16,8},{20,12},{24,0},{28,4},{1,25},{... | collective-permute-start | bytes 393224 | tf_op jit(solution)/shard_map/ppermute | solution.py:296
  23.2 35.7 %collective-permute-start.6 = (bf16[16,8,512]{2,1,0:T(8,128)(2,1)S(1)}, bf16[16,8,512]{2,1,0:T(8,128)(2,1)S(1)}, u32[]{:S(2)}, u32[]{:S(2)}) collective-permute-start(bf16[16,8,512]{2,1,0:T(8,128)(2,1)S(1)} %get-tuple-element.78), channel_id=1, source_target_pairs={{0,8},{4,12},{8,0},{12,4},{16,24},{20,28},{24,16},{28,20},{1,9},{5... | collective-permute-start | bytes 393224 | tf_op jit(solution)/shard_map/ppermute | solution.py:296
  29.4 32.1 %collective-permute-start.9 = (bf16[16,8,512]{2,1,0:T(8,128)(2,1)S(1)}, bf16[16,8,512]{2,1,0:T(8,128)(2,1)S(1)}, u32[]{:S(2)}, u32[]{:S(2)}) collective-permute-start(bf16[16,8,512]{2,1,0:T(8,128)(2,1)S(1)} %get-tuple-element.84), channel_id=1, source_target_pairs={{0,16},{4,20},{8,24},{12,28},{16,0},{20,4},{24,8},{28,12},{1,17},{... | collective-permute-start | bytes 393224 | tf_op jit(solution)/shard_map/ppermute | solution.py:296
  58.9 9.7 %collective-permute-start.7 = (bf16[8,24,512]{2,1,0:T(8,128)(2,1)S(1)}, bf16[8,24,512]{2,1,0:T(8,128)(2,1)S(1)}, u32[]{:S(2)}, u32[]{:S(2)}) collective-permute-start(bf16[8,24,512]{2,1,0:T(8,128)(2,1)S(1)} %get-tuple-element.79), channel_id=1, source_target_pairs={{0,24},{4,28},{8,16},{12,20},{16,8},{20,12},{24,0},{28,4},{1,25},{... | collective-permute-start | bytes 589832 | tf_op jit(solution)/shard_map/ppermute | solution.py:296
  61.5 11.3 %collective-permute-start.8 = (bf16[8,24,512]{2,1,0:T(8,128)(2,1)S(1)}, bf16[8,24,512]{2,1,0:T(8,128)(2,1)S(1)}, u32[]{:S(2)}, u32[]{:S(2)}) collective-permute-start(bf16[8,24,512]{2,1,0:T(8,128)(2,1)S(1)} %get-tuple-element.80), channel_id=1, source_target_pairs={{0,8},{4,12},{8,0},{12,4},{16,24},{20,28},{24,16},{28,20},{1,9},{5... | collective-permute-start | bytes 589832 | tf_op jit(solution)/shard_map/ppermute | solution.py:296
  61.5 15.0 %collective-permute-start.10 = (bf16[8,24,512]{2,1,0:T(8,128)(2,1)S(1)}, bf16[8,24,512]{2,1,0:T(8,128)(2,1)S(1)}, u32[]{:S(2)}, u32[]{:S(2)}) collective-permute-start(bf16[8,24,512]{2,1,0:T(8,128)(2,1)S(1)} %get-tuple-element.90), channel_id=1, source_target_pairs={{0,16},{4,20},{8,24},{12,28},{16,0},{20,4},{24,8},{28,12},{1,17},{... | collective-permute-start | bytes 589832 | tf_op jit(solution)/shard_map/ppermute | solution.py:296
  66.7 25.3 %copy-start.6 = (f32[3,3,512]{2,1,0:T(4,128)S(1)}, f32[3,3,512]{2,1,0:T(4,128)}, u32[]{:S(2)}) copy-start(f32[3,3,512]{2,1,0:T(4,128)} %refs_12_.1) | copy-start | bytes 55300
  76.5 5.6 %collective-permute-start.11 = (bf16[4,4,24,512]{3,2,1,0:T(8,128)(2,1)S(1)}, bf16[4,4,24,512]{3,2,1,0:T(8,128)(2,1)S(1)}, u32[]{:S(2)}, u32[]{:S(2)}) collective-permute-start(bf16[4,4,24,512]{3,2,1,0:T(8,128)(2,1)S(1)} %stack_back.1), channel_id=1, source_target_pairs={{0,4},{4,0},{8,12},{12,8},{16,20},{20,16},{24,28},{28,24},{1,5},{5... | collective-permute-start | bytes 1179656 | tf_op jit(solution)/shard_map/ppermute | solution.py:296
  76.6 1.9 %collective-permute-start.12 = (bf16[4,4,8,512]{3,2,1,0:T(8,128)(2,1)S(1)}, bf16[4,4,8,512]{3,2,1,0:T(8,128)(2,1)S(1)}, u32[]{:S(2)}, u32[]{:S(2)}) collective-permute-start(bf16[4,4,8,512]{3,2,1,0:T(8,128)(2,1)S(1)} %get-tuple-element.95), channel_id=1, source_target_pairs={{0,4},{4,0},{8,12},{12,8},{16,20},{20,16},{24,28},{28,24},{1,5},{5... | collective-permute-start | bytes 393224 | tf_op jit(solution)/shard_map/ppermute | solution.py:296
  78.5 4.3 %collective-permute-start.14 = (bf16[2,4,8,512]{3,2,1,0:T(8,128)(2,1)S(1)}, bf16[2,4,8,512]{3,2,1,0:T(8,128)(2,1)S(1)}, u32[]{:S(2)}, u32[]{:S(2)}) collective-permute-start(bf16[2,4,8,512]{3,2,1,0:T(8,128)(2,1)S(1)} %get-tuple-element.99), channel_id=1, source_target_pairs={{0,8},{4,12},{8,0},{12,4},{16,24},{20,28},{24,16},{28,20},{1,9},{5... | collective-permute-start | bytes 196616 | tf_op jit(solution)/shard_map/ppermute | solution.py:296
  78.5 9.0 %collective-permute-start.13 = (bf16[2,4,8,512]{3,2,1,0:T(8,128)(2,1)S(1)}, bf16[2,4,8,512]{3,2,1,0:T(8,128)(2,1)S(1)}, u32[]{:S(2)}, u32[]{:S(2)}) collective-permute-start(bf16[2,4,8,512]{3,2,1,0:T(8,128)(2,1)S(1)} %get-tuple-element.96), channel_id=1, source_target_pairs={{0,24},{4,28},{8,16},{12,20},{16,8},{20,12},{24,0},{28,4},{1,25},{... | collective-permute-start | bytes 196616 | tf_op jit(solution)/shard_map/ppermute | solution.py:296
  79.9 8.1 %collective-permute-start.15 = (bf16[2,4,8,512]{3,2,1,0:T(8,128)(2,1)S(1)}, bf16[2,4,8,512]{3,2,1,0:T(8,128)(2,1)S(1)}, u32[]{:S(2)}, u32[]{:S(2)}) collective-permute-start(bf16[2,4,8,512]{3,2,1,0:T(8,128)(2,1)S(1)} %get-tuple-element.101), channel_id=1, source_target_pairs={{0,16},{4,20},{8,24},{12,28},{16,0},{20,4},{24,8},{28,12},{1,17},{... | collective-permute-start | bytes 196616 | tf_op jit(solution)/shard_map/ppermute | solution.py:296
  82.8 5.3 %collective-permute-start.16 = (bf16[8,4,512]{2,1,0:T(4,128)(2,1)S(1)}, bf16[8,4,512]{2,1,0:T(4,128)(2,1)S(1)}, u32[]{:S(2)}, u32[]{:S(2)}) collective-permute-start(bf16[8,4,512]{2,1,0:T(4,128)(2,1)S(1)} %get-tuple-element.103), channel_id=1, source_target_pairs={{0,1},{1,2},{2,3},{4,5},{5,6},{6,7},{8,9},{9,10},{10,11},{12,13},{... | collective-permute-start | bytes 98312 | tf_op jit(solution)/shard_map/ppermute | solution.py:364
  86.2 5.8 %collective-permute-start.17 = (bf16[8,4,512]{2,1,0:T(4,128)(2,1)S(1)}, bf16[8,4,512]{2,1,0:T(4,128)(2,1)S(1)}, u32[]{:S(2)}, u32[]{:S(2)}) collective-permute-start(bf16[8,4,512]{2,1,0:T(4,128)(2,1)S(1)} %get-tuple-element.104), channel_id=1, source_target_pairs={{1,0},{2,1},{3,2},{5,4},{6,5},{7,6},{9,8},{10,9},{11,10},{13,12},{... | collective-permute-start | bytes 98312 | tf_op jit(solution)/shard_map/ppermute | solution.py:365

commit v10 on v8

--- a/solution.py
+++ b/solution.py
@@ -72,23 +72,72 @@
     )(video)
 
 
-def attend_frames(pieces, gain, bias, weights, normed, projected, attended, mixed):
+def groups_of(piece):
+    wide = piece[...].astype(jnp.float32)
+    return [wide[:, begin : begin + GROUP] for begin in range(0, wide.shape[1], GROUP)]
+
+
+def normalized(x, gain):
+    x = x.reshape(-1, x.shape[-1])
+    x = x * lax.rsqrt(jnp.mean(x * x, axis=-1, keepdims=True) + epsilon) * gain
+    return x.astype(jnp.bfloat16)
+
+
+def project_kernel(inward, n_early, n_in, *refs):
+    gain, w_query, w_key, w_value, out, normed = refs[n_in:]
+    at = 0
+    for piece, _ in inward(refs[:n_in])[:n_early]:
+        for x in groups_of(piece):
+            count = x.shape[0] * GROUP
+            normed[at : at + count] = normalized(x, gain[...])
+            at += count
+    for index, weight in enumerate((w_query, w_key, w_value)):
+        out[index] = jnp.dot(normed[...], weight[...], preferred_element_type=jnp.float32).astype(jnp.bfloat16)
+
+
+def project(inward, n_early, pieces, weights, span):
+    cols, channels = pieces[0].shape[-2:]
+    rows = n_early * span * cols
+    norm_gain, *matrices = weights
+    return pl.pallas_call(
+        functools.partial(project_kernel, inward, n_early, len(pieces)),
+        out_shape=jax.ShapeDtypeStruct((3, rows, channels), jnp.bfloat16),
+        in_specs=[INSIDE] * (len(pieces) + 4),
+        out_specs=INSIDE,
+        scratch_shapes=[pltpu.VMEM((rows, channels), jnp.bfloat16)],
+        compiler_params=pltpu.CompilerParams(vmem_limit_bytes=20 * MIB),
+        cost_estimate=pl.CostEstimate(
+            flops=6 * rows * channels * channels, bytes_accessed=8 * rows * channels, transcendentals=0
+        ),
+        name="project_early",
+    )(*pieces, norm_gain[None], *matrices[:3])
+
+
+def attend_frames(pieces, early, n_early, gain, bias, weights, normed, projected, attended, mixed):
     w_query, w_key, w_value, w_out, w_time = weights
     groups, frames, _, channels = mixed.shape
     frames = frames - 2
     rows = frames * GROUP
-    for piece, first in pieces:
-        wide = piece[...].astype(jnp.float32)
-        span = wide.shape[0]
-        for group in range(groups):
-            x = wide[:, group * GROUP : (group + 1) * GROUP]
+    places = []
+    at = 0
+    for number, (piece, first) in enumerate(pieces):
+        if number == n_early:
+            at = 0
+        for group, x in enumerate(groups_of(piece)):
+            span = x.shape[0]
+            count = span * GROUP
             mixed[group, pl.ds(first + 1, span)] = x
-            x = x.reshape(span * GROUP, channels)
-            x = x * lax.rsqrt(jnp.mean(x * x, axis=-1, keepdims=True) + epsilon) * gain
-            begin = pl.multiple_of(group * rows + first * GROUP, span * GROUP)
-            normed[pl.ds(begin, span * GROUP)] = x.astype(jnp.bfloat16)
+            begin = pl.multiple_of(group * rows + first * GROUP, count)
+            if number < n_early:
+                projected[:, pl.ds(begin, count)] = early[:, at : at + count]
+            else:
+                normed[at : at + count] = normalized(x, gain)
+                places.append((begin, at, count))
+            at += count
     for index, weight in enumerate((w_query, w_key, w_value)):
-        projected[index] = jnp.dot(normed[...], weight[...], preferred_element_type=jnp.float32).astype(jnp.bfloat16)
+        result = jnp.dot(normed[...], weight[...], preferred_element_type=jnp.float32).astype(jnp.bfloat16)
+        for begin, at, count in places:
+            projected[index, pl.ds(begin, count)] = result[at : at + count]
     queries, key_proj, values = projected.at[0], projected.at[1], projected.at[2]
     height = rows // BLOCKS
     power = math.log2(math.e) / math.sqrt(channels)
@@ -132,14 +181,16 @@
     return (summed / (1.0 + jnp.exp(-summed))).reshape(groups, frames // 2, GROUP, channels)
 
 
-def attend_kernel(inward, hops, paired, n_in, *refs):
+def attend_kernel(inward, hops, paired, n_early, n_in, *refs):
     gain, *weights = refs[n_in : n_in + 6]
-    *results, done, bias, normed, projected, attended, mixed = refs[n_in + 6 :]
+    early = refs[n_in + 6] if n_early else None
+    *results, done, bias, normed, projected, attended, mixed = refs[n_in + 6 + (n_early > 0) :]
     to_row = lax.broadcasted_iota(jnp.int32, bias.shape, 0)
     from_row = lax.broadcasted_iota(jnp.int32, bias.shape, 1)
     allowed = (from_row <= to_row) & (((from_row ^ to_row) & (GROUP - 1)) == 0)
     bias[...] = jnp.where(allowed, 0.0, -1e30)
-    made = attend_frames(inward(refs[:n_in]), gain[...], bias, weights, normed, projected, attended, mixed)
+    pieces = inward(refs[:n_in])
+    made = attend_frames(pieces, early, n_early, gain[...], bias, weights, normed, projected, attended, mixed)
     done[...] = jnp.concatenate([made[g] for g in range(made.shape[0])], axis=1).astype(jnp.bfloat16)
     me = lax.axis_index("frm")
     for i, (hop, result) in enumerate(zip(hops, results)):
@@ -151,7 +202,7 @@
             results[-1][i] = done[pl.ds((me ^ hop ^ 1) * span, span)]
 
 
-def attend(inward, hops, paired, pieces, weights, frames, name):
+def attend(inward, hops, paired, pieces, weights, frames, name, n_early=0, early=()):
     cols, channels = pieces[0].shape[-2:]
     rows = frames * cols
     made = frames // 2
@@ -161,14 +212,14 @@
         shapes.append((len(hops), size, cols, channels))
     norm_gain, *matrices = weights
     return pl.pallas_call(
-        functools.partial(attend_kernel, inward, hops, paired, len(pieces)),
+        functools.partial(attend_kernel, inward, hops, paired, n_early, len(pieces)),
         out_shape=[jax.ShapeDtypeStruct(shape, jnp.bfloat16) for shape in shapes],
-        in_specs=[INSIDE] * (len(pieces) + 6),
+        in_specs=[INSIDE] * (len(pieces) + 6 + len(early)),
         out_specs=[INSIDE] * len(shapes),
         scratch_shapes=[
             pltpu.VMEM((made, cols, channels), jnp.bfloat16),
             pltpu.VMEM((frames * GROUP, frames * GROUP), jnp.float32),
-            pltpu.VMEM((rows, channels), jnp.bfloat16),
+            pltpu.VMEM((rows - rows * n_early // (2 * len(hops)), channels), jnp.bfloat16),
             pltpu.VMEM((3, rows, channels), jnp.bfloat16),
             pltpu.VMEM((rows, channels), jnp.bfloat16),
             pltpu.VMEM((cols // GROUP, frames + 2, GROUP, channels), jnp.float32),
@@ -176,7 +227,7 @@
         compiler_params=pltpu.CompilerParams(vmem_limit_bytes=24 * MIB),
         cost_estimate=SMALL,
         name=name,
-    )(*pieces, norm_gain[None], *matrices)
+    )(*pieces, norm_gain[None], *matrices, *early)
 
 
 def outer_rows(hops, pieces, taken):
@@ -322,21 +373,36 @@
     outer_far[0], *inner_far = lax.optimization_barrier((outer_far[0], *inner_far))
     inner_far = [swap(piece, k) for k, piece in zip(hops, inner_far)]
 
+    late = list(range(2, len(far))) or [len(far) - 1]
+    soon = [i for i in range(len(far)) if i not in late]
+    n_early = 2 * len(soon) + 2
+
     def inward(pieces):
         me = lax.axis_index("frm")
         *pieces, own, other = pieces
-        pairs = []
-        for k, piece in zip(hops, pieces):
-            pairs.append((piece.at[pl.ds(0, span)], (me ^ k) * span))
-            pairs.append((piece.at[pl.ds(span, span)], (me ^ k ^ 1) * span))
-        return pairs + [(own, me * span), (other.at[len(far)], (me ^ 1) * span)]
+
+        def halves(numbers):
+            return [
+                (pieces[i].at[pl.ds(j * span, span)], (me ^ hops[i] ^ j) * span) for i in numbers for j in range(2)
+            ]
+
+        return [(own, me * span), (other.at[len(far)], (me ^ 1) * span), *halves(soon), *halves(late)]
+
+    def inward_soon(pieces):
+        *pieces, own, other = pieces
+        blocks = [pieces[i].at[pl.ds(j * span, span)] for i in range(len(soon)) for j in range(2)]
+        return [(block, None) for block in [own, other.at[len(far)], *blocks]]
 
     outer = list(attend(inward, hops, True, [*outer_far, outer[-1], outer_other], weights, frames, "attend_outer"))
-    outer[:2], inner_far[0] = lax.optimization_barrier((outer[:2], inner_far[0]))
+    near = [inner[-1], inner_other]
+    early = project(inward_soon, n_early, [*[inner_far[i] for i in soon], *near], weights, span)
+    outer[:2], early = lax.optimization_barrier((outer[:2], early))
     for i in range(2, len(far)):
         outer[i], inner_far[i] = lax.optimization_barrier((outer[i], inner_far[i]))
     outer = [swap(piece, k) for k, piece in zip(hops, outer)]
-    *keep, give = attend(inward, hops, False, [*inner_far, inner[-1], inner_other], weights, frames, "attend_inner")
+    *keep, give = attend(
+        inward, hops, False, [*inner_far, *near], weights, frames, "attend_inner", n_early, [early]
+    )
 
     outer[:2], give = lax.optimization_barrier((outer[:2], give))
     taken = swap(give, 1)

time: 85.1 us -> 84.2 us (0.989)
  waiting for transfers between devices: 42.5 us -> 36.5 us
  starting transfers between devices: 25.4 us -> 30.6 us
    ppermute x16, waiting for transfers between devices: 42.5 us -> 36.4 us  [swap(): lax.ppermute(block, 'frm', [(i, i ^ k) for i in range(count)])]
    ppermute x16, starting transfers between devices: 20.7 us -> 25.9 us  [swap(): lax.ppermute(block, 'frm', [(i, i ^ k) for i in range(count)])]
    pallas_call x2 -> x3, Pallas kernels: 12.3 us -> 12.3 us  [the longest x2 10.8 us: attend(): pl.pallas_call(functools.partial(attend_kernel, inward, hops, paired, n_e...]
where the time goes in v10:
time: 84.2 us; the launch traced here: 84 us
  waiting for transfers between devices  36.5 us (43%)
  starting transfers between devices  30.6 us (36%)
  Pallas kernels  15.1 us (18%)
  local copies, waits for them, and re-layouts  1.76 us (2%)
    ppermute x16, waiting for transfers between devices, swap(): lax.ppermute(block, 'frm', [(i, i ^ k) for i in range(count)])  36.4 us
    ppermute x16, starting transfers between devices, swap(): lax.ppermute(block, 'frm', [(i, i ^ k) for i in range(count)])  25.9 us
    pallas_call x2, Pallas kernels, attend(): pl.pallas_call(functools.partial(attend_kernel, inward, hops, paired, n_e...  10.8 us
    ppermute x1, starting transfers between devices, local(): left = lax.ppermute(high_side, 'col', upward)  3.39 us
    pallas_call x1, Pallas kernels, depth_filter(): pl.pallas_call(functools.partial(filter_kernel, hops), out_shape=jax.Shap...  2.38 us
    unnamed x16, local copies, waits for them, and re-layouts  1.76 us
  transfers between devices with their start and end apart: 18, of which 7 were waited for; matrix products, arithmetic and copies ran while one was open for 0% of the time, Pallas kernels for 15%

profile of v10, /device:TPU:0, one launch (start us, length us, event | category | flops | bytes accessed | tf_op | source)
XLA Modules:
  0.0 84.0 jit_solution(7506261642480520315)
XLA Ops:
  0.0 0.0 copy-start.3
  0.0 0.0 copy-start.2
  0.0 0.0 copy-start.1
  0.0 0.0 copy-start
  0.0 0.0 copy-start.4
  0.0 0.0 copy-start.5
  0.0 1.7 %copy-done.5 = bf16[8,8,32,512]{3,2,1,0:T(8,128)(2,1)S(1)} copy-done((bf16[8,8,32,512]{3,2,1,0:T(8,128)(2,1)S(1)}, bf16[8,8,32,512]{3,2,1,0:T(8,128)(2,1)}, u32[]{:S(2)}) %copy-start.5) | copy-done | bytes 2097176
  1.8 0.0 copy-start.7
  1.8 0.1 cut.1
  1.9 0.5 collective-permute-start
  2.4 1.5 %collective-permute-done.refs_3_.refs_4_ = bf16[4,8,16,512]{3,2,1,0:T(8,128)(2,1)S(1)} collective-permute-done((bf16[4,8,16,512]{3,2,1,0:T(8,128)(2,1)S(1)}, bf16[4,8,16,512]{3,2,1,0:T(8,128)(2,1)S(1)}, u32[]{:S(2)}, u32[]{:S(2)}) %collective-permute-start) | collective-permute-done | bytes 524320 | tf_op jit(solution)/shard_map/ppermute | solution.py:347
  4.0 0.1 join_outer.1
  4.0 0.4 collective-permute-start.2
  4.5 4.7 %collective-permute-start.1 = (bf16[16,16,512]{2,1,0:T(8,128)(2,1)S(1)}, bf16[16,16,512]{2,1,0:T(8,128)(2,1)S(1)}, u32[]{:S(2)}, u32[]{:S(2)}) collective-permute-start(bf16[16,16,512]{2,1,0:T(8,128)(2,1)S(1)} %get-tuple-element.62), channel_id=1, source_target_pairs={{0,24},{4,28},{8,16},{12,20},{16,8},{20,12},{24,0},{28,4},{1,25},{... | collective-permute-start | bytes 786440 | tf_op jit(solution)/shard_map/ppermute | solution.py:347
  9.2 0.0 collective-permute-start.3
  9.2 0.6 collective-permute-start.4
  9.8 0.0 collective-permute-done.2.refs_3_.refs_4_
  9.8 0.1 join_inner.1
  9.8 6.6 %collective-permute-done.1.refs_0_ = bf16[16,16,512]{2,1,0:T(8,128)(2,1)S(1)} collective-permute-done((bf16[16,16,512]{2,1,0:T(8,128)(2,1)S(1)}, bf16[16,16,512]{2,1,0:T(8,128)(2,1)S(1)}, u32[]{:S(2)}, u32[]{:S(2)}) %collective-permute-start.1) | collective-permute-done | bytes 262176 | tf_op jit(solution)/shard_map/ppermute | solution.py:347
  16.4 3.7 %collective-permute-start.5 = (bf16[16,16,512]{2,1,0:T(8,128)(2,1)S(1)}, bf16[16,16,512]{2,1,0:T(8,128)(2,1)S(1)}, u32[]{:S(2)}, u32[]{:S(2)}) collective-permute-start(bf16[16,16,512]{2,1,0:T(8,128)(2,1)S(1)} %get-tuple-element.76), channel_id=1, source_target_pairs={{0,24},{4,28},{8,16},{12,20},{16,8},{20,12},{24,0},{28,4},{1,25},{... | collective-permute-start | bytes 786440 | tf_op jit(solution)/shard_map/ppermute | solution.py:347
  20.2 3.3 %collective-permute-start.6 = (bf16[16,16,512]{2,1,0:T(8,128)(2,1)S(1)}, bf16[16,16,512]{2,1,0:T(8,128)(2,1)S(1)}, u32[]{:S(2)}, u32[]{:S(2)}) collective-permute-start(bf16[16,16,512]{2,1,0:T(8,128)(2,1)S(1)} %get-tuple-element.77), channel_id=1, source_target_pairs={{0,8},{4,12},{8,0},{12,4},{16,24},{20,28},{24,16},{28,20},{1,9},{5... | collective-permute-start | bytes 786440 | tf_op jit(solution)/shard_map/ppermute | solution.py:347
  23.5 0.0 collective-permute-start.9
  23.5 0.0 collective-permute-done.3.refs_1_
  23.5 14.8 %collective-permute-done.4.refs_2_ = bf16[16,16,512]{2,1,0:T(8,128)(2,1)S(1)} collective-permute-done((bf16[16,16,512]{2,1,0:T(8,128)(2,1)S(1)}, bf16[16,16,512]{2,1,0:T(8,128)(2,1)S(1)}, u32[]{:S(2)}, u32[]{:S(2)}) %collective-permute-start.4) | collective-permute-done | bytes 262176 | tf_op jit(solution)/shard_map/ppermute | solution.py:347
  38.3 0.0 copy-done.3
  38.3 0.0 copy-done.2
  38.3 0.0 copy-done.1
  38.3 0.0 copy-done
  38.3 0.0 copy-done.4
  38.3 0.0 copy-done.7
  38.3 5.9 %attend_outer.1 = (bf16[8,16,512]{2,1,0:T(8,128)(2,1)S(1)}, bf16[8,16,512]{2,1,0:T(8,128)(2,1)S(1)}, bf16[8,16,512]{2,1,0:T(8,128)(2,1)S(1)}, bf16[8,16,512]{2,1,0:T(8,128)(2,1)S(1)}) custom-call(bf16[16,16,512]{2,1,0:T(8,128)(2,1)S(1)} %collective-permute-done.1.refs_0_, bf16[16,16,512]{2,1,0:T(8,128)(2,1)S(1)} %collective-permute-done.3.refs_1_, ...), custom_call_target="tpu_custom_call" | custom-call | flops 1 | bytes 1 | tf_op jit(solution)/shard_map/attend_outer/pallas_call | solution.py:214
  44.3 0.0 collective-permute-done.5.refs_0_
  44.3 0.0 collective-permute-done.6.refs_1_
  44.3 1.5 %project_early.1.refs_11_ = bf16[3,768,512]{2,1,0:T(8,128)(2,1)S(1)} custom-call(bf16[16,16,512]{2,1,0:T(8,128)(2,1)S(1)} %collective-permute-done.5.refs_0_, bf16[16,16,512]{2,1,0:T(8,128)(2,1)S(1)} %collective-permute-done.6.refs_1_, bf16[8,16,512]{2,1,0:T(8,128)(2,1)S(1)} %get-tuple-element.78.refs_2_.refs_3_, ...), custom_call_target="tpu_custom_call" | custom-call | flops 1207959552 | bytes 3145728 | tf_op jit(solution)/shard_map/project_early/pallas_call | solution.py:102
  45.8 2.5 %collective-permute-start.7 = (bf16[8,16,512]{2,1,0:T(8,128)(2,1)S(1)}, bf16[8,16,512]{2,1,0:T(8,128)(2,1)S(1)}, u32[]{:S(2)}, u32[]{:S(2)}) collective-permute-start(bf16[8,16,512]{2,1,0:T(8,128)(2,1)S(1)} %get-tuple-element.79), channel_id=1, source_target_pairs={{0,24},{4,28},{8,16},{12,20},{16,8},{20,12},{24,0},{28,4},{1,25},{... | collective-permute-start | bytes 393224 | tf_op jit(solution)/shard_map/ppermute | solution.py:347
  48.3 6.3 %collective-permute-start.8 = (bf16[8,16,512]{2,1,0:T(8,128)(2,1)S(1)}, bf16[8,16,512]{2,1,0:T(8,128)(2,1)S(1)}, u32[]{:S(2)}, u32[]{:S(2)}) collective-permute-start(bf16[8,16,512]{2,1,0:T(8,128)(2,1)S(1)} %get-tuple-element.80), channel_id=1, source_target_pairs={{0,8},{4,12},{8,0},{12,4},{16,24},{20,28},{24,16},{28,20},{1,9},{5... | collective-permute-start | bytes 393224 | tf_op jit(solution)/shard_map/ppermute | solution.py:347
  54.6 3.4 %collective-permute-done.9.refs_2_ = bf16[16,16,512]{2,1,0:T(8,128)(2,1)S(1)} collective-permute-done((bf16[16,16,512]{2,1,0:T(8,128)(2,1)S(1)}, bf16[16,16,512]{2,1,0:T(8,128)(2,1)S(1)}, u32[]{:S(2)}, u32[]{:S(2)}) %collective-permute-start.9) | collective-permute-done | bytes 262176 | tf_op jit(solution)/shard_map/ppermute | solution.py:347
  58.0 0.0 copy-start.6
  58.0 0.0 collective-permute-start.10
  58.0 4.8 %attend_inner.1 = (bf16[4,16,512]{2,1,0:T(8,128)(2,1)S(1)}, bf16[4,16,512]{2,1,0:T(8,128)(2,1)S(1)}, bf16[4,16,512]{2,1,0:T(8,128)(2,1)S(1)}, bf16[4,16,512]{2,1,0:T(8,128)(2,1)S(1)}, bf16[4,4,16,512]{3,2,1,0:T(8,128)(2,1)S(1)}) custom-call(bf16[16,16,512]{2,1,0:T(8,128)(2,1)S(1)} %collective-permute-done.5.refs_0_, ...), custom_call_target="tpu_custom_call" | custom-call | flops 1 | bytes 1 | tf_op jit(solution)/shard_map/attend_inner/pallas_call | solution.py:214
  62.8 0.0 collective-permute-done.7.refs_0_
  62.8 0.0 collective-permute-done.8.refs_1_
  62.8 0.1 collective-permute-start.12
  62.9 3.0 %collective-permute-done.10.refs_2_ = bf16[8,16,512]{2,1,0:T(8,128)(2,1)S(1)} collective-permute-done((bf16[8,16,512]{2,1,0:T(8,128)(2,1)S(1)}, bf16[8,16,512]{2,1,0:T(8,128)(2,1)S(1)}, u32[]{:S(2)}, u32[]{:S(2)}) %collective-permute-start.10) | collective-permute-done | bytes 131104 | tf_op jit(solution)/shard_map/ppermute | solution.py:347
  65.9 0.1 collective-permute-start.11
  66.0 0.0 collective-permute-done.12.refs_3_.refs_9_
  66.1 1.5 %collective-permute-start.14 = (bf16[2,4,16,512]{3,2,1,0:T(8,128)(2,1)S(1)}, bf16[2,4,16,512]{3,2,1,0:T(8,128)(2,1)S(1)}, u32[]{:S(2)}, u32[]{:S(2)}) collective-permute-start(bf16[2,4,16,512]{3,2,1,0:T(8,128)(2,1)S(1)} %get-tuple-element.97), channel_id=1, source_target_pairs={{0,8},{4,12},{8,0},{12,4},{16,24},{20,28},{24,16},{28,20},{1,9},{5... | collective-permute-start | bytes 393224 | tf_op jit(solution)/shard_map/ppermute | solution.py:347
  67.6 1.4 %collective-permute-start.13 = (bf16[2,4,16,512]{3,2,1,0:T(8,128)(2,1)S(1)}, bf16[2,4,16,512]{3,2,1,0:T(8,128)(2,1)S(1)}, u32[]{:S(2)}, u32[]{:S(2)}) collective-permute-start(bf16[2,4,16,512]{3,2,1,0:T(8,128)(2,1)S(1)} %get-tuple-element.94), channel_id=1, source_target_pairs={{0,24},{4,28},{8,16},{12,20},{16,8},{20,12},{24,0},{28,4},{1,25},{... | collective-permute-start | bytes 393224 | tf_op jit(solution)/shard_map/ppermute | solution.py:347
  68.9 0.7 collective-permute-start.15
  69.6 0.0 collective-permute-done.11.refs_4_
  69.6 0.1 rim.1
  69.7 2.3 %collective-permute-done.14.refs_6_ = bf16[2,4,16,512]{3,2,1,0:T(8,128)(2,1)S(1)} collective-permute-done((bf16[2,4,16,512]{3,2,1,0:T(8,128)(2,1)S(1)}, bf16[2,4,16,512]{3,2,1,0:T(8,128)(2,1)S(1)}, u32[]{:S(2)}, u32[]{:S(2)}) %collective-permute-start.14) | collective-permute-done | bytes 131104 | tf_op jit(solution)/shard_map/ppermute | solution.py:347
  72.0 3.4 %collective-permute-start.16 = (bf16[8,4,512]{2,1,0:T(4,128)(2,1)S(1)}, bf16[8,4,512]{2,1,0:T(4,128)(2,1)S(1)}, u32[]{:S(2)}, u32[]{:S(2)}) collective-permute-start(bf16[8,4,512]{2,1,0:T(4,128)(2,1)S(1)} %get-tuple-element.101), channel_id=1, source_target_pairs={{0,1},{1,2},{2,3},{4,5},{5,6},{6,7},{8,9},{9,10},{10,11},{12,13},{... | collective-permute-start | bytes 98312 | tf_op jit(solution)/shard_map/ppermute | solution.py:430
  75.4 1.3 %collective-permute-start.17 = (bf16[8,4,512]{2,1,0:T(4,128)(2,1)S(1)}, bf16[8,4,512]{2,1,0:T(4,128)(2,1)S(1)}, u32[]{:S(2)}, u32[]{:S(2)}) collective-permute-start(bf16[8,4,512]{2,1,0:T(4,128)(2,1)S(1)} %get-tuple-element.102), channel_id=1, source_target_pairs={{1,0},{2,1},{3,2},{5,4},{6,5},{7,6},{9,8},{10,9},{11,10},{13,12},{... | collective-permute-start | bytes 98312 | tf_op jit(solution)/shard_map/ppermute | solution.py:431
  76.7 0.0 collective-permute-done.13.refs_5_
  76.7 4.9 %collective-permute-done.15.refs_7_ = bf16[2,4,16,512]{3,2,1,0:T(8,128)(2,1)S(1)} collective-permute-done((bf16[2,4,16,512]{3,2,1,0:T(8,128)(2,1)S(1)}, bf16[2,4,16,512]{3,2,1,0:T(8,128)(2,1)S(1)}, u32[]{:S(2)}, u32[]{:S(2)}) %collective-permute-start.15) | collective-permute-done | bytes 131104 | tf_op jit(solution)/shard_map/ppermute | solution.py:347
  81.6 0.0 collective-permute-done.16.refs_10_
  81.6 0.0 collective-permute-done.17.refs_11_
  81.6 0.0 copy-done.6
  81.6 2.4 %depth_filter.1 = bf16[4,8,32,512]{3,2,1,0:T(8,128)(2,1)} custom-call(bf16[8,16,512]{2,1,0:T(8,128)(2,1)S(1)} %collective-permute-done.7.refs_0_, bf16[8,16,512]{2,1,0:T(8,128)(2,1)S(1)} %collective-permute-done.8.refs_1_, bf16[8,16,512]{2,1,0:T(8,128)(2,1)S(1)} %collective-permute-done.10.refs_2_, bf16[8,16,512]{2,1,0:T(8,128)(2,1)S(1)} %get-tuple-element.89.refs_3_, ...), custom_call_target="tpu_custom_call" | custom-call | flops 1 | bytes 1 | tf_op jit(solution)/shard_map/depth_filter/pallas_call | solution.py:320
  (2 shorter events, 0.0 us)
Async XLA Ops:
  0.0 38.3 %copy-start.3 = (bf16[512,512]{1,0:T(8,128)(2,1)S(1)}, bf16[512,512]{1,0:T(8,128)(2,1)}, u32[]{:S(2)}) copy-start(bf16[512,512]{1,0:T(8,128)(2,1)} %refs_8_.3) | copy-start | bytes 1572868
  0.0 38.3 %copy-start.2 = (bf16[512,512]{1,0:T(8,128)(2,1)S(1)}, bf16[512,512]{1,0:T(8,128)(2,1)}, u32[]{:S(2)}) copy-start(bf16[512,512]{1,0:T(8,128)(2,1)} %refs_7_.5) | copy-start | bytes 1572868
  0.0 38.3 %copy-start.1 = (bf16[512,512]{1,0:T(8,128)(2,1)S(1)}, bf16[512,512]{1,0:T(8,128)(2,1)}, u32[]{:S(2)}) copy-start(bf16[512,512]{1,0:T(8,128)(2,1)} %refs_6_.5) | copy-start | bytes 1572868
  0.0 38.3 %copy-start = (bf16[3,512,512]{2,1,0:T(8,128)(2,1)S(1)}, bf16[3,512,512]{2,1,0:T(8,128)(2,1)}, u32[]{:S(2)}) copy-start(bf16[3,512,512]{2,1,0:T(8,128)(2,1)} %refs_10_.3) | copy-start | bytes 4718596
  0.0 38.3 %copy-start.4 = (bf16[512,512]{1,0:T(8,128)(2,1)S(1)}, bf16[512,512]{1,0:T(8,128)(2,1)}, u32[]{:S(2)}) copy-start(bf16[512,512]{1,0:T(8,128)(2,1)} %refs_9_.3) | copy-start | bytes 1572868
  0.0 1.7 %copy-start.5 = (bf16[8,8,32,512]{3,2,1,0:T(8,128)(2,1)S(1)}, bf16[8,8,32,512]{3,2,1,0:T(8,128)(2,1)}, u32[]{:S(2)}) copy-start(bf16[8,8,32,512]{3,2,1,0:T(8,128)(2,1)} %video.1) | copy-start | bytes 6291460
  1.8 36.5 %copy-start.7 = (f32[512]{0:T(512)S(1)}, f32[512]{0:T(512)}, u32[]{:S(2)}) copy-start(f32[512]{0:T(512)} %param.9) | copy-start | bytes 6148
  1.9 2.1 %collective-permute-start = (bf16[4,8,16,512]{3,2,1,0:T(8,128)(2,1)S(1)}, bf16[4,8,16,512]{3,2,1,0:T(8,128)(2,1)S(1)}, u32[]{:S(2)}, u32[]{:S(2)}) collective-permute-start(bf16[4,8,16,512]{3,2,1,0:T(8,128)(2,1)S(1)} %get-tuple-element.57), channel_id=1, source_target_pairs={{0,4},{4,0},{8,12},{12,8},{16,20},{20,16},{24,28},{28,24},{1,5},{5... | collective-permute-start | bytes 1572872 | tf_op jit(solution)/shard_map/ppermute | solution.py:347
  4.0 5.8 %collective-permute-start.2 = (bf16[4,8,16,512]{3,2,1,0:T(8,128)(2,1)S(1)}, bf16[4,8,16,512]{3,2,1,0:T(8,128)(2,1)S(1)}, u32[]{:S(2)}, u32[]{:S(2)}) collective-permute-start(bf16[4,8,16,512]{3,2,1,0:T(8,128)(2,1)S(1)} %get-tuple-element.66), channel_id=1, source_target_pairs={{0,4},{4,0},{8,12},{12,8},{16,20},{20,16},{24,28},{28,24},{1,5},{5... | collective-permute-start | bytes 1572872 | tf_op jit(solution)/shard_map/ppermute | solution.py:347
  4.5 12.0 %collective-permute-start.1 = (bf16[16,16,512]{2,1,0:T(8,128)(2,1)S(1)}, bf16[16,16,512]{2,1,0:T(8,128)(2,1)S(1)}, u32[]{:S(2)}, u32[]{:S(2)}) collective-permute-start(bf16[16,16,512]{2,1,0:T(8,128)(2,1)S(1)} %get-tuple-element.62), channel_id=1, source_target_pairs={{0,24},{4,28},{8,16},{12,20},{16,8},{20,12},{24,0},{28,4},{1,25},{... | collective-permute-start | bytes 786440 | tf_op jit(solution)/shard_map/ppermute | solution.py:347
  9.2 14.3 %collective-permute-start.3 = (bf16[16,16,512]{2,1,0:T(8,128)(2,1)S(1)}, bf16[16,16,512]{2,1,0:T(8,128)(2,1)S(1)}, u32[]{:S(2)}, u32[]{:S(2)}) collective-permute-start(bf16[16,16,512]{2,1,0:T(8,128)(2,1)S(1)} %get-tuple-element.71), channel_id=1, source_target_pairs={{0,8},{4,12},{8,0},{12,4},{16,24},{20,28},{24,16},{28,20},{1,9},{5... | collective-permute-start | bytes 786440 | tf_op jit(solution)/shard_map/ppermute | solution.py:347
  9.2 29.0 %collective-permute-start.4 = (bf16[16,16,512]{2,1,0:T(8,128)(2,1)S(1)}, bf16[16,16,512]{2,1,0:T(8,128)(2,1)S(1)}, u32[]{:S(2)}, u32[]{:S(2)}) collective-permute-start(bf16[16,16,512]{2,1,0:T(8,128)(2,1)S(1)} %get-tuple-element.72), channel_id=1, source_target_pairs={{0,16},{4,20},{8,24},{12,28},{16,0},{20,4},{24,8},{28,12},{1,17},{... | collective-permute-start | bytes 786440 | tf_op jit(solution)/shard_map/ppermute | solution.py:347
  16.4 27.8 %collective-permute-start.5 = (bf16[16,16,512]{2,1,0:T(8,128)(2,1)S(1)}, bf16[16,16,512]{2,1,0:T(8,128)(2,1)S(1)}, u32[]{:S(2)}, u32[]{:S(2)}) collective-permute-start(bf16[16,16,512]{2,1,0:T(8,128)(2,1)S(1)} %get-tuple-element.76), channel_id=1, source_target_pairs={{0,24},{4,28},{8,16},{12,20},{16,8},{20,12},{24,0},{28,4},{1,25},{... | collective-permute-start | bytes 786440 | tf_op jit(solution)/shard_map/ppermute | solution.py:347
  20.2 24.1 %collective-permute-start.6 = (bf16[16,16,512]{2,1,0:T(8,128)(2,1)S(1)}, bf16[16,16,512]{2,1,0:T(8,128)(2,1)S(1)}, u32[]{:S(2)}, u32[]{:S(2)}) collective-permute-start(bf16[16,16,512]{2,1,0:T(8,128)(2,1)S(1)} %get-tuple-element.77), channel_id=1, source_target_pairs={{0,8},{4,12},{8,0},{12,4},{16,24},{20,28},{24,16},{28,20},{1,9},{5... | collective-permute-start | bytes 786440 | tf_op jit(solution)/shard_map/ppermute | solution.py:347
  23.5 34.5 %collective-permute-start.9 = (bf16[16,16,512]{2,1,0:T(8,128)(2,1)S(1)}, bf16[16,16,512]{2,1,0:T(8,128)(2,1)S(1)}, u32[]{:S(2)}, u32[]{:S(2)}) collective-permute-start(bf16[16,16,512]{2,1,0:T(8,128)(2,1)S(1)} %get-tuple-element.82), channel_id=1, source_target_pairs={{0,16},{4,20},{8,24},{12,28},{16,0},{20,4},{24,8},{28,12},{1,17},{... | collective-permute-start | bytes 786440 | tf_op jit(solution)/shard_map/ppermute | solution.py:347
  45.8 17.0 %collective-permute-start.7 = (bf16[8,16,512]{2,1,0:T(8,128)(2,1)S(1)}, bf16[8,16,512]{2,1,0:T(8,128)(2,1)S(1)}, u32[]{:S(2)}, u32[]{:S(2)}) collective-permute-start(bf16[8,16,512]{2,1,0:T(8,128)(2,1)S(1)} %get-tuple-element.79), channel_id=1, source_target_pairs={{0,24},{4,28},{8,16},{12,20},{16,8},{20,12},{24,0},{28,4},{1,25},{... | collective-permute-start | bytes 393224 | tf_op jit(solution)/shard_map/ppermute | solution.py:347
  48.3 14.5 %collective-permute-start.8 = (bf16[8,16,512]{2,1,0:T(8,128)(2,1)S(1)}, bf16[8,16,512]{2,1,0:T(8,128)(2,1)S(1)}, u32[]{:S(2)}, u32[]{:S(2)}) collective-permute-start(bf16[8,16,512]{2,1,0:T(8,128)(2,1)S(1)} %get-tuple-element.80), channel_id=1, source_target_pairs={{0,8},{4,12},{8,0},{12,4},{16,24},{20,28},{24,16},{28,20},{1,9},{5... | collective-permute-start | bytes 393224 | tf_op jit(solution)/shard_map/ppermute | solution.py:347
  58.0 23.7 %copy-start.6 = (f32[3,3,512]{2,1,0:T(4,128)S(1)}, f32[3,3,512]{2,1,0:T(4,128)}, u32[]{:S(2)}) copy-start(f32[3,3,512]{2,1,0:T(4,128)} %refs_12_.1) | copy-start | bytes 55300
  58.0 7.9 %collective-permute-start.10 = (bf16[8,16,512]{2,1,0:T(8,128)(2,1)S(1)}, bf16[8,16,512]{2,1,0:T(8,128)(2,1)S(1)}, u32[]{:S(2)}, u32[]{:S(2)}) collective-permute-start(bf16[8,16,512]{2,1,0:T(8,128)(2,1)S(1)} %get-tuple-element.88), channel_id=1, source_target_pairs={{0,16},{4,20},{8,24},{12,28},{16,0},{20,4},{24,8},{28,12},{1,17},{... | collective-permute-start | bytes 393224 | tf_op jit(solution)/shard_map/ppermute | solution.py:347
  62.8 3.2 %collective-permute-start.12 = (bf16[4,4,16,512]{3,2,1,0:T(8,128)(2,1)S(1)}, bf16[4,4,16,512]{3,2,1,0:T(8,128)(2,1)S(1)}, u32[]{:S(2)}, u32[]{:S(2)}) collective-permute-start(bf16[4,4,16,512]{3,2,1,0:T(8,128)(2,1)S(1)} %get-tuple-element.93), channel_id=1, source_target_pairs={{0,4},{4,0},{8,12},{12,8},{16,20},{20,16},{24,28},{28,24},{1,5},{5... | collective-permute-start | bytes 786440 | tf_op jit(solution)/shard_map/ppermute | solution.py:347
  65.9 3.7 %collective-permute-start.11 = (bf16[4,4,16,512]{3,2,1,0:T(8,128)(2,1)S(1)}, bf16[4,4,16,512]{3,2,1,0:T(8,128)(2,1)S(1)}, u32[]{:S(2)}, u32[]{:S(2)}) collective-permute-start(bf16[4,4,16,512]{3,2,1,0:T(8,128)(2,1)S(1)} %stack_back.1), channel_id=1, source_target_pairs={{0,4},{4,0},{8,12},{12,8},{16,20},{20,16},{24,28},{28,24},{1,5},{5... | collective-permute-start | bytes 786440 | tf_op jit(solution)/shard_map/ppermute | solution.py:347
  66.1 6.0 %collective-permute-start.14 = (bf16[2,4,16,512]{3,2,1,0:T(8,128)(2,1)S(1)}, bf16[2,4,16,512]{3,2,1,0:T(8,128)(2,1)S(1)}, u32[]{:S(2)}, u32[]{:S(2)}) collective-permute-start(bf16[2,4,16,512]{3,2,1,0:T(8,128)(2,1)S(1)} %get-tuple-element.97), channel_id=1, source_target_pairs={{0,8},{4,12},{8,0},{12,4},{16,24},{20,28},{24,16},{28,20},{1,9},{5... | collective-permute-start | bytes 393224 | tf_op jit(solution)/shard_map/ppermute | solution.py:347
  67.6 9.2 %collective-permute-start.13 = (bf16[2,4,16,512]{3,2,1,0:T(8,128)(2,1)S(1)}, bf16[2,4,16,512]{3,2,1,0:T(8,128)(2,1)S(1)}, u32[]{:S(2)}, u32[]{:S(2)}) collective-permute-start(bf16[2,4,16,512]{3,2,1,0:T(8,128)(2,1)S(1)} %get-tuple-element.94), channel_id=1, source_target_pairs={{0,24},{4,28},{8,16},{12,20},{16,8},{20,12},{24,0},{28,4},{1,25},{... | collective-permute-start | bytes 393224 | tf_op jit(solution)/shard_map/ppermute | solution.py:347
  68.9 12.7 %collective-permute-start.15 = (bf16[2,4,16,512]{3,2,1,0:T(8,128)(2,1)S(1)}, bf16[2,4,16,512]{3,2,1,0:T(8,128)(2,1)S(1)}, u32[]{:S(2)}, u32[]{:S(2)}) collective-permute-start(bf16[2,4,16,512]{3,2,1,0:T(8,128)(2,1)S(1)} %get-tuple-element.99), channel_id=1, source_target_pairs={{0,16},{4,20},{8,24},{12,28},{16,0},{20,4},{24,8},{28,12},{1,17},{... | collective-permute-start | bytes 393224 | tf_op jit(solution)/shard_map/ppermute | solution.py:347
  72.0 9.6 %collective-permute-start.16 = (bf16[8,4,512]{2,1,0:T(4,128)(2,1)S(1)}, bf16[8,4,512]{2,1,0:T(4,128)(2,1)S(1)}, u32[]{:S(2)}, u32[]{:S(2)}) collective-permute-start(bf16[8,4,512]{2,1,0:T(4,128)(2,1)S(1)} %get-tuple-element.101), channel_id=1, source_target_pairs={{0,1},{1,2},{2,3},{4,5},{5,6},{6,7},{8,9},{9,10},{10,11},{12,13},{... | collective-permute-start | bytes 98312 | tf_op jit(solution)/shard_map/ppermute | solution.py:430
  75.4 6.2 %collective-permute-start.17 = (bf16[8,4,512]{2,1,0:T(4,128)(2,1)S(1)}, bf16[8,4,512]{2,1,0:T(4,128)(2,1)S(1)}, u32[]{:S(2)}, u32[]{:S(2)}) collective-permute-start(bf16[8,4,512]{2,1,0:T(4,128)(2,1)S(1)} %get-tuple-element.102), channel_id=1, source_target_pairs={{1,0},{2,1},{3,2},{5,4},{6,5},{7,6},{9,8},{10,9},{11,10},{13,12},{... | collective-permute-start | bytes 98312 | tf_op jit(solution)/shard_map/ppermute | solution.py:431

commit v11 on v10

--- a/solution.py
+++ b/solution.py
@@ -367,7 +367,6 @@
     outer_far = join(outer, outer_other, "join_outer")
     *outer_far, inner_stack = lax.optimization_barrier((*outer_far, inner_stack))
     outer_far = [swap(piece, k) for k, piece in zip(hops, outer_far)]
-    nearest = far.index(1)
     inner_other = swap(inner_stack, 1)
     inner_far = join(inner, inner_other, "join_inner")
     outer_far[0], *inner_far = lax.optimization_barrier((outer_far[0], *inner_far))
@@ -424,7 +423,6 @@
     (stack,) = gather(for_mate, outer, [(chips, made, width, channels)], "stack_back")
     halves = swap(stack, 1)
     low_side, high_side = rim(hops, outer, halves)
-    low_side, high_side, inner[nearest] = lax.optimization_barrier((low_side, high_side, inner[nearest]))
     line = lax.axis_size("col")
     upward = [(i, i + 1) for i in range(line - 1)]
     left = lax.ppermute(high_side, "col", upward)

time: 84.2 us -> 83.5 us (level)
  waiting for transfers between devices: 36.5 us -> 34.9 us
  starting transfers between devices: 30.6 us -> 31.5 us
    ppermute x16, waiting for transfers between devices: 36.4 us -> 30.4 us  [swap(): lax.ppermute(block, 'frm', [(i, i ^ k) for i in range(count)])]
    ppermute x1, waiting for transfers between devices: 0.01 us -> 4.23 us  [local(): right = lax.ppermute(low_side, 'col', [(b, a) for a, b in upward])]
    ppermute x16, starting transfers between devices: 25.9 us -> 26.8 us  [swap(): lax.ppermute(block, 'frm', [(i, i ^ k) for i in range(count)])]
  transfers between devices with their start and end apart: 18 -> 18, of which waited for: 7 -> 8; matrix products, arithmetic and copies ran while one was open for 0% -> 0% of each run, Pallas kernels for 15% -> 15%
where the time goes in v11:
time: 83.5 us; the launch traced here: 83.3 us
  waiting for transfers between devices  34.9 us (42%)
  starting transfers between devices  31.5 us (38%)
  Pallas kernels  15 us (18%)
  local copies, waits for them, and re-layouts  1.76 us (2%)
    ppermute x16, waiting for transfers between devices, swap(): lax.ppermute(block, 'frm', [(i, i ^ k) for i in range(count)])  30.4 us
    ppermute x16, starting transfers between devices, swap(): lax.ppermute(block, 'frm', [(i, i ^ k) for i in range(count)])  26.8 us
    pallas_call x2, Pallas kernels, attend(): pl.pallas_call(functools.partial(attend_kernel, inward, hops, paired, n_e...  10.8 us
    ppermute x1, waiting for transfers between devices, local(): right = lax.ppermute(low_side, 'col', [(b, a) for a, b in upward])  4.23 us
    ppermute x1, starting transfers between devices, local(): left = lax.ppermute(high_side, 'col', upward)  3.4 us
    pallas_call x1, Pallas kernels, depth_filter(): pl.pallas_call(functools.partial(filter_kernel, hops), out_shape=jax.Shap...  2.37 us
    unnamed x16, local copies, waits for them, and re-layouts  1.76 us
  transfers between devices with their start and end apart: 18, of which 8 were waited for; matrix products, arithmetic and copies ran while one was open for 0% of the time, Pallas kernels for 15%

profile of v11, /device:TPU:0, one launch (start us, length us, event | category | flops | bytes accessed | tf_op | source)
XLA Modules:
  0.0 83.3 jit_solution(4036105918892086200)
XLA Ops:
  0.0 0.0 copy-start.3
  0.0 0.0 copy-start.2
  0.0 0.0 copy-start.1
  0.0 0.0 copy-start
  0.0 0.0 copy-start.4
  0.0 0.0 copy-start.5
  0.0 1.7 %copy-done.5 = bf16[8,8,32,512]{3,2,1,0:T(8,128)(2,1)S(1)} copy-done((bf16[8,8,32,512]{3,2,1,0:T(8,128)(2,1)S(1)}, bf16[8,8,32,512]{3,2,1,0:T(8,128)(2,1)}, u32[]{:S(2)}) %copy-start.5) | copy-done | bytes 2097176
  1.8 0.0 copy-start.7
  1.8 0.1 cut.1
  1.9 0.5 collective-permute-start
  2.4 1.5 %collective-permute-done.refs_3_.refs_4_ = bf16[4,8,16,512]{3,2,1,0:T(8,128)(2,1)S(1)} collective-permute-done((bf16[4,8,16,512]{3,2,1,0:T(8,128)(2,1)S(1)}, bf16[4,8,16,512]{3,2,1,0:T(8,128)(2,1)S(1)}, u32[]{:S(2)}, u32[]{:S(2)}) %collective-permute-start) | collective-permute-done | bytes 524320 | tf_op jit(solution)/shard_map/ppermute | solution.py:347
  4.0 0.1 join_outer.1
  4.0 0.4 collective-permute-start.2
  4.5 4.7 %collective-permute-start.1 = (bf16[16,16,512]{2,1,0:T(8,128)(2,1)S(1)}, bf16[16,16,512]{2,1,0:T(8,128)(2,1)S(1)}, u32[]{:S(2)}, u32[]{:S(2)}) collective-permute-start(bf16[16,16,512]{2,1,0:T(8,128)(2,1)S(1)} %get-tuple-element.59), channel_id=1, source_target_pairs={{0,24},{4,28},{8,16},{12,20},{16,8},{20,12},{24,0},{28,4},{1,25},{... | collective-permute-start | bytes 786440 | tf_op jit(solution)/shard_map/ppermute | solution.py:347
  9.2 0.0 collective-permute-start.3
  9.2 0.6 collective-permute-start.4
  9.8 0.0 collective-permute-done.2.refs_3_.refs_4_
  9.8 0.1 join_inner.1
  9.8 6.6 %collective-permute-done.1.refs_0_ = bf16[16,16,512]{2,1,0:T(8,128)(2,1)S(1)} collective-permute-done((bf16[16,16,512]{2,1,0:T(8,128)(2,1)S(1)}, bf16[16,16,512]{2,1,0:T(8,128)(2,1)S(1)}, u32[]{:S(2)}, u32[]{:S(2)}) %collective-permute-start.1) | collective-permute-done | bytes 262176 | tf_op jit(solution)/shard_map/ppermute | solution.py:347
  16.4 3.7 %collective-permute-start.5 = (bf16[16,16,512]{2,1,0:T(8,128)(2,1)S(1)}, bf16[16,16,512]{2,1,0:T(8,128)(2,1)S(1)}, u32[]{:S(2)}, u32[]{:S(2)}) collective-permute-start(bf16[16,16,512]{2,1,0:T(8,128)(2,1)S(1)} %get-tuple-element.73), channel_id=1, source_target_pairs={{0,24},{4,28},{8,16},{12,20},{16,8},{20,12},{24,0},{28,4},{1,25},{... | collective-permute-start | bytes 786440 | tf_op jit(solution)/shard_map/ppermute | solution.py:347
  20.2 3.3 %collective-permute-start.6 = (bf16[16,16,512]{2,1,0:T(8,128)(2,1)S(1)}, bf16[16,16,512]{2,1,0:T(8,128)(2,1)S(1)}, u32[]{:S(2)}, u32[]{:S(2)}) collective-permute-start(bf16[16,16,512]{2,1,0:T(8,128)(2,1)S(1)} %get-tuple-element.74), channel_id=1, source_target_pairs={{0,8},{4,12},{8,0},{12,4},{16,24},{20,28},{24,16},{28,20},{1,9},{5... | collective-permute-start | bytes 786440 | tf_op jit(solution)/shard_map/ppermute | solution.py:347
  23.5 0.0 collective-permute-start.9
  23.5 0.0 collective-permute-done.3.refs_1_
  23.5 14.8 %collective-permute-done.4.refs_2_ = bf16[16,16,512]{2,1,0:T(8,128)(2,1)S(1)} collective-permute-done((bf16[16,16,512]{2,1,0:T(8,128)(2,1)S(1)}, bf16[16,16,512]{2,1,0:T(8,128)(2,1)S(1)}, u32[]{:S(2)}, u32[]{:S(2)}) %collective-permute-start.4) | collective-permute-done | bytes 262176 | tf_op jit(solution)/shard_map/ppermute | solution.py:347
  38.3 0.0 copy-done.3
  38.3 0.0 copy-done.2
  38.3 0.0 copy-done.1
  38.3 0.0 copy-done
  38.3 0.0 copy-done.4
  38.3 0.0 copy-done.7
  38.3 5.9 %attend_outer.1 = (bf16[8,16,512]{2,1,0:T(8,128)(2,1)S(1)}, bf16[8,16,512]{2,1,0:T(8,128)(2,1)S(1)}, bf16[8,16,512]{2,1,0:T(8,128)(2,1)S(1)}, bf16[8,16,512]{2,1,0:T(8,128)(2,1)S(1)}) custom-call(bf16[16,16,512]{2,1,0:T(8,128)(2,1)S(1)} %collective-permute-done.1.refs_0_, bf16[16,16,512]{2,1,0:T(8,128)(2,1)S(1)} %collective-permute-done.3.refs_1_, ...), custom_call_target="tpu_custom_call" | custom-call | flops 1 | bytes 1 | tf_op jit(solution)/shard_map/attend_outer/pallas_call | solution.py:214
  44.3 0.0 collective-permute-done.5.refs_0_
  44.3 0.0 collective-permute-done.6.refs_1_
  44.3 1.5 %project_early.1.refs_11_ = bf16[3,768,512]{2,1,0:T(8,128)(2,1)S(1)} custom-call(bf16[16,16,512]{2,1,0:T(8,128)(2,1)S(1)} %collective-permute-done.5.refs_0_, bf16[16,16,512]{2,1,0:T(8,128)(2,1)S(1)} %collective-permute-done.6.refs_1_, bf16[8,16,512]{2,1,0:T(8,128)(2,1)S(1)} %get-tuple-element.75.refs_2_.refs_3_, ...), custom_call_target="tpu_custom_call" | custom-call | flops 1207959552 | bytes 3145728 | tf_op jit(solution)/shard_map/project_early/pallas_call | solution.py:102
  45.8 2.5 %collective-permute-start.7 = (bf16[8,16,512]{2,1,0:T(8,128)(2,1)S(1)}, bf16[8,16,512]{2,1,0:T(8,128)(2,1)S(1)}, u32[]{:S(2)}, u32[]{:S(2)}) collective-permute-start(bf16[8,16,512]{2,1,0:T(8,128)(2,1)S(1)} %get-tuple-element.76), channel_id=1, source_target_pairs={{0,24},{4,28},{8,16},{12,20},{16,8},{20,12},{24,0},{28,4},{1,25},{... | collective-permute-start | bytes 393224 | tf_op jit(solution)/shard_map/ppermute | solution.py:347
  48.3 6.3 %collective-permute-start.8 = (bf16[8,16,512]{2,1,0:T(8,128)(2,1)S(1)}, bf16[8,16,512]{2,1,0:T(8,128)(2,1)S(1)}, u32[]{:S(2)}, u32[]{:S(2)}) collective-permute-start(bf16[8,16,512]{2,1,0:T(8,128)(2,1)S(1)} %get-tuple-element.77), channel_id=1, source_target_pairs={{0,8},{4,12},{8,0},{12,4},{16,24},{20,28},{24,16},{28,20},{1,9},{5... | collective-permute-start | bytes 393224 | tf_op jit(solution)/shard_map/ppermute | solution.py:347
  54.6 3.4 %collective-permute-done.9.refs_2_ = bf16[16,16,512]{2,1,0:T(8,128)(2,1)S(1)} collective-permute-done((bf16[16,16,512]{2,1,0:T(8,128)(2,1)S(1)}, bf16[16,16,512]{2,1,0:T(8,128)(2,1)S(1)}, u32[]{:S(2)}, u32[]{:S(2)}) %collective-permute-start.9) | collective-permute-done | bytes 262176 | tf_op jit(solution)/shard_map/ppermute | solution.py:347
  58.0 0.0 copy-start.6
  58.0 0.0 collective-permute-start.10
  58.0 4.8 %attend_inner.1 = (bf16[4,16,512]{2,1,0:T(8,128)(2,1)S(1)}, bf16[4,16,512]{2,1,0:T(8,128)(2,1)S(1)}, bf16[4,16,512]{2,1,0:T(8,128)(2,1)S(1)}, bf16[4,16,512]{2,1,0:T(8,128)(2,1)S(1)}, bf16[4,4,16,512]{3,2,1,0:T(8,128)(2,1)S(1)}) custom-call(bf16[16,16,512]{2,1,0:T(8,128)(2,1)S(1)} %collective-permute-done.5.refs_0_, ...), custom_call_target="tpu_custom_call" | custom-call | flops 1 | bytes 1 | tf_op jit(solution)/shard_map/attend_inner/pallas_call | solution.py:214
  62.8 0.0 collective-permute-done.7.refs_0_
  62.8 0.0 collective-permute-done.8.refs_1_
  62.8 0.1 collective-permute-start.12
  62.9 3.0 %collective-permute-done.10.refs_2_ = bf16[8,16,512]{2,1,0:T(8,128)(2,1)S(1)} collective-permute-done((bf16[8,16,512]{2,1,0:T(8,128)(2,1)S(1)}, bf16[8,16,512]{2,1,0:T(8,128)(2,1)S(1)}, u32[]{:S(2)}, u32[]{:S(2)}) %collective-permute-start.10) | collective-permute-done | bytes 131104 | tf_op jit(solution)/shard_map/ppermute | solution.py:347
  65.9 0.1 collective-permute-start.11
  66.0 0.0 collective-permute-done.12.refs_3_.refs_9_
  66.1 2.5 %collective-permute-start.13 = (bf16[2,4,16,512]{3,2,1,0:T(8,128)(2,1)S(1)}, bf16[2,4,16,512]{3,2,1,0:T(8,128)(2,1)S(1)}, u32[]{:S(2)}, u32[]{:S(2)}) collective-permute-start(bf16[2,4,16,512]{3,2,1,0:T(8,128)(2,1)S(1)} %get-tuple-element.91), channel_id=1, source_target_pairs={{0,24},{4,28},{8,16},{12,20},{16,8},{20,12},{24,0},{28,4},{1,25},{... | collective-permute-start | bytes 393224 | tf_op jit(solution)/shard_map/ppermute | solution.py:347
  68.5 0.0 collective-permute-start.14
  68.5 2.0 %collective-permute-start.15 = (bf16[2,4,16,512]{3,2,1,0:T(8,128)(2,1)S(1)}, bf16[2,4,16,512]{3,2,1,0:T(8,128)(2,1)S(1)}, u32[]{:S(2)}, u32[]{:S(2)}) collective-permute-start(bf16[2,4,16,512]{3,2,1,0:T(8,128)(2,1)S(1)} %get-tuple-element.93), channel_id=1, source_target_pairs={{0,16},{4,20},{8,24},{12,28},{16,0},{20,4},{24,8},{28,12},{1,17},{... | collective-permute-start | bytes 393224 | tf_op jit(solution)/shard_map/ppermute | solution.py:347
  70.5 0.0 collective-permute-done.11.refs_4_
  70.5 0.1 rim.1
  70.6 3.4 %collective-permute-start.16 = (bf16[8,4,512]{2,1,0:T(4,128)(2,1)S(1)}, bf16[8,4,512]{2,1,0:T(4,128)(2,1)S(1)}, u32[]{:S(2)}, u32[]{:S(2)}) collective-permute-start(bf16[8,4,512]{2,1,0:T(4,128)(2,1)S(1)} %get-tuple-element.95), channel_id=1, source_target_pairs={{0,1},{1,2},{2,3},{4,5},{5,6},{6,7},{8,9},{9,10},{10,11},{12,13},{... | collective-permute-start | bytes 98312 | tf_op jit(solution)/shard_map/ppermute | solution.py:428
  74.0 1.3 %collective-permute-start.17 = (bf16[8,4,512]{2,1,0:T(4,128)(2,1)S(1)}, bf16[8,4,512]{2,1,0:T(4,128)(2,1)S(1)}, u32[]{:S(2)}, u32[]{:S(2)}) collective-permute-start(bf16[8,4,512]{2,1,0:T(4,128)(2,1)S(1)} %get-tuple-element.96), channel_id=1, source_target_pairs={{1,0},{2,1},{3,2},{5,4},{6,5},{7,6},{9,8},{10,9},{11,10},{13,12},{... | collective-permute-start | bytes 98312 | tf_op jit(solution)/shard_map/ppermute | solution.py:429
  75.3 0.3 collective-permute-done.16.refs_10_
  75.6 4.2 %collective-permute-done.17.refs_11_ = bf16[8,4,512]{2,1,0:T(4,128)(2,1)S(1)} collective-permute-done((bf16[8,4,512]{2,1,0:T(4,128)(2,1)S(1)}, bf16[8,4,512]{2,1,0:T(4,128)(2,1)S(1)}, u32[]{:S(2)}, u32[]{:S(2)}) %collective-permute-start.17) | collective-permute-done | bytes 32800 | tf_op jit(solution)/shard_map/ppermute | solution.py:429
  79.9 0.0 collective-permute-done.13.refs_5_
  79.9 0.0 collective-permute-done.14.refs_6_
  79.9 1.1 %collective-permute-done.15.refs_7_ = bf16[2,4,16,512]{3,2,1,0:T(8,128)(2,1)S(1)} collective-permute-done((bf16[2,4,16,512]{3,2,1,0:T(8,128)(2,1)S(1)}, bf16[2,4,16,512]{3,2,1,0:T(8,128)(2,1)S(1)}, u32[]{:S(2)}, u32[]{:S(2)}) %collective-permute-start.15) | collective-permute-done | bytes 131104 | tf_op jit(solution)/shard_map/ppermute | solution.py:347
  81.0 0.0 copy-done.6
  81.0 2.4 %depth_filter.1 = bf16[4,8,32,512]{3,2,1,0:T(8,128)(2,1)} custom-call(bf16[8,16,512]{2,1,0:T(8,128)(2,1)S(1)} %collective-permute-done.7.refs_0_, bf16[8,16,512]{2,1,0:T(8,128)(2,1)S(1)} %collective-permute-done.8.refs_1_, bf16[8,16,512]{2,1,0:T(8,128)(2,1)S(1)} %collective-permute-done.10.refs_2_, bf16[8,16,512]{2,1,0:T(8,128)(2,1)S(1)} %get-tuple-element.86.refs_3_, ...), custom_call_target="tpu_custom_call" | custom-call | flops 1 | bytes 1 | tf_op jit(solution)/shard_map/depth_filter/pallas_call | solution.py:320
  (2 shorter events, 0.0 us)
Async XLA Ops:
  0.0 38.3 %copy-start.3 = (bf16[512,512]{1,0:T(8,128)(2,1)S(1)}, bf16[512,512]{1,0:T(8,128)(2,1)}, u32[]{:S(2)}) copy-start(bf16[512,512]{1,0:T(8,128)(2,1)} %refs_8_.3) | copy-start | bytes 1572868
  0.0 38.3 %copy-start.2 = (bf16[512,512]{1,0:T(8,128)(2,1)S(1)}, bf16[512,512]{1,0:T(8,128)(2,1)}, u32[]{:S(2)}) copy-start(bf16[512,512]{1,0:T(8,128)(2,1)} %refs_7_.5) | copy-start | bytes 1572868
  0.0 38.3 %copy-start.1 = (bf16[512,512]{1,0:T(8,128)(2,1)S(1)}, bf16[512,512]{1,0:T(8,128)(2,1)}, u32[]{:S(2)}) copy-start(bf16[512,512]{1,0:T(8,128)(2,1)} %refs_6_.5) | copy-start | bytes 1572868
  0.0 38.3 %copy-start = (bf16[3,512,512]{2,1,0:T(8,128)(2,1)S(1)}, bf16[3,512,512]{2,1,0:T(8,128)(2,1)}, u32[]{:S(2)}) copy-start(bf16[3,512,512]{2,1,0:T(8,128)(2,1)} %refs_10_.3) | copy-start | bytes 4718596
  0.0 38.3 %copy-start.4 = (bf16[512,512]{1,0:T(8,128)(2,1)S(1)}, bf16[512,512]{1,0:T(8,128)(2,1)}, u32[]{:S(2)}) copy-start(bf16[512,512]{1,0:T(8,128)(2,1)} %refs_9_.3) | copy-start | bytes 1572868
  0.0 1.7 %copy-start.5 = (bf16[8,8,32,512]{3,2,1,0:T(8,128)(2,1)S(1)}, bf16[8,8,32,512]{3,2,1,0:T(8,128)(2,1)}, u32[]{:S(2)}) copy-start(bf16[8,8,32,512]{3,2,1,0:T(8,128)(2,1)} %video.1) | copy-start | bytes 6291460
  1.8 36.5 %copy-start.7 = (f32[512]{0:T(512)S(1)}, f32[512]{0:T(512)}, u32[]{:S(2)}) copy-start(f32[512]{0:T(512)} %param.9) | copy-start | bytes 6148
  1.9 2.1 %collective-permute-start = (bf16[4,8,16,512]{3,2,1,0:T(8,128)(2,1)S(1)}, bf16[4,8,16,512]{3,2,1,0:T(8,128)(2,1)S(1)}, u32[]{:S(2)}, u32[]{:S(2)}) collective-permute-start(bf16[4,8,16,512]{3,2,1,0:T(8,128)(2,1)S(1)} %get-tuple-element.54), channel_id=1, source_target_pairs={{0,4},{4,0},{8,12},{12,8},{16,20},{20,16},{24,28},{28,24},{1,5},{5... | collective-permute-start | bytes 1572872 | tf_op jit(solution)/shard_map/ppermute | solution.py:347
  4.0 5.8 %collective-permute-start.2 = (bf16[4,8,16,512]{3,2,1,0:T(8,128)(2,1)S(1)}, bf16[4,8,16,512]{3,2,1,0:T(8,128)(2,1)S(1)}, u32[]{:S(2)}, u32[]{:S(2)}) collective-permute-start(bf16[4,8,16,512]{3,2,1,0:T(8,128)(2,1)S(1)} %get-tuple-element.63), channel_id=1, source_target_pairs={{0,4},{4,0},{8,12},{12,8},{16,20},{20,16},{24,28},{28,24},{1,5},{5... | collective-permute-start | bytes 1572872 | tf_op jit(solution)/shard_map/ppermute | solution.py:347
  4.5 12.0 %collective-permute-start.1 = (bf16[16,16,512]{2,1,0:T(8,128)(2,1)S(1)}, bf16[16,16,512]{2,1,0:T(8,128)(2,1)S(1)}, u32[]{:S(2)}, u32[]{:S(2)}) collective-permute-start(bf16[16,16,512]{2,1,0:T(8,128)(2,1)S(1)} %get-tuple-element.59), channel_id=1, source_target_pairs={{0,24},{4,28},{8,16},{12,20},{16,8},{20,12},{24,0},{28,4},{1,25},{... | collective-permute-start | bytes 786440 | tf_op jit(solution)/shard_map/ppermute | solution.py:347
  9.2 14.3 %collective-permute-start.3 = (bf16[16,16,512]{2,1,0:T(8,128)(2,1)S(1)}, bf16[16,16,512]{2,1,0:T(8,128)(2,1)S(1)}, u32[]{:S(2)}, u32[]{:S(2)}) collective-permute-start(bf16[16,16,512]{2,1,0:T(8,128)(2,1)S(1)} %get-tuple-element.68), channel_id=1, source_target_pairs={{0,8},{4,12},{8,0},{12,4},{16,24},{20,28},{24,16},{28,20},{1,9},{5... | collective-permute-start | bytes 786440 | tf_op jit(solution)/shard_map/ppermute | solution.py:347
  9.2 29.0 %collective-permute-start.4 = (bf16[16,16,512]{2,1,0:T(8,128)(2,1)S(1)}, bf16[16,16,512]{2,1,0:T(8,128)(2,1)S(1)}, u32[]{:S(2)}, u32[]{:S(2)}) collective-permute-start(bf16[16,16,512]{2,1,0:T(8,128)(2,1)S(1)} %get-tuple-element.69), channel_id=1, source_target_pairs={{0,16},{4,20},{8,24},{12,28},{16,0},{20,4},{24,8},{28,12},{1,17},{... | collective-permute-start | bytes 786440 | tf_op jit(solution)/shard_map/ppermute | solution.py:347
  16.4 27.8 %collective-permute-start.5 = (bf16[16,16,512]{2,1,0:T(8,128)(2,1)S(1)}, bf16[16,16,512]{2,1,0:T(8,128)(2,1)S(1)}, u32[]{:S(2)}, u32[]{:S(2)}) collective-permute-start(bf16[16,16,512]{2,1,0:T(8,128)(2,1)S(1)} %get-tuple-element.73), channel_id=1, source_target_pairs={{0,24},{4,28},{8,16},{12,20},{16,8},{20,12},{24,0},{28,4},{1,25},{... | collective-permute-start | bytes 786440 | tf_op jit(solution)/shard_map/ppermute | solution.py:347
  20.2 24.1 %collective-permute-start.6 = (bf16[16,16,512]{2,1,0:T(8,128)(2,1)S(1)}, bf16[16,16,512]{2,1,0:T(8,128)(2,1)S(1)}, u32[]{:S(2)}, u32[]{:S(2)}) collective-permute-start(bf16[16,16,512]{2,1,0:T(8,128)(2,1)S(1)} %get-tuple-element.74), channel_id=1, source_target_pairs={{0,8},{4,12},{8,0},{12,4},{16,24},{20,28},{24,16},{28,20},{1,9},{5... | collective-permute-start | bytes 786440 | tf_op jit(solution)/shard_map/ppermute | solution.py:347
  23.5 34.5 %collective-permute-start.9 = (bf16[16,16,512]{2,1,0:T(8,128)(2,1)S(1)}, bf16[16,16,512]{2,1,0:T(8,128)(2,1)S(1)}, u32[]{:S(2)}, u32[]{:S(2)}) collective-permute-start(bf16[16,16,512]{2,1,0:T(8,128)(2,1)S(1)} %get-tuple-element.79), channel_id=1, source_target_pairs={{0,16},{4,20},{8,24},{12,28},{16,0},{20,4},{24,8},{28,12},{1,17},{... | collective-permute-start | bytes 786440 | tf_op jit(solution)/shard_map/ppermute | solution.py:347
  45.8 17.0 %collective-permute-start.7 = (bf16[8,16,512]{2,1,0:T(8,128)(2,1)S(1)}, bf16[8,16,512]{2,1,0:T(8,128)(2,1)S(1)}, u32[]{:S(2)}, u32[]{:S(2)}) collective-permute-start(bf16[8,16,512]{2,1,0:T(8,128)(2,1)S(1)} %get-tuple-element.76), channel_id=1, source_target_pairs={{0,24},{4,28},{8,16},{12,20},{16,8},{20,12},{24,0},{28,4},{1,25},{... | collective-permute-start | bytes 393224 | tf_op jit(solution)/shard_map/ppermute | solution.py:347
  48.3 14.5 %collective-permute-start.8 = (bf16[8,16,512]{2,1,0:T(8,128)(2,1)S(1)}, bf16[8,16,512]{2,1,0:T(8,128)(2,1)S(1)}, u32[]{:S(2)}, u32[]{:S(2)}) collective-permute-start(bf16[8,16,512]{2,1,0:T(8,128)(2,1)S(1)} %get-tuple-element.77), channel_id=1, source_target_pairs={{0,8},{4,12},{8,0},{12,4},{16,24},{20,28},{24,16},{28,20},{1,9},{5... | collective-permute-start | bytes 393224 | tf_op jit(solution)/shard_map/ppermute | solution.py:347
  58.0 23.0 %copy-start.6 = (f32[3,3,512]{2,1,0:T(4,128)S(1)}, f32[3,3,512]{2,1,0:T(4,128)}, u32[]{:S(2)}) copy-start(f32[3,3,512]{2,1,0:T(4,128)} %refs_12_.1) | copy-start | bytes 55300
  58.0 7.9 %collective-permute-start.10 = (bf16[8,16,512]{2,1,0:T(8,128)(2,1)S(1)}, bf16[8,16,512]{2,1,0:T(8,128)(2,1)S(1)}, u32[]{:S(2)}, u32[]{:S(2)}) collective-permute-start(bf16[8,16,512]{2,1,0:T(8,128)(2,1)S(1)} %get-tuple-element.85), channel_id=1, source_target_pairs={{0,16},{4,20},{8,24},{12,28},{16,0},{20,4},{24,8},{28,12},{1,17},{... | collective-permute-start | bytes 393224 | tf_op jit(solution)/shard_map/ppermute | solution.py:347
  62.8 3.2 %collective-permute-start.12 = (bf16[4,4,16,512]{3,2,1,0:T(8,128)(2,1)S(1)}, bf16[4,4,16,512]{3,2,1,0:T(8,128)(2,1)S(1)}, u32[]{:S(2)}, u32[]{:S(2)}) collective-permute-start(bf16[4,4,16,512]{3,2,1,0:T(8,128)(2,1)S(1)} %get-tuple-element.90), channel_id=1, source_target_pairs={{0,4},{4,0},{8,12},{12,8},{16,20},{20,16},{24,28},{28,24},{1,5},{5... | collective-permute-start | bytes 786440 | tf_op jit(solution)/shard_map/ppermute | solution.py:347
  65.9 4.6 %collective-permute-start.11 = (bf16[4,4,16,512]{3,2,1,0:T(8,128)(2,1)S(1)}, bf16[4,4,16,512]{3,2,1,0:T(8,128)(2,1)S(1)}, u32[]{:S(2)}, u32[]{:S(2)}) collective-permute-start(bf16[4,4,16,512]{3,2,1,0:T(8,128)(2,1)S(1)} %stack_back.1), channel_id=1, source_target_pairs={{0,4},{4,0},{8,12},{12,8},{16,20},{20,16},{24,28},{28,24},{1,5},{5... | collective-permute-start | bytes 786440 | tf_op jit(solution)/shard_map/ppermute | solution.py:347
  66.1 13.8 %collective-permute-start.13 = (bf16[2,4,16,512]{3,2,1,0:T(8,128)(2,1)S(1)}, bf16[2,4,16,512]{3,2,1,0:T(8,128)(2,1)S(1)}, u32[]{:S(2)}, u32[]{:S(2)}) collective-permute-start(bf16[2,4,16,512]{3,2,1,0:T(8,128)(2,1)S(1)} %get-tuple-element.91), channel_id=1, source_target_pairs={{0,24},{4,28},{8,16},{12,20},{16,8},{20,12},{24,0},{28,4},{1,25},{... | collective-permute-start | bytes 393224 | tf_op jit(solution)/shard_map/ppermute | solution.py:347
  68.5 11.3 %collective-permute-start.14 = (bf16[2,4,16,512]{3,2,1,0:T(8,128)(2,1)S(1)}, bf16[2,4,16,512]{3,2,1,0:T(8,128)(2,1)S(1)}, u32[]{:S(2)}, u32[]{:S(2)}) collective-permute-start(bf16[2,4,16,512]{3,2,1,0:T(8,128)(2,1)S(1)} %get-tuple-element.92), channel_id=1, source_target_pairs={{0,8},{4,12},{8,0},{12,4},{16,24},{20,28},{24,16},{28,20},{1,9},{5... | collective-permute-start | bytes 393224 | tf_op jit(solution)/shard_map/ppermute | solution.py:347
  68.5 12.4 %collective-permute-start.15 = (bf16[2,4,16,512]{3,2,1,0:T(8,128)(2,1)S(1)}, bf16[2,4,16,512]{3,2,1,0:T(8,128)(2,1)S(1)}, u32[]{:S(2)}, u32[]{:S(2)}) collective-permute-start(bf16[2,4,16,512]{3,2,1,0:T(8,128)(2,1)S(1)} %get-tuple-element.93), channel_id=1, source_target_pairs={{0,16},{4,20},{8,24},{12,28},{16,0},{20,4},{24,8},{28,12},{1,17},{... | collective-permute-start | bytes 393224 | tf_op jit(solution)/shard_map/ppermute | solution.py:347
  70.6 5.0 %collective-permute-start.16 = (bf16[8,4,512]{2,1,0:T(4,128)(2,1)S(1)}, bf16[8,4,512]{2,1,0:T(4,128)(2,1)S(1)}, u32[]{:S(2)}, u32[]{:S(2)}) collective-permute-start(bf16[8,4,512]{2,1,0:T(4,128)(2,1)S(1)} %get-tuple-element.95), channel_id=1, source_target_pairs={{0,1},{1,2},{2,3},{4,5},{5,6},{6,7},{8,9},{9,10},{10,11},{12,13},{... | collective-permute-start | bytes 98312 | tf_op jit(solution)/shard_map/ppermute | solution.py:428
  74.0 5.8 %collective-permute-start.17 = (bf16[8,4,512]{2,1,0:T(4,128)(2,1)S(1)}, bf16[8,4,512]{2,1,0:T(4,128)(2,1)S(1)}, u32[]{:S(2)}, u32[]{:S(2)}) collective-permute-start(bf16[8,4,512]{2,1,0:T(4,128)(2,1)S(1)} %get-tuple-element.96), channel_id=1, source_target_pairs={{1,0},{2,1},{3,2},{5,4},{6,5},{7,6},{9,8},{10,9},{11,10},{13,12},{... | collective-permute-start | bytes 98312 | tf_op jit(solution)/shard_map/ppermute | solution.py:429

commit v12 on v11

--- a/solution.py
+++ b/solution.py
@@ -395,9 +395,7 @@
     outer = list(attend(inward, hops, True, [*outer_far, outer[-1], outer_other], weights, frames, "attend_outer"))
     near = [inner[-1], inner_other]
     early = project(inward_soon, n_early, [*[inner_far[i] for i in soon], *near], weights, span)
-    outer[:2], early = lax.optimization_barrier((outer[:2], early))
-    for i in range(2, len(far)):
-        outer[i], inner_far[i] = lax.optimization_barrier((outer[i], inner_far[i]))
+    outer, early = lax.optimization_barrier((outer, early))
     outer = [swap(piece, k) for k, piece in zip(hops, outer)]
     *keep, give = attend(
         inward, hops, False, [*inner_far, *near], weights, frames, "attend_inner", n_early, [early]

time: 83.5 us -> 83.7 us (level)
  no operation moved by 1% of the time
where the time goes in v12:
time: 83.7 us; the launch traced here: 83.5 us
  waiting for transfers between devices  34.7 us (41%)
  starting transfers between devices  31.8 us (38%)
  Pallas kernels  15.1 us (18%)
  local copies, waits for them, and re-layouts  1.76 us (2%)
    ppermute x16, waiting for transfers between devices, swap(): lax.ppermute(block, 'frm', [(i, i ^ k) for i in range(count)])  30.2 us
    ppermute x16, starting transfers between devices, swap(): lax.ppermute(block, 'frm', [(i, i ^ k) for i in range(count)])  27.2 us
    pallas_call x2, Pallas kernels, attend(): pl.pallas_call(functools.partial(attend_kernel, inward, hops, paired, n_e...  10.8 us
    ppermute x1, waiting for transfers between devices, local(): right = lax.ppermute(low_side, 'col', [(b, a) for a, b in upward])  4.23 us
    ppermute x1, starting transfers between devices, local(): left = lax.ppermute(high_side, 'col', upward)  3.4 us
    pallas_call x1, Pallas kernels, depth_filter(): pl.pallas_call(functools.partial(filter_kernel, hops), out_shape=jax.Shap...  2.38 us
    unnamed x16, local copies, waits for them, and re-layouts  1.76 us
  transfers between devices with their start and end apart: 18, of which 8 were waited for; matrix products, arithmetic and copies ran while one was open for 0% of the time, Pallas kernels for 15%

profile of v12, /device:TPU:0, one launch (start us, length us, event | category | flops | bytes accessed | tf_op | source)
XLA Modules:
  0.0 83.5 jit_solution(4619515684989778149)
XLA Ops:
  0.0 0.0 copy-start.3
  0.0 0.0 copy-start.2
  0.0 0.0 copy-start.1
  0.0 0.0 copy-start
  0.0 0.0 copy-start.4
  0.0 0.0 copy-start.5
  0.0 1.7 %copy-done.5 = bf16[8,8,32,512]{3,2,1,0:T(8,128)(2,1)S(1)} copy-done((bf16[8,8,32,512]{3,2,1,0:T(8,128)(2,1)S(1)}, bf16[8,8,32,512]{3,2,1,0:T(8,128)(2,1)}, u32[]{:S(2)}) %copy-start.5) | copy-done | bytes 2097176
  1.8 0.0 copy-start.7
  1.8 0.1 cut.1
  1.9 0.5 collective-permute-start
  2.4 1.5 %collective-permute-done.refs_3_.refs_4_ = bf16[4,8,16,512]{3,2,1,0:T(8,128)(2,1)S(1)} collective-permute-done((bf16[4,8,16,512]{3,2,1,0:T(8,128)(2,1)S(1)}, bf16[4,8,16,512]{3,2,1,0:T(8,128)(2,1)S(1)}, u32[]{:S(2)}, u32[]{:S(2)}) %collective-permute-start) | collective-permute-done | bytes 524320 | tf_op jit(solution)/shard_map/ppermute | solution.py:347
  4.0 0.1 join_outer.1
  4.0 0.4 collective-permute-start.2
  4.5 4.7 %collective-permute-start.1 = (bf16[16,16,512]{2,1,0:T(8,128)(2,1)S(1)}, bf16[16,16,512]{2,1,0:T(8,128)(2,1)S(1)}, u32[]{:S(2)}, u32[]{:S(2)}) collective-permute-start(bf16[16,16,512]{2,1,0:T(8,128)(2,1)S(1)} %get-tuple-element.59), channel_id=1, source_target_pairs={{0,24},{4,28},{8,16},{12,20},{16,8},{20,12},{24,0},{28,4},{1,25},{... | collective-permute-start | bytes 786440 | tf_op jit(solution)/shard_map/ppermute | solution.py:347
  9.2 0.0 collective-permute-start.3
  9.2 0.6 collective-permute-start.4
  9.8 0.0 collective-permute-done.2.refs_3_.refs_4_
  9.8 0.1 join_inner.1
  9.8 6.6 %collective-permute-done.1.refs_0_ = bf16[16,16,512]{2,1,0:T(8,128)(2,1)S(1)} collective-permute-done((bf16[16,16,512]{2,1,0:T(8,128)(2,1)S(1)}, bf16[16,16,512]{2,1,0:T(8,128)(2,1)S(1)}, u32[]{:S(2)}, u32[]{:S(2)}) %collective-permute-start.1) | collective-permute-done | bytes 262176 | tf_op jit(solution)/shard_map/ppermute | solution.py:347
  16.4 3.7 %collective-permute-start.5 = (bf16[16,16,512]{2,1,0:T(8,128)(2,1)S(1)}, bf16[16,16,512]{2,1,0:T(8,128)(2,1)S(1)}, u32[]{:S(2)}, u32[]{:S(2)}) collective-permute-start(bf16[16,16,512]{2,1,0:T(8,128)(2,1)S(1)} %get-tuple-element.75), channel_id=1, source_target_pairs={{0,24},{4,28},{8,16},{12,20},{16,8},{20,12},{24,0},{28,4},{1,25},{... | collective-permute-start | bytes 786440 | tf_op jit(solution)/shard_map/ppermute | solution.py:347
  20.2 3.3 %collective-permute-start.6 = (bf16[16,16,512]{2,1,0:T(8,128)(2,1)S(1)}, bf16[16,16,512]{2,1,0:T(8,128)(2,1)S(1)}, u32[]{:S(2)}, u32[]{:S(2)}) collective-permute-start(bf16[16,16,512]{2,1,0:T(8,128)(2,1)S(1)} %get-tuple-element.76), channel_id=1, source_target_pairs={{0,8},{4,12},{8,0},{12,4},{16,24},{20,28},{24,16},{28,20},{1,9},{5... | collective-permute-start | bytes 786440 | tf_op jit(solution)/shard_map/ppermute | solution.py:347
  23.5 0.0 collective-permute-start.9
  23.5 0.0 collective-permute-done.3.refs_1_
  23.5 14.8 %collective-permute-done.4.refs_2_ = bf16[16,16,512]{2,1,0:T(8,128)(2,1)S(1)} collective-permute-done((bf16[16,16,512]{2,1,0:T(8,128)(2,1)S(1)}, bf16[16,16,512]{2,1,0:T(8,128)(2,1)S(1)}, u32[]{:S(2)}, u32[]{:S(2)}) %collective-permute-start.4) | collective-permute-done | bytes 262176 | tf_op jit(solution)/shard_map/ppermute | solution.py:347
  38.3 0.0 copy-done.3
  38.3 0.0 copy-done.2
  38.3 0.0 copy-done.1
  38.3 0.0 copy-done
  38.3 0.0 copy-done.4
  38.3 0.0 copy-done.7
  38.3 5.9 %attend_outer.1 = (bf16[8,16,512]{2,1,0:T(8,128)(2,1)S(1)}, bf16[8,16,512]{2,1,0:T(8,128)(2,1)S(1)}, bf16[8,16,512]{2,1,0:T(8,128)(2,1)S(1)}, bf16[8,16,512]{2,1,0:T(8,128)(2,1)S(1)}) custom-call(bf16[16,16,512]{2,1,0:T(8,128)(2,1)S(1)} %collective-permute-done.1.refs_0_, bf16[16,16,512]{2,1,0:T(8,128)(2,1)S(1)} %collective-permute-done.3.refs_1_, ...), custom_call_target="tpu_custom_call" | custom-call | flops 1 | bytes 1 | tf_op jit(solution)/shard_map/attend_outer/pallas_call | solution.py:214
  44.3 0.0 collective-permute-done.5.refs_0_
  44.3 0.0 collective-permute-done.6.refs_1_
  44.3 1.5 %project_early.1.refs_11_ = bf16[3,768,512]{2,1,0:T(8,128)(2,1)S(1)} custom-call(bf16[16,16,512]{2,1,0:T(8,128)(2,1)S(1)} %collective-permute-done.5.refs_0_, bf16[16,16,512]{2,1,0:T(8,128)(2,1)S(1)} %collective-permute-done.6.refs_1_, bf16[8,16,512]{2,1,0:T(8,128)(2,1)S(1)} %get-tuple-element.77.refs_2_.refs_3_, ...), custom_call_target="tpu_custom_call" | custom-call | flops 1207959552 | bytes 3145728 | tf_op jit(solution)/shard_map/project_early/pallas_call | solution.py:102
  45.8 0.0 copy-start.6
  45.8 2.5 %collective-permute-start.7 = (bf16[8,16,512]{2,1,0:T(8,128)(2,1)S(1)}, bf16[8,16,512]{2,1,0:T(8,128)(2,1)S(1)}, u32[]{:S(2)}, u32[]{:S(2)}) collective-permute-start(bf16[8,16,512]{2,1,0:T(8,128)(2,1)S(1)} %get-tuple-element.78), channel_id=1, source_target_pairs={{0,24},{4,28},{8,16},{12,20},{16,8},{20,12},{24,0},{28,4},{1,25},{... | collective-permute-start | bytes 393224 | tf_op jit(solution)/shard_map/ppermute | solution.py:347
  48.3 6.3 %collective-permute-start.8 = (bf16[8,16,512]{2,1,0:T(8,128)(2,1)S(1)}, bf16[8,16,512]{2,1,0:T(8,128)(2,1)S(1)}, u32[]{:S(2)}, u32[]{:S(2)}) collective-permute-start(bf16[8,16,512]{2,1,0:T(8,128)(2,1)S(1)} %get-tuple-element.79), channel_id=1, source_target_pairs={{0,8},{4,12},{8,0},{12,4},{16,24},{20,28},{24,16},{28,20},{1,9},{5... | collective-permute-start | bytes 393224 | tf_op jit(solution)/shard_map/ppermute | solution.py:347
  54.6 0.0 collective-permute-start.10
  54.6 6.2 %collective-permute-done.9.refs_2_ = bf16[16,16,512]{2,1,0:T(8,128)(2,1)S(1)} collective-permute-done((bf16[16,16,512]{2,1,0:T(8,128)(2,1)S(1)}, bf16[16,16,512]{2,1,0:T(8,128)(2,1)S(1)}, u32[]{:S(2)}, u32[]{:S(2)}) %collective-permute-start.9) | collective-permute-done | bytes 262176 | tf_op jit(solution)/shard_map/ppermute | solution.py:347
  60.8 4.8 %attend_inner.1 = (bf16[4,16,512]{2,1,0:T(8,128)(2,1)S(1)}, bf16[4,16,512]{2,1,0:T(8,128)(2,1)S(1)}, bf16[4,16,512]{2,1,0:T(8,128)(2,1)S(1)}, bf16[4,16,512]{2,1,0:T(8,128)(2,1)S(1)}, bf16[4,4,16,512]{3,2,1,0:T(8,128)(2,1)S(1)}) custom-call(bf16[16,16,512]{2,1,0:T(8,128)(2,1)S(1)} %collective-permute-done.5.refs_0_, ...), custom_call_target="tpu_custom_call" | custom-call | flops 1 | bytes 1 | tf_op jit(solution)/shard_map/attend_inner/pallas_call | solution.py:214
  65.7 0.0 collective-permute-done.7.refs_0_
  65.7 0.0 collective-permute-done.8.refs_1_
  65.7 0.1 collective-permute-start.12
  65.8 0.1 collective-permute-done.10.refs_2_
  65.9 0.4 collective-permute-start.11
  66.3 0.9 %collective-permute-done.12.refs_3_.refs_9_ = bf16[4,4,16,512]{3,2,1,0:T(8,128)(2,1)S(1)} collective-permute-done((bf16[4,4,16,512]{3,2,1,0:T(8,128)(2,1)S(1)}, bf16[4,4,16,512]{3,2,1,0:T(8,128)(2,1)S(1)}, u32[]{:S(2)}, u32[]{:S(2)}) %collective-permute-start.12) | collective-permute-done | bytes 262176 | tf_op jit(solution)/shard_map/ppermute | solution.py:347
  67.3 2.5 %collective-permute-start.13 = (bf16[2,4,16,512]{3,2,1,0:T(8,128)(2,1)S(1)}, bf16[2,4,16,512]{3,2,1,0:T(8,128)(2,1)S(1)}, u32[]{:S(2)}, u32[]{:S(2)}) collective-permute-start(bf16[2,4,16,512]{3,2,1,0:T(8,128)(2,1)S(1)} %get-tuple-element.91), channel_id=1, source_target_pairs={{0,24},{4,28},{8,16},{12,20},{16,8},{20,12},{24,0},{28,4},{1,25},{... | collective-permute-start | bytes 393224 | tf_op jit(solution)/shard_map/ppermute | solution.py:347
  69.8 0.0 collective-permute-start.14
  69.9 1.9 %collective-permute-start.15 = (bf16[2,4,16,512]{3,2,1,0:T(8,128)(2,1)S(1)}, bf16[2,4,16,512]{3,2,1,0:T(8,128)(2,1)S(1)}, u32[]{:S(2)}, u32[]{:S(2)}) collective-permute-start(bf16[2,4,16,512]{3,2,1,0:T(8,128)(2,1)S(1)} %get-tuple-element.93), channel_id=1, source_target_pairs={{0,16},{4,20},{8,24},{12,28},{16,0},{20,4},{24,8},{28,12},{1,17},{... | collective-permute-start | bytes 393224 | tf_op jit(solution)/shard_map/ppermute | solution.py:347
  71.8 0.0 collective-permute-done.11.refs_4_
  71.8 0.1 rim.1
  71.9 3.4 %collective-permute-start.16 = (bf16[8,4,512]{2,1,0:T(4,128)(2,1)S(1)}, bf16[8,4,512]{2,1,0:T(4,128)(2,1)S(1)}, u32[]{:S(2)}, u32[]{:S(2)}) collective-permute-start(bf16[8,4,512]{2,1,0:T(4,128)(2,1)S(1)} %get-tuple-element.95), channel_id=1, source_target_pairs={{0,1},{1,2},{2,3},{4,5},{5,6},{6,7},{8,9},{9,10},{10,11},{12,13},{... | collective-permute-start | bytes 98312 | tf_op jit(solution)/shard_map/ppermute | solution.py:426
  75.3 1.3 %collective-permute-start.17 = (bf16[8,4,512]{2,1,0:T(4,128)(2,1)S(1)}, bf16[8,4,512]{2,1,0:T(4,128)(2,1)S(1)}, u32[]{:S(2)}, u32[]{:S(2)}) collective-permute-start(bf16[8,4,512]{2,1,0:T(4,128)(2,1)S(1)} %get-tuple-element.96), channel_id=1, source_target_pairs={{1,0},{2,1},{3,2},{5,4},{6,5},{7,6},{9,8},{10,9},{11,10},{13,12},{... | collective-permute-start | bytes 98312 | tf_op jit(solution)/shard_map/ppermute | solution.py:427
  76.6 0.3 collective-permute-done.16.refs_10_
  76.9 4.2 %collective-permute-done.17.refs_11_ = bf16[8,4,512]{2,1,0:T(4,128)(2,1)S(1)} collective-permute-done((bf16[8,4,512]{2,1,0:T(4,128)(2,1)S(1)}, bf16[8,4,512]{2,1,0:T(4,128)(2,1)S(1)}, u32[]{:S(2)}, u32[]{:S(2)}) %collective-permute-start.17) | collective-permute-done | bytes 32800 | tf_op jit(solution)/shard_map/ppermute | solution.py:427
  81.1 0.0 collective-permute-done.13.refs_5_
  81.1 0.0 collective-permute-done.14.refs_6_
  81.1 0.0 collective-permute-done.15.refs_7_
  81.1 0.0 copy-done.6
  81.1 2.4 %depth_filter.1 = bf16[4,8,32,512]{3,2,1,0:T(8,128)(2,1)} custom-call(bf16[8,16,512]{2,1,0:T(8,128)(2,1)S(1)} %collective-permute-done.7.refs_0_, bf16[8,16,512]{2,1,0:T(8,128)(2,1)S(1)} %collective-permute-done.8.refs_1_, bf16[8,16,512]{2,1,0:T(8,128)(2,1)S(1)} %collective-permute-done.10.refs_2_, bf16[8,16,512]{2,1,0:T(8,128)(2,1)S(1)} %get-tuple-element.86.refs_3_, ...), custom_call_target="tpu_custom_call" | custom-call | flops 1 | bytes 1 | tf_op jit(solution)/shard_map/depth_filter/pallas_call | solution.py:320
  (2 shorter events, 0.0 us)
Async XLA Ops:
  0.0 38.3 %copy-start.3 = (bf16[512,512]{1,0:T(8,128)(2,1)S(1)}, bf16[512,512]{1,0:T(8,128)(2,1)}, u32[]{:S(2)}) copy-start(bf16[512,512]{1,0:T(8,128)(2,1)} %refs_8_.3) | copy-start | bytes 1572868
  0.0 38.3 %copy-start.2 = (bf16[512,512]{1,0:T(8,128)(2,1)S(1)}, bf16[512,512]{1,0:T(8,128)(2,1)}, u32[]{:S(2)}) copy-start(bf16[512,512]{1,0:T(8,128)(2,1)} %refs_7_.5) | copy-start | bytes 1572868
  0.0 38.3 %copy-start.1 = (bf16[512,512]{1,0:T(8,128)(2,1)S(1)}, bf16[512,512]{1,0:T(8,128)(2,1)}, u32[]{:S(2)}) copy-start(bf16[512,512]{1,0:T(8,128)(2,1)} %refs_6_.5) | copy-start | bytes 1572868
  0.0 38.3 %copy-start = (bf16[3,512,512]{2,1,0:T(8,128)(2,1)S(1)}, bf16[3,512,512]{2,1,0:T(8,128)(2,1)}, u32[]{:S(2)}) copy-start(bf16[3,512,512]{2,1,0:T(8,128)(2,1)} %refs_10_.3) | copy-start | bytes 4718596
  0.0 38.3 %copy-start.4 = (bf16[512,512]{1,0:T(8,128)(2,1)S(1)}, bf16[512,512]{1,0:T(8,128)(2,1)}, u32[]{:S(2)}) copy-start(bf16[512,512]{1,0:T(8,128)(2,1)} %refs_9_.3) | copy-start | bytes 1572868
  0.0 1.7 %copy-start.5 = (bf16[8,8,32,512]{3,2,1,0:T(8,128)(2,1)S(1)}, bf16[8,8,32,512]{3,2,1,0:T(8,128)(2,1)}, u32[]{:S(2)}) copy-start(bf16[8,8,32,512]{3,2,1,0:T(8,128)(2,1)} %video.1) | copy-start | bytes 6291460
  1.8 36.5 %copy-start.7 = (f32[512]{0:T(512)S(1)}, f32[512]{0:T(512)}, u32[]{:S(2)}) copy-start(f32[512]{0:T(512)} %param.9) | copy-start | bytes 6148
  1.9 2.1 %collective-permute-start = (bf16[4,8,16,512]{3,2,1,0:T(8,128)(2,1)S(1)}, bf16[4,8,16,512]{3,2,1,0:T(8,128)(2,1)S(1)}, u32[]{:S(2)}, u32[]{:S(2)}) collective-permute-start(bf16[4,8,16,512]{3,2,1,0:T(8,128)(2,1)S(1)} %get-tuple-element.54), channel_id=1, source_target_pairs={{0,4},{4,0},{8,12},{12,8},{16,20},{20,16},{24,28},{28,24},{1,5},{5... | collective-permute-start | bytes 1572872 | tf_op jit(solution)/shard_map/ppermute | solution.py:347
  4.0 5.8 %collective-permute-start.2 = (bf16[4,8,16,512]{3,2,1,0:T(8,128)(2,1)S(1)}, bf16[4,8,16,512]{3,2,1,0:T(8,128)(2,1)S(1)}, u32[]{:S(2)}, u32[]{:S(2)}) collective-permute-start(bf16[4,8,16,512]{3,2,1,0:T(8,128)(2,1)S(1)} %get-tuple-element.63), channel_id=1, source_target_pairs={{0,4},{4,0},{8,12},{12,8},{16,20},{20,16},{24,28},{28,24},{1,5},{5... | collective-permute-start | bytes 1572872 | tf_op jit(solution)/shard_map/ppermute | solution.py:347
  4.5 12.0 %collective-permute-start.1 = (bf16[16,16,512]{2,1,0:T(8,128)(2,1)S(1)}, bf16[16,16,512]{2,1,0:T(8,128)(2,1)S(1)}, u32[]{:S(2)}, u32[]{:S(2)}) collective-permute-start(bf16[16,16,512]{2,1,0:T(8,128)(2,1)S(1)} %get-tuple-element.59), channel_id=1, source_target_pairs={{0,24},{4,28},{8,16},{12,20},{16,8},{20,12},{24,0},{28,4},{1,25},{... | collective-permute-start | bytes 786440 | tf_op jit(solution)/shard_map/ppermute | solution.py:347
  9.2 14.3 %collective-permute-start.3 = (bf16[16,16,512]{2,1,0:T(8,128)(2,1)S(1)}, bf16[16,16,512]{2,1,0:T(8,128)(2,1)S(1)}, u32[]{:S(2)}, u32[]{:S(2)}) collective-permute-start(bf16[16,16,512]{2,1,0:T(8,128)(2,1)S(1)} %get-tuple-element.68), channel_id=1, source_target_pairs={{0,8},{4,12},{8,0},{12,4},{16,24},{20,28},{24,16},{28,20},{1,9},{5... | collective-permute-start | bytes 786440 | tf_op jit(solution)/shard_map/ppermute | solution.py:347
  9.2 29.0 %collective-permute-start.4 = (bf16[16,16,512]{2,1,0:T(8,128)(2,1)S(1)}, bf16[16,16,512]{2,1,0:T(8,128)(2,1)S(1)}, u32[]{:S(2)}, u32[]{:S(2)}) collective-permute-start(bf16[16,16,512]{2,1,0:T(8,128)(2,1)S(1)} %get-tuple-element.69), channel_id=1, source_target_pairs={{0,16},{4,20},{8,24},{12,28},{16,0},{20,4},{24,8},{28,12},{1,17},{... | collective-permute-start | bytes 786440 | tf_op jit(solution)/shard_map/ppermute | solution.py:347
  16.4 27.8 %collective-permute-start.5 = (bf16[16,16,512]{2,1,0:T(8,128)(2,1)S(1)}, bf16[16,16,512]{2,1,0:T(8,128)(2,1)S(1)}, u32[]{:S(2)}, u32[]{:S(2)}) collective-permute-start(bf16[16,16,512]{2,1,0:T(8,128)(2,1)S(1)} %get-tuple-element.75), channel_id=1, source_target_pairs={{0,24},{4,28},{8,16},{12,20},{16,8},{20,12},{24,0},{28,4},{1,25},{... | collective-permute-start | bytes 786440 | tf_op jit(solution)/shard_map/ppermute | solution.py:347
  20.2 24.1 %collective-permute-start.6 = (bf16[16,16,512]{2,1,0:T(8,128)(2,1)S(1)}, bf16[16,16,512]{2,1,0:T(8,128)(2,1)S(1)}, u32[]{:S(2)}, u32[]{:S(2)}) collective-permute-start(bf16[16,16,512]{2,1,0:T(8,128)(2,1)S(1)} %get-tuple-element.76), channel_id=1, source_target_pairs={{0,8},{4,12},{8,0},{12,4},{16,24},{20,28},{24,16},{28,20},{1,9},{5... | collective-permute-start | bytes 786440 | tf_op jit(solution)/shard_map/ppermute | solution.py:347
  23.5 37.3 %collective-permute-start.9 = (bf16[16,16,512]{2,1,0:T(8,128)(2,1)S(1)}, bf16[16,16,512]{2,1,0:T(8,128)(2,1)S(1)}, u32[]{:S(2)}, u32[]{:S(2)}) collective-permute-start(bf16[16,16,512]{2,1,0:T(8,128)(2,1)S(1)} %get-tuple-element.80), channel_id=1, source_target_pairs={{0,16},{4,20},{8,24},{12,28},{16,0},{20,4},{24,8},{28,12},{1,17},{... | collective-permute-start | bytes 786440 | tf_op jit(solution)/shard_map/ppermute | solution.py:347
  45.8 35.3 %copy-start.6 = (f32[3,3,512]{2,1,0:T(4,128)S(1)}, f32[3,3,512]{2,1,0:T(4,128)}, u32[]{:S(2)}) copy-start(f32[3,3,512]{2,1,0:T(4,128)} %refs_12_.1) | copy-start | bytes 55300
  45.8 19.9 %collective-permute-start.7 = (bf16[8,16,512]{2,1,0:T(8,128)(2,1)S(1)}, bf16[8,16,512]{2,1,0:T(8,128)(2,1)S(1)}, u32[]{:S(2)}, u32[]{:S(2)}) collective-permute-start(bf16[8,16,512]{2,1,0:T(8,128)(2,1)S(1)} %get-tuple-element.78), channel_id=1, source_target_pairs={{0,24},{4,28},{8,16},{12,20},{16,8},{20,12},{24,0},{28,4},{1,25},{... | collective-permute-start | bytes 393224 | tf_op jit(solution)/shard_map/ppermute | solution.py:347
  48.3 17.3 %collective-permute-start.8 = (bf16[8,16,512]{2,1,0:T(8,128)(2,1)S(1)}, bf16[8,16,512]{2,1,0:T(8,128)(2,1)S(1)}, u32[]{:S(2)}, u32[]{:S(2)}) collective-permute-start(bf16[8,16,512]{2,1,0:T(8,128)(2,1)S(1)} %get-tuple-element.79), channel_id=1, source_target_pairs={{0,8},{4,12},{8,0},{12,4},{16,24},{20,28},{24,16},{28,20},{1,9},{5... | collective-permute-start | bytes 393224 | tf_op jit(solution)/shard_map/ppermute | solution.py:347
  54.6 11.3 %collective-permute-start.10 = (bf16[8,16,512]{2,1,0:T(8,128)(2,1)S(1)}, bf16[8,16,512]{2,1,0:T(8,128)(2,1)S(1)}, u32[]{:S(2)}, u32[]{:S(2)}) collective-permute-start(bf16[8,16,512]{2,1,0:T(8,128)(2,1)S(1)} %get-tuple-element.85), channel_id=1, source_target_pairs={{0,16},{4,20},{8,24},{12,28},{16,0},{20,4},{24,8},{28,12},{1,17},{... | collective-permute-start | bytes 393224 | tf_op jit(solution)/shard_map/ppermute | solution.py:347
  65.7 1.6 %collective-permute-start.12 = (bf16[4,4,16,512]{3,2,1,0:T(8,128)(2,1)S(1)}, bf16[4,4,16,512]{3,2,1,0:T(8,128)(2,1)S(1)}, u32[]{:S(2)}, u32[]{:S(2)}) collective-permute-start(bf16[4,4,16,512]{3,2,1,0:T(8,128)(2,1)S(1)} %get-tuple-element.90), channel_id=1, source_target_pairs={{0,4},{4,0},{8,12},{12,8},{16,20},{20,16},{24,28},{28,24},{1,5},{5... | collective-permute-start | bytes 786440 | tf_op jit(solution)/shard_map/ppermute | solution.py:347
  65.9 5.9 %collective-permute-start.11 = (bf16[4,4,16,512]{3,2,1,0:T(8,128)(2,1)S(1)}, bf16[4,4,16,512]{3,2,1,0:T(8,128)(2,1)S(1)}, u32[]{:S(2)}, u32[]{:S(2)}) collective-permute-start(bf16[4,4,16,512]{3,2,1,0:T(8,128)(2,1)S(1)} %stack_back.1), channel_id=1, source_target_pairs={{0,4},{4,0},{8,12},{12,8},{16,20},{20,16},{24,28},{28,24},{1,5},{5... | collective-permute-start | bytes 786440 | tf_op jit(solution)/shard_map/ppermute | solution.py:347
  67.3 13.8 %collective-permute-start.13 = (bf16[2,4,16,512]{3,2,1,0:T(8,128)(2,1)S(1)}, bf16[2,4,16,512]{3,2,1,0:T(8,128)(2,1)S(1)}, u32[]{:S(2)}, u32[]{:S(2)}) collective-permute-start(bf16[2,4,16,512]{3,2,1,0:T(8,128)(2,1)S(1)} %get-tuple-element.91), channel_id=1, source_target_pairs={{0,24},{4,28},{8,16},{12,20},{16,8},{20,12},{24,0},{28,4},{1,25},{... | collective-permute-start | bytes 393224 | tf_op jit(solution)/shard_map/ppermute | solution.py:347
  69.8 11.3 %collective-permute-start.14 = (bf16[2,4,16,512]{3,2,1,0:T(8,128)(2,1)S(1)}, bf16[2,4,16,512]{3,2,1,0:T(8,128)(2,1)S(1)}, u32[]{:S(2)}, u32[]{:S(2)}) collective-permute-start(bf16[2,4,16,512]{3,2,1,0:T(8,128)(2,1)S(1)} %get-tuple-element.92), channel_id=1, source_target_pairs={{0,8},{4,12},{8,0},{12,4},{16,24},{20,28},{24,16},{28,20},{1,9},{5... | collective-permute-start | bytes 393224 | tf_op jit(solution)/shard_map/ppermute | solution.py:347
  69.9 11.3 %collective-permute-start.15 = (bf16[2,4,16,512]{3,2,1,0:T(8,128)(2,1)S(1)}, bf16[2,4,16,512]{3,2,1,0:T(8,128)(2,1)S(1)}, u32[]{:S(2)}, u32[]{:S(2)}) collective-permute-start(bf16[2,4,16,512]{3,2,1,0:T(8,128)(2,1)S(1)} %get-tuple-element.93), channel_id=1, source_target_pairs={{0,16},{4,20},{8,24},{12,28},{16,0},{20,4},{24,8},{28,12},{1,17},{... | collective-permute-start | bytes 393224 | tf_op jit(solution)/shard_map/ppermute | solution.py:347
  71.9 5.0 %collective-permute-start.16 = (bf16[8,4,512]{2,1,0:T(4,128)(2,1)S(1)}, bf16[8,4,512]{2,1,0:T(4,128)(2,1)S(1)}, u32[]{:S(2)}, u32[]{:S(2)}) collective-permute-start(bf16[8,4,512]{2,1,0:T(4,128)(2,1)S(1)} %get-tuple-element.95), channel_id=1, source_target_pairs={{0,1},{1,2},{2,3},{4,5},{5,6},{6,7},{8,9},{9,10},{10,11},{12,13},{... | collective-permute-start | bytes 98312 | tf_op jit(solution)/shard_map/ppermute | solution.py:426
  75.3 5.8 %collective-permute-start.17 = (bf16[8,4,512]{2,1,0:T(4,128)(2,1)S(1)}, bf16[8,4,512]{2,1,0:T(4,128)(2,1)S(1)}, u32[]{:S(2)}, u32[]{:S(2)}) collective-permute-start(bf16[8,4,512]{2,1,0:T(4,128)(2,1)S(1)} %get-tuple-element.96), channel_id=1, source_target_pairs={{1,0},{2,1},{3,2},{5,4},{6,5},{7,6},{9,8},{10,9},{11,10},{13,12},{... | collective-permute-start | bytes 98312 | tf_op jit(solution)/shard_map/ppermute | solution.py:427

commit v13 on v11

--- a/solution.py
+++ b/solution.py
@@ -265,13 +265,13 @@
     )(*pieces, taken)
 
 
-def filter_kernel(hops, *refs):
+def filter_kernel(hops, back, *refs):
     count = len(hops) + 1
     left, right, w_depth, result, outer, inner, out, sems = refs[2 * count :]
     me = lax.axis_index("frm")
     for k, piece in outer_rows(hops, refs[: count - 1], refs[count - 1]):
         outer[me ^ k] = piece[...]
-    for k, piece in inner_rows(hops, refs[count : 2 * count - 1], refs[2 * count - 1]):
+    for k, piece in inner_rows(back, refs[count : 2 * count - 1], refs[2 * count - 1]):
         inner[me ^ k] = piece[...]
     frames, height, cols, channels = out.shape
     edge = cols // 4
@@ -312,13 +312,13 @@
         copy.wait()
 
 
-def depth_filter(hops, outer, inner, left, right, w_depth):
+def depth_filter(hops, back, outer, inner, left, right, w_depth):
     height, frames, channels = left.shape
     width = inner[-1].shape[2]
     cols = 2 * width
     size = frames * height * cols * channels
     return pl.pallas_call(
-        functools.partial(filter_kernel, hops),
+        functools.partial(filter_kernel, hops, back),
         out_shape=jax.ShapeDtypeStruct((frames, height, cols, channels), jnp.bfloat16),
         in_specs=[INSIDE] * (2 * len(hops) + 5),
         out_specs=pl.BlockSpec(memory_space=pl.ANY),
@@ -414,7 +414,9 @@
         return pairs
 
     inner = gather(joined_back, [*keep[:-1], taken], [(2, made, width, channels)] * len(far), "join_back")
-    inner = [swap(piece, k) for k, piece in zip(hops, inner)]
+    turn = sorted(range(len(far)), key=lambda i: far[i] == 1)
+    back = [hops[i] for i in turn] + [0]
+    inner = [swap(inner[i], hops[i]) for i in turn]
 
     def for_mate(ins, outs):
         _, core = place()
@@ -427,7 +429,7 @@
     upward = [(i, i + 1) for i in range(line - 1)]
     left = lax.ppermute(high_side, "col", upward)
     right = lax.ppermute(low_side, "col", [(b, a) for a, b in upward])
-    return depth_filter(hops, [*outer, halves], [*inner, keep[-1], taken], left, right, w_depth)
+    return depth_filter(hops, back, [*outer, halves], [*inner, keep[-1], taken], left, right, w_depth)
 
 
 def solution(mesh):

time: 83.5 us -> 83.5 us (level)
  no operation moved by 1% of the time
where the time goes in v13:
time: 83.5 us; the launch traced here: 83.3 us
  waiting for transfers between devices  34.9 us (42%)
  starting transfers between devices  31.5 us (38%)
  Pallas kernels  15.1 us (18%)
  local copies, waits for them, and re-layouts  1.76 us (2%)
    ppermute x16, waiting for transfers between devices, swap(): lax.ppermute(block, 'frm', [(i, i ^ k) for i in range(count)])  30.4 us
    ppermute x16, starting transfers between devices, swap(): lax.ppermute(block, 'frm', [(i, i ^ k) for i in range(count)])  26.8 us
    pallas_call x2, Pallas kernels, attend(): pl.pallas_call(functools.partial(attend_kernel, inward, hops, paired, n_e...  10.8 us
    ppermute x1, waiting for transfers between devices, local(): right = lax.ppermute(low_side, 'col', [(b, a) for a, b in upward])  4.23 us
    ppermute x1, starting transfers between devices, local(): left = lax.ppermute(high_side, 'col', upward)  3.4 us
    pallas_call x1, Pallas kernels, depth_filter(): pl.pallas_call(functools.partial(filter_kernel, hops, back), out_shape=ja...  2.37 us
    unnamed x16, local copies, waits for them, and re-layouts  1.76 us
  transfers between devices with their start and end apart: 18, of which 8 were waited for; matrix products, arithmetic and copies ran while one was open for 0% of the time, Pallas kernels for 15%

profile of v13, /device:TPU:0, one launch (start us, length us, event | category | flops | bytes accessed | tf_op | source)
XLA Modules:
  0.0 83.3 jit_solution(10416091736839147348)
XLA Ops:
  0.0 0.0 copy-start.3
  0.0 0.0 copy-start.2
  0.0 0.0 copy-start.1
  0.0 0.0 copy-start
  0.0 0.0 copy-start.4
  0.0 0.0 copy-start.5
  0.0 1.7 %copy-done.5 = bf16[8,8,32,512]{3,2,1,0:T(8,128)(2,1)S(1)} copy-done((bf16[8,8,32,512]{3,2,1,0:T(8,128)(2,1)S(1)}, bf16[8,8,32,512]{3,2,1,0:T(8,128)(2,1)}, u32[]{:S(2)}) %copy-start.5) | copy-done | bytes 2097176
  1.8 0.0 copy-start.7
  1.8 0.1 cut.1
  1.9 0.5 collective-permute-start
  2.4 1.5 %collective-permute-done.refs_3_.refs_4_ = bf16[4,8,16,512]{3,2,1,0:T(8,128)(2,1)S(1)} collective-permute-done((bf16[4,8,16,512]{3,2,1,0:T(8,128)(2,1)S(1)}, bf16[4,8,16,512]{3,2,1,0:T(8,128)(2,1)S(1)}, u32[]{:S(2)}, u32[]{:S(2)}) %collective-permute-start) | collective-permute-done | bytes 524320 | tf_op jit(solution)/shard_map/ppermute | solution.py:347
  4.0 0.1 join_outer.1
  4.0 0.4 collective-permute-start.2
  4.5 4.7 %collective-permute-start.1 = (bf16[16,16,512]{2,1,0:T(8,128)(2,1)S(1)}, bf16[16,16,512]{2,1,0:T(8,128)(2,1)S(1)}, u32[]{:S(2)}, u32[]{:S(2)}) collective-permute-start(bf16[16,16,512]{2,1,0:T(8,128)(2,1)S(1)} %get-tuple-element.59), channel_id=1, source_target_pairs={{0,24},{4,28},{8,16},{12,20},{16,8},{20,12},{24,0},{28,4},{1,25},{... | collective-permute-start | bytes 786440 | tf_op jit(solution)/shard_map/ppermute | solution.py:347
  9.2 0.0 collective-permute-start.3
  9.2 0.6 collective-permute-start.4
  9.8 0.0 collective-permute-done.2.refs_3_.refs_4_
  9.8 0.1 join_inner.1
  9.8 6.6 %collective-permute-done.1.refs_0_ = bf16[16,16,512]{2,1,0:T(8,128)(2,1)S(1)} collective-permute-done((bf16[16,16,512]{2,1,0:T(8,128)(2,1)S(1)}, bf16[16,16,512]{2,1,0:T(8,128)(2,1)S(1)}, u32[]{:S(2)}, u32[]{:S(2)}) %collective-permute-start.1) | collective-permute-done | bytes 262176 | tf_op jit(solution)/shard_map/ppermute | solution.py:347
  16.4 3.7 %collective-permute-start.5 = (bf16[16,16,512]{2,1,0:T(8,128)(2,1)S(1)}, bf16[16,16,512]{2,1,0:T(8,128)(2,1)S(1)}, u32[]{:S(2)}, u32[]{:S(2)}) collective-permute-start(bf16[16,16,512]{2,1,0:T(8,128)(2,1)S(1)} %get-tuple-element.73), channel_id=1, source_target_pairs={{0,24},{4,28},{8,16},{12,20},{16,8},{20,12},{24,0},{28,4},{1,25},{... | collective-permute-start | bytes 786440 | tf_op jit(solution)/shard_map/ppermute | solution.py:347
  20.2 3.3 %collective-permute-start.6 = (bf16[16,16,512]{2,1,0:T(8,128)(2,1)S(1)}, bf16[16,16,512]{2,1,0:T(8,128)(2,1)S(1)}, u32[]{:S(2)}, u32[]{:S(2)}) collective-permute-start(bf16[16,16,512]{2,1,0:T(8,128)(2,1)S(1)} %get-tuple-element.74), channel_id=1, source_target_pairs={{0,8},{4,12},{8,0},{12,4},{16,24},{20,28},{24,16},{28,20},{1,9},{5... | collective-permute-start | bytes 786440 | tf_op jit(solution)/shard_map/ppermute | solution.py:347
  23.5 0.0 collective-permute-start.9
  23.5 0.0 collective-permute-done.3.refs_1_
  23.5 14.8 %collective-permute-done.4.refs_2_ = bf16[16,16,512]{2,1,0:T(8,128)(2,1)S(1)} collective-permute-done((bf16[16,16,512]{2,1,0:T(8,128)(2,1)S(1)}, bf16[16,16,512]{2,1,0:T(8,128)(2,1)S(1)}, u32[]{:S(2)}, u32[]{:S(2)}) %collective-permute-start.4) | collective-permute-done | bytes 262176 | tf_op jit(solution)/shard_map/ppermute | solution.py:347
  38.3 0.0 copy-done.3
  38.3 0.0 copy-done.2
  38.3 0.0 copy-done.1
  38.3 0.0 copy-done
  38.3 0.0 copy-done.4
  38.3 0.0 copy-done.7
  38.3 5.9 %attend_outer.1 = (bf16[8,16,512]{2,1,0:T(8,128)(2,1)S(1)}, bf16[8,16,512]{2,1,0:T(8,128)(2,1)S(1)}, bf16[8,16,512]{2,1,0:T(8,128)(2,1)S(1)}, bf16[8,16,512]{2,1,0:T(8,128)(2,1)S(1)}) custom-call(bf16[16,16,512]{2,1,0:T(8,128)(2,1)S(1)} %collective-permute-done.1.refs_0_, bf16[16,16,512]{2,1,0:T(8,128)(2,1)S(1)} %collective-permute-done.3.refs_1_, ...), custom_call_target="tpu_custom_call" | custom-call | flops 1 | bytes 1 | tf_op jit(solution)/shard_map/attend_outer/pallas_call | solution.py:214
  44.3 0.0 collective-permute-done.5.refs_0_
  44.3 0.0 collective-permute-done.6.refs_1_
  44.3 1.5 %project_early.1.refs_11_ = bf16[3,768,512]{2,1,0:T(8,128)(2,1)S(1)} custom-call(bf16[16,16,512]{2,1,0:T(8,128)(2,1)S(1)} %collective-permute-done.5.refs_0_, bf16[16,16,512]{2,1,0:T(8,128)(2,1)S(1)} %collective-permute-done.6.refs_1_, bf16[8,16,512]{2,1,0:T(8,128)(2,1)S(1)} %get-tuple-element.75.refs_2_.refs_3_, ...), custom_call_target="tpu_custom_call" | custom-call | flops 1207959552 | bytes 3145728 | tf_op jit(solution)/shard_map/project_early/pallas_call | solution.py:102
  45.8 2.5 %collective-permute-start.7 = (bf16[8,16,512]{2,1,0:T(8,128)(2,1)S(1)}, bf16[8,16,512]{2,1,0:T(8,128)(2,1)S(1)}, u32[]{:S(2)}, u32[]{:S(2)}) collective-permute-start(bf16[8,16,512]{2,1,0:T(8,128)(2,1)S(1)} %get-tuple-element.76), channel_id=1, source_target_pairs={{0,24},{4,28},{8,16},{12,20},{16,8},{20,12},{24,0},{28,4},{1,25},{... | collective-permute-start | bytes 393224 | tf_op jit(solution)/shard_map/ppermute | solution.py:347
  48.3 6.3 %collective-permute-start.8 = (bf16[8,16,512]{2,1,0:T(8,128)(2,1)S(1)}, bf16[8,16,512]{2,1,0:T(8,128)(2,1)S(1)}, u32[]{:S(2)}, u32[]{:S(2)}) collective-permute-start(bf16[8,16,512]{2,1,0:T(8,128)(2,1)S(1)} %get-tuple-element.77), channel_id=1, source_target_pairs={{0,8},{4,12},{8,0},{12,4},{16,24},{20,28},{24,16},{28,20},{1,9},{5... | collective-permute-start | bytes 393224 | tf_op jit(solution)/shard_map/ppermute | solution.py:347
  54.6 3.4 %collective-permute-done.9.refs_2_ = bf16[16,16,512]{2,1,0:T(8,128)(2,1)S(1)} collective-permute-done((bf16[16,16,512]{2,1,0:T(8,128)(2,1)S(1)}, bf16[16,16,512]{2,1,0:T(8,128)(2,1)S(1)}, u32[]{:S(2)}, u32[]{:S(2)}) %collective-permute-start.9) | collective-permute-done | bytes 262176 | tf_op jit(solution)/shard_map/ppermute | solution.py:347
  58.0 0.0 copy-start.6
  58.0 0.0 collective-permute-start.10
  58.0 4.8 %attend_inner.1 = (bf16[4,16,512]{2,1,0:T(8,128)(2,1)S(1)}, bf16[4,16,512]{2,1,0:T(8,128)(2,1)S(1)}, bf16[4,16,512]{2,1,0:T(8,128)(2,1)S(1)}, bf16[4,16,512]{2,1,0:T(8,128)(2,1)S(1)}, bf16[4,4,16,512]{3,2,1,0:T(8,128)(2,1)S(1)}) custom-call(bf16[16,16,512]{2,1,0:T(8,128)(2,1)S(1)} %collective-permute-done.5.refs_0_, ...), custom_call_target="tpu_custom_call" | custom-call | flops 1 | bytes 1 | tf_op jit(solution)/shard_map/attend_inner/pallas_call | solution.py:214
  62.8 0.0 collective-permute-done.7.refs_0_
  62.8 0.0 collective-permute-done.8.refs_1_
  62.8 0.1 collective-permute-start.12
  62.9 3.0 %collective-permute-done.10.refs_2_ = bf16[8,16,512]{2,1,0:T(8,128)(2,1)S(1)} collective-permute-done((bf16[8,16,512]{2,1,0:T(8,128)(2,1)S(1)}, bf16[8,16,512]{2,1,0:T(8,128)(2,1)S(1)}, u32[]{:S(2)}, u32[]{:S(2)}) %collective-permute-start.10) | collective-permute-done | bytes 131104 | tf_op jit(solution)/shard_map/ppermute | solution.py:347
  65.9 0.1 collective-permute-start.11
  66.0 0.0 collective-permute-done.12.refs_3_.refs_9_
  66.1 2.5 %collective-permute-start.13 = (bf16[2,4,16,512]{3,2,1,0:T(8,128)(2,1)S(1)}, bf16[2,4,16,512]{3,2,1,0:T(8,128)(2,1)S(1)}, u32[]{:S(2)}, u32[]{:S(2)}) collective-permute-start(bf16[2,4,16,512]{3,2,1,0:T(8,128)(2,1)S(1)} %get-tuple-element.91), channel_id=1, source_target_pairs={{0,24},{4,28},{8,16},{12,20},{16,8},{20,12},{24,0},{28,4},{1,25},{... | collective-permute-start | bytes 393224 | tf_op jit(solution)/shard_map/ppermute | solution.py:347
  68.5 0.5 collective-permute-start.14
  69.0 1.5 %collective-permute-start.15 = (bf16[2,4,16,512]{3,2,1,0:T(8,128)(2,1)S(1)}, bf16[2,4,16,512]{3,2,1,0:T(8,128)(2,1)S(1)}, u32[]{:S(2)}, u32[]{:S(2)}) collective-permute-start(bf16[2,4,16,512]{3,2,1,0:T(8,128)(2,1)S(1)} %get-tuple-element.93), channel_id=1, source_target_pairs={{0,8},{4,12},{8,0},{12,4},{16,24},{20,28},{24,16},{28,20},{1,9},{5... | collective-permute-start | bytes 393224 | tf_op jit(solution)/shard_map/ppermute | solution.py:347
  70.5 0.0 collective-permute-done.11.refs_4_
  70.5 0.1 rim.1
  70.6 3.4 %collective-permute-start.16 = (bf16[8,4,512]{2,1,0:T(4,128)(2,1)S(1)}, bf16[8,4,512]{2,1,0:T(4,128)(2,1)S(1)}, u32[]{:S(2)}, u32[]{:S(2)}) collective-permute-start(bf16[8,4,512]{2,1,0:T(4,128)(2,1)S(1)} %get-tuple-element.95), channel_id=1, source_target_pairs={{0,1},{1,2},{2,3},{4,5},{5,6},{6,7},{8,9},{9,10},{10,11},{12,13},{... | collective-permute-start | bytes 98312 | tf_op jit(solution)/shard_map/ppermute | solution.py:430
  74.0 1.3 %collective-permute-start.17 = (bf16[8,4,512]{2,1,0:T(4,128)(2,1)S(1)}, bf16[8,4,512]{2,1,0:T(4,128)(2,1)S(1)}, u32[]{:S(2)}, u32[]{:S(2)}) collective-permute-start(bf16[8,4,512]{2,1,0:T(4,128)(2,1)S(1)} %get-tuple-element.96), channel_id=1, source_target_pairs={{1,0},{2,1},{3,2},{5,4},{6,5},{7,6},{9,8},{10,9},{11,10},{13,12},{... | collective-permute-start | bytes 98312 | tf_op jit(solution)/shard_map/ppermute | solution.py:431
  75.3 0.3 collective-permute-done.16.refs_10_
  75.6 4.2 %collective-permute-done.17.refs_11_ = bf16[8,4,512]{2,1,0:T(4,128)(2,1)S(1)} collective-permute-done((bf16[8,4,512]{2,1,0:T(4,128)(2,1)S(1)}, bf16[8,4,512]{2,1,0:T(4,128)(2,1)S(1)}, u32[]{:S(2)}, u32[]{:S(2)}) %collective-permute-start.17) | collective-permute-done | bytes 32800 | tf_op jit(solution)/shard_map/ppermute | solution.py:431
  79.9 0.0 collective-permute-done.13.refs_5_
  79.9 1.1 %collective-permute-done.14.refs_6_ = bf16[2,4,16,512]{3,2,1,0:T(8,128)(2,1)S(1)} collective-permute-done((bf16[2,4,16,512]{3,2,1,0:T(8,128)(2,1)S(1)}, bf16[2,4,16,512]{3,2,1,0:T(8,128)(2,1)S(1)}, u32[]{:S(2)}, u32[]{:S(2)}) %collective-permute-start.14) | collective-permute-done | bytes 131104 | tf_op jit(solution)/shard_map/ppermute | solution.py:347
  81.0 0.0 collective-permute-done.15.refs_7_
  81.0 0.0 copy-done.6
  81.0 2.4 %depth_filter.1 = bf16[4,8,32,512]{3,2,1,0:T(8,128)(2,1)} custom-call(bf16[8,16,512]{2,1,0:T(8,128)(2,1)S(1)} %collective-permute-done.7.refs_0_, bf16[8,16,512]{2,1,0:T(8,128)(2,1)S(1)} %collective-permute-done.8.refs_1_, bf16[8,16,512]{2,1,0:T(8,128)(2,1)S(1)} %collective-permute-done.10.refs_2_, bf16[8,16,512]{2,1,0:T(8,128)(2,1)S(1)} %get-tuple-element.86.refs_3_, ...), custom_call_target="tpu_custom_call" | custom-call | flops 1 | bytes 1 | tf_op jit(solution)/shard_map/depth_filter/pallas_call | solution.py:320
  (2 shorter events, 0.0 us)
Async XLA Ops:
  0.0 38.3 %copy-start.3 = (bf16[512,512]{1,0:T(8,128)(2,1)S(1)}, bf16[512,512]{1,0:T(8,128)(2,1)}, u32[]{:S(2)}) copy-start(bf16[512,512]{1,0:T(8,128)(2,1)} %refs_8_.3) | copy-start | bytes 1572868
  0.0 38.3 %copy-start.2 = (bf16[512,512]{1,0:T(8,128)(2,1)S(1)}, bf16[512,512]{1,0:T(8,128)(2,1)}, u32[]{:S(2)}) copy-start(bf16[512,512]{1,0:T(8,128)(2,1)} %refs_7_.5) | copy-start | bytes 1572868
  0.0 38.3 %copy-start.1 = (bf16[512,512]{1,0:T(8,128)(2,1)S(1)}, bf16[512,512]{1,0:T(8,128)(2,1)}, u32[]{:S(2)}) copy-start(bf16[512,512]{1,0:T(8,128)(2,1)} %refs_6_.5) | copy-start | bytes 1572868
  0.0 38.3 %copy-start = (bf16[3,512,512]{2,1,0:T(8,128)(2,1)S(1)}, bf16[3,512,512]{2,1,0:T(8,128)(2,1)}, u32[]{:S(2)}) copy-start(bf16[3,512,512]{2,1,0:T(8,128)(2,1)} %refs_10_.3) | copy-start | bytes 4718596
  0.0 38.3 %copy-start.4 = (bf16[512,512]{1,0:T(8,128)(2,1)S(1)}, bf16[512,512]{1,0:T(8,128)(2,1)}, u32[]{:S(2)}) copy-start(bf16[512,512]{1,0:T(8,128)(2,1)} %refs_9_.3) | copy-start | bytes 1572868
  0.0 1.7 %copy-start.5 = (bf16[8,8,32,512]{3,2,1,0:T(8,128)(2,1)S(1)}, bf16[8,8,32,512]{3,2,1,0:T(8,128)(2,1)}, u32[]{:S(2)}) copy-start(bf16[8,8,32,512]{3,2,1,0:T(8,128)(2,1)} %video.1) | copy-start | bytes 6291460
  1.8 36.5 %copy-start.7 = (f32[512]{0:T(512)S(1)}, f32[512]{0:T(512)}, u32[]{:S(2)}) copy-start(f32[512]{0:T(512)} %param.9) | copy-start | bytes 6148
  1.9 2.1 %collective-permute-start = (bf16[4,8,16,512]{3,2,1,0:T(8,128)(2,1)S(1)}, bf16[4,8,16,512]{3,2,1,0:T(8,128)(2,1)S(1)}, u32[]{:S(2)}, u32[]{:S(2)}) collective-permute-start(bf16[4,8,16,512]{3,2,1,0:T(8,128)(2,1)S(1)} %get-tuple-element.54), channel_id=1, source_target_pairs={{0,4},{4,0},{8,12},{12,8},{16,20},{20,16},{24,28},{28,24},{1,5},{5... | collective-permute-start | bytes 1572872 | tf_op jit(solution)/shard_map/ppermute | solution.py:347
  4.0 5.8 %collective-permute-start.2 = (bf16[4,8,16,512]{3,2,1,0:T(8,128)(2,1)S(1)}, bf16[4,8,16,512]{3,2,1,0:T(8,128)(2,1)S(1)}, u32[]{:S(2)}, u32[]{:S(2)}) collective-permute-start(bf16[4,8,16,512]{3,2,1,0:T(8,128)(2,1)S(1)} %get-tuple-element.63), channel_id=1, source_target_pairs={{0,4},{4,0},{8,12},{12,8},{16,20},{20,16},{24,28},{28,24},{1,5},{5... | collective-permute-start | bytes 1572872 | tf_op jit(solution)/shard_map/ppermute | solution.py:347
  4.5 12.0 %collective-permute-start.1 = (bf16[16,16,512]{2,1,0:T(8,128)(2,1)S(1)}, bf16[16,16,512]{2,1,0:T(8,128)(2,1)S(1)}, u32[]{:S(2)}, u32[]{:S(2)}) collective-permute-start(bf16[16,16,512]{2,1,0:T(8,128)(2,1)S(1)} %get-tuple-element.59), channel_id=1, source_target_pairs={{0,24},{4,28},{8,16},{12,20},{16,8},{20,12},{24,0},{28,4},{1,25},{... | collective-permute-start | bytes 786440 | tf_op jit(solution)/shard_map/ppermute | solution.py:347
  9.2 14.3 %collective-permute-start.3 = (bf16[16,16,512]{2,1,0:T(8,128)(2,1)S(1)}, bf16[16,16,512]{2,1,0:T(8,128)(2,1)S(1)}, u32[]{:S(2)}, u32[]{:S(2)}) collective-permute-start(bf16[16,16,512]{2,1,0:T(8,128)(2,1)S(1)} %get-tuple-element.68), channel_id=1, source_target_pairs={{0,8},{4,12},{8,0},{12,4},{16,24},{20,28},{24,16},{28,20},{1,9},{5... | collective-permute-start | bytes 786440 | tf_op jit(solution)/shard_map/ppermute | solution.py:347
  9.2 29.0 %collective-permute-start.4 = (bf16[16,16,512]{2,1,0:T(8,128)(2,1)S(1)}, bf16[16,16,512]{2,1,0:T(8,128)(2,1)S(1)}, u32[]{:S(2)}, u32[]{:S(2)}) collective-permute-start(bf16[16,16,512]{2,1,0:T(8,128)(2,1)S(1)} %get-tuple-element.69), channel_id=1, source_target_pairs={{0,16},{4,20},{8,24},{12,28},{16,0},{20,4},{24,8},{28,12},{1,17},{... | collective-permute-start | bytes 786440 | tf_op jit(solution)/shard_map/ppermute | solution.py:347
  16.4 27.8 %collective-permute-start.5 = (bf16[16,16,512]{2,1,0:T(8,128)(2,1)S(1)}, bf16[16,16,512]{2,1,0:T(8,128)(2,1)S(1)}, u32[]{:S(2)}, u32[]{:S(2)}) collective-permute-start(bf16[16,16,512]{2,1,0:T(8,128)(2,1)S(1)} %get-tuple-element.73), channel_id=1, source_target_pairs={{0,24},{4,28},{8,16},{12,20},{16,8},{20,12},{24,0},{28,4},{1,25},{... | collective-permute-start | bytes 786440 | tf_op jit(solution)/shard_map/ppermute | solution.py:347
  20.2 24.1 %collective-permute-start.6 = (bf16[16,16,512]{2,1,0:T(8,128)(2,1)S(1)}, bf16[16,16,512]{2,1,0:T(8,128)(2,1)S(1)}, u32[]{:S(2)}, u32[]{:S(2)}) collective-permute-start(bf16[16,16,512]{2,1,0:T(8,128)(2,1)S(1)} %get-tuple-element.74), channel_id=1, source_target_pairs={{0,8},{4,12},{8,0},{12,4},{16,24},{20,28},{24,16},{28,20},{1,9},{5... | collective-permute-start | bytes 786440 | tf_op jit(solution)/shard_map/ppermute | solution.py:347
  23.5 34.5 %collective-permute-start.9 = (bf16[16,16,512]{2,1,0:T(8,128)(2,1)S(1)}, bf16[16,16,512]{2,1,0:T(8,128)(2,1)S(1)}, u32[]{:S(2)}, u32[]{:S(2)}) collective-permute-start(bf16[16,16,512]{2,1,0:T(8,128)(2,1)S(1)} %get-tuple-element.79), channel_id=1, source_target_pairs={{0,16},{4,20},{8,24},{12,28},{16,0},{20,4},{24,8},{28,12},{1,17},{... | collective-permute-start | bytes 786440 | tf_op jit(solution)/shard_map/ppermute | solution.py:347
  45.8 17.0 %collective-permute-start.7 = (bf16[8,16,512]{2,1,0:T(8,128)(2,1)S(1)}, bf16[8,16,512]{2,1,0:T(8,128)(2,1)S(1)}, u32[]{:S(2)}, u32[]{:S(2)}) collective-permute-start(bf16[8,16,512]{2,1,0:T(8,128)(2,1)S(1)} %get-tuple-element.76), channel_id=1, source_target_pairs={{0,24},{4,28},{8,16},{12,20},{16,8},{20,12},{24,0},{28,4},{1,25},{... | collective-permute-start | bytes 393224 | tf_op jit(solution)/shard_map/ppermute | solution.py:347
  48.3 14.5 %collective-permute-start.8 = (bf16[8,16,512]{2,1,0:T(8,128)(2,1)S(1)}, bf16[8,16,512]{2,1,0:T(8,128)(2,1)S(1)}, u32[]{:S(2)}, u32[]{:S(2)}) collective-permute-start(bf16[8,16,512]{2,1,0:T(8,128)(2,1)S(1)} %get-tuple-element.77), channel_id=1, source_target_pairs={{0,8},{4,12},{8,0},{12,4},{16,24},{20,28},{24,16},{28,20},{1,9},{5... | collective-permute-start | bytes 393224 | tf_op jit(solution)/shard_map/ppermute | solution.py:347
  58.0 23.0 %copy-start.6 = (f32[3,3,512]{2,1,0:T(4,128)S(1)}, f32[3,3,512]{2,1,0:T(4,128)}, u32[]{:S(2)}) copy-start(f32[3,3,512]{2,1,0:T(4,128)} %refs_12_.1) | copy-start | bytes 55300
  58.0 7.9 %collective-permute-start.10 = (bf16[8,16,512]{2,1,0:T(8,128)(2,1)S(1)}, bf16[8,16,512]{2,1,0:T(8,128)(2,1)S(1)}, u32[]{:S(2)}, u32[]{:S(2)}) collective-permute-start(bf16[8,16,512]{2,1,0:T(8,128)(2,1)S(1)} %get-tuple-element.85), channel_id=1, source_target_pairs={{0,16},{4,20},{8,24},{12,28},{16,0},{20,4},{24,8},{28,12},{1,17},{... | collective-permute-start | bytes 393224 | tf_op jit(solution)/shard_map/ppermute | solution.py:347
  62.8 3.2 %collective-permute-start.12 = (bf16[4,4,16,512]{3,2,1,0:T(8,128)(2,1)S(1)}, bf16[4,4,16,512]{3,2,1,0:T(8,128)(2,1)S(1)}, u32[]{:S(2)}, u32[]{:S(2)}) collective-permute-start(bf16[4,4,16,512]{3,2,1,0:T(8,128)(2,1)S(1)} %get-tuple-element.90), channel_id=1, source_target_pairs={{0,4},{4,0},{8,12},{12,8},{16,20},{20,16},{24,28},{28,24},{1,5},{5... | collective-permute-start | bytes 786440 | tf_op jit(solution)/shard_map/ppermute | solution.py:347
  65.9 4.6 %collective-permute-start.11 = (bf16[4,4,16,512]{3,2,1,0:T(8,128)(2,1)S(1)}, bf16[4,4,16,512]{3,2,1,0:T(8,128)(2,1)S(1)}, u32[]{:S(2)}, u32[]{:S(2)}) collective-permute-start(bf16[4,4,16,512]{3,2,1,0:T(8,128)(2,1)S(1)} %stack_back.1), channel_id=1, source_target_pairs={{0,4},{4,0},{8,12},{12,8},{16,20},{20,16},{24,28},{28,24},{1,5},{5... | collective-permute-start | bytes 786440 | tf_op jit(solution)/shard_map/ppermute | solution.py:347
  66.1 13.8 %collective-permute-start.13 = (bf16[2,4,16,512]{3,2,1,0:T(8,128)(2,1)S(1)}, bf16[2,4,16,512]{3,2,1,0:T(8,128)(2,1)S(1)}, u32[]{:S(2)}, u32[]{:S(2)}) collective-permute-start(bf16[2,4,16,512]{3,2,1,0:T(8,128)(2,1)S(1)} %get-tuple-element.91), channel_id=1, source_target_pairs={{0,24},{4,28},{8,16},{12,20},{16,8},{20,12},{24,0},{28,4},{1,25},{... | collective-permute-start | bytes 393224 | tf_op jit(solution)/shard_map/ppermute | solution.py:347
  68.5 12.4 %collective-permute-start.14 = (bf16[2,4,16,512]{3,2,1,0:T(8,128)(2,1)S(1)}, bf16[2,4,16,512]{3,2,1,0:T(8,128)(2,1)S(1)}, u32[]{:S(2)}, u32[]{:S(2)}) collective-permute-start(bf16[2,4,16,512]{3,2,1,0:T(8,128)(2,1)S(1)} %get-tuple-element.92), channel_id=1, source_target_pairs={{0,16},{4,20},{8,24},{12,28},{16,0},{20,4},{24,8},{28,12},{1,17},{... | collective-permute-start | bytes 393224 | tf_op jit(solution)/shard_map/ppermute | solution.py:347
  69.0 11.9 %collective-permute-start.15 = (bf16[2,4,16,512]{3,2,1,0:T(8,128)(2,1)S(1)}, bf16[2,4,16,512]{3,2,1,0:T(8,128)(2,1)S(1)}, u32[]{:S(2)}, u32[]{:S(2)}) collective-permute-start(bf16[2,4,16,512]{3,2,1,0:T(8,128)(2,1)S(1)} %get-tuple-element.93), channel_id=1, source_target_pairs={{0,8},{4,12},{8,0},{12,4},{16,24},{20,28},{24,16},{28,20},{1,9},{5... | collective-permute-start | bytes 393224 | tf_op jit(solution)/shard_map/ppermute | solution.py:347
  70.6 5.0 %collective-permute-start.16 = (bf16[8,4,512]{2,1,0:T(4,128)(2,1)S(1)}, bf16[8,4,512]{2,1,0:T(4,128)(2,1)S(1)}, u32[]{:S(2)}, u32[]{:S(2)}) collective-permute-start(bf16[8,4,512]{2,1,0:T(4,128)(2,1)S(1)} %get-tuple-element.95), channel_id=1, source_target_pairs={{0,1},{1,2},{2,3},{4,5},{5,6},{6,7},{8,9},{9,10},{10,11},{12,13},{... | collective-permute-start | bytes 98312 | tf_op jit(solution)/shard_map/ppermute | solution.py:430
  74.0 5.8 %collective-permute-start.17 = (bf16[8,4,512]{2,1,0:T(4,128)(2,1)S(1)}, bf16[8,4,512]{2,1,0:T(4,128)(2,1)S(1)}, u32[]{:S(2)}, u32[]{:S(2)}) collective-permute-start(bf16[8,4,512]{2,1,0:T(4,128)(2,1)S(1)} %get-tuple-element.96), channel_id=1, source_target_pairs={{1,0},{2,1},{3,2},{5,4},{6,5},{7,6},{9,8},{10,9},{11,10},{13,12},{... | collective-permute-start | bytes 98312 | tf_op jit(solution)/shard_map/ppermute | solution.py:431
